TPU v7x, 512 devices: a whole 4x4x16 slice. The times are simulated.
512 devices in a mesh: sample: 8 (over y, z_hi), space: 64 (over z_lo, x, core).
Axes of the slice: x: 4, y: 4, z: 16 (z_hi: 2, z_lo: 8; z = z_hi * 8 + z_lo), core: 2. Of those that a mesh axis runs over, the one named last changes fastest.
Arguments:
- activations: bfloat16 [8, 64, 16, 16, 128], P('sample', 'space'), may hold values from -6 to 6
- conv_weight: bfloat16 [3456, 256], replicated, may hold values from -0.109375 to 0.109375
- conv_bias: float32 [256], replicated, may hold values from -3 to 3
- cotangent: bfloat16 [8, 64, 16, 16, 256], P('sample', 'space'), may hold values from -6 to 6
- basis_panels: bfloat16 [8, 432, 3456], P('sample', None, 'space'), may hold values from -0.109375 to 0.109375
- panel_owner: int32 [8], replicated, may hold values from 0 to 7, each once
- output_basis: float32 [256, 256], replicated, may hold values from -0.375 to 0.375
- input_eigen: float32 [3456], P('space'), may hold values from 0.001 to 1
- output_eigen: float32 [256], replicated, may hold values from 0.001 to 1
Outputs:
- data_grad: bfloat16 [8, 64, 16, 16, 128], P('sample', 'space')
- update: float32 [3456, 256], P('space')
Inputs may be any that keep to these rules, and one draw needn't show every extreme that they name: Every sample index stores exactly one row panel: panel j of the basis sits in slot panel_owner[j].
All inputs are finite; a program needn't handle non-finite values.
Results may differ from a plain program's by a relative error of at most 0.0055.
Values may be sent and summed in bfloat16 or wider, within the bound.
No kernel may reach another device: no remote copies, remote signals or barrier semaphores. Data moves between devices by JAX's collectives and lax.ppermute only.
A program may use at most 64 MiB of HBM per device.

v0:
```python
import jax
import jax.numpy as jnp
from jax import lax
from jax.sharding import PartitionSpec as P

DAMPING = 0.001


def extended(block, sides, width):
    for axis, dim in sides:
        count = lax.axis_size(axis)
        forward = [(i, i + 1) for i in range(count - 1)]
        backward = [(target, source) for source, target in forward]
        low = lax.ppermute(
            lax.slice_in_dim(block, block.shape[dim] - width, None, axis=dim), axis, forward
        )
        high = lax.ppermute(lax.slice_in_dim(block, 0, width, axis=dim), axis, backward)
        block = jnp.concatenate([low, block, high], axis=dim)
    return block


def spread(shard, axis, root):
    mine = lax.axis_index(axis) == root
    return lax.psum(jnp.where(mine, shard, jnp.zeros_like(shard)), axis)


def tap_matrix(padded, flipped):
    planes = padded.shape[0] - 2
    height = padded.shape[1] - 2
    breadth = padded.shape[2] - 2
    pieces = []
    for z_step in range(3):
        for y_step in range(3):
            for x_step in range(3):
                z_from = 2 - z_step if flipped else z_step
                y_from = 2 - y_step if flipped else y_step
                x_from = 2 - x_step if flipped else x_step
                pieces.append(
                    padded[
                        z_from : z_from + planes,
                        y_from : y_from + height,
                        x_from : x_from + breadth,
                        :,
                    ]
                )
    stacked = jnp.concatenate(pieces, axis=-1)
    return stacked.reshape(planes * height * breadth, stacked.shape[-1])


def pad_plane(volume):
    return jnp.pad(volume, ((0, 0), (1, 1), (1, 1), (0, 0)))


def delta_of(pre_act, cot_rows):
    logistic = jax.nn.sigmoid(pre_act)
    return (cot_rows.astype(jnp.float32) * logistic * (1.0 + pre_act * (1.0 - logistic))).astype(
        jnp.bfloat16
    )


def per_device(
    activations,
    conv_weight,
    conv_bias,
    cotangent,
    basis_panels,
    panel_owner,
    output_basis,
    input_eigen,
    output_eigen,
):
    in_width = activations.shape[-1]
    out_width = conv_weight.shape[1]
    volume = activations[0]
    dims = volume.shape
    rimmed = extended(volume, (("space", 0),), 1)
    patches = tap_matrix(pad_plane(rimmed), False)
    pre_act = jnp.dot(patches, conv_weight, preferred_element_type=jnp.float32) + conv_bias
    delta = delta_of(pre_act, cotangent[0].reshape(-1, out_width))
    grad_part = lax.dot_general(
        patches, delta, (((0,), (0,)), ((), ())), preferred_element_type=jnp.float32
    )
    cells = (
        patches.shape[0] * activations.shape[0] * lax.axis_size("sample") * lax.axis_size("space")
    )
    weight_grad = lax.psum(grad_part, ("sample", "space")) / cells
    weight_back = (
        conv_weight.reshape(27, in_width, out_width)
        .transpose(0, 2, 1)
        .reshape(27 * out_width, in_width)
    )
    delta_rimmed = extended(delta.reshape(dims[0], dims[1], dims[2], out_width), (("space", 0),), 1)
    back = tap_matrix(pad_plane(delta_rimmed), True)
    data = jnp.dot(back, weight_back, preferred_element_type=jnp.float32).astype(jnp.bfloat16)
    data_grad = data.reshape(dims)[None]
    stored = basis_panels[0]
    received = []
    for panel_index in range(lax.axis_size("sample")):
        received.append(spread(stored, "sample", panel_owner[panel_index]))
    column_block = jnp.concatenate(received, axis=0)
    highest = lax.Precision.HIGHEST
    block_float = column_block.astype(jnp.float32)
    rotated = lax.dot_general(block_float, weight_grad, (((0,), (0,)), ((), ())), precision=highest)
    rotated = jnp.dot(rotated, output_basis, precision=highest)
    scaled = rotated / (input_eigen[:, None] * output_eigen[None, :] + DAMPING)
    turned = jnp.dot(scaled, output_basis.T, precision=highest)
    update = lax.psum_scatter(
        jnp.dot(block_float, turned, precision=highest), "space", scatter_dimension=0, tiled=True
    )
    return (data_grad, update)


def solution(mesh):
    return jax.shard_map(
        per_device,
        mesh=mesh,
        in_specs=(
            P("sample", "space", None, None, None),
            P(),
            P(),
            P("sample", "space", None, None, None),
            P("sample", None, "space"),
            P(),
            P(),
            P("space"),
            P(),
        ),
        out_specs=(P("sample", "space", None, None, None), P("space", None)),
        check_vma=False,
    )
```

profile of v0, /device:TPU:1, one launch (start us, length us, event | category | flops | bytes accessed | tf_op | source)
XLA Modules:
  0.0 960.4 jit_solution(1489800768144665098)
XLA Ops:
  7.2 4.6 collective-permute-start
  11.9 5.6 collective-permute-start.1
  17.5 1.6 fusion.23
  24.1 1.6 select_bitcast_fusion
  25.8 2.8 copy.12
  28.6 1.3 dynamic-slice.4
  31.8 0.8 copy-done.1
  33.2 1.9 collective-permute-start.2
  35.2 2.4 collective-permute-start.3
  37.6 2.5 fusion.24
  40.1 1.4 collective-permute-done.3
  42.8 0.7 constant_dynamic-update-slice_fusion.52
  43.5 0.7 constant_dynamic-update-slice_fusion.51
  45.6 0.7 constant_dynamic-update-slice_fusion.48
  46.3 0.7 constant_dynamic-update-slice_fusion.47
  49.1 0.7 constant_dynamic-update-slice_fusion.43
  50.4 0.7 constant_dynamic-update-slice_fusion.41
  51.8 0.7 constant_dynamic-update-slice_fusion.39
  53.2 0.7 constant_dynamic-update-slice_fusion.37
  54.6 0.7 constant_dynamic-update-slice_fusion.35
  60.0 0.7 constant_dynamic-update-slice_fusion.27
  60.7 153.4 %all-reduce.10.cloned.1.call-done = (bf16[432,54]{0,1:T(8,128)(2,1)}, bf16[432,54]{0,1:T(8,128)(2,1)}, bf16[432,54]{0,1:T(8,128)(2,1)}, bf16[432,54]{0,1:T(8,128...) async-done(((bf16[432,54]{0,1:T(8,128)(2,1)}, bf16[432,54]{0,1:T(8,128)(2,1)}, ...) | async-done | bytes 373264 | tf_op jit(solution)/shard_map/psum | solution.py:24
  214.1 1.3 concatenate.180
  215.5 485.2 %all-reduce.8.cloned.1.call-done = f32[3456,256]{1,0:T(8,128)} async-done(((f32[3456,256]{1,0:T(8,128)}), f32[3456,256]{1,0:T(8,128)}) %all-reduce.8.cloned.1.call-update) | async-done | bytes 3538960 | tf_op jit(solution)/shard_map/psum | solution.py:86
  700.6 3.4 fusion.1
  704.6 3.4 fusion.26
  708.0 232.6 %fusion = f32[56,256]{1,0:T(8,128)S(1)} fusion(f32[3456,256]{1,0:T(8,128)} %fusion.26), kind=kCustom, calls=%all-reduce-scatter | all-reduce-scatter fusion | flops 917505 | bytes 3598336
  940.6 1.9 collective-permute-start.4
  942.5 1.3 collective-permute-start.5
  943.8 1.3 collective-permute-start.6
  945.1 3.7 convolution_convert_fusion
  948.8 3.6 collective-permute-done.4
  (78 shorter events, 15.6 us)
Async XLA Ops:
  7.2 696.8 %copy-start = (f32[256,256]{1,0:T(8,128)S(1)}, f32[256,256]{1,0:T(8,128)}, u32[]{:S(2)}) copy-start(f32[256,256]{1,0:T(8,128)} %param.15) | copy-start | bytes 786436
  7.2 207.0 %all-reduce.10.cloned.1.call-start = ((), (), s32[]{:S(2)}) async-start(), calls=%async_computation.1 | async-start | bytes 917504 | tf_op jit(solution)/shard_map/psum | solution.py:24
  7.2 23.4 %collective-permute-start = (bf16[1,16,16,128]{3,2,1,0:T(8,128)(2,1)}, bf16[1,16,16,128]{3,2,1,0:T(8,128)(2,1)S(1)}, u32[]{:S(2)}, u32[]{:S(2)}) collective-permute-start(bf16[1,16,16,128]{3,2,1,0:T(8,128)(2,1)} %bitcast.157), channel_id=1, source_target_pairs={{0,1},{1,2},{2,3},{3,4},{4,5},{5,6},{6,7},{7,8},{8,9},{9,10},{10,1... | collective-permute-start | bytes 196616 | tf_op jit(solution)/shard_map/ppermute | solution.py:14
  11.9 18.8 %collective-permute-start.1 = (bf16[1,16,16,128]{3,2,1,0:T(8,128)(2,1)}, bf16[1,16,16,128]{3,2,1,0:T(8,128)(2,1)S(1)}, u32[]{:S(2)}, u32[]{:S(2)}) collective-permute-start(bf16[1,16,16,128]{3,2,1,0:T(8,128)(2,1)} %bitcast.158), channel_id=1, source_target_pairs={{1,0},{2,1},{3,2},{4,3},{5,4},{6,5},{7,6},{8,7},{9,8},{10,9},{11,1... | collective-permute-start | bytes 196616 | tf_op jit(solution)/shard_map/ppermute | solution.py:17
  25.7 674.9 %all-reduce.8.cloned.1.call-start = ((), (), s32[]{:S(2)}) async-start(), calls=%async_computation | async-start | bytes 7077888 | tf_op jit(solution)/shard_map/psum | solution.py:86
  25.8 4.9 copy-start.2
  31.1 1.5 copy-start.1
  31.1 1.5 copy-start.5
  31.1 1.5 copy-start.6
  33.2 6.8 collective-permute-start.2
  35.2 6.3 collective-permute-start.3
  215.4 488.6 %copy-start.3 = (f32[256]{0:T(256)S(1)}, f32[256]{0:T(256)}, u32[]{:S(2)}) copy-start(f32[256]{0:T(256)} %param.17) | copy-start | bytes 3076
  215.4 488.6 %copy-start.4 = (f32[54]{0:T(128)S(1)}, f32[54]{0:T(128)}, u32[]{:S(2)}) copy-start(f32[54]{0:T(128)} %param.16) | copy-start | bytes 652
  940.6 11.9 %collective-permute-start.4 = (f32[56,256]{1,0:T(8,128)S(1)}, f32[56,256]{1,0:T(8,128)S(1)}, u32[]{:S(2)}, u32[]{:S(2)}) collective-permute-start(f32[56,256]{1,0:T(8,128)S(1)} %fusion), channel_id=1, source_target_pairs={{0,1},{1,2},{2,3},{3,4},{4,5},{5,6},{6,7},{7,8},{8,9},{9,10},{10,1... | collective-permute-start | bytes 172040
  942.5 9.9 %collective-permute-start.5 = (f32[56,256]{1,0:T(8,128)S(1)}, f32[56,256]{1,0:T(8,128)S(1)}, u32[]{:S(2)}, u32[]{:S(2)}) collective-permute-start(f32[56,256]{1,0:T(8,128)S(1)} %fusion), channel_id=1, source_target_pairs={{0,2},{1,3},{2,4},{3,5},{4,6},{5,7},{6,8},{7,9},{8,10},{9,11},{10,... | collective-permute-start | bytes 172040
  943.8 5.0 collective-permute-start.6
Sparse Core Ops, SparseCore 0:
  25.9 188.2 all-reduce.9
  220.4 480.1 all-reduce.7
where the time goes:
time: 964 us; the launch traced here: 960 us
  waiting for transfers between devices  644 us (67%)
  blocking collectives  233 us (24%)
  local copies, waits for them, and re-layouts  28.7 us (3%)
  between operations  20.3 us (2%)
  starting transfers between devices  19.1 us (2%)
  matrix products  14.2 us (1%)
    psum x1, waiting for transfers between devices, per_device(): weight_grad = lax.psum(grad_part, ('sample', 'space')) / cells  485 us
    unnamed x1, blocking collectives  233 us
    psum x1, waiting for transfers between devices, spread(): return lax.psum(jnp.where(mine, shard, jnp.zeros_like(shard)), axis)  153 us
    unnamed x70, local copies, waits for them, and re-layouts  21.6 us
  transfers between devices with their start and end apart: 9, of which 4 were waited for; matrix products, arithmetic and copies ran while one was open for 4% of the time, Pallas kernels for 0%

commit v1 on v0

v1 whole, which is shorter than its diff:
```python
import functools

import jax
import jax.numpy as jnp
from jax import lax
from jax.experimental import pallas as pl
from jax.experimental.pallas import tpu as pltpu
from jax.sharding import Mesh
from jax.sharding import PartitionSpec as P

DAMPING = 0.001
CELLS = 131072
BF16 = jnp.bfloat16
F32 = jnp.float32
VMEM = pl.BlockSpec(memory_space=pltpu.VMEM)
SMEM = pl.BlockSpec(memory_space=pltpu.SMEM)
LIMIT = 48 * 1024 * 1024
YS = ("y", "zh")
ZS = ("zh", "zl")
XC = ("x", "c")
YXC = ("y", "x", "c")
SPACE = ("zl", "x", "c")


def call(body, out_shape, inputs, scratch=(), smem=0, flops=0):
    specs = [SMEM] * smem + [VMEM] * (len(inputs) - smem)
    many = isinstance(out_shape, (list, tuple))
    return pl.pallas_call(
        body,
        out_shape=out_shape,
        in_specs=specs,
        out_specs=[VMEM] * len(out_shape) if many else VMEM,
        scratch_shapes=list(scratch),
        compiler_params=pltpu.CompilerParams(vmem_limit_bytes=LIMIT),
        cost_estimate=pl.CostEstimate(
            flops=flops,
            bytes_accessed=sum(a.size * a.dtype.itemsize for a in inputs),
            transcendentals=0,
        ),
    )(*inputs)


def shape(dims, dtype):
    return jax.ShapeDtypeStruct(dims, dtype)


def iota(dims, axis):
    return lax.broadcasted_iota(jnp.int32, dims, axis)


def exchange(x, axes):
    return lax.all_to_all(x, axes, 0, 0)


def contract0(a, b):
    return lax.dot_general(a, b, (((0,), (0,)), ((), ())), preferred_element_type=F32)


def x_shifted(rows, step):
    if step == 0:
        return rows
    x = iota(rows.shape, 0) & 15
    inside = (x + step >= 0) & (x + step < 16)
    return jnp.where(inside, pltpu.roll(rows, (-step) % 256, 0), 0.0)


def basis_body(panel_ref, eigen_ref, out_ref):
    panel = panel_ref[...]
    eigen = eigen_ref[...]
    first = eigen.astype(BF16).astype(F32)
    second = (eigen - first).astype(BF16).astype(F32)
    third = eigen - first - second
    for pair in range(4):
        row = iota((432, 128), 0)
        lane = iota((432, 128), 1)
        pick = ((row & 7) == 2 * pair + (lane >> 6)) & ((row >> 3) == (lane & 63))
        block = contract0(panel, jnp.where(pick, 1.0, 0.0).astype(BF16))
        block = jnp.concatenate([block, jnp.zeros((10, 128), F32)], axis=0)
        if pair == 0:
            at = iota((64, 128), 1)
            block = jnp.where(at == 54, first, block)
            block = jnp.where(at == 55, second, block)
            block = jnp.where(at == 56, third, block)
        out_ref[pair] = block.astype(BF16)


def forward_body(place_ref, low_ref, mine_ref, high_ref, weight_ref, bias_ref, cot_ref, delta_ref, send_ref, patches):
    planes = (low_ref[...], mine_ref[...], high_ref[...])
    none = jnp.zeros((16, 128), BF16)
    for a in range(3):
        wide = planes[a].astype(F32)
        for c in range(3):
            moved = x_shifted(wide, c - 1).astype(BF16)
            for b in range(3):
                at = (9 * a + 3 * b + c) * 128
                if b == 0:
                    shifted = jnp.concatenate([none, moved[:240]], axis=0)
                elif b == 2:
                    shifted = jnp.concatenate([moved[16:], none], axis=0)
                else:
                    shifted = moved
                patches[:, at : at + 128] = shifted
    pre = jnp.dot(patches[...], weight_ref[...], preferred_element_type=F32) + bias_ref[...]
    logistic = 1.0 / (1.0 + jnp.exp(-pre))
    delta = (cot_ref[...].astype(F32) * logistic * (1.0 + pre * (1.0 - logistic))).astype(BF16)
    delta_ref[...] = delta
    rim = jnp.where(place_ref[0] < 4, planes[0].astype(F32), planes[2].astype(F32))
    act_t = planes[1].astype(F32).T.astype(BF16)
    rim_t = rim.T.astype(BF16)
    for x in range(4):
        for c in range(2):
            to = 2 * x + c
            for half in range(2):
                lanes = slice(128 * half, 128 * half + 128)
                rows = slice(32 * x, 32 * x + 32)
                send_ref[to, 32 * half : 32 * half + 32] = act_t[rows, lanes]
                send_ref[to, 64 + 32 * half : 96 + 32 * half] = rim_t[rows, lanes]
            send_ref[to, 128:] = delta[:, 128 * c : 128 * c + 128]


def weight_grad_body(got_ref, out_ref, moved, deltas):
    pieces = []
    for plane, at in [(0, 64)] + [(e, 0) for e in range(8)] + [(7, 64)]:
        pieces.append(got_ref[plane, at : at + 32].astype(F32))
        pieces.append(got_ref[plane, at + 32 : at + 64].astype(F32))
    acts = jnp.concatenate(pieces, axis=1)
    lane = iota((32, 2560), 1)
    x = lane & 15
    y = (lane >> 4) & 15
    for b in range(3):
        for c in range(3):
            step = 16 * (b - 1) + (c - 1)
            turned = pltpu.roll(acts, (-step) % 2560, 1) if step else acts
            inside = (x + c >= 1) & (x + c < 17) & (y + b >= 1) & (y + b < 17)
            moved[32 * (3 * b + c) : 32 * (3 * b + c) + 32, :] = jnp.where(inside, turned, 0.0).astype(BF16)
    for e in range(8):
        deltas[256 * e : 256 * e + 256, :] = got_ref[e, 128:]
    rows = [
        jnp.dot(moved[:, 256 * a : 256 * a + 2048], deltas[...], preferred_element_type=F32) for a in range(3)
    ]
    whole = jnp.concatenate(rows, axis=0).reshape(27, 4, 8, 128)
    for to in range(4):
        part = jnp.concatenate([whole[:, to].reshape(216, 128), jnp.zeros((8, 128), F32)], axis=0)
        out_ref[to] = part.astype(BF16)


def over_y_body(got_ref, out_ref, total):
    total[...] = sum(got_ref[i].astype(F32) for i in range(4)) * (1.0 / CELLS)
    for r in range(8):
        rows = total[pl.ds(r, 28, stride=8), :]
        rows = jnp.concatenate([rows, jnp.zeros((4, 128), F32)], axis=0).astype(BF16)
        out_ref[r] = rows
        out_ref[8 + r] = rows


def over_z_body(got_ref, out_ref):
    total = sum(got_ref[i].astype(F32) for i in range(16)).astype(BF16)
    for to in range(32):
        out_ref[to] = total


def rotate_body(owner_ref, place_ref, got_ref, basis_ref, out_ref):
    zh, zl = place_ref[0], place_ref[1]
    groups = [
        jnp.concatenate([got_ref[2 * g], got_ref[2 * g + 1]], axis=1) for g in range(16)
    ]
    grads = jnp.concatenate(groups, axis=0)
    row = iota((512, 512), 0)
    h = 54 * (row >> 6) + (row & 63)
    source = (4 * (h & 3) + ((h >> 2) & 3)) * 32 + (h >> 4)
    pick = ((row & 63) < 54) & (source == iota((512, 512), 1))
    ordered = jnp.dot(jnp.where(pick, 1.0, 0.0).astype(BF16), grads, preferred_element_type=F32).astype(BF16)
    half = (iota((64, 128), 1) >> 6) == (zl & 1)
    total = jnp.zeros((64, 256), F32)
    for j in range(8):
        block = basis_ref[8 * zh + owner_ref[j], zl >> 1]
        block = jnp.where(half, block.astype(F32), 0.0).astype(BF16)
        rows = ordered[64 * j : 64 * j + 64]
        total = total + jnp.dot(block, jnp.concatenate([rows, rows], axis=0), preferred_element_type=F32)
    total = jnp.concatenate([total[:56, :128], total[:56, 128:]], axis=0).astype(BF16)
    for to in range(16):
        out_ref[to] = total


def update_body(owner_ref, place_ref, got_ref, basis_ref, out_basis_ref, out_eigen_ref, out_ref):
    zl = place_ref[1]
    slot = owner_ref[zl]
    highest = lax.Precision.HIGHEST
    whole = jnp.zeros((512, 256), F32)
    for zh in range(2):
        total = sum(got_ref[8 * zh + i].astype(F32) for i in range(8))
        rotated = jnp.concatenate([total[:56], total[56:]], axis=1)
        rotated = jnp.concatenate([rotated, jnp.zeros((8, 256), F32)], axis=0)
        rotated = jnp.dot(rotated, out_basis_ref[...], precision=highest, preferred_element_type=F32)
        terms = basis_ref[8 * zh, 0].astype(F32)
        eigen = (terms[:, 54:55] + terms[:, 55:56]) + terms[:, 56:57]
        scaled = rotated / (eigen * out_eigen_ref[...] + DAMPING)
        scaled = jnp.where(iota((64, 256), 0) < 54, scaled, 0.0)
        turned = lax.dot_general(
            scaled, out_basis_ref[...], (((1,), (1,)), ((), ())), precision=highest, preferred_element_type=F32
        )
        high = turned.astype(BF16)
        rest = (turned - high.astype(F32)).astype(BF16)
        parts = []
        for pair in range(4):
            block = basis_ref[8 * zh + slot, pair]
            parts.append(contract0(block, high) + contract0(block, rest))
        whole = whole + jnp.concatenate(parts, axis=0)
    row = iota((512, 512), 0)
    t = 54 * (row >> 6) + (row & 63)
    source = 64 * (t & 7) + (t >> 3)
    pick = ((row & 63) < 54) & (source == iota((512, 512), 1))
    ordered = jnp.dot(jnp.where(pick, 1.0, 0.0).astype(BF16), whole.astype(BF16), preferred_element_type=F32)
    out_ref[...] = ordered.astype(BF16).reshape(8, 64, 256)


def over_xc_body(got_ref, out_ref):
    total = sum(got_ref[i].astype(F32) for i in range(8))[:56]
    for to in range(4):
        out_ref[to] = total


def last_body(got_ref, out_ref):
    out_ref[...] = ((got_ref[0] + got_ref[1]) + (got_ref[2] + got_ref[3]))[:54]


def data_grad_body(low_ref, mine_ref, high_ref, weight_ref, out_ref, back):
    none = jnp.zeros((16, 256), BF16)
    total = jnp.zeros((256, 128), F32)
    for a in range(3):
        wide = (high_ref, mine_ref, low_ref)[a][...].astype(F32)
        for c in range(3):
            moved = x_shifted(wide, 1 - c).astype(BF16)
            for b in range(3):
                if b == 2:
                    shifted = jnp.concatenate([none, moved[:240]], axis=0)
                elif b == 0:
                    shifted = jnp.concatenate([moved[16:], none], axis=0)
                else:
                    shifted = moved
                tap = 9 * a + 3 * b + c
                total = total + lax.dot_general(
                    shifted,
                    weight_ref[128 * tap : 128 * tap + 128, :],
                    (((1,), (1,)), ((), ())),
                    preferred_element_type=F32,
                )
    out_ref[...] = total.astype(BF16)


def neighbours(block):
    count = 64
    up = [(i, i + 1) for i in range(count - 1)]
    down = [(i + 1, i) for i in range(count - 1)]
    return lax.ppermute(block, SPACE, up), lax.ppermute(block, SPACE, down)


def per_device(
    activations,
    conv_weight,
    conv_bias,
    cotangent,
    basis_panels,
    panel_owner,
    output_basis,
    input_eigen,
    output_eigen,
):
    place = jnp.stack([lax.axis_index("zh"), lax.axis_index("zl")]).astype(jnp.int32)
    inner = lax.axis_index(XC).astype(jnp.int32).reshape(1)
    plane = activations.reshape(256, 128)
    low, high = neighbours(plane)

    eigen = jnp.pad(input_eigen, (0, 10), constant_values=1.0).reshape(64, 1)
    stored = call(basis_body, shape((4, 64, 128), BF16), (basis_panels[0], eigen))
    turn = [(8 * a + b, 8 * b + a) for a in range(8) for b in range(8)]
    stored = lax.ppermute(stored, ("y", "zh", "zl"), turn)
    basis = lax.all_gather(stored, ZS)

    delta, send = call(
        forward_body,
        [shape((256, 256), BF16), shape((8, 384, 128), BF16)],
        (inner, low, plane, high, conv_weight, conv_bias.reshape(1, 256), cotangent.reshape(256, 256)),
        [pltpu.VMEM((256, 3456), BF16)],
        smem=1,
        flops=2 * 256 * 3456 * 256,
    )
    delta_low, delta_high = neighbours(delta)
    got = exchange(send, XC)
    part = call(
        weight_grad_body,
        shape((4, 224, 128), BF16),
        (got,),
        [pltpu.VMEM((288, 2560), BF16), pltpu.VMEM((2048, 128), BF16)],
        flops=2 * 864 * 2048 * 128,
    )
    part = call(
        over_y_body, shape((16, 32, 128), BF16), (exchange(part, "y"),), [pltpu.VMEM((224, 128), F32)]
    )
    part = call(over_z_body, shape((32, 32, 128), BF16), (exchange(part, ZS),))
    grads = exchange(part, YXC)
    data = call(
        data_grad_body,
        shape((256, 128), BF16),
        (delta_low, delta, delta_high, conv_weight),
        [pltpu.VMEM((256, 256), BF16)],
        flops=2 * 256 * 3456 * 256,
    )
    rotated = call(
        rotate_body, shape((16, 112, 128), BF16), (panel_owner, place, grads, basis), smem=2
    )
    rotated = exchange(rotated, ZS)
    part = call(
        update_body,
        shape((8, 64, 256), BF16),
        (panel_owner, place, rotated, basis, output_basis, output_eigen.reshape(1, 256)),
        smem=2,
    )
    part = call(over_xc_body, shape((4, 56, 256), F32), (exchange(part, XC),))
    update = call(last_body, shape((54, 256), F32), (exchange(part, "y"),))
    return (data.reshape(1, 1, 16, 16, 128), update)


def solution(mesh):
    fine = Mesh(mesh.devices.reshape(4, 2, 8, 4, 2), ("y", "zh", "zl", "x", "c"))
    both = P(YS, SPACE, None, None, None)
    return jax.shard_map(
        per_device,
        mesh=fine,
        in_specs=(both, P(), P(), both, P(YS, None, SPACE), P(), P(), P(SPACE), P()),
        out_specs=(both, P(SPACE, None)),
        check_vma=False,
    )
```

time: 964 us -> 177 us (0.18)
  waiting for transfers between devices: 644 us -> 14.7 us
  blocking collectives: 233 us -> 90 us
  local copies, waits for them, and re-layouts: 28.7 us -> 7.49 us
  starting transfers between devices: 19.1 us -> 38.6 us
  matrix products: 14.2 us -> 0 us
  Pallas kernels: 0 us -> 10.8 us
    psum x2 -> x0, waiting for transfers between devices: 639 us -> none  [the longest x1 485 us: per_device(): weight_grad = lax.psum(grad_part, ('sample', 'space')) / cells]
    unnamed x1 -> x0, blocking collectives: 233 us -> none
    all_to_all x0 -> x4, blocking collectives: none -> 90 us  [exchange(): return lax.all_to_all(x, axes, 0, 0)]
    all_to_all x0 -> x3, starting transfers between devices: none -> 22.4 us  [exchange(): return lax.all_to_all(x, axes, 0, 0)]
    unnamed x70 -> x23, local copies, waits for them, and re-layouts: 21.6 us -> 6.72 us
    dot_general x7 -> x0, matrix products: 14.2 us -> none  [the longest x1 3.7 us: per_device(): jnp.dot(back, weight_back, preferred_element_type=jnp.float32)]
    all_to_all x0 -> x3, waiting for transfers between devices: none -> 13.6 us  [exchange(): return lax.all_to_all(x, axes, 0, 0)]
    pallas_call x0 -> x10, Pallas kernels: none -> 10.8 us  [call(): pl.pallas_call(body, out_shape=out_shape, in_specs=specs, out_specs=[VMEM...]
  transfers between devices with their start and end apart: 9 -> 9, of which waited for: 4 -> 4; matrix products, arithmetic and copies ran while one was open for 4% -> 0% of each run, Pallas kernels for 0% -> 3%
where the time goes in v1:
time: 177 us; the launch traced here: 176 us
  blocking collectives  90 us (51%)
  starting transfers between devices  38.6 us (22%)
  waiting for transfers between devices  14.7 us (8%)
  between operations  14.2 us (8%)
  Pallas kernels  10.8 us (6%)
  local copies, waits for them, and re-layouts  7.49 us (4%)
    all_to_all x4, blocking collectives, exchange(): return lax.all_to_all(x, axes, 0, 0)  90 us
    all_to_all x3, starting transfers between devices, exchange(): return lax.all_to_all(x, axes, 0, 0)  22.4 us
    ppermute x4, starting transfers between devices, neighbours(): return (lax.ppermute(block, SPACE, up), lax.ppermute(block, SPACE, down))  15.5 us
    all_to_all x3, waiting for transfers between devices, exchange(): return lax.all_to_all(x, axes, 0, 0)  13.6 us
    pallas_call x10, Pallas kernels, call(): pl.pallas_call(body, out_shape=out_shape, in_specs=specs, out_specs=[VMEM...  10.8 us
    unnamed x23, local copies, waits for them, and re-layouts  6.72 us
  transfers between devices with their start and end apart: 9, of which 4 were waited for; matrix products, arithmetic and copies ran while one was open for 0% of the time, Pallas kernels for 3%

profile of v1, /device:TPU:1, one launch (start us, length us, event | category | flops | bytes accessed | tf_op | source)
XLA Modules:
  0.0 175.9 jit_solution(11759201633622841465)
XLA Ops:
  7.2 1.0 copy.13
  8.2 0.7 pad_bitcast_fusion
  9.2 0.7 collective-permute-start.4
  9.9 0.6 copy-done.10
  10.6 4.5 %collective-permute-start = (bf16[256,128]{1,0:T(8,128)(2,1)}, bf16[256,128]{1,0:T(8,128)(2,1)S(1)}, u32[]{:S(2)}, u32[]{:S(2)}) collective-permute-start(bf16[256,128]{1,0:T(8,128)(2,1)} %bitcast.16), channel_id=1, source_target_pairs={{0,1},{1,2},{2,3},{3,4},{4,5},{5,6},{6,7},{7,8},{8,9},{9,10},{10,1... | collective-permute-start | bytes 196616 | tf_op jit(solution)/shard_map/ppermute | solution.py:255
  15.1 5.6 %collective-permute-start.1 = (bf16[256,128]{1,0:T(8,128)(2,1)}, bf16[256,128]{1,0:T(8,128)(2,1)S(1)}, u32[]{:S(2)}, u32[]{:S(2)}) collective-permute-start(bf16[256,128]{1,0:T(8,128)(2,1)} %bitcast.17), channel_id=1, source_target_pairs={{1,0},{2,1},{3,2},{4,3},{5,4},{6,5},{7,6},{8,7},{9,8},{10,9},{11,1... | collective-permute-start | bytes 196616 | tf_op jit(solution)/shard_map/ppermute | solution.py:255
  20.7 1.1 collective-permute-done.1.high_ref
  21.8 1.5 copy-done
  23.2 0.9 copy-done.5
  24.2 0.8 copy-done.6
  25.0 0.7 copy-done.8
  25.7 0.8 shard_map.104
  26.5 33.7 %all_to_all.35.got_ref = bf16[8,384,128]{2,1,0:T(8,128)(2,1)S(1)} all-to-all(bf16[8,384,128]{2,1,0:T(8,128)(2,1)S(1)} %get-tuple-element.5), channel_id=1, replica_groups=mesh['y'=4,'zh'=2,'zl'=8,'x'=4,'c'=2] {'x','c'}, dimensions={0} | all-to-all | bytes 1572864 | tf_op jit(solution)/shard_map/all_to_all | solution.py:52
  60.2 1.3 shard_map.106
  61.5 7.7 %all_to_all.36.got_ref = bf16[4,224,128]{2,1,0:T(8,128)(2,1)S(1)} all-to-all(bf16[4,224,128]{2,1,0:T(8,128)(2,1)S(1)} %shard_map.106), channel_id=1, replica_groups=mesh['y'=4,'zh'=2,'zl'=8,'x'=4,'c'=2] {'y'}, dimensions={0} | all-to-all | bytes 458752 | tf_op jit(solution)/shard_map/all_to_all | solution.py:52
  69.3 24.9 %all_to_all.37.got_ref = bf16[16,32,128]{2,1,0:T(8,128)(2,1)S(1)} all-to-all(bf16[16,32,128]{2,1,0:T(8,128)(2,1)S(1)} %shard_map.107), channel_id=1, replica_groups=mesh['y'=4,'zh'=2,'zl'=8,'x'=4,'c'=2] {'zh','zl'}, dimensions={0} | all-to-all | bytes 262144 | tf_op jit(solution)/shard_map/all_to_all | solution.py:52
  94.2 0.7 shard_map.108
  94.9 8.6 %all-to-all-start.3 = ((bf16[32,32,128]{2,1,0:T(8,128)(2,1)}), bf16[32,32,128]{2,1,0:T(8,128)(2,1)S(1)}, u32[]{:S(2)}, u32[]{:S(2)}) async-start(bf16[32,32,128]{2,1,0:T(8,128)(2,1)} %shard_map.108), calls=%async_computation.3 | async-start | bytes 524288 | tf_op jit(solution)/shard_map/all_to_all | solution.py:52
  103.6 8.9 %all-to-all-done.3.got_ref = bf16[32,32,128]{2,1,0:T(8,128)(2,1)S(1)} async-done(((bf16[32,32,128]{2,1,0:T(8,128)(2,1)}), bf16[32,32,128]{2,1,0:T(8,128)(2,1)S(1)}, u32[]{:S(2)}, u32[]{:S(2)}) %all-to-all-start.3) | async-done | bytes 262176 | tf_op jit(solution)/shard_map/all_to_all | solution.py:52
  112.5 1.2 copy-done.2
  113.8 1.1 shard_map.110
  114.9 23.7 %all_to_all.38.got_ref = bf16[16,112,128]{2,1,0:T(8,128)(2,1)S(1)} all-to-all(bf16[16,112,128]{2,1,0:T(8,128)(2,1)S(1)} %shard_map.110), channel_id=1, replica_groups=mesh['y'=4,'zh'=2,'zl'=8,'x'=4,'c'=2] {'zh','zl'}, dimensions={0} | all-to-all | bytes 917504 | tf_op jit(solution)/shard_map/all_to_all | solution.py:52
  138.6 3.5 %shard_map.111 = bf16[8,64,256]{2,1,0:T(8,128)(2,1)} custom-call(s32[8]{0:T(128)S(1)} %copy-done.7, s32[2]{0:T(128)S(1)} %pad_add_fusion.place_ref, bf16[16,112,128]{2,1,0:T(8,128)(2,1)S(1)} %all_to_all.38.got_ref, bf16[16,4,64,128]{3,2,1,0:T(8,128)(2,1)S(1)} %bitcast.13, f32[256,256]{1,0:T(8,128)S(1)} %copy-done.4, f32[1,256]{1,0:T(1,128)S(1)} %bitcast.20), custom_call_target="tpu_custom_call" | custom-call | bytes 1770536 | tf_op jit(solution)/shard_map/pallas_call | solution.py:28
  142.1 10.4 %all-to-all-start.5 = ((bf16[8,64,256]{2,1,0:T(8,128)(2,1)}), bf16[8,64,256]{2,1,0:T(8,128)(2,1)S(1)}, u32[]{:S(2)}, u32[]{:S(2)}) async-start(bf16[8,64,256]{2,1,0:T(8,128)(2,1)} %shard_map.111), calls=%async_computation.5 | async-start | bytes 524288 | tf_op jit(solution)/shard_map/all_to_all | solution.py:52
  152.5 3.5 %collective-permute-start.2 = (bf16[256,256]{1,0:T(8,128)(2,1)S(1)}, bf16[256,256]{1,0:T(8,128)(2,1)S(1)}, u32[]{:S(2)}, u32[]{:S(2)}) collective-permute-start(bf16[256,256]{1,0:T(8,128)(2,1)S(1)} %get-tuple-element.4.mine_ref), channel_id=1, source_target_pairs={{0,1},{1,2},{2,3},{3,4},{4,5},{5,6},{6,7},{7,8},{8,9},{9,10},{10,1... | collective-permute-start | bytes 393224 | tf_op jit(solution)/shard_map/ppermute | solution.py:255
  156.0 1.9 %collective-permute-start.3 = (bf16[256,256]{1,0:T(8,128)(2,1)S(1)}, bf16[256,256]{1,0:T(8,128)(2,1)S(1)}, u32[]{:S(2)}, u32[]{:S(2)}) collective-permute-start(bf16[256,256]{1,0:T(8,128)(2,1)S(1)} %get-tuple-element.4.mine_ref), channel_id=1, source_target_pairs={{1,0},{2,1},{3,2},{4,3},{5,4},{6,5},{7,6},{8,7},{9,8},{10,9},{11,1... | collective-permute-start | bytes 393224 | tf_op jit(solution)/shard_map/ppermute | solution.py:255
  158.0 1.1 all-to-all-done.5.got_ref
  159.0 0.7 shard_map.112
  159.7 3.4 %all-to-all-start.6 = ((f32[4,56,256]{2,1,0:T(8,128)}), f32[4,56,256]{2,1,0:T(8,128)S(1)}, u32[]{:S(2)}, u32[]{:S(2)}) async-start(f32[4,56,256]{2,1,0:T(8,128)} %shard_map.112), calls=%async_computation.6 | async-start | bytes 458752 | tf_op jit(solution)/shard_map/all_to_all | solution.py:52
  163.2 1.7 shard_map.105
  164.9 3.6 %all-to-all-done.6.got_ref = f32[4,56,256]{2,1,0:T(8,128)S(1)} async-done(((f32[4,56,256]{2,1,0:T(8,128)}), f32[4,56,256]{2,1,0:T(8,128)S(1)}, u32[]{:S(2)}, u32[]{:S(2)}) %all-to-all-start.6) | async-done | bytes 229408 | tf_op jit(solution)/shard_map/all_to_all | solution.py:52
  168.4 0.6 shard_map.113
  (27 shorter events, 0.6 us)
Async XLA Ops:
  7.2 105.4 %all-gather.3.cloned.1.call-start = ((), (), s32[]{:S(2)}) async-start(), calls=%async_computation.7 | async-start | bytes 1114112 | tf_op jit(solution)/shard_map/all_gather | solution.py:278
  9.2 0.7 collective-permute-start.4
  9.9 0.6 copy-start.10
  10.6 10.1 %collective-permute-start = (bf16[256,128]{1,0:T(8,128)(2,1)}, bf16[256,128]{1,0:T(8,128)(2,1)S(1)}, u32[]{:S(2)}, u32[]{:S(2)}) collective-permute-start(bf16[256,128]{1,0:T(8,128)(2,1)} %bitcast.16), channel_id=1, source_target_pairs={{0,1},{1,2},{2,3},{3,4},{4,5},{5,6},{6,7},{7,8},{8,9},{9,10},{10,1... | collective-permute-start | bytes 196616 | tf_op jit(solution)/shard_map/ppermute | solution.py:255
  15.1 6.7 %collective-permute-start.1 = (bf16[256,128]{1,0:T(8,128)(2,1)}, bf16[256,128]{1,0:T(8,128)(2,1)S(1)}, u32[]{:S(2)}, u32[]{:S(2)}) collective-permute-start(bf16[256,128]{1,0:T(8,128)(2,1)} %bitcast.17), channel_id=1, source_target_pairs={{1,0},{2,1},{3,2},{4,3},{5,4},{6,5},{7,6},{8,7},{9,8},{10,9},{11,1... | collective-permute-start | bytes 196616 | tf_op jit(solution)/shard_map/ppermute | solution.py:255
  21.8 1.5 copy-start
  23.2 0.9 copy-start.5
  24.1 0.8 copy-start.6
  25.0 0.7 copy-start.8
  60.2 52.4 %copy-start.7 = (s32[8]{0:T(128)S(1)}, s32[8]{0:T(128)}, u32[]{:S(2)}) copy-start(s32[8]{0:T(128)} %owner_ref.3) | copy-start | bytes 100
  94.2 44.4 %copy-start.4 = (f32[256,256]{1,0:T(8,128)S(1)}, f32[256,256]{1,0:T(8,128)}, u32[]{:S(2)}) copy-start(f32[256,256]{1,0:T(8,128)} %out_basis_ref.1) | copy-start | bytes 786436
  94.2 44.4 %copy-start.9 = (f32[256]{0:T(256)S(1)}, f32[256]{0:T(256)}, u32[]{:S(2)}) copy-start(f32[256]{0:T(256)} %param.17) | copy-start | bytes 3076
  94.9 17.6 %all-to-all-start.3 = ((bf16[32,32,128]{2,1,0:T(8,128)(2,1)}), bf16[32,32,128]{2,1,0:T(8,128)(2,1)S(1)}, u32[]{:S(2)}, u32[]{:S(2)}) async-start(bf16[32,32,128]{2,1,0:T(8,128)(2,1)} %shard_map.108), calls=%async_computation.3 | async-start | bytes 524288 | tf_op jit(solution)/shard_map/all_to_all | solution.py:52
  112.5 1.2 copy-start.2
  113.8 24.8 %copy-start.3 = (bf16[64,64,128]{2,1,0:T(8,128)(2,1)S(1)}, bf16[64,64,128]{2,1,0:T(8,128)(2,1)}, u32[]{:S(2)}) copy-start(bf16[64,64,128]{2,1,0:T(8,128)(2,1)} %all-gather.3.cloned.1.call-done) | copy-start | bytes 3145732
  138.6 24.6 %copy-start.1 = (bf16[3456,256]{1,0:T(8,128)(2,1)S(1)}, bf16[3456,256]{1,0:T(8,128)(2,1)}, u32[]{:S(2)}) copy-start(bf16[3456,256]{1,0:T(8,128)(2,1)} %weight_ref.3) | copy-start | bytes 5308420
  142.1 16.9 %all-to-all-start.5 = ((bf16[8,64,256]{2,1,0:T(8,128)(2,1)}), bf16[8,64,256]{2,1,0:T(8,128)(2,1)S(1)}, u32[]{:S(2)}, u32[]{:S(2)}) async-start(bf16[8,64,256]{2,1,0:T(8,128)(2,1)} %shard_map.111), calls=%async_computation.5 | async-start | bytes 524288 | tf_op jit(solution)/shard_map/all_to_all | solution.py:52
  152.5 10.6 %collective-permute-start.2 = (bf16[256,256]{1,0:T(8,128)(2,1)S(1)}, bf16[256,256]{1,0:T(8,128)(2,1)S(1)}, u32[]{:S(2)}, u32[]{:S(2)}) collective-permute-start(bf16[256,256]{1,0:T(8,128)(2,1)S(1)} %get-tuple-element.4.mine_ref), channel_id=1, source_target_pairs={{0,1},{1,2},{2,3},{3,4},{4,5},{5,6},{6,7},{7,8},{8,9},{9,10},{10,1... | collective-permute-start | bytes 393224 | tf_op jit(solution)/shard_map/ppermute | solution.py:255
  156.0 7.1 %collective-permute-start.3 = (bf16[256,256]{1,0:T(8,128)(2,1)S(1)}, bf16[256,256]{1,0:T(8,128)(2,1)S(1)}, u32[]{:S(2)}, u32[]{:S(2)}) collective-permute-start(bf16[256,256]{1,0:T(8,128)(2,1)S(1)} %get-tuple-element.4.mine_ref), channel_id=1, source_target_pairs={{1,0},{2,1},{3,2},{4,3},{5,4},{6,5},{7,6},{8,7},{9,8},{10,9},{11,1... | collective-permute-start | bytes 393224 | tf_op jit(solution)/shard_map/ppermute | solution.py:255
  159.7 8.7 %all-to-all-start.6 = ((f32[4,56,256]{2,1,0:T(8,128)}), f32[4,56,256]{2,1,0:T(8,128)S(1)}, u32[]{:S(2)}, u32[]{:S(2)}) async-start(f32[4,56,256]{2,1,0:T(8,128)} %shard_map.112), calls=%async_computation.6 | async-start | bytes 458752 | tf_op jit(solution)/shard_map/all_to_all | solution.py:52
Sparse Core Ops, SparseCore 0:
  10.7 81.3 all-gather.2

commit v2 on v1

v2 whole, which is shorter than its diff:
```python
import jax
import jax.numpy as jnp
from jax import lax
from jax.experimental import pallas as pl
from jax.experimental.pallas import tpu as pltpu
from jax.sharding import Mesh
from jax.sharding import PartitionSpec as P

DAMPING = 0.001
CELLS = 131072
BF16 = jnp.bfloat16
F32 = jnp.float32
VMEM = pl.BlockSpec(memory_space=pltpu.VMEM)
SMEM = pl.BlockSpec(memory_space=pltpu.SMEM)
LIMIT = 48 * 1024 * 1024
ANY = pl.BlockSpec(memory_space=pl.ANY)
AXES = ("y", "zh", "zg", "zl", "x", "c")
SIZES = (4, 2, 2, 4, 4, 2)
SAMPLE = ("y", "zh")
XC = ("x", "c")
YXC = ("y", "x", "c")
SPACE = ("zg", "zl", "x", "c")


def call(body, out_shape, scalars=(), arrays=(), remote=(), scratch=(), flops=0):
    many = isinstance(out_shape, (list, tuple))
    inputs = (*scalars, *arrays, *remote)
    return pl.pallas_call(
        body,
        out_shape=out_shape,
        in_specs=[SMEM] * len(scalars) + [VMEM] * len(arrays) + [ANY] * len(remote),
        out_specs=[VMEM] * len(out_shape) if many else VMEM,
        scratch_shapes=list(scratch),
        compiler_params=pltpu.CompilerParams(vmem_limit_bytes=LIMIT),
        cost_estimate=pl.CostEstimate(
            flops=flops,
            bytes_accessed=sum(a.size * a.dtype.itemsize for a in inputs),
            transcendentals=0,
        ),
    )(*inputs)


def shape(dims, dtype):
    return jax.ShapeDtypeStruct(dims, dtype)


def iota(dims, axis):
    return lax.broadcasted_iota(jnp.int32, dims, axis)


def exchange(x, axes):
    return lax.all_to_all(x, axes, 0, 0)


def started(copies):
    for copy in copies:
        copy.start()
    return copies


def x_shifted(rows, step):
    if step == 0:
        return rows
    x = iota(rows.shape, 0) & 15
    inside = (x + step >= 0) & (x + step < 16)
    return jnp.where(inside, pltpu.roll(rows, (-step) % 256, 0), 0.0)


def basis_body(panel, eigen_any, out_ref, eigen, sem):
    copy = pltpu.make_async_copy(eigen_any, eigen, sem)
    copy.start()
    copy.wait()
    row = iota((54, 54), 0)
    column = jnp.sum(jnp.where(row == iota((54, 54), 1), eigen[...], 0.0), axis=1, keepdims=True)
    column = jnp.concatenate([column, jnp.ones((10, 1), F32)], axis=0)
    first = column.astype(BF16).astype(F32)
    second = (column - first).astype(BF16).astype(F32)
    third = column - first - second
    for r in range(4):
        pick = iota((432, 128), 0) == 4 * iota((432, 128), 1) + r
        block = jnp.dot(panel[...], jnp.where(pick, 1.0, 0.0).astype(BF16), preferred_element_type=F32)
        block = jnp.concatenate([block, jnp.zeros((10, 128), F32)], axis=0)
        if r == 0:
            at = iota((64, 128), 1)
            block = jnp.where(at == 108, first, block)
            block = jnp.where(at == 109, second, block)
            block = jnp.where(at == 110, third, block)
        out_ref[r] = block.astype(BF16)


def pack_body(own_ref, other_ref, after_ref, out_ref):
    out_ref[0] = own_ref[...]
    out_ref[1] = other_ref[...]
    out_ref[2] = own_ref[...]
    out_ref[3] = other_ref[...]


def forward_body(
    place_ref, low_ref, high_ref, mine_any, weight_any, bias_any, cot_any,
    delta_ref, send_ref, patches, mine, weight, bias, cot, sems,
):
    copies = started(
        [
            pltpu.make_async_copy(source, target, sems.at[i])
            for i, (source, target) in enumerate(
                [(mine_any, mine), (weight_any, weight), (bias_any, bias), (cot_any, cot)]
            )
        ]
    )
    none = jnp.zeros((16, 128), BF16)
    for a in (0, 2, 1):
        if a == 1:
            copies[0].wait()
        wide = (low_ref, mine, high_ref)[a][...].astype(F32)
        for c in range(3):
            moved = x_shifted(wide, c - 1).astype(BF16)
            for b in range(3):
                at = (9 * a + 3 * b + c) * 128
                if b == 0:
                    shifted = jnp.concatenate([none, moved[:240]], axis=0)
                elif b == 2:
                    shifted = jnp.concatenate([moved[16:], none], axis=0)
                else:
                    shifted = moved
                patches[:, at : at + 128] = shifted
    for copy in copies[1:]:
        copy.wait()
    pre = jnp.dot(patches[...], weight[...], preferred_element_type=F32) + bias[...]
    logistic = 1.0 / (1.0 + jnp.exp(-pre))
    delta = (cot[...].astype(F32) * logistic * (1.0 + pre * (1.0 - logistic))).astype(BF16)
    delta_ref[...] = delta
    rim = jnp.where(place_ref[0] < 4, low_ref[...].astype(F32), high_ref[...].astype(F32))
    act_t = mine[...].astype(F32).T.astype(BF16)
    rim_t = rim.T.astype(BF16)
    for x in range(4):
        for c in range(2):
            to = 2 * x + c
            for half in range(2):
                lanes = slice(128 * half, 128 * half + 128)
                rows = slice(32 * x, 32 * x + 32)
                send_ref[to, 32 * half : 32 * half + 32] = act_t[rows, lanes]
                send_ref[to, 64 + 32 * half : 96 + 32 * half] = rim_t[rows, lanes]
            send_ref[to, 128:] = delta[:, 128 * c : 128 * c + 128]


def weight_grad_body(got_ref, out_ref, moved, deltas, whole):
    pieces = []
    for plane, at in [(0, 64)] + [(e, 0) for e in range(8)] + [(7, 64)]:
        pieces.append(got_ref[plane, at : at + 32].astype(F32))
        pieces.append(got_ref[plane, at + 32 : at + 64].astype(F32))
    acts = jnp.concatenate(pieces, axis=1)
    lane = iota((32, 2560), 1)
    x = lane & 15
    y = (lane >> 4) & 15
    for b in range(3):
        for c in range(3):
            step = 16 * (b - 1) + (c - 1)
            turned = pltpu.roll(acts, (-step) % 2560, 1) if step else acts
            inside = (x + c >= 1) & (x + c < 17) & (y + b >= 1) & (y + b < 17)
            moved[32 * (3 * b + c) : 32 * (3 * b + c) + 32, :] = jnp.where(inside, turned, 0.0).astype(BF16)
    for e in range(8):
        deltas[256 * e : 256 * e + 256, :] = got_ref[e, 128:]
    for a in range(3):
        whole[288 * a : 288 * a + 288, :] = jnp.dot(
            moved[:, 256 * a : 256 * a + 2048], deltas[...], preferred_element_type=F32
        )
    none = jnp.zeros((5, 128), F32)
    for y_to in range(4):
        for z_to in range(4):
            parts = []
            for e in range(2):
                parts.append(whole[pl.ds(8 * y_to + 4 * e + z_to, 27, stride=32), :])
                parts.append(none)
            out_ref[4 * y_to + z_to] = jnp.concatenate(parts, axis=0).astype(BF16)


def over_y_zl_body(got_ref, out_ref):
    total = sum(got_ref[i].astype(F32) for i in range(16)) * (1.0 / CELLS)
    for to in range(4):
        out_ref[to] = total.astype(BF16)


def over_zh_zg_body(got_ref, out_ref):
    total = ((got_ref[0].astype(F32) + got_ref[1].astype(F32)) + (got_ref[2].astype(F32) + got_ref[3].astype(F32))).astype(BF16)
    for to in range(32):
        out_ref[to] = total


def slot_of(owner, zh):
    return owner >> 1, (owner & 1) ^ zh


def rotate_body(owner_ref, place_ref, got_ref, basis_any, out_ref, basis, grads, ordered, sems):
    zh, zl = place_ref[0], place_ref[1]
    copies = []
    for j in range(8):
        first, second = slot_of(owner_ref[j], zh)
        copies.append(pltpu.make_async_copy(basis_any.at[first, second, zl], basis.at[j], sems.at[j]))
    started(copies)
    for y in range(4):
        for x in range(4):
            at = 32 * (8 * x + 2 * y)
            for c in range(2):
                grads[c, at : at + 64, :] = got_ref[8 * y + 2 * x + c].astype(F32)
    for tap in range(27):
        for c in range(2):
            ordered[32 * tap : 32 * tap + 32, 128 * c : 128 * c + 128] = grads[c, pl.ds(tap, 32, stride=32), :]
    ordered[864:, :] = jnp.zeros((32, 256), F32)
    inside = iota((64, 128), 1) < 108
    total = jnp.zeros((64, 256), F32)
    for j in range(8):
        copies[j].wait()
        block = jnp.where(inside, basis[j].astype(F32), 0.0).astype(BF16)
        rows = ordered[108 * j : 108 * j + 128, :].astype(BF16)
        total = total + jnp.dot(block, rows, preferred_element_type=F32)
    for to in range(4):
        out_ref[to] = total[:56]


def update_body(
    owner_ref, place_ref, got_ref, basis_any, out_basis_any, out_eigen_any,
    out_ref, basis, out_basis, out_eigen, ordered, sems,
):
    zh, zl = place_ref[0], place_ref[1]
    copies = [
        pltpu.make_async_copy(out_basis_any, out_basis, sems.at[0]),
        pltpu.make_async_copy(out_eigen_any, out_eigen, sems.at[1]),
    ]
    for g in range(2):
        first, second = slot_of(owner_ref[zl + 4 * g], zh)
        copies.append(pltpu.make_async_copy(basis_any.at[first, second], basis.at[g], sems.at[2 + g]))
    started(copies)
    highest = lax.Precision.HIGHEST
    rotated = (got_ref[0] + got_ref[1]) + (got_ref[2] + got_ref[3])
    rotated = jnp.concatenate([rotated, jnp.zeros((8, 256), F32)], axis=0)
    for copy in copies:
        copy.wait()
    rotated = jnp.dot(rotated, out_basis[...], precision=highest, preferred_element_type=F32)
    terms = basis[0, 0].astype(F32)
    eigen = (terms[:, 108:109] + terms[:, 109:110]) + terms[:, 110:111]
    scaled = rotated / (eigen * out_eigen[...] + DAMPING)
    scaled = jnp.where(iota((64, 256), 0) < 54, scaled, 0.0)
    turned = lax.dot_general(
        scaled, out_basis[...], (((1,), (1,)), ((), ())), precision=highest, preferred_element_type=F32
    )
    high = turned.astype(BF16)
    rest = (turned - high.astype(F32)).astype(BF16)
    for g in range(2):
        for r in range(4):
            block = basis[g, r].astype(F32).T.astype(BF16)
            rows = jnp.dot(block, high, preferred_element_type=F32) + jnp.dot(block, rest, preferred_element_type=F32)
            for c in range(2):
                ordered[g, c, pl.ds(r, 108, stride=4), :] = rows[:108, 128 * c : 128 * c + 128]
        for c in range(2):
            ordered[g, c, 432:, :] = jnp.zeros((8, 128), F32)
    for c in range(2):
        for to in range(8):
            rows = [ordered[g, c, 54 * to : 54 * to + 56, :] for g in range(2)]
            out_ref[to, :, 128 * c : 128 * c + 128] = jnp.concatenate(rows, axis=0).astype(BF16)


def over_xc_body(got_ref, out_ref):
    total = sum(got_ref[i].astype(F32) for i in range(8))
    for g in range(2):
        rows = total[56 * g : 56 * g + 56]
        rows = jnp.concatenate([rows[:, :128], rows[:, 128:]], axis=0).astype(BF16)
        for y in range(4):
            out_ref[4 * g + y] = rows


def last_body(got_ref, out_ref):
    total = sum(got_ref[i].astype(F32) for i in range(8))
    out_ref[...] = jnp.concatenate([total[:54], total[56:110]], axis=1)


def data_grad_body(low_ref, high_ref, mine_ref, weight_any, out_ref, weight, sem):
    copy = pltpu.make_async_copy(weight_any, weight, sem)
    copy.start()
    none = jnp.zeros((16, 256), BF16)
    total = jnp.zeros((256, 128), F32)
    for a in range(3):
        wide = (high_ref, mine_ref, low_ref)[a][...].astype(F32)
        if a == 0:
            copy.wait()
        for c in range(3):
            moved = x_shifted(wide, 1 - c).astype(BF16)
            for b in range(3):
                if b == 2:
                    shifted = jnp.concatenate([none, moved[:240]], axis=0)
                elif b == 0:
                    shifted = jnp.concatenate([moved[16:], none], axis=0)
                else:
                    shifted = moved
                tap = 9 * a + 3 * b + c
                total = total + lax.dot_general(
                    shifted,
                    weight[128 * tap : 128 * tap + 128, :],
                    (((1,), (1,)), ((), ())),
                    preferred_element_type=F32,
                )
    out_ref[...] = total.astype(BF16)


def neighbours(block):
    count = 64
    up = [(i, i + 1) for i in range(count - 1)]
    down = [(i + 1, i) for i in range(count - 1)]
    return lax.ppermute(block, SPACE, up), lax.ppermute(block, SPACE, down)


def turned(block, flip):
    pairs = [
        (8 * y + 4 * zh + z, 8 * z + 4 * (zh ^ flip) + y) for y in range(4) for zh in range(2) for z in range(4)
    ]
    return lax.ppermute(block, ("y", "zh", "zl"), pairs)


def per_device(
    activations,
    conv_weight,
    conv_bias,
    cotangent,
    basis_panels,
    panel_owner,
    output_basis,
    input_eigen,
    output_eigen,
):
    dma = pltpu.SemaphoreType.DMA
    place = jnp.stack([lax.axis_index("zh"), lax.axis_index("zl")]).astype(jnp.int32)
    inner = lax.axis_index(XC).astype(jnp.int32).reshape(1)
    plane = activations.reshape(256, 128)
    low, high = neighbours(plane)

    stored = call(
        basis_body,
        shape((4, 64, 128), BF16),
        arrays=(basis_panels[0].T,),
        remote=(input_eigen.reshape(1, 54),),
        scratch=[pltpu.VMEM((1, 54), F32), dma],
    )
    own, other = turned(stored, 0), turned(stored, 1)

    delta, send = call(
        forward_body,
        [shape((256, 256), BF16), shape((8, 384, 128), BF16)],
        (inner,),
        (low, high),
        (plane, conv_weight, conv_bias.reshape(1, 256), cotangent.reshape(256, 256)),
        [
            pltpu.VMEM((256, 3456), BF16),
            pltpu.VMEM((256, 128), BF16),
            pltpu.VMEM((3456, 256), BF16),
            pltpu.VMEM((1, 256), F32),
            pltpu.VMEM((256, 256), BF16),
            dma((4,)),
        ],
        flops=2 * 256 * 3456 * 256,
    )
    packed = call(pack_body, shape((4, 4, 64, 128), BF16), arrays=(own, other), remote=(delta,))
    basis = lax.all_gather(packed, "zl")
    delta_low, delta_high = neighbours(delta)
    got = exchange(send, XC)
    part = call(
        weight_grad_body,
        shape((16, 64, 128), BF16),
        arrays=(got,),
        scratch=[pltpu.VMEM((288, 2560), BF16), pltpu.VMEM((2048, 128), BF16), pltpu.VMEM((864, 128), F32)],
        flops=2 * 864 * 2048 * 128,
    )
    part = call(over_y_zl_body, shape((4, 64, 128), BF16), arrays=(exchange(part, ("y", "zl")),))
    part = call(over_zh_zg_body, shape((32, 64, 128), BF16), arrays=(exchange(part, ("zh", "zg")),))
    grads = exchange(part, YXC)
    data = call(
        data_grad_body,
        shape((256, 128), BF16),
        arrays=(delta_low, delta_high, delta),
        remote=(conv_weight,),
        scratch=[pltpu.VMEM((3456, 256), BF16), dma],
        flops=2 * 256 * 3456 * 256,
    )
    rotated = call(
        rotate_body,
        shape((4, 56, 256), F32),
        (panel_owner, place),
        (grads,),
        (basis,),
        [
            pltpu.VMEM((8, 64, 128), BF16),
            pltpu.VMEM((2, 1024, 128), F32),
            pltpu.VMEM((896, 256), F32),
            dma((8,)),
        ],
    )
    part = call(
        update_body,
        shape((8, 112, 256), BF16),
        (panel_owner, place),
        (exchange(rotated, "zl"),),
        (basis, output_basis, output_eigen.reshape(1, 256)),
        [
            pltpu.VMEM((2, 4, 64, 128), BF16),
            pltpu.VMEM((256, 256), F32),
            pltpu.VMEM((1, 256), F32),
            pltpu.VMEM((2, 2, 440, 128), F32),
            dma((4,)),
        ],
    )
    part = call(over_xc_body, shape((8, 112, 128), BF16), arrays=(exchange(part, XC),))
    update = call(last_body, shape((54, 256), F32), arrays=(exchange(part, ("zg", "y")),))
    return (data.reshape(1, 1, 16, 16, 128), update)


def solution(mesh):
    fine = Mesh(mesh.devices.reshape(SIZES), AXES)
    both = P(SAMPLE, SPACE, None, None, None)
    return jax.shard_map(
        per_device,
        mesh=fine,
        in_specs=(both, P(), P(), both, P(SAMPLE, None, SPACE), P(), P(), P(SPACE), P()),
        out_specs=(both, P(SPACE, None)),
        check_vma=False,
    )
```

time: 177 us -> 184 us (1.040)
  blocking collectives: 90 us -> 65.8 us
  starting transfers between devices: 38.6 us -> 58 us
  waiting for transfers between devices: 14.7 us -> 26.4 us
  Pallas kernels: 10.8 us -> 13.3 us
  local copies, waits for them, and re-layouts: 7.49 us -> 5.16 us
    all_to_all x4, blocking collectives: 90 us -> 65.8 us  [exchange(): return lax.all_to_all(x, axes, 0, 0)]
    ppermute x1 -> x2, starting transfers between devices: 0.66 us -> 11.3 us  [turned(): return lax.ppermute(block, ('y', 'zh', 'zl'), pairs)]
    all_to_all x3, starting transfers between devices: 22.4 us -> 31.7 us  [exchange(): return lax.all_to_all(x, axes, 0, 0)]
    all_gather x1, waiting for transfers between devices: 0.01 us -> 6.68 us  [per_device(): basis = lax.all_gather(packed, 'zl')]
    ppermute x4, waiting for transfers between devices: 1.08 us -> 5.43 us  [neighbours(): return (lax.ppermute(block, SPACE, up), lax.ppermute(block, SPACE, down))]
    ppermute x1 -> x2, waiting for transfers between devices: 0.01 us -> 3.19 us  [turned(): return lax.ppermute(block, ('y', 'zh', 'zl'), pairs)]
    pallas_call x10 -> x11, Pallas kernels: 10.8 us -> 13.3 us  [call(): pl.pallas_call(body, out_shape=out_shape, in_specs=[SMEM] * len(scalars)...]
    all_to_all x3, waiting for transfers between devices: 13.6 us -> 11.1 us  [exchange(): return lax.all_to_all(x, axes, 0, 0)]
  transfers between devices with their start and end apart: 9 -> 10, of which waited for: 4 -> 6; matrix products, arithmetic and copies ran while one was open for 0% -> 0% of each run, Pallas kernels for 3% -> 2%
where the time goes in v2:
time: 184 us; the launch traced here: 183 us
  blocking collectives  65.8 us (36%)
  starting transfers between devices  58 us (32%)
  waiting for transfers between devices  26.4 us (14%)
  between operations  14.2 us (8%)
  Pallas kernels  13.3 us (7%)
  local copies, waits for them, and re-layouts  5.16 us (3%)
    all_to_all x4, blocking collectives, exchange(): return lax.all_to_all(x, axes, 0, 0)  65.8 us
    all_to_all x3, starting transfers between devices, exchange(): return lax.all_to_all(x, axes, 0, 0)  31.7 us
    ppermute x4, starting transfers between devices, neighbours(): return (lax.ppermute(block, SPACE, up), lax.ppermute(block, SPACE, down))  15 us
    pallas_call x11, Pallas kernels, call(): pl.pallas_call(body, out_shape=out_shape, in_specs=[SMEM] * len(scalars)...  13.3 us
    ppermute x2, starting transfers between devices, turned(): return lax.ppermute(block, ('y', 'zh', 'zl'), pairs)  11.3 us
    all_to_all x3, waiting for transfers between devices, exchange(): return lax.all_to_all(x, axes, 0, 0)  11.1 us
    all_gather x1, waiting for transfers between devices, per_device(): basis = lax.all_gather(packed, 'zl')  6.68 us
    ppermute x4, waiting for transfers between devices, neighbours(): return (lax.ppermute(block, SPACE, up), lax.ppermute(block, SPACE, down))  5.43 us
  transfers between devices with their start and end apart: 10, of which 6 were waited for; matrix products, arithmetic and copies ran while one was open for 0% of the time, Pallas kernels for 2%

profile of v2, /device:TPU:1, one launch (start us, length us, event | category | flops | bytes accessed | tf_op | source)
XLA Modules:
  0.0 183.1 jit_solution(9168106932343650678)
XLA Ops:
  7.2 4.5 %collective-permute-start = (bf16[256,128]{1,0:T(8,128)(2,1)}, bf16[256,128]{1,0:T(8,128)(2,1)S(1)}, u32[]{:S(2)}, u32[]{:S(2)}) collective-permute-start(bf16[256,128]{1,0:T(8,128)(2,1)} %bitcast.16), channel_id=1, source_target_pairs={{0,1},{1,2},{2,3},{3,4},{4,5},{5,6},{6,7},{7,8},{8,9},{9,10},{10,1... | collective-permute-start | bytes 196616 | tf_op jit(solution)/shard_map/ppermute | solution.py:308
  11.7 5.6 %collective-permute-start.1 = (bf16[256,128]{1,0:T(8,128)(2,1)}, bf16[256,128]{1,0:T(8,128)(2,1)S(1)}, u32[]{:S(2)}, u32[]{:S(2)}) collective-permute-start(bf16[256,128]{1,0:T(8,128)(2,1)} %bitcast.17), channel_id=1, source_target_pairs={{1,0},{2,1},{3,2},{4,3},{5,4},{6,5},{7,6},{8,7},{9,8},{10,9},{11,1... | collective-permute-start | bytes 196616 | tf_op jit(solution)/shard_map/ppermute | solution.py:308
  17.3 1.1 collective-permute-done.1.high_ref
  18.4 1.5 copy-done
  19.8 0.9 copy-done.5
  20.7 0.8 copy-done.6
  21.6 0.7 copy-done.9
  22.3 1.6 shard_map.104
  23.9 17.9 %all_to_all.35.got_ref = bf16[8,384,128]{2,1,0:T(8,128)(2,1)S(1)} all-to-all(bf16[8,384,128]{2,1,0:T(8,128)(2,1)S(1)} %get-tuple-element.5), channel_id=1, replica_groups=mesh['y'=4,'zh'=2,'zg'=2,'zl'=4,'x'=4,'c'=2] {'x','c'}, dimensions={0} | all-to-all | bytes 1572864 | tf_op jit(solution)/shard_map/all_to_all | solution.py:52
  41.8 2.2 %shard_map.106 = bf16[16,64,128]{2,1,0:T(8,128)(2,1)} custom-call(bf16[8,384,128]{2,1,0:T(8,128)(2,1)S(1)} %all_to_all.35.got_ref), custom_call_target="tpu_custom_call" | custom-call | flops 452984832 | bytes 786432 | tf_op jit(solution)/shard_map/pallas_call | solution.py:28
  43.9 10.9 %all-to-all-start.1 = ((bf16[16,64,128]{2,1,0:T(8,128)(2,1)}), bf16[16,64,128]{2,1,0:T(8,128)(2,1)S(1)}, u32[]{:S(2)}, u32[]{:S(2)}) async-start(bf16[16,64,128]{2,1,0:T(8,128)(2,1)} %shard_map.106), calls=%async_computation.1 | async-start | bytes 524288 | tf_op jit(solution)/shard_map/all_to_all | solution.py:52
  55.2 0.7 collective-permute-start.4
  55.9 10.6 %collective-permute-start.5 = (bf16[4,64,128]{2,1,0:T(8,128)(2,1)S(1)}, bf16[4,64,128]{2,1,0:T(8,128)(2,1)S(1)}, u32[]{:S(2)}, u32[]{:S(2)}) collective-permute-start(bf16[4,64,128]{2,1,0:T(8,128)(2,1)S(1)} %shard_map.109), channel_id=1, source_target_pairs={{0,64},{8,192},{16,320},{24,448},{64,0},{72,128},{80,256},{88,384}... | collective-permute-start | bytes 196616 | tf_op jit(solution)/shard_map/ppermute | solution.py:315
  66.6 3.2 %collective-permute-done.5.other_ref = bf16[4,64,128]{2,1,0:T(8,128)(2,1)S(1)} collective-permute-done((bf16[4,64,128]{2,1,0:T(8,128)(2,1)S(1)}, bf16[4,64,128]{2,1,0:T(8,128)(2,1)S(1)}, u32[]{:S(2)}, u32[]{:S(2)}) %collective-permute-start.5) | collective-permute-done | bytes 65568 | tf_op jit(solution)/shard_map/ppermute | solution.py:315
  69.8 0.8 shard_map.110
  70.6 21.8 %all_to_all.36.got_ref = bf16[4,64,128]{2,1,0:T(8,128)(2,1)S(1)} all-to-all(bf16[4,64,128]{2,1,0:T(8,128)(2,1)S(1)} %shard_map.107), channel_id=1, replica_groups=mesh['y'=4,'zh'=2,'zg'=2,'zl'=4,'x'=4,'c'=2] {'zh','zg'}, dimensions={0} | all-to-all | bytes 131072 | tf_op jit(solution)/shard_map/all_to_all | solution.py:52
  92.4 0.9 shard_map.108
  93.3 17.3 %all-to-all-start.3 = ((bf16[32,64,128]{2,1,0:T(8,128)(2,1)}), bf16[32,64,128]{2,1,0:T(8,128)(2,1)S(1)}, u32[]{:S(2)}, u32[]{:S(2)}) async-start(bf16[32,64,128]{2,1,0:T(8,128)(2,1)} %shard_map.108), calls=%async_computation.3 | async-start | bytes 1048576 | tf_op jit(solution)/shard_map/all_to_all | solution.py:52
  110.7 6.7 %all-gather.3.cloned.1.call-done = bf16[16,4,64,128]{3,2,1,0:T(8,128)(2,1)} async-done(((bf16[4,4,64,128]{3,2,1,0:T(8,128)(2,1)}), bf16[16,4,64,128]{3,2,1,0:T(8,128)(2,1)}) %all-gather.3.cloned.1.call-update) | async-done | bytes 1048592 | tf_op jit(solution)/shard_map/all_gather | solution.py:361
  117.4 4.8 %all-to-all-done.3.got_ref = bf16[32,64,128]{2,1,0:T(8,128)(2,1)S(1)} async-done(((bf16[32,64,128]{2,1,0:T(8,128)(2,1)}), bf16[32,64,128]{2,1,0:T(8,128)(2,1)S(1)}, u32[]{:S(2)}, u32[]{:S(2)}) %all-to-all-start.3) | async-done | bytes 524320 | tf_op jit(solution)/shard_map/all_to_all | solution.py:52
  122.2 1.2 copy-done.2
  123.4 1.9 %shard_map.111 = f32[4,56,256]{2,1,0:T(8,128)S(1)} custom-call(s32[8]{0:T(128)S(1)} %copy-done.8, s32[2]{0:T(128)S(1)} %pad_add_fusion.place_ref, bf16[32,64,128]{2,1,0:T(8,128)(2,1)S(1)} %all-to-all-done.3.got_ref, bf16[4,4,4,64,128]{4,3,2,1,0:T(8,128)(2,1)S(1)} %bitcast.13), custom_call_target="tpu_custom_call" | custom-call | bytes 1572904 | tf_op jit(solution)/shard_map/pallas_call | solution.py:28
  125.3 12.1 %all_to_all.37.got_ref = f32[4,56,256]{2,1,0:T(8,128)S(1)} all-to-all(f32[4,56,256]{2,1,0:T(8,128)S(1)} %shard_map.111), channel_id=1, replica_groups=mesh['y'=4,'zh'=2,'zg'=2,'zl'=4,'x'=4,'c'=2] {'zl'}, dimensions={0} | all-to-all | bytes 458752 | tf_op jit(solution)/shard_map/all_to_all | solution.py:52
  137.4 2.2 %shard_map.112 = bf16[8,112,256]{2,1,0:T(8,128)(2,1)S(1)} custom-call(s32[8]{0:T(128)S(1)} %copy-done.8, s32[2]{0:T(128)S(1)} %pad_add_fusion.place_ref, f32[4,56,256]{2,1,0:T(8,128)S(1)} %all_to_all.37.got_ref, bf16[4,4,4,64,128]{4,3,2,1,0:T(8,128)(2,1)S(1)} %bitcast.14, f32[256,256]{1,0:T(8,128)S(1)} %copy-done.4, f32[1,256]{1,0:T(1,128)S(1)} %bitcast.21), custom_call_target="tpu_custom_call" | custom-call | bytes 1541160 | tf_op jit(solution)/shard_map/pallas_call | solution.py:28
  139.6 14.0 %all_to_all.38.got_ref = bf16[8,112,256]{2,1,0:T(8,128)(2,1)S(1)} all-to-all(bf16[8,112,256]{2,1,0:T(8,128)(2,1)S(1)} %shard_map.112), channel_id=1, replica_groups=mesh['y'=4,'zh'=2,'zg'=2,'zl'=4,'x'=4,'c'=2] {'x','c'}, dimensions={0} | all-to-all | bytes 917504 | tf_op jit(solution)/shard_map/all_to_all | solution.py:52
  153.6 0.8 shard_map.113
  154.4 3.4 %all-to-all-start.6 = ((bf16[8,112,128]{2,1,0:T(8,128)(2,1)}), bf16[8,112,128]{2,1,0:T(8,128)(2,1)S(1)}, u32[]{:S(2)}, u32[]{:S(2)}) async-start(bf16[8,112,128]{2,1,0:T(8,128)(2,1)} %shard_map.113), calls=%async_computation.6 | async-start | bytes 458752 | tf_op jit(solution)/shard_map/all_to_all | solution.py:52
  157.8 3.0 %collective-permute-start.2 = (bf16[256,256]{1,0:T(8,128)(2,1)S(1)}, bf16[256,256]{1,0:T(8,128)(2,1)S(1)}, u32[]{:S(2)}, u32[]{:S(2)}) collective-permute-start(bf16[256,256]{1,0:T(8,128)(2,1)S(1)} %get-tuple-element.4.mine_ref.after_ref), channel_id=1, source_target_pairs={{0,1},{1,2},{2,3},{3,4},{4,5},{5,6},{6,7},{7,8},{8,9},{9,10},{10,1... | collective-permute-start | bytes 393224 | tf_op jit(solution)/shard_map/ppermute | solution.py:308
  160.8 1.9 %collective-permute-start.3 = (bf16[256,256]{1,0:T(8,128)(2,1)S(1)}, bf16[256,256]{1,0:T(8,128)(2,1)S(1)}, u32[]{:S(2)}, u32[]{:S(2)}) collective-permute-start(bf16[256,256]{1,0:T(8,128)(2,1)S(1)} %get-tuple-element.4.mine_ref.after_ref), channel_id=1, source_target_pairs={{1,0},{2,1},{3,2},{4,3},{5,4},{6,5},{7,6},{8,7},{9,8},{10,9},{11,1... | collective-permute-start | bytes 393224 | tf_op jit(solution)/shard_map/ppermute | solution.py:308
  162.8 4.3 %collective-permute-done.3.high_ref = bf16[256,256]{1,0:T(8,128)(2,1)S(1)} collective-permute-done((bf16[256,256]{1,0:T(8,128)(2,1)S(1)}, bf16[256,256]{1,0:T(8,128)(2,1)S(1)}, u32[]{:S(2)}, u32[]{:S(2)}) %collective-permute-start.3) | collective-permute-done | bytes 131104 | tf_op jit(solution)/shard_map/ppermute | solution.py:308
  167.1 2.1 %shard_map.105 = bf16[256,128]{1,0:T(8,128)(2,1)} custom-call(bf16[256,256]{1,0:T(8,128)(2,1)S(1)} %collective-permute-done.2.low_ref, bf16[256,256]{1,0:T(8,128)(2,1)S(1)} %collective-permute-done.3.high_ref, bf16[256,256]{1,0:T(8,128)(2,1)S(1)} %get-tuple-element.4.mine_ref.after_ref, bf16[3456,256]{1,0:T(8,128)(2,1)S(1)} %copy-done.1), custom_call_target="tpu_custom_call" | custom-call | flops 452984832 | bytes 2162688 | tf_op jit(solution)/shard_map/pallas_call | solution.py:28
  169.2 6.3 %all-to-all-done.6.got_ref = bf16[8,112,128]{2,1,0:T(8,128)(2,1)S(1)} async-done(((bf16[8,112,128]{2,1,0:T(8,128)(2,1)}), bf16[8,112,128]{2,1,0:T(8,128)(2,1)S(1)}, u32[]{:S(2)}, u32[]{:S(2)}) %all-to-all-start.6) | async-done | bytes 229408 | tf_op jit(solution)/shard_map/all_to_all | solution.py:52
  (29 shorter events, 1.2 us)
Async XLA Ops:
  7.2 10.1 %collective-permute-start = (bf16[256,128]{1,0:T(8,128)(2,1)}, bf16[256,128]{1,0:T(8,128)(2,1)S(1)}, u32[]{:S(2)}, u32[]{:S(2)}) collective-permute-start(bf16[256,128]{1,0:T(8,128)(2,1)} %bitcast.16), channel_id=1, source_target_pairs={{0,1},{1,2},{2,3},{3,4},{4,5},{5,6},{6,7},{7,8},{8,9},{9,10},{10,1... | collective-permute-start | bytes 196616 | tf_op jit(solution)/shard_map/ppermute | solution.py:308
  11.7 6.7 %collective-permute-start.1 = (bf16[256,128]{1,0:T(8,128)(2,1)}, bf16[256,128]{1,0:T(8,128)(2,1)S(1)}, u32[]{:S(2)}, u32[]{:S(2)}) collective-permute-start(bf16[256,128]{1,0:T(8,128)(2,1)} %bitcast.17), channel_id=1, source_target_pairs={{1,0},{2,1},{3,2},{4,3},{5,4},{6,5},{7,6},{8,7},{9,8},{10,9},{11,1... | collective-permute-start | bytes 196616 | tf_op jit(solution)/shard_map/ppermute | solution.py:308
  18.3 1.5 copy-start
  19.8 0.9 copy-start.5
  20.7 0.8 copy-start.6
  21.6 0.7 copy-start.9
  23.9 31.0 %copy-start.7 = (bf16[1,432,54]{1,2,0:T(8,128)(2,1)S(1)}, bf16[1,432,54]{1,2,0:T(8,128)(2,1)}, u32[]{:S(2)}) copy-start(bf16[1,432,54]{1,2,0:T(8,128)(2,1)} %param.13) | copy-start | bytes 139972
  23.9 31.0 %copy-start.11 = (f32[54]{0:T(128)S(1)}, f32[54]{0:T(128)}, u32[]{:S(2)}) copy-start(f32[54]{0:T(128)} %param.16) | copy-start | bytes 652
  43.9 78.2 %copy-start.8 = (s32[8]{0:T(128)S(1)}, s32[8]{0:T(128)}, u32[]{:S(2)}) copy-start(s32[8]{0:T(128)} %owner_ref.3) | copy-start | bytes 100
  43.9 26.6 %all-to-all-start.1 = ((bf16[16,64,128]{2,1,0:T(8,128)(2,1)}), bf16[16,64,128]{2,1,0:T(8,128)(2,1)S(1)}, u32[]{:S(2)}, u32[]{:S(2)}) async-start(bf16[16,64,128]{2,1,0:T(8,128)(2,1)} %shard_map.106), calls=%async_computation.1 | async-start | bytes 524288 | tf_op jit(solution)/shard_map/all_to_all | solution.py:52
  54.9 62.5 %all-gather.3.cloned.1.call-start = ((), (), s32[]{:S(2)}) async-start(), calls=%async_computation.7 | async-start | bytes 1310720 | tf_op jit(solution)/shard_map/all_gather | solution.py:361
  55.2 11.3 %collective-permute-start.4 = (bf16[4,64,128]{2,1,0:T(8,128)(2,1)S(1)}, bf16[4,64,128]{2,1,0:T(8,128)(2,1)S(1)}, u32[]{:S(2)}, u32[]{:S(2)}) collective-permute-start(bf16[4,64,128]{2,1,0:T(8,128)(2,1)S(1)} %shard_map.109), channel_id=1, source_target_pairs={{0,0},{8,128},{16,256},{24,384},{64,64},{72,192},{80,320},{88,448}... | collective-permute-start | bytes 196616 | tf_op jit(solution)/shard_map/ppermute | solution.py:315
  55.9 13.8 %collective-permute-start.5 = (bf16[4,64,128]{2,1,0:T(8,128)(2,1)S(1)}, bf16[4,64,128]{2,1,0:T(8,128)(2,1)S(1)}, u32[]{:S(2)}, u32[]{:S(2)}) collective-permute-start(bf16[4,64,128]{2,1,0:T(8,128)(2,1)S(1)} %shard_map.109), channel_id=1, source_target_pairs={{0,64},{8,192},{16,320},{24,448},{64,0},{72,128},{80,256},{88,384}... | collective-permute-start | bytes 196616 | tf_op jit(solution)/shard_map/ppermute | solution.py:315
  93.2 44.2 %copy-start.4 = (f32[256,256]{1,0:T(8,128)S(1)}, f32[256,256]{1,0:T(8,128)}, u32[]{:S(2)}) copy-start(f32[256,256]{1,0:T(8,128)} %out_basis_any.1) | copy-start | bytes 786436
  93.2 44.2 %copy-start.10 = (f32[256]{0:T(256)S(1)}, f32[256]{0:T(256)}, u32[]{:S(2)}) copy-start(f32[256]{0:T(256)} %param.17) | copy-start | bytes 3076
  93.3 28.9 %all-to-all-start.3 = ((bf16[32,64,128]{2,1,0:T(8,128)(2,1)}), bf16[32,64,128]{2,1,0:T(8,128)(2,1)S(1)}, u32[]{:S(2)}, u32[]{:S(2)}) async-start(bf16[32,64,128]{2,1,0:T(8,128)(2,1)} %shard_map.108), calls=%async_computation.3 | async-start | bytes 1048576 | tf_op jit(solution)/shard_map/all_to_all | solution.py:52
  122.2 1.2 copy-start.2
  123.4 14.0 %copy-start.3 = (bf16[16,4,64,128]{3,2,1,0:T(8,128)(2,1)S(1)}, bf16[16,4,64,128]{3,2,1,0:T(8,128)(2,1)}, u32[]{:S(2)}) copy-start(bf16[16,4,64,128]{3,2,1,0:T(8,128)(2,1)} %all-gather.3.cloned.1.call-done) | copy-start | bytes 3145732
  137.4 29.7 %copy-start.1 = (bf16[3456,256]{1,0:T(8,128)(2,1)S(1)}, bf16[3456,256]{1,0:T(8,128)(2,1)}, u32[]{:S(2)}) copy-start(bf16[3456,256]{1,0:T(8,128)(2,1)} %weight_any.3) | copy-start | bytes 5308420
  154.4 21.2 %all-to-all-start.6 = ((bf16[8,112,128]{2,1,0:T(8,128)(2,1)}), bf16[8,112,128]{2,1,0:T(8,128)(2,1)S(1)}, u32[]{:S(2)}, u32[]{:S(2)}) async-start(bf16[8,112,128]{2,1,0:T(8,128)(2,1)} %shard_map.113), calls=%async_computation.6 | async-start | bytes 458752 | tf_op jit(solution)/shard_map/all_to_all | solution.py:52
  157.8 5.0 %collective-permute-start.2 = (bf16[256,256]{1,0:T(8,128)(2,1)S(1)}, bf16[256,256]{1,0:T(8,128)(2,1)S(1)}, u32[]{:S(2)}, u32[]{:S(2)}) collective-permute-start(bf16[256,256]{1,0:T(8,128)(2,1)S(1)} %get-tuple-element.4.mine_ref.after_ref), channel_id=1, source_target_pairs={{0,1},{1,2},{2,3},{3,4},{4,5},{5,6},{6,7},{7,8},{8,9},{9,10},{10,1... | collective-permute-start | bytes 393224 | tf_op jit(solution)/shard_map/ppermute | solution.py:308
  160.8 6.3 %collective-permute-start.3 = (bf16[256,256]{1,0:T(8,128)(2,1)S(1)}, bf16[256,256]{1,0:T(8,128)(2,1)S(1)}, u32[]{:S(2)}, u32[]{:S(2)}) collective-permute-start(bf16[256,256]{1,0:T(8,128)(2,1)S(1)} %get-tuple-element.4.mine_ref.after_ref), channel_id=1, source_target_pairs={{1,0},{2,1},{3,2},{4,3},{5,4},{6,5},{7,6},{8,7},{9,8},{10,9},{11,1... | collective-permute-start | bytes 393224 | tf_op jit(solution)/shard_map/ppermute | solution.py:308
Sparse Core Ops, SparseCore 0:
  70.6 46.6 all-gather.2

commit v3 on v2

--- a/solution.py
+++ b/solution.py
@@ -22,16 +22,21 @@
 SPACE = ("zg", "zl", "x", "c")
 
 
-def call(body, out_shape, scalars=(), arrays=(), remote=(), scratch=(), flops=0):
+def call(body, out_shape, scalars=(), arrays=(), remote=(), after=(), scratch=(), flops=0, limit=LIMIT):
     many = isinstance(out_shape, (list, tuple))
-    inputs = (*scalars, *arrays, *remote)
+    inputs = (*scalars, *arrays, *remote, *after)
+    kept = len(inputs) - len(after)
+
+    def kernel(*refs):
+        body(*refs[:kept], *refs[len(inputs) :])
+
     return pl.pallas_call(
-        body,
+        kernel,
         out_shape=out_shape,
-        in_specs=[SMEM] * len(scalars) + [VMEM] * len(arrays) + [ANY] * len(remote),
+        in_specs=[SMEM] * len(scalars) + [VMEM] * len(arrays) + [ANY] * (len(remote) + len(after)),
         out_specs=[VMEM] * len(out_shape) if many else VMEM,
         scratch_shapes=list(scratch),
-        compiler_params=pltpu.CompilerParams(vmem_limit_bytes=LIMIT),
+        compiler_params=pltpu.CompilerParams(vmem_limit_bytes=limit),
         cost_estimate=pl.CostEstimate(
             flops=flops,
             bytes_accessed=sum(a.size * a.dtype.itemsize for a in inputs),
@@ -88,7 +93,7 @@
         out_ref[r] = block.astype(BF16)
 
 
-def pack_body(own_ref, other_ref, after_ref, out_ref):
+def pack_body(own_ref, other_ref, out_ref):
     out_ref[0] = own_ref[...]
     out_ref[1] = other_ref[...]
     out_ref[2] = own_ref[...]
@@ -190,12 +195,15 @@
     return owner >> 1, (owner & 1) ^ zh
 
 
-def rotate_body(owner_ref, place_ref, got_ref, basis_any, out_ref, basis, grads, ordered, sems):
+def rotate_body(owner_ref, place_ref, got_ref, basis_any, out_ref, panels_ref, basis, grads, ordered, sems):
     zh, zl = place_ref[0], place_ref[1]
     copies = []
     for j in range(8):
         first, second = slot_of(owner_ref[j], zh)
         copies.append(pltpu.make_async_copy(basis_any.at[first, second, zl], basis.at[j], sems.at[j]))
+    for g in range(2):
+        first, second = slot_of(owner_ref[zl + 4 * g], zh)
+        copies.append(pltpu.make_async_copy(basis_any.at[first, second], panels_ref.at[g], sems.at[8 + g]))
     started(copies)
     for y in range(4):
         for x in range(4):
@@ -215,20 +223,17 @@
         total = total + jnp.dot(block, rows, preferred_element_type=F32)
     for to in range(4):
         out_ref[to] = total[:56]
+    for copy in copies[8:]:
+        copy.wait()
 
 
 def update_body(
-    owner_ref, place_ref, got_ref, basis_any, out_basis_any, out_eigen_any,
-    out_ref, basis, out_basis, out_eigen, ordered, sems,
+    got_ref, basis, out_basis_any, out_eigen_any, out_ref, out_basis, out_eigen, ordered, sems
 ):
-    zh, zl = place_ref[0], place_ref[1]
     copies = [
         pltpu.make_async_copy(out_basis_any, out_basis, sems.at[0]),
         pltpu.make_async_copy(out_eigen_any, out_eigen, sems.at[1]),
     ]
-    for g in range(2):
-        first, second = slot_of(owner_ref[zl + 4 * g], zh)
-        copies.append(pltpu.make_async_copy(basis_any.at[first, second], basis.at[g], sems.at[2 + g]))
     started(copies)
     highest = lax.Precision.HIGHEST
     rotated = (got_ref[0] + got_ref[1]) + (got_ref[2] + got_ref[3])
@@ -273,7 +278,7 @@
     out_ref[...] = jnp.concatenate([total[:54], total[56:110]], axis=1)
 
 
-def data_grad_body(low_ref, high_ref, mine_ref, weight_any, out_ref, weight, sem):
+def data_grad_body(low_ref, high_ref, mine_ref, weight_any, out_ref, token_ref, weight, sem):
     copy = pltpu.make_async_copy(weight_any, weight, sem)
     copy.start()
     none = jnp.zeros((16, 256), BF16)
@@ -299,6 +304,7 @@
                     preferred_element_type=F32,
                 )
     out_ref[...] = total.astype(BF16)
+    token_ref[...] = jnp.zeros((8, 128), F32)
 
 
 def neighbours(block):
@@ -338,6 +344,7 @@
         arrays=(basis_panels[0].T,),
         remote=(input_eigen.reshape(1, 54),),
         scratch=[pltpu.VMEM((1, 54), F32), dma],
+        flops=4_000_000_000,
     )
     own, other = turned(stored, 0), turned(stored, 1)
 
@@ -347,6 +354,7 @@
         (inner,),
         (low, high),
         (plane, conv_weight, conv_bias.reshape(1, 256), cotangent.reshape(256, 256)),
+        (own,),
         [
             pltpu.VMEM((256, 3456), BF16),
             pltpu.VMEM((256, 128), BF16),
@@ -357,53 +365,55 @@
         ],
         flops=2 * 256 * 3456 * 256,
     )
-    packed = call(pack_body, shape((4, 4, 64, 128), BF16), arrays=(own, other), remote=(delta,))
-    basis = lax.all_gather(packed, "zl")
     delta_low, delta_high = neighbours(delta)
     got = exchange(send, XC)
     part = call(
         weight_grad_body,
         shape((16, 64, 128), BF16),
         arrays=(got,),
+        after=(other, delta_low, delta_high),
         scratch=[pltpu.VMEM((288, 2560), BF16), pltpu.VMEM((2048, 128), BF16), pltpu.VMEM((864, 128), F32)],
         flops=2 * 864 * 2048 * 128,
     )
-    part = call(over_y_zl_body, shape((4, 64, 128), BF16), arrays=(exchange(part, ("y", "zl")),))
+    packed = call(pack_body, shape((4, 4, 64, 128), BF16), arrays=(own, other), after=(part,))
+    basis = lax.all_gather(packed, "zl")
+    data, token = call(
+        data_grad_body,
+        [shape((256, 128), BF16), shape((8, 128), F32)],
+        arrays=(delta_low, delta_high, delta),
+        remote=(conv_weight,),
+        after=(part,),
+        scratch=[pltpu.VMEM((3456, 256), BF16), dma],
+        flops=2 * 256 * 3456 * 256,
+    )
+    part = call(over_y_zl_body, shape((4, 64, 128), BF16), arrays=(exchange(part, ("y", "zl")),), after=(token,))
     part = call(over_zh_zg_body, shape((32, 64, 128), BF16), arrays=(exchange(part, ("zh", "zg")),))
     grads = exchange(part, YXC)
-    data = call(
-        data_grad_body,
-        shape((256, 128), BF16),
-        arrays=(delta_low, delta_high, delta),
-        remote=(conv_weight,),
-        scratch=[pltpu.VMEM((3456, 256), BF16), dma],
-        flops=2 * 256 * 3456 * 256,
-    )
-    rotated = call(
+    rotated, panels = call(
         rotate_body,
-        shape((4, 56, 256), F32),
+        [shape((4, 56, 256), F32), shape((2, 4, 64, 128), BF16)],
         (panel_owner, place),
         (grads,),
         (basis,),
-        [
+        scratch=[
             pltpu.VMEM((8, 64, 128), BF16),
             pltpu.VMEM((2, 1024, 128), F32),
             pltpu.VMEM((896, 256), F32),
-            dma((8,)),
+            dma((10,)),
         ],
+        limit=LIMIT + 15_000_000,
     )
     part = call(
         update_body,
         shape((8, 112, 256), BF16),
-        (panel_owner, place),
-        (exchange(rotated, "zl"),),
-        (basis, output_basis, output_eigen.reshape(1, 256)),
-        [
-            pltpu.VMEM((2, 4, 64, 128), BF16),
+        (),
+        (exchange(rotated, "zl"), panels),
+        (output_basis, output_eigen.reshape(1, 256)),
+        scratch=[
             pltpu.VMEM((256, 256), F32),
             pltpu.VMEM((1, 256), F32),
             pltpu.VMEM((2, 2, 440, 128), F32),
-            dma((4,)),
+            dma((2,)),
         ],
     )
     part = call(over_xc_body, shape((8, 112, 128), BF16), arrays=(exchange(part, XC),))

time: 184 us -> 183 us (level)
  starting transfers between devices: 58 us -> 64.3 us
  waiting for transfers between devices: 26.4 us -> 20.2 us
  local copies, waits for them, and re-layouts: 5.16 us -> 3.19 us
    ppermute x2, starting transfers between devices: 11.3 us -> 16.2 us  [turned(): return lax.ppermute(block, ('y', 'zh', 'zl'), pairs)]
    all_gather x1, waiting for transfers between devices: 6.68 us -> 2.11 us  [per_device(): basis = lax.all_gather(packed, 'zl')]
    ppermute x4, waiting for transfers between devices: 5.43 us -> 0.86 us  [neighbours(): return (lax.ppermute(block, SPACE, up), lax.ppermute(block, SPACE, down))]
    all_to_all x3, waiting for transfers between devices: 11.1 us -> 15.5 us  [exchange(): return lax.all_to_all(x, axes, 0, 0)]
    unnamed x24 -> x20, local copies, waits for them, and re-layouts: 5.16 us -> 3.19 us
  transfers between devices with their start and end apart: 10 -> 10, of which waited for: 6 -> 5; matrix products, arithmetic and copies ran while one was open for 0% -> 0% of each run, Pallas kernels for 2% -> 2%
where the time goes in v3:
time: 183 us; the launch traced here: 182 us
  blocking collectives  65.9 us (36%)
  starting transfers between devices  64.3 us (35%)
  waiting for transfers between devices  20.2 us (11%)
  between operations  14.2 us (8%)
  Pallas kernels  14.1 us (8%)
  local copies, waits for them, and re-layouts  3.19 us (2%)
    all_to_all x4, blocking collectives, exchange(): return lax.all_to_all(x, axes, 0, 0)  65.9 us
    all_to_all x3, starting transfers between devices, exchange(): return lax.all_to_all(x, axes, 0, 0)  32.5 us
    ppermute x2, starting transfers between devices, turned(): return lax.ppermute(block, ('y', 'zh', 'zl'), pairs)  16.2 us
    all_to_all x3, waiting for transfers between devices, exchange(): return lax.all_to_all(x, axes, 0, 0)  15.5 us
    ppermute x4, starting transfers between devices, neighbours(): return (lax.ppermute(block, SPACE, up), lax.ppermute(block, SPACE, down))  15.5 us
    pallas_call x11, Pallas kernels, call(): pl.pallas_call(kernel, out_shape=out_shape, in_specs=[SMEM] * len(scalars...  14.1 us
  transfers between devices with their start and end apart: 10, of which 5 were waited for; matrix products, arithmetic and copies ran while one was open for 0% of the time, Pallas kernels for 2%

profile of v3, /device:TPU:1, one launch (start us, length us, event | category | flops | bytes accessed | tf_op | source)
XLA Modules:
  0.0 182.5 jit_solution(11900818169042157479)
XLA Ops:
  7.2 0.8 copy-done.7
  8.0 0.7 copy-done.8
  8.7 0.3 shard_map.104
  9.0 0.8 collective-permute-start.2
  9.8 4.5 %collective-permute-start = (bf16[256,128]{1,0:T(8,128)(2,1)S(1)}, bf16[256,128]{1,0:T(8,128)(2,1)S(1)}, u32[]{:S(2)}, u32[]{:S(2)}) collective-permute-start(bf16[256,128]{1,0:T(8,128)(2,1)S(1)} %bitcast.14), channel_id=1, source_target_pairs={{0,1},{1,2},{2,3},{3,4},{4,5},{5,6},{6,7},{7,8},{8,9},{9,10},{10,1... | collective-permute-start | bytes 196616 | tf_op jit(solution)/shard_map/ppermute | solution.py:314
  14.3 5.6 %collective-permute-start.1 = (bf16[256,128]{1,0:T(8,128)(2,1)S(1)}, bf16[256,128]{1,0:T(8,128)(2,1)S(1)}, u32[]{:S(2)}, u32[]{:S(2)}) collective-permute-start(bf16[256,128]{1,0:T(8,128)(2,1)S(1)} %bitcast.15), channel_id=1, source_target_pairs={{1,0},{2,1},{3,2},{4,3},{5,4},{6,5},{7,6},{8,7},{9,8},{10,9},{11,1... | collective-permute-start | bytes 196616 | tf_op jit(solution)/shard_map/ppermute | solution.py:314
  19.9 0.9 collective-permute-done.1.refs_2_
  20.8 2.5 %shard_map.105 = (bf16[256,256]{1,0:T(8,128)(2,1)S(1)}, bf16[8,384,128]{2,1,0:T(8,128)(2,1)}) custom-call(s32[1]{0:T(128)} %bitcast.refs_0_, bf16[256,128]{1,0:T(8,128)(2,1)S(1)} %collective-permute-done.refs_1_, bf16[256,128]{1,0:T(8,128)(2,1)S(1)} %collective-permute-done.1.refs_2_, bf16[256,128]{1,0:T(8,128)(2,1)S(1)} %bitcast.16, ...), custom_call_target="tpu_custom_call" | custom-call | flops 452984832 | bytes 2163716 | tf_op jit(solution)/shard_map/pallas_call | solution.py:33
  23.3 8.1 %all-to-all-start = ((bf16[8,384,128]{2,1,0:T(8,128)(2,1)}), bf16[8,384,128]{2,1,0:T(8,128)(2,1)S(1)}, u32[]{:S(2)}, u32[]{:S(2)}) async-start(bf16[8,384,128]{2,1,0:T(8,128)(2,1)} %get-tuple-element.9), calls=%async_computation | async-start | bytes 1572864 | tf_op jit(solution)/shard_map/all_to_all | solution.py:57
  31.4 3.5 %collective-permute-start.3 = (bf16[256,256]{1,0:T(8,128)(2,1)S(1)}, bf16[256,256]{1,0:T(8,128)(2,1)S(1)}, u32[]{:S(2)}, u32[]{:S(2)}) collective-permute-start(bf16[256,256]{1,0:T(8,128)(2,1)S(1)} %get-tuple-element.8.refs_2_), channel_id=1, source_target_pairs={{0,1},{1,2},{2,3},{3,4},{4,5},{5,6},{6,7},{7,8},{8,9},{9,10},{10,1... | collective-permute-start | bytes 393224 | tf_op jit(solution)/shard_map/ppermute | solution.py:314
  35.0 1.9 %collective-permute-start.4 = (bf16[256,256]{1,0:T(8,128)(2,1)S(1)}, bf16[256,256]{1,0:T(8,128)(2,1)S(1)}, u32[]{:S(2)}, u32[]{:S(2)}) collective-permute-start(bf16[256,256]{1,0:T(8,128)(2,1)S(1)} %get-tuple-element.8.refs_2_), channel_id=1, source_target_pairs={{1,0},{2,1},{3,2},{4,3},{5,4},{6,5},{7,6},{8,7},{9,8},{10,9},{11,1... | collective-permute-start | bytes 393224 | tf_op jit(solution)/shard_map/ppermute | solution.py:314
  36.9 15.4 %collective-permute-start.5 = (bf16[4,64,128]{2,1,0:T(8,128)(2,1)S(1)}, bf16[4,64,128]{2,1,0:T(8,128)(2,1)S(1)}, u32[]{:S(2)}, u32[]{:S(2)}) collective-permute-start(bf16[4,64,128]{2,1,0:T(8,128)(2,1)S(1)} %shard_map.104), channel_id=1, source_target_pairs={{0,64},{8,192},{16,320},{24,448},{64,0},{72,128},{80,256},{88,384}... | collective-permute-start | bytes 196616 | tf_op jit(solution)/shard_map/ppermute | solution.py:321
  52.3 1.7 collective-permute-done.5.refs_1_
  54.0 2.2 %shard_map.106.refs_4_.refs_2_ = bf16[16,64,128]{2,1,0:T(8,128)(2,1)} custom-call(bf16[8,384,128]{2,1,0:T(8,128)(2,1)S(1)} %all-to-all-done.refs_0_, bf16[4,64,128]{2,1,0:T(8,128)(2,1)S(1)} %collective-permute-done.5.refs_1_, bf16[256,256]{1,0:T(8,128)(2,1)S(1)} %collective-permute-done.3.refs_2_.refs_0_, ...), custom_call_target="tpu_custom_call" | custom-call | flops 452984832 | bytes 1114112 | tf_op jit(solution)/shard_map/pallas_call | solution.py:33
  56.2 16.1 %all-to-all-start.1 = ((bf16[16,64,128]{2,1,0:T(8,128)(2,1)}), bf16[16,64,128]{2,1,0:T(8,128)(2,1)S(1)}, u32[]{:S(2)}, u32[]{:S(2)}) async-start(bf16[16,64,128]{2,1,0:T(8,128)(2,1)} %shard_map.106.refs_4_.refs_2_), calls=%async_computation.1 | async-start | bytes 524288 | tf_op jit(solution)/shard_map/all_to_all | solution.py:57
  72.4 0.8 shard_map.110
  73.2 2.1 %shard_map.107 = (bf16[256,128]{1,0:T(8,128)(2,1)}, f32[8,128]{1,0:T(8,128)S(1)}) custom-call(bf16[256,256]{1,0:T(8,128)(2,1)S(1)} %collective-permute-done.3.refs_2_.refs_0_, bf16[256,256]{1,0:T(8,128)(2,1)S(1)} %collective-permute-done.4.refs_3_.refs_1_, bf16[256,256]{1,0:T(8,128)(2,1)S(1)} %get-tuple-element.8.refs_2_, bf16[3456,256]{1,0:T(8,128)(2,1)S(1)} %copy-done, ...), custom_call_target="tpu_custom_call" | custom-call | flops 452984832 | bytes 2424832 | tf_op jit(solution)/shard_map/pallas_call | solution.py:33
  75.3 6.8 %all-to-all-done.1.refs_0_ = bf16[16,64,128]{2,1,0:T(8,128)(2,1)S(1)} async-done(((bf16[16,64,128]{2,1,0:T(8,128)(2,1)}), bf16[16,64,128]{2,1,0:T(8,128)(2,1)S(1)}, u32[]{:S(2)}, u32[]{:S(2)}) %all-to-all-start.1) | async-done | bytes 262176 | tf_op jit(solution)/shard_map/all_to_all | solution.py:57
  82.1 22.0 %all_to_all.35.refs_0_ = bf16[4,64,128]{2,1,0:T(8,128)(2,1)S(1)} all-to-all(bf16[4,64,128]{2,1,0:T(8,128)(2,1)S(1)} %shard_map.108), channel_id=1, replica_groups=mesh['y'=4,'zh'=2,'zg'=2,'zl'=4,'x'=4,'c'=2] {'zh','zg'}, dimensions={0} | all-to-all | bytes 131072 | tf_op jit(solution)/shard_map/all_to_all | solution.py:57
  104.1 0.9 shard_map.109
  105.0 8.2 %all-to-all-start.3 = ((bf16[32,64,128]{2,1,0:T(8,128)(2,1)}), bf16[32,64,128]{2,1,0:T(8,128)(2,1)S(1)}, u32[]{:S(2)}, u32[]{:S(2)}) async-start(bf16[32,64,128]{2,1,0:T(8,128)(2,1)} %shard_map.109), calls=%async_computation.3 | async-start | bytes 1048576 | tf_op jit(solution)/shard_map/all_to_all | solution.py:57
  113.2 0.7 pad_add_fusion.refs_1_
  113.9 2.1 %all-gather.3.cloned.1.call-done = bf16[16,4,64,128]{3,2,1,0:T(8,128)(2,1)} async-done(((bf16[4,4,64,128]{3,2,1,0:T(8,128)(2,1)}), bf16[16,4,64,128]{3,2,1,0:T(8,128)(2,1)}) %all-gather.3.cloned.1.call-update) | async-done | bytes 1048592 | tf_op jit(solution)/shard_map/all_gather | solution.py:379
  116.0 8.8 %all-to-all-done.3.refs_2_ = bf16[32,64,128]{2,1,0:T(8,128)(2,1)S(1)} async-done(((bf16[32,64,128]{2,1,0:T(8,128)(2,1)}), bf16[32,64,128]{2,1,0:T(8,128)(2,1)S(1)}, u32[]{:S(2)}, u32[]{:S(2)}) %all-to-all-start.3) | async-done | bytes 524320 | tf_op jit(solution)/shard_map/all_to_all | solution.py:57
  124.8 0.8 copy-done.9
  125.6 3.2 %shard_map.111 = (f32[4,56,256]{2,1,0:T(8,128)}, bf16[2,4,64,128]{3,2,1,0:T(8,128)(2,1)}) custom-call(s32[8]{0:T(128)} %refs_0_.1, s32[2]{0:T(128)} %pad_add_fusion.refs_1_, bf16[32,64,128]{2,1,0:T(8,128)(2,1)} %copy-done.9, bf16[4,4,4,64,128]{4,3,2,1,0:T(8,128)(2,1)} %bitcast.21), custom_call_target="tpu_custom_call" | custom-call | bytes 1572904 | tf_op jit(solution)/shard_map/pallas_call | solution.py:33
  128.7 9.8 %all_to_all.36.refs_0_ = f32[4,56,256]{2,1,0:T(8,128)S(1)} all-to-all(f32[4,56,256]{2,1,0:T(8,128)} %get-tuple-element.12), channel_id=1, replica_groups=mesh['y'=4,'zh'=2,'zg'=2,'zl'=4,'x'=4,'c'=2] {'zl'}, dimensions={0} | all-to-all | bytes 458752 | tf_op jit(solution)/shard_map/all_to_all | solution.py:57
  138.5 0.9 copy-done.3
  139.4 1.4 shard_map.112
  140.8 14.0 %all_to_all.37.refs_0_ = bf16[8,112,256]{2,1,0:T(8,128)(2,1)S(1)} all-to-all(bf16[8,112,256]{2,1,0:T(8,128)(2,1)S(1)} %shard_map.112), channel_id=1, replica_groups=mesh['y'=4,'zh'=2,'zg'=2,'zl'=4,'x'=4,'c'=2] {'x','c'}, dimensions={0} | all-to-all | bytes 917504 | tf_op jit(solution)/shard_map/all_to_all | solution.py:57
  154.9 20.1 %all_to_all.38.refs_0_ = bf16[8,112,128]{2,1,0:T(8,128)(2,1)S(1)} all-to-all(bf16[8,112,128]{2,1,0:T(8,128)(2,1)S(1)} %shard_map.113), channel_id=1, replica_groups=mesh['y'=4,'zh'=2,'zg'=2,'zl'=4,'x'=4,'c'=2] {'zg','y'}, dimensions={0} | all-to-all | bytes 458752 | tf_op jit(solution)/shard_map/all_to_all | solution.py:57
  175.0 0.7 shard_map.114
  (25 shorter events, 0.2 us)
Async XLA Ops:
  7.2 0.8 copy-start.7
  8.0 0.7 copy-start.8
  8.6 1.1 copy-start.4
  8.6 12.1 %copy-start = (bf16[3456,256]{1,0:T(8,128)(2,1)S(1)}, bf16[3456,256]{1,0:T(8,128)(2,1)}, u32[]{:S(2)}) copy-start(bf16[3456,256]{1,0:T(8,128)(2,1)} %refs_3_.1) | copy-start | bytes 5308420
  8.6 12.1 %copy-start.2 = (bf16[1,1,16,16,256]{4,3,2,1,0:T(8,128)(2,1)S(1)}, bf16[1,1,16,16,256]{4,3,2,1,0:T(8,128)(2,1)}, u32[]{:S(2)}) copy-start(bf16[1,1,16,16,256]{4,3,2,1,0:T(8,128)(2,1)} %param.12) | copy-start | bytes 393220
  8.6 12.1 %copy-start.5 = (f32[256]{0:T(256)S(1)}, f32[256]{0:T(256)}, u32[]{:S(2)}) copy-start(f32[256]{0:T(256)} %param.11) | copy-start | bytes 3076
  9.0 10.9 %collective-permute-start.2 = (bf16[4,64,128]{2,1,0:T(8,128)(2,1)S(1)}, bf16[4,64,128]{2,1,0:T(8,128)(2,1)S(1)}, u32[]{:S(2)}, u32[]{:S(2)}) collective-permute-start(bf16[4,64,128]{2,1,0:T(8,128)(2,1)S(1)} %shard_map.104), channel_id=1, source_target_pairs={{0,0},{8,128},{16,256},{24,384},{64,64},{72,192},{80,320},{88,448}... | collective-permute-start | bytes 196616 | tf_op jit(solution)/shard_map/ppermute | solution.py:321
  9.8 10.1 %collective-permute-start = (bf16[256,128]{1,0:T(8,128)(2,1)S(1)}, bf16[256,128]{1,0:T(8,128)(2,1)S(1)}, u32[]{:S(2)}, u32[]{:S(2)}) collective-permute-start(bf16[256,128]{1,0:T(8,128)(2,1)S(1)} %bitcast.14), channel_id=1, source_target_pairs={{0,1},{1,2},{2,3},{3,4},{4,5},{5,6},{6,7},{7,8},{8,9},{9,10},{10,1... | collective-permute-start | bytes 196616 | tf_op jit(solution)/shard_map/ppermute | solution.py:314
  14.3 6.5 %collective-permute-start.1 = (bf16[256,128]{1,0:T(8,128)(2,1)S(1)}, bf16[256,128]{1,0:T(8,128)(2,1)S(1)}, u32[]{:S(2)}, u32[]{:S(2)}) collective-permute-start(bf16[256,128]{1,0:T(8,128)(2,1)S(1)} %bitcast.15), channel_id=1, source_target_pairs={{1,0},{2,1},{3,2},{4,3},{5,4},{6,5},{7,6},{8,7},{9,8},{10,9},{11,1... | collective-permute-start | bytes 196616 | tf_op jit(solution)/shard_map/ppermute | solution.py:314
  23.3 30.7 %all-to-all-start = ((bf16[8,384,128]{2,1,0:T(8,128)(2,1)}), bf16[8,384,128]{2,1,0:T(8,128)(2,1)S(1)}, u32[]{:S(2)}, u32[]{:S(2)}) async-start(bf16[8,384,128]{2,1,0:T(8,128)(2,1)} %get-tuple-element.9), calls=%async_computation | async-start | bytes 1572864 | tf_op jit(solution)/shard_map/all_to_all | solution.py:57
  31.4 22.6 %collective-permute-start.3 = (bf16[256,256]{1,0:T(8,128)(2,1)S(1)}, bf16[256,256]{1,0:T(8,128)(2,1)S(1)}, u32[]{:S(2)}, u32[]{:S(2)}) collective-permute-start(bf16[256,256]{1,0:T(8,128)(2,1)S(1)} %get-tuple-element.8.refs_2_), channel_id=1, source_target_pairs={{0,1},{1,2},{2,3},{3,4},{4,5},{5,6},{6,7},{7,8},{8,9},{9,10},{10,1... | collective-permute-start | bytes 393224 | tf_op jit(solution)/shard_map/ppermute | solution.py:314
  35.0 19.1 %collective-permute-start.4 = (bf16[256,256]{1,0:T(8,128)(2,1)S(1)}, bf16[256,256]{1,0:T(8,128)(2,1)S(1)}, u32[]{:S(2)}, u32[]{:S(2)}) collective-permute-start(bf16[256,256]{1,0:T(8,128)(2,1)S(1)} %get-tuple-element.8.refs_2_), channel_id=1, source_target_pairs={{1,0},{2,1},{3,2},{4,3},{5,4},{6,5},{7,6},{8,7},{9,8},{10,9},{11,1... | collective-permute-start | bytes 393224 | tf_op jit(solution)/shard_map/ppermute | solution.py:314
  36.9 17.1 %collective-permute-start.5 = (bf16[4,64,128]{2,1,0:T(8,128)(2,1)S(1)}, bf16[4,64,128]{2,1,0:T(8,128)(2,1)S(1)}, u32[]{:S(2)}, u32[]{:S(2)}) collective-permute-start(bf16[4,64,128]{2,1,0:T(8,128)(2,1)S(1)} %shard_map.104), channel_id=1, source_target_pairs={{0,64},{8,192},{16,320},{24,448},{64,0},{72,128},{80,256},{88,384}... | collective-permute-start | bytes 196616 | tf_op jit(solution)/shard_map/ppermute | solution.py:321
  56.2 25.8 %all-to-all-start.1 = ((bf16[16,64,128]{2,1,0:T(8,128)(2,1)}), bf16[16,64,128]{2,1,0:T(8,128)(2,1)S(1)}, u32[]{:S(2)}, u32[]{:S(2)}) async-start(bf16[16,64,128]{2,1,0:T(8,128)(2,1)} %shard_map.106.refs_4_.refs_2_), calls=%async_computation.1 | async-start | bytes 524288 | tf_op jit(solution)/shard_map/all_to_all | solution.py:57
  72.3 43.7 %all-gather.3.cloned.1.call-start = ((), (), s32[]{:S(2)}) async-start(), calls=%async_computation.7 | async-start | bytes 1310720 | tf_op jit(solution)/shard_map/all_gather | solution.py:379
  104.1 34.4 %copy-start.1 = (f32[256,256]{1,0:T(8,128)S(1)}, f32[256,256]{1,0:T(8,128)}, u32[]{:S(2)}) copy-start(f32[256,256]{1,0:T(8,128)} %refs_2_.1) | copy-start | bytes 786436
  104.1 34.4 %copy-start.6 = (f32[256]{0:T(256)S(1)}, f32[256]{0:T(256)}, u32[]{:S(2)}) copy-start(f32[256]{0:T(256)} %param.17) | copy-start | bytes 3076
  105.0 19.8 %all-to-all-start.3 = ((bf16[32,64,128]{2,1,0:T(8,128)(2,1)}), bf16[32,64,128]{2,1,0:T(8,128)(2,1)S(1)}, u32[]{:S(2)}, u32[]{:S(2)}) async-start(bf16[32,64,128]{2,1,0:T(8,128)(2,1)} %shard_map.109), calls=%async_computation.3 | async-start | bytes 1048576 | tf_op jit(solution)/shard_map/all_to_all | solution.py:57
  124.8 0.8 copy-start.9
  138.5 0.9 copy-start.3
Sparse Core Ops, SparseCore 0:
  75.3 40.6 all-gather.2

commit v4 on v3

--- a/solution.py
+++ b/solution.py
@@ -93,16 +93,9 @@
         out_ref[r] = block.astype(BF16)
 
 
-def pack_body(own_ref, other_ref, out_ref):
-    out_ref[0] = own_ref[...]
-    out_ref[1] = other_ref[...]
-    out_ref[2] = own_ref[...]
-    out_ref[3] = other_ref[...]
-
-
 def forward_body(
-    place_ref, low_ref, high_ref, mine_any, weight_any, bias_any, cot_any,
-    delta_ref, send_ref, patches, mine, weight, bias, cot, sems,
+    place_ref, low_ref, high_ref, basis_ref, mine_any, weight_any, bias_any, cot_any,
+    delta_ref, send_ref, twice_ref, patches, mine, weight, bias, cot, sems,
 ):
     copies = started(
         [
@@ -112,6 +105,8 @@
             )
         ]
     )
+    twice_ref[0] = basis_ref[...]
+    twice_ref[1] = basis_ref[...]
     none = jnp.zeros((16, 128), BF16)
     for a in (0, 2, 1):
         if a == 1:
@@ -191,19 +186,19 @@
         out_ref[to] = total
 
 
-def slot_of(owner, zh):
-    return owner >> 1, (owner & 1) ^ zh
+def slot_of(owner):
+    return 4 * (owner & 1) + (owner >> 1)
 
 
 def rotate_body(owner_ref, place_ref, got_ref, basis_any, out_ref, panels_ref, basis, grads, ordered, sems):
-    zh, zl = place_ref[0], place_ref[1]
+    zl = place_ref[0]
     copies = []
     for j in range(8):
-        first, second = slot_of(owner_ref[j], zh)
-        copies.append(pltpu.make_async_copy(basis_any.at[first, second, zl], basis.at[j], sems.at[j]))
+        slot = slot_of(owner_ref[j])
+        copies.append(pltpu.make_async_copy(basis_any.at[slot, 0, zl], basis.at[j], sems.at[j]))
     for g in range(2):
-        first, second = slot_of(owner_ref[zl + 4 * g], zh)
-        copies.append(pltpu.make_async_copy(basis_any.at[first, second], panels_ref.at[g], sems.at[8 + g]))
+        slot = slot_of(owner_ref[zl + 4 * g])
+        copies.append(pltpu.make_async_copy(basis_any.at[slot, 0], panels_ref.at[g], sems.at[8 + g]))
     started(copies)
     for y in range(4):
         for x in range(4):
@@ -314,11 +309,8 @@
     return lax.ppermute(block, SPACE, up), lax.ppermute(block, SPACE, down)
 
 
-def turned(block, flip):
-    pairs = [
-        (8 * y + 4 * zh + z, 8 * z + 4 * (zh ^ flip) + y) for y in range(4) for zh in range(2) for z in range(4)
-    ]
-    return lax.ppermute(block, ("y", "zh", "zl"), pairs)
+def turned(block):
+    return lax.ppermute(block, ("y", "zl"), [(4 * y + z, 4 * z + y) for y in range(4) for z in range(4)])
 
 
 def per_device(
@@ -333,7 +325,7 @@
     output_eigen,
 ):
     dma = pltpu.SemaphoreType.DMA
-    place = jnp.stack([lax.axis_index("zh"), lax.axis_index("zl")]).astype(jnp.int32)
+    place = lax.axis_index("zl").astype(jnp.int32).reshape(1)
     inner = lax.axis_index(XC).astype(jnp.int32).reshape(1)
     plane = activations.reshape(256, 128)
     low, high = neighbours(plane)
@@ -346,16 +338,14 @@
         scratch=[pltpu.VMEM((1, 54), F32), dma],
         flops=4_000_000_000,
     )
-    own, other = turned(stored, 0), turned(stored, 1)
-
-    delta, send = call(
+
+    delta, send, twice = call(
         forward_body,
-        [shape((256, 256), BF16), shape((8, 384, 128), BF16)],
+        [shape((256, 256), BF16), shape((8, 384, 128), BF16), shape((2, 4, 64, 128), BF16)],
         (inner,),
-        (low, high),
+        (low, high, turned(stored)),
         (plane, conv_weight, conv_bias.reshape(1, 256), cotangent.reshape(256, 256)),
-        (own,),
-        [
+        scratch=[
             pltpu.VMEM((256, 3456), BF16),
             pltpu.VMEM((256, 128), BF16),
             pltpu.VMEM((3456, 256), BF16),
@@ -365,18 +355,17 @@
         ],
         flops=2 * 256 * 3456 * 256,
     )
+    basis = lax.all_gather(twice, ("zh", "zl"))
     delta_low, delta_high = neighbours(delta)
     got = exchange(send, XC)
     part = call(
         weight_grad_body,
         shape((16, 64, 128), BF16),
         arrays=(got,),
-        after=(other, delta_low, delta_high),
+        after=(delta_low, delta_high),
         scratch=[pltpu.VMEM((288, 2560), BF16), pltpu.VMEM((2048, 128), BF16), pltpu.VMEM((864, 128), F32)],
         flops=2 * 864 * 2048 * 128,
     )
-    packed = call(pack_body, shape((4, 4, 64, 128), BF16), arrays=(own, other), after=(part,))
-    basis = lax.all_gather(packed, "zl")
     data, token = call(
         data_grad_body,
         [shape((256, 128), BF16), shape((8, 128), F32)],

time: 183 us -> 176 us (0.962)
  starting transfers between devices: 64.3 us -> 44.4 us
  blocking collectives: 65.9 us -> 75 us
  waiting for transfers between devices: 20.2 us -> 25.1 us
    ppermute x2 -> x1, starting transfers between devices: 16.2 us -> 0.8 us  [turned(): lax.ppermute(block, ('y', 'zl'), [(4 * y + z, 4 * z + y) for y in range(4...]
    all_to_all x4, blocking collectives: 65.9 us -> 75 us  [exchange(): return lax.all_to_all(x, axes, 0, 0)]
    ppermute x4, waiting for transfers between devices: 0.86 us -> 7.18 us  [neighbours(): return (lax.ppermute(block, SPACE, up), lax.ppermute(block, SPACE, down))]
    all_to_all x3, starting transfers between devices: 32.5 us -> 28.1 us  [exchange(): return lax.all_to_all(x, axes, 0, 0)]
    all_to_all x3, waiting for transfers between devices: 15.5 us -> 17.9 us  [exchange(): return lax.all_to_all(x, axes, 0, 0)]
    all_gather x1, waiting for transfers between devices: 2.11 us -> 0.02 us  [per_device(): basis = lax.all_gather(twice, ('zh', 'zl'))]
    pallas_call x11 -> x10, Pallas kernels: 14.1 us -> 13.4 us  [call(): pl.pallas_call(kernel, out_shape=out_shape, in_specs=[SMEM] * len(scalars...]
  transfers between devices with their start and end apart: 10 -> 9, of which waited for: 5 -> 4; matrix products, arithmetic and copies ran while one was open for 0% -> 0% of each run, Pallas kernels for 2% -> 3%
where the time goes in v4:
time: 176 us
  blocking collectives  75 us (43%)
  starting transfers between devices  44.4 us (25%)
  waiting for transfers between devices  25.1 us (14%)
  between operations  14.2 us (8%)
  Pallas kernels  13.4 us (8%)
  local copies, waits for them, and re-layouts  3.52 us (2%)
    all_to_all x4, blocking collectives, exchange(): return lax.all_to_all(x, axes, 0, 0)  75 us
    all_to_all x3, starting transfers between devices, exchange(): return lax.all_to_all(x, axes, 0, 0)  28.1 us
    all_to_all x3, waiting for transfers between devices, exchange(): return lax.all_to_all(x, axes, 0, 0)  17.9 us
    ppermute x4, starting transfers between devices, neighbours(): return (lax.ppermute(block, SPACE, up), lax.ppermute(block, SPACE, down))  15.5 us
    pallas_call x10, Pallas kernels, call(): pl.pallas_call(kernel, out_shape=out_shape, in_specs=[SMEM] * len(scalars...  13.4 us
    ppermute x4, waiting for transfers between devices, neighbours(): return (lax.ppermute(block, SPACE, up), lax.ppermute(block, SPACE, down))  7.18 us
  transfers between devices with their start and end apart: 9, of which 4 were waited for; matrix products, arithmetic and copies ran while one was open for 0% of the time, Pallas kernels for 3%

profile of v4, /device:TPU:1, one launch (start us, length us, event | category | flops | bytes accessed | tf_op | source)
XLA Modules:
  0.0 175.6 jit_solution(14859266461068012666)
XLA Ops:
  7.2 4.5 %collective-permute-start = (bf16[256,128]{1,0:T(8,128)(2,1)}, bf16[256,128]{1,0:T(8,128)(2,1)S(1)}, u32[]{:S(2)}, u32[]{:S(2)}) collective-permute-start(bf16[256,128]{1,0:T(8,128)(2,1)} %bitcast.13), channel_id=1, source_target_pairs={{0,1},{1,2},{2,3},{3,4},{4,5},{5,6},{6,7},{7,8},{8,9},{9,10},{10,1... | collective-permute-start | bytes 196616 | tf_op jit(solution)/shard_map/ppermute | solution.py:309
  11.7 5.6 %collective-permute-start.1 = (bf16[256,128]{1,0:T(8,128)(2,1)}, bf16[256,128]{1,0:T(8,128)(2,1)S(1)}, u32[]{:S(2)}, u32[]{:S(2)}) collective-permute-start(bf16[256,128]{1,0:T(8,128)(2,1)} %bitcast.14), channel_id=1, source_target_pairs={{1,0},{2,1},{3,2},{4,3},{5,4},{6,5},{7,6},{8,7},{9,8},{10,9},{11,1... | collective-permute-start | bytes 196616 | tf_op jit(solution)/shard_map/ppermute | solution.py:309
  17.3 0.8 copy-done.7
  18.1 0.7 copy-done.8
  18.7 0.3 shard_map.104
  19.1 0.8 collective-permute-start.2
  19.9 0.3 copy-done
  20.2 2.6 %shard_map.105 = (bf16[256,256]{1,0:T(8,128)(2,1)S(1)}, bf16[8,384,128]{2,1,0:T(8,128)(2,1)}, bf16[2,4,64,128]{3,2,1,0:T(8,128)(2,1)}) custom-call(s32[1]{0:T(128)} %bitcast.refs_0_, bf16[256,128]{1,0:T(8,128)(2,1)S(1)} %collective-permute-done.refs_1_, bf16[256,128]{1,0:T(8,128)(2,1)S(1)} %collective-permute-done.1.refs_2_, ...), custom_call_target="tpu_custom_call" | custom-call | flops 452984832 | bytes 2163716 | tf_op jit(solution)/shard_map/pallas_call | solution.py:33
  22.8 3.9 %all-to-all-start = ((bf16[8,384,128]{2,1,0:T(8,128)(2,1)}), bf16[8,384,128]{2,1,0:T(8,128)(2,1)S(1)}, u32[]{:S(2)}, u32[]{:S(2)}) async-start(bf16[8,384,128]{2,1,0:T(8,128)(2,1)} %get-tuple-element.10), calls=%async_computation | async-start | bytes 1572864 | tf_op jit(solution)/shard_map/all_to_all | solution.py:57
  26.7 3.5 %collective-permute-start.3 = (bf16[256,256]{1,0:T(8,128)(2,1)S(1)}, bf16[256,256]{1,0:T(8,128)(2,1)S(1)}, u32[]{:S(2)}, u32[]{:S(2)}) collective-permute-start(bf16[256,256]{1,0:T(8,128)(2,1)S(1)} %get-tuple-element.9.refs_2_), channel_id=1, source_target_pairs={{0,1},{1,2},{2,3},{3,4},{4,5},{5,6},{6,7},{7,8},{8,9},{9,10},{10,1... | collective-permute-start | bytes 393224 | tf_op jit(solution)/shard_map/ppermute | solution.py:309
  30.2 1.9 %collective-permute-start.4 = (bf16[256,256]{1,0:T(8,128)(2,1)S(1)}, bf16[256,256]{1,0:T(8,128)(2,1)S(1)}, u32[]{:S(2)}, u32[]{:S(2)}) collective-permute-start(bf16[256,256]{1,0:T(8,128)(2,1)S(1)} %get-tuple-element.9.refs_2_), channel_id=1, source_target_pairs={{1,0},{2,1},{3,2},{4,3},{5,4},{6,5},{7,6},{8,7},{9,8},{10,9},{11,1... | collective-permute-start | bytes 393224 | tf_op jit(solution)/shard_map/ppermute | solution.py:309
  32.2 0.0 all-gather.3.cloned.1.call-update
  32.2 5.1 %collective-permute-done.3.refs_1_.refs_0_ = bf16[256,256]{1,0:T(8,128)(2,1)S(1)} collective-permute-done((bf16[256,256]{1,0:T(8,128)(2,1)S(1)}, bf16[256,256]{1,0:T(8,128)(2,1)S(1)}, u32[]{:S(2)}, u32[]{:S(2)}) %collective-permute-start.3) | collective-permute-done | bytes 131104 | tf_op jit(solution)/shard_map/ppermute | solution.py:309
  37.3 2.1 %collective-permute-done.4.refs_2_.refs_1_ = bf16[256,256]{1,0:T(8,128)(2,1)S(1)} collective-permute-done((bf16[256,256]{1,0:T(8,128)(2,1)S(1)}, bf16[256,256]{1,0:T(8,128)(2,1)S(1)}, u32[]{:S(2)}, u32[]{:S(2)}) %collective-permute-start.4) | collective-permute-done | bytes 131104 | tf_op jit(solution)/shard_map/ppermute | solution.py:309
  39.4 2.2 %shard_map.106.refs_4_ = bf16[16,64,128]{2,1,0:T(8,128)(2,1)} custom-call(bf16[8,384,128]{2,1,0:T(8,128)(2,1)S(1)} %all-to-all-done.refs_0_, bf16[256,256]{1,0:T(8,128)(2,1)S(1)} %collective-permute-done.3.refs_1_.refs_0_, bf16[256,256]{1,0:T(8,128)(2,1)S(1)} %collective-permute-done.4.refs_2_.refs_1_), custom_call_target="tpu_custom_call" | custom-call | flops 452984832 | bytes 1048576 | tf_op jit(solution)/shard_map/pallas_call | solution.py:33
  41.6 14.5 %all-to-all-start.1 = ((bf16[16,64,128]{2,1,0:T(8,128)(2,1)}), bf16[16,64,128]{2,1,0:T(8,128)(2,1)S(1)}, u32[]{:S(2)}, u32[]{:S(2)}) async-start(bf16[16,64,128]{2,1,0:T(8,128)(2,1)} %shard_map.106.refs_4_), calls=%async_computation.1 | async-start | bytes 524288 | tf_op jit(solution)/shard_map/all_to_all | solution.py:57
  56.1 2.1 %shard_map.107 = (bf16[256,128]{1,0:T(8,128)(2,1)}, f32[8,128]{1,0:T(8,128)S(1)}) custom-call(bf16[256,256]{1,0:T(8,128)(2,1)S(1)} %collective-permute-done.3.refs_1_.refs_0_, bf16[256,256]{1,0:T(8,128)(2,1)S(1)} %collective-permute-done.4.refs_2_.refs_1_, bf16[256,256]{1,0:T(8,128)(2,1)S(1)} %get-tuple-element.9.refs_2_, bf16[3456,256]{1,0:T(8,128)(2,1)S(1)} %copy-done, ...), custom_call_target="tpu_custom_call" | custom-call | flops 452984832 | bytes 2424832 | tf_op jit(solution)/shard_map/pallas_call | solution.py:33
  58.2 6.4 %all-to-all-done.1.refs_0_ = bf16[16,64,128]{2,1,0:T(8,128)(2,1)S(1)} async-done(((bf16[16,64,128]{2,1,0:T(8,128)(2,1)}), bf16[16,64,128]{2,1,0:T(8,128)(2,1)S(1)}, u32[]{:S(2)}, u32[]{:S(2)}) %all-to-all-start.1) | async-done | bytes 262176 | tf_op jit(solution)/shard_map/all_to_all | solution.py:57
  64.6 31.2 %all_to_all.35.refs_0_ = bf16[4,64,128]{2,1,0:T(8,128)(2,1)S(1)} all-to-all(bf16[4,64,128]{2,1,0:T(8,128)(2,1)S(1)} %shard_map.108), channel_id=1, replica_groups=mesh['y'=4,'zh'=2,'zg'=2,'zl'=4,'x'=4,'c'=2] {'zh','zg'}, dimensions={0} | all-to-all | bytes 131072 | tf_op jit(solution)/shard_map/all_to_all | solution.py:57
  95.8 0.9 shard_map.109
  96.7 9.7 %all-to-all-start.3 = ((bf16[32,64,128]{2,1,0:T(8,128)(2,1)}), bf16[32,64,128]{2,1,0:T(8,128)(2,1)S(1)}, u32[]{:S(2)}, u32[]{:S(2)}) async-start(bf16[32,64,128]{2,1,0:T(8,128)(2,1)} %shard_map.109), calls=%async_computation.3 | async-start | bytes 1048576 | tf_op jit(solution)/shard_map/all_to_all | solution.py:57
  106.4 0.0 all-gather.3.cloned.1.call-done
  106.4 11.5 %all-to-all-done.3.refs_2_ = bf16[32,64,128]{2,1,0:T(8,128)(2,1)S(1)} async-done(((bf16[32,64,128]{2,1,0:T(8,128)(2,1)}), bf16[32,64,128]{2,1,0:T(8,128)(2,1)S(1)}, u32[]{:S(2)}, u32[]{:S(2)}) %all-to-all-start.3) | async-done | bytes 524320 | tf_op jit(solution)/shard_map/all_to_all | solution.py:57
  117.9 0.8 copy-done.9
  118.7 3.2 %shard_map.110 = (f32[4,56,256]{2,1,0:T(8,128)}, bf16[2,4,64,128]{3,2,1,0:T(8,128)(2,1)}) custom-call(s32[8]{0:T(128)} %refs_0_.1, s32[1]{0:T(128)} %bitcast.8.refs_1_, bf16[32,64,128]{2,1,0:T(8,128)(2,1)} %copy-done.9, bf16[8,2,4,64,128]{4,3,2,1,0:T(8,128)(2,1)} %bitcast.20), custom_call_target="tpu_custom_call" | custom-call | bytes 1572900 | tf_op jit(solution)/shard_map/pallas_call | solution.py:33
  121.9 9.8 %all_to_all.36.refs_0_ = f32[4,56,256]{2,1,0:T(8,128)S(1)} all-to-all(f32[4,56,256]{2,1,0:T(8,128)} %get-tuple-element.14), channel_id=1, replica_groups=mesh['y'=4,'zh'=2,'zg'=2,'zl'=4,'x'=4,'c'=2] {'zl'}, dimensions={0} | all-to-all | bytes 458752 | tf_op jit(solution)/shard_map/all_to_all | solution.py:57
  131.7 0.9 copy-done.3
  132.6 1.4 shard_map.111
  134.0 14.0 %all_to_all.37.refs_0_ = bf16[8,112,256]{2,1,0:T(8,128)(2,1)S(1)} all-to-all(bf16[8,112,256]{2,1,0:T(8,128)(2,1)S(1)} %shard_map.111), channel_id=1, replica_groups=mesh['y'=4,'zh'=2,'zg'=2,'zl'=4,'x'=4,'c'=2] {'x','c'}, dimensions={0} | all-to-all | bytes 917504 | tf_op jit(solution)/shard_map/all_to_all | solution.py:57
  148.0 0.1 shard_map.112
  148.1 20.1 %all_to_all.38.refs_0_ = bf16[8,112,128]{2,1,0:T(8,128)(2,1)S(1)} all-to-all(bf16[8,112,128]{2,1,0:T(8,128)(2,1)S(1)} %shard_map.112), channel_id=1, replica_groups=mesh['y'=4,'zh'=2,'zg'=2,'zl'=4,'x'=4,'c'=2] {'zg','y'}, dimensions={0} | all-to-all | bytes 458752 | tf_op jit(solution)/shard_map/all_to_all | solution.py:57
  168.1 0.7 shard_map.113
  (21 shorter events, 0.1 us)
Async XLA Ops:
  7.2 12.7 %collective-permute-start = (bf16[256,128]{1,0:T(8,128)(2,1)}, bf16[256,128]{1,0:T(8,128)(2,1)S(1)}, u32[]{:S(2)}, u32[]{:S(2)}) collective-permute-start(bf16[256,128]{1,0:T(8,128)(2,1)} %bitcast.13), channel_id=1, source_target_pairs={{0,1},{1,2},{2,3},{3,4},{4,5},{5,6},{6,7},{7,8},{8,9},{9,10},{10,1... | collective-permute-start | bytes 196616 | tf_op jit(solution)/shard_map/ppermute | solution.py:309
  11.7 8.2 %collective-permute-start.1 = (bf16[256,128]{1,0:T(8,128)(2,1)}, bf16[256,128]{1,0:T(8,128)(2,1)S(1)}, u32[]{:S(2)}, u32[]{:S(2)}) collective-permute-start(bf16[256,128]{1,0:T(8,128)(2,1)} %bitcast.14), channel_id=1, source_target_pairs={{1,0},{2,1},{3,2},{4,3},{5,4},{6,5},{7,6},{8,7},{9,8},{10,9},{11,1... | collective-permute-start | bytes 196616 | tf_op jit(solution)/shard_map/ppermute | solution.py:309
  17.3 0.8 copy-start.7
  18.1 0.7 copy-start.8
  18.7 1.5 copy-start
  18.7 1.5 copy-start.2
  18.7 1.5 copy-start.4
  18.7 1.5 copy-start.5
  19.1 0.8 collective-permute-start.2
  22.8 16.6 %all-to-all-start = ((bf16[8,384,128]{2,1,0:T(8,128)(2,1)}), bf16[8,384,128]{2,1,0:T(8,128)(2,1)S(1)}, u32[]{:S(2)}, u32[]{:S(2)}) async-start(bf16[8,384,128]{2,1,0:T(8,128)(2,1)} %get-tuple-element.10), calls=%async_computation | async-start | bytes 1572864 | tf_op jit(solution)/shard_map/all_to_all | solution.py:57
  26.7 79.7 %all-gather.3.cloned.1.call-start = ((), (), s32[]{:S(2)}) async-start(), calls=%async_computation.7 | async-start | bytes 1179648 | tf_op jit(solution)/shard_map/all_gather | solution.py:358
  26.7 10.6 %collective-permute-start.3 = (bf16[256,256]{1,0:T(8,128)(2,1)S(1)}, bf16[256,256]{1,0:T(8,128)(2,1)S(1)}, u32[]{:S(2)}, u32[]{:S(2)}) collective-permute-start(bf16[256,256]{1,0:T(8,128)(2,1)S(1)} %get-tuple-element.9.refs_2_), channel_id=1, source_target_pairs={{0,1},{1,2},{2,3},{3,4},{4,5},{5,6},{6,7},{7,8},{8,9},{9,10},{10,1... | collective-permute-start | bytes 393224 | tf_op jit(solution)/shard_map/ppermute | solution.py:309
  30.2 9.1 %collective-permute-start.4 = (bf16[256,256]{1,0:T(8,128)(2,1)S(1)}, bf16[256,256]{1,0:T(8,128)(2,1)S(1)}, u32[]{:S(2)}, u32[]{:S(2)}) collective-permute-start(bf16[256,256]{1,0:T(8,128)(2,1)S(1)} %get-tuple-element.9.refs_2_), channel_id=1, source_target_pairs={{1,0},{2,1},{3,2},{4,3},{5,4},{6,5},{7,6},{8,7},{9,8},{10,9},{11,1... | collective-permute-start | bytes 393224 | tf_op jit(solution)/shard_map/ppermute | solution.py:309
  41.6 23.0 %all-to-all-start.1 = ((bf16[16,64,128]{2,1,0:T(8,128)(2,1)}), bf16[16,64,128]{2,1,0:T(8,128)(2,1)S(1)}, u32[]{:S(2)}, u32[]{:S(2)}) async-start(bf16[16,64,128]{2,1,0:T(8,128)(2,1)} %shard_map.106.refs_4_), calls=%async_computation.1 | async-start | bytes 524288 | tf_op jit(solution)/shard_map/all_to_all | solution.py:57
  95.8 35.9 %copy-start.1 = (f32[256,256]{1,0:T(8,128)S(1)}, f32[256,256]{1,0:T(8,128)}, u32[]{:S(2)}) copy-start(f32[256,256]{1,0:T(8,128)} %refs_2_.1) | copy-start | bytes 786436
  95.8 35.9 %copy-start.6 = (f32[256]{0:T(256)S(1)}, f32[256]{0:T(256)}, u32[]{:S(2)}) copy-start(f32[256]{0:T(256)} %param.17) | copy-start | bytes 3076
  96.7 21.3 %all-to-all-start.3 = ((bf16[32,64,128]{2,1,0:T(8,128)(2,1)}), bf16[32,64,128]{2,1,0:T(8,128)(2,1)S(1)}, u32[]{:S(2)}, u32[]{:S(2)}) async-start(bf16[32,64,128]{2,1,0:T(8,128)(2,1)} %shard_map.109), calls=%async_computation.3 | async-start | bytes 1048576 | tf_op jit(solution)/shard_map/all_to_all | solution.py:57
  117.9 0.8 copy-start.9
  131.7 0.9 copy-start.3
Sparse Core Ops, SparseCore 0:
  32.3 70.4 all-gather.2

commit v5 on v4

--- a/solution.py
+++ b/solution.py
@@ -94,8 +94,8 @@
 
 
 def forward_body(
-    place_ref, low_ref, high_ref, basis_ref, mine_any, weight_any, bias_any, cot_any,
-    delta_ref, send_ref, twice_ref, patches, mine, weight, bias, cot, sems,
+    place_ref, low_ref, high_ref, mine_any, weight_any, bias_any, cot_any,
+    delta_ref, send_ref, patches, mine, weight, bias, cot, sems,
 ):
     copies = started(
         [
@@ -105,8 +105,6 @@
             )
         ]
     )
-    twice_ref[0] = basis_ref[...]
-    twice_ref[1] = basis_ref[...]
     none = jnp.zeros((16, 128), BF16)
     for a in (0, 2, 1):
         if a == 1:
@@ -187,18 +185,18 @@
 
 
 def slot_of(owner):
-    return 4 * (owner & 1) + (owner >> 1)
+    return owner & 1, owner >> 1
 
 
 def rotate_body(owner_ref, place_ref, got_ref, basis_any, out_ref, panels_ref, basis, grads, ordered, sems):
-    zl = place_ref[0]
+    zg, zl = place_ref[0], place_ref[1]
     copies = []
     for j in range(8):
-        slot = slot_of(owner_ref[j])
-        copies.append(pltpu.make_async_copy(basis_any.at[slot, 0, zl], basis.at[j], sems.at[j]))
+        zh, z = slot_of(owner_ref[j])
+        copies.append(pltpu.make_async_copy(basis_any.at[zh, zg, z, zl], basis.at[j], sems.at[j]))
     for g in range(2):
-        slot = slot_of(owner_ref[zl + 4 * g])
-        copies.append(pltpu.make_async_copy(basis_any.at[slot, 0], panels_ref.at[g], sems.at[8 + g]))
+        zh, z = slot_of(owner_ref[zl + 4 * g])
+        copies.append(pltpu.make_async_copy(basis_any.at[zh, zg, z], panels_ref.at[g], sems.at[8 + g]))
     started(copies)
     for y in range(4):
         for x in range(4):
@@ -325,7 +323,7 @@
     output_eigen,
 ):
     dma = pltpu.SemaphoreType.DMA
-    place = lax.axis_index("zl").astype(jnp.int32).reshape(1)
+    place = jnp.stack([lax.axis_index("zg"), lax.axis_index("zl")]).astype(jnp.int32)
     inner = lax.axis_index(XC).astype(jnp.int32).reshape(1)
     plane = activations.reshape(256, 128)
     low, high = neighbours(plane)
@@ -339,12 +337,15 @@
         flops=4_000_000_000,
     )
 
-    delta, send, twice = call(
+    stored = turned(stored)
+    basis = lax.all_gather(stored, ("zh", "zg", "zl")).reshape(2, 2, 4, 4, 64, 128)
+    delta, send = call(
         forward_body,
-        [shape((256, 256), BF16), shape((8, 384, 128), BF16), shape((2, 4, 64, 128), BF16)],
+        [shape((256, 256), BF16), shape((8, 384, 128), BF16)],
         (inner,),
-        (low, high, turned(stored)),
+        (low, high),
         (plane, conv_weight, conv_bias.reshape(1, 256), cotangent.reshape(256, 256)),
+        (stored,),
         scratch=[
             pltpu.VMEM((256, 3456), BF16),
             pltpu.VMEM((256, 128), BF16),
@@ -355,7 +356,6 @@
         ],
         flops=2 * 256 * 3456 * 256,
     )
-    basis = lax.all_gather(twice, ("zh", "zl"))
     delta_low, delta_high = neighbours(delta)
     got = exchange(send, XC)
     part = call(

time: 176 us -> 176 us (level)
  blocking collectives: 75 us -> 71.6 us
  waiting for transfers between devices: 25.1 us -> 26.9 us
    all_to_all x4, blocking collectives: 75 us -> 71.6 us  [exchange(): return lax.all_to_all(x, axes, 0, 0)]
    all_gather x1, waiting for transfers between devices: 0.02 us -> 2.17 us  [per_device(): lax.all_gather(stored, ('zh', 'zg', 'zl')).reshape(2, 2, 4, 4, 64, 128)]
  transfers between devices with their start and end apart: 9 -> 9, of which waited for: 4 -> 5; matrix products, arithmetic and copies ran while one was open for 0% -> 0% of each run, Pallas kernels for 3% -> 3%
where the time goes in v5:
time: 176 us; the launch traced here: 175 us
  blocking collectives  71.6 us (41%)
  starting transfers between devices  44.6 us (25%)
  waiting for transfers between devices  26.9 us (15%)
  between operations  14.2 us (8%)
  Pallas kernels  13.3 us (8%)
  local copies, waits for them, and re-layouts  3.49 us (2%)
    all_to_all x4, blocking collectives, exchange(): return lax.all_to_all(x, axes, 0, 0)  71.6 us
    all_to_all x3, starting transfers between devices, exchange(): return lax.all_to_all(x, axes, 0, 0)  28.3 us
    all_to_all x3, waiting for transfers between devices, exchange(): return lax.all_to_all(x, axes, 0, 0)  17.6 us
    ppermute x4, starting transfers between devices, neighbours(): return (lax.ppermute(block, SPACE, up), lax.ppermute(block, SPACE, down))  15.5 us
    pallas_call x10, Pallas kernels, call(): pl.pallas_call(kernel, out_shape=out_shape, in_specs=[SMEM] * len(scalars...  13.3 us
    ppermute x4, waiting for transfers between devices, neighbours(): return (lax.ppermute(block, SPACE, up), lax.ppermute(block, SPACE, down))  6.47 us
  transfers between devices with their start and end apart: 9, of which 5 were waited for; matrix products, arithmetic and copies ran while one was open for 0% of the time, Pallas kernels for 3%

profile of v5, /device:TPU:1, one launch (start us, length us, event | category | flops | bytes accessed | tf_op | source)
XLA Modules:
  0.0 174.8 jit_solution(12019702068389367585)
XLA Ops:
  7.2 4.5 %collective-permute-start = (bf16[256,128]{1,0:T(8,128)(2,1)}, bf16[256,128]{1,0:T(8,128)(2,1)S(1)}, u32[]{:S(2)}, u32[]{:S(2)}) collective-permute-start(bf16[256,128]{1,0:T(8,128)(2,1)} %bitcast.14), channel_id=1, source_target_pairs={{0,1},{1,2},{2,3},{3,4},{4,5},{5,6},{6,7},{7,8},{8,9},{9,10},{10,1... | collective-permute-start | bytes 196616 | tf_op jit(solution)/shard_map/ppermute | solution.py:307
  11.7 5.6 %collective-permute-start.1 = (bf16[256,128]{1,0:T(8,128)(2,1)}, bf16[256,128]{1,0:T(8,128)(2,1)S(1)}, u32[]{:S(2)}, u32[]{:S(2)}) collective-permute-start(bf16[256,128]{1,0:T(8,128)(2,1)} %bitcast.15), channel_id=1, source_target_pairs={{1,0},{2,1},{3,2},{4,3},{5,4},{6,5},{7,6},{8,7},{9,8},{10,9},{11,1... | collective-permute-start | bytes 196616 | tf_op jit(solution)/shard_map/ppermute | solution.py:307
  17.3 0.8 copy-done.8
  18.1 0.7 copy-done.9
  18.7 0.3 shard_map.104
  19.1 0.8 collective-permute-start.2
  19.9 0.3 copy-done
  20.2 2.5 %shard_map.105 = (bf16[256,256]{1,0:T(8,128)(2,1)S(1)}, bf16[8,384,128]{2,1,0:T(8,128)(2,1)}) custom-call(s32[1]{0:T(128)} %bitcast.refs_0_, bf16[256,128]{1,0:T(8,128)(2,1)S(1)} %collective-permute-done.refs_1_, bf16[256,128]{1,0:T(8,128)(2,1)S(1)} %collective-permute-done.1.refs_2_, bf16[256,128]{1,0:T(8,128)(2,1)S(1)} %bitcast.16, ...), custom_call_target="tpu_custom_call" | custom-call | flops 452984832 | bytes 2163716 | tf_op jit(solution)/shard_map/pallas_call | solution.py:33
  22.8 3.9 %all-to-all-start = ((bf16[8,384,128]{2,1,0:T(8,128)(2,1)}), bf16[8,384,128]{2,1,0:T(8,128)(2,1)S(1)}, u32[]{:S(2)}, u32[]{:S(2)}) async-start(bf16[8,384,128]{2,1,0:T(8,128)(2,1)} %get-tuple-element.9), calls=%async_computation | async-start | bytes 1572864 | tf_op jit(solution)/shard_map/all_to_all | solution.py:57
  26.7 0.7 all-gather.3.cloned.1.call-update
  27.4 3.5 %collective-permute-start.3 = (bf16[256,256]{1,0:T(8,128)(2,1)S(1)}, bf16[256,256]{1,0:T(8,128)(2,1)S(1)}, u32[]{:S(2)}, u32[]{:S(2)}) collective-permute-start(bf16[256,256]{1,0:T(8,128)(2,1)S(1)} %get-tuple-element.8.refs_2_), channel_id=1, source_target_pairs={{0,1},{1,2},{2,3},{3,4},{4,5},{5,6},{6,7},{7,8},{8,9},{9,10},{10,1... | collective-permute-start | bytes 393224 | tf_op jit(solution)/shard_map/ppermute | solution.py:307
  31.0 1.9 %collective-permute-start.4 = (bf16[256,256]{1,0:T(8,128)(2,1)S(1)}, bf16[256,256]{1,0:T(8,128)(2,1)S(1)}, u32[]{:S(2)}, u32[]{:S(2)}) collective-permute-start(bf16[256,256]{1,0:T(8,128)(2,1)S(1)} %get-tuple-element.8.refs_2_), channel_id=1, source_target_pairs={{1,0},{2,1},{3,2},{4,3},{5,4},{6,5},{7,6},{8,7},{9,8},{10,9},{11,1... | collective-permute-start | bytes 393224 | tf_op jit(solution)/shard_map/ppermute | solution.py:307
  32.9 4.4 %collective-permute-done.3.refs_1_.refs_0_ = bf16[256,256]{1,0:T(8,128)(2,1)S(1)} collective-permute-done((bf16[256,256]{1,0:T(8,128)(2,1)S(1)}, bf16[256,256]{1,0:T(8,128)(2,1)S(1)}, u32[]{:S(2)}, u32[]{:S(2)}) %collective-permute-start.3) | collective-permute-done | bytes 131104 | tf_op jit(solution)/shard_map/ppermute | solution.py:307
  37.3 2.1 %collective-permute-done.4.refs_2_.refs_1_ = bf16[256,256]{1,0:T(8,128)(2,1)S(1)} collective-permute-done((bf16[256,256]{1,0:T(8,128)(2,1)S(1)}, bf16[256,256]{1,0:T(8,128)(2,1)S(1)}, u32[]{:S(2)}, u32[]{:S(2)}) %collective-permute-start.4) | collective-permute-done | bytes 131104 | tf_op jit(solution)/shard_map/ppermute | solution.py:307
  39.4 2.2 %shard_map.106.refs_4_ = bf16[16,64,128]{2,1,0:T(8,128)(2,1)} custom-call(bf16[8,384,128]{2,1,0:T(8,128)(2,1)S(1)} %all-to-all-done.refs_0_, bf16[256,256]{1,0:T(8,128)(2,1)S(1)} %collective-permute-done.3.refs_1_.refs_0_, bf16[256,256]{1,0:T(8,128)(2,1)S(1)} %collective-permute-done.4.refs_2_.refs_1_), custom_call_target="tpu_custom_call" | custom-call | flops 452984832 | bytes 1048576 | tf_op jit(solution)/shard_map/pallas_call | solution.py:33
  41.5 14.5 %all-to-all-start.1 = ((bf16[16,64,128]{2,1,0:T(8,128)(2,1)}), bf16[16,64,128]{2,1,0:T(8,128)(2,1)S(1)}, u32[]{:S(2)}, u32[]{:S(2)}) async-start(bf16[16,64,128]{2,1,0:T(8,128)(2,1)} %shard_map.106.refs_4_), calls=%async_computation.1 | async-start | bytes 524288 | tf_op jit(solution)/shard_map/all_to_all | solution.py:57
  56.0 2.1 %shard_map.107 = (bf16[256,128]{1,0:T(8,128)(2,1)}, f32[8,128]{1,0:T(8,128)S(1)}) custom-call(bf16[256,256]{1,0:T(8,128)(2,1)S(1)} %collective-permute-done.3.refs_1_.refs_0_, bf16[256,256]{1,0:T(8,128)(2,1)S(1)} %collective-permute-done.4.refs_2_.refs_1_, bf16[256,256]{1,0:T(8,128)(2,1)S(1)} %get-tuple-element.8.refs_2_, bf16[3456,256]{1,0:T(8,128)(2,1)S(1)} %copy-done, ...), custom_call_target="tpu_custom_call" | custom-call | flops 452984832 | bytes 2424832 | tf_op jit(solution)/shard_map/pallas_call | solution.py:33
  58.1 8.9 %all-to-all-done.1.refs_0_ = bf16[16,64,128]{2,1,0:T(8,128)(2,1)S(1)} async-done(((bf16[16,64,128]{2,1,0:T(8,128)(2,1)}), bf16[16,64,128]{2,1,0:T(8,128)(2,1)S(1)}, u32[]{:S(2)}, u32[]{:S(2)}) %all-to-all-start.1) | async-done | bytes 262176 | tf_op jit(solution)/shard_map/all_to_all | solution.py:57
  67.0 22.9 %all_to_all.35.refs_0_ = bf16[4,64,128]{2,1,0:T(8,128)(2,1)S(1)} all-to-all(bf16[4,64,128]{2,1,0:T(8,128)(2,1)S(1)} %shard_map.108), channel_id=1, replica_groups=mesh['y'=4,'zh'=2,'zg'=2,'zl'=4,'x'=4,'c'=2] {'zh','zg'}, dimensions={0} | all-to-all | bytes 131072 | tf_op jit(solution)/shard_map/all_to_all | solution.py:57
  89.9 0.9 shard_map.109
  90.8 9.8 %all-to-all-start.3 = ((bf16[32,64,128]{2,1,0:T(8,128)(2,1)}), bf16[32,64,128]{2,1,0:T(8,128)(2,1)S(1)}, u32[]{:S(2)}, u32[]{:S(2)}) async-start(bf16[32,64,128]{2,1,0:T(8,128)(2,1)} %shard_map.109), calls=%async_computation.3 | async-start | bytes 1048576 | tf_op jit(solution)/shard_map/all_to_all | solution.py:57
  100.7 0.7 pad_add_fusion.refs_1_
  101.3 2.2 %all-gather.3.cloned.1.call-done = bf16[64,64,128]{2,1,0:T(8,128)(2,1)} async-done(((bf16[4,64,128]{2,1,0:T(8,128)(2,1)}), bf16[64,64,128]{2,1,0:T(8,128)(2,1)}) %all-gather.3.cloned.1.call-update) | async-done | bytes 1048592 | tf_op jit(solution)/shard_map/all_gather | solution.py:341
  103.5 8.7 %all-to-all-done.3.refs_2_ = bf16[32,64,128]{2,1,0:T(8,128)(2,1)S(1)} async-done(((bf16[32,64,128]{2,1,0:T(8,128)(2,1)}), bf16[32,64,128]{2,1,0:T(8,128)(2,1)S(1)}, u32[]{:S(2)}, u32[]{:S(2)}) %all-to-all-start.3) | async-done | bytes 524320 | tf_op jit(solution)/shard_map/all_to_all | solution.py:57
  112.2 0.8 copy-done.10
  113.0 3.2 %shard_map.110 = (f32[4,56,256]{2,1,0:T(8,128)}, bf16[2,4,64,128]{3,2,1,0:T(8,128)(2,1)}) custom-call(s32[8]{0:T(128)} %refs_0_.1, s32[2]{0:T(128)} %pad_add_fusion.refs_1_, bf16[32,64,128]{2,1,0:T(8,128)(2,1)} %copy-done.10, bf16[2,2,4,4,64,128]{5,4,3,2,1,0:T(8,128)(2,1)} %bitcast.21), custom_call_target="tpu_custom_call" | custom-call | bytes 1572904 | tf_op jit(solution)/shard_map/pallas_call | solution.py:33
  116.2 9.6 %all_to_all.36.refs_0_ = f32[4,56,256]{2,1,0:T(8,128)S(1)} all-to-all(f32[4,56,256]{2,1,0:T(8,128)} %get-tuple-element.12), channel_id=1, replica_groups=mesh['y'=4,'zh'=2,'zg'=2,'zl'=4,'x'=4,'c'=2] {'zl'}, dimensions={0} | all-to-all | bytes 458752 | tf_op jit(solution)/shard_map/all_to_all | solution.py:57
  125.8 0.9 copy-done.4
  126.7 1.4 shard_map.111
  128.1 15.2 %all_to_all.37.refs_0_ = bf16[8,112,256]{2,1,0:T(8,128)(2,1)S(1)} all-to-all(bf16[8,112,256]{2,1,0:T(8,128)(2,1)S(1)} %shard_map.111), channel_id=1, replica_groups=mesh['y'=4,'zh'=2,'zg'=2,'zl'=4,'x'=4,'c'=2] {'x','c'}, dimensions={0} | all-to-all | bytes 917504 | tf_op jit(solution)/shard_map/all_to_all | solution.py:57
  143.3 24.0 %all_to_all.38.refs_0_ = bf16[8,112,128]{2,1,0:T(8,128)(2,1)S(1)} all-to-all(bf16[8,112,128]{2,1,0:T(8,128)(2,1)S(1)} %shard_map.112), channel_id=1, replica_groups=mesh['y'=4,'zh'=2,'zg'=2,'zl'=4,'x'=4,'c'=2] {'zg','y'}, dimensions={0} | all-to-all | bytes 458752 | tf_op jit(solution)/shard_map/all_to_all | solution.py:57
  167.3 0.7 shard_map.113
  (24 shorter events, 0.2 us)
Async XLA Ops:
  7.2 12.7 %collective-permute-start = (bf16[256,128]{1,0:T(8,128)(2,1)}, bf16[256,128]{1,0:T(8,128)(2,1)S(1)}, u32[]{:S(2)}, u32[]{:S(2)}) collective-permute-start(bf16[256,128]{1,0:T(8,128)(2,1)} %bitcast.14), channel_id=1, source_target_pairs={{0,1},{1,2},{2,3},{3,4},{4,5},{5,6},{6,7},{7,8},{8,9},{9,10},{10,1... | collective-permute-start | bytes 196616 | tf_op jit(solution)/shard_map/ppermute | solution.py:307
  11.7 8.2 %collective-permute-start.1 = (bf16[256,128]{1,0:T(8,128)(2,1)}, bf16[256,128]{1,0:T(8,128)(2,1)S(1)}, u32[]{:S(2)}, u32[]{:S(2)}) collective-permute-start(bf16[256,128]{1,0:T(8,128)(2,1)} %bitcast.15), channel_id=1, source_target_pairs={{1,0},{2,1},{3,2},{4,3},{5,4},{6,5},{7,6},{8,7},{9,8},{10,9},{11,1... | collective-permute-start | bytes 196616 | tf_op jit(solution)/shard_map/ppermute | solution.py:307
  17.3 0.8 copy-start.8
  18.1 0.7 copy-start.9
  18.7 1.5 copy-start
  18.7 1.5 copy-start.3
  18.7 1.5 copy-start.5
  18.7 1.5 copy-start.6
  19.1 0.8 collective-permute-start.2
  19.9 2.9 %copy-start.2 = (bf16[4,64,128]{2,1,0:T(8,128)(2,1)}, bf16[4,64,128]{2,1,0:T(8,128)(2,1)S(1)}, u32[]{:S(2)}) copy-start(bf16[4,64,128]{2,1,0:T(8,128)(2,1)S(1)} %collective-permute-done.2.refs_7_) | copy-start | bytes 196612
  22.8 16.6 %all-to-all-start = ((bf16[8,384,128]{2,1,0:T(8,128)(2,1)}), bf16[8,384,128]{2,1,0:T(8,128)(2,1)S(1)}, u32[]{:S(2)}, u32[]{:S(2)}) async-start(bf16[8,384,128]{2,1,0:T(8,128)(2,1)} %get-tuple-element.9), calls=%async_computation | async-start | bytes 1572864 | tf_op jit(solution)/shard_map/all_to_all | solution.py:57
  26.7 76.8 %all-gather.3.cloned.1.call-start = ((), (), s32[]{:S(2)}) async-start(), calls=%async_computation.7 | async-start | bytes 1114112 | tf_op jit(solution)/shard_map/all_gather | solution.py:341
  27.4 9.9 %collective-permute-start.3 = (bf16[256,256]{1,0:T(8,128)(2,1)S(1)}, bf16[256,256]{1,0:T(8,128)(2,1)S(1)}, u32[]{:S(2)}, u32[]{:S(2)}) collective-permute-start(bf16[256,256]{1,0:T(8,128)(2,1)S(1)} %get-tuple-element.8.refs_2_), channel_id=1, source_target_pairs={{0,1},{1,2},{2,3},{3,4},{4,5},{5,6},{6,7},{7,8},{8,9},{9,10},{10,1... | collective-permute-start | bytes 393224 | tf_op jit(solution)/shard_map/ppermute | solution.py:307
  31.0 8.4 %collective-permute-start.4 = (bf16[256,256]{1,0:T(8,128)(2,1)S(1)}, bf16[256,256]{1,0:T(8,128)(2,1)S(1)}, u32[]{:S(2)}, u32[]{:S(2)}) collective-permute-start(bf16[256,256]{1,0:T(8,128)(2,1)S(1)} %get-tuple-element.8.refs_2_), channel_id=1, source_target_pairs={{1,0},{2,1},{3,2},{4,3},{5,4},{6,5},{7,6},{8,7},{9,8},{10,9},{11,1... | collective-permute-start | bytes 393224 | tf_op jit(solution)/shard_map/ppermute | solution.py:307
  41.5 25.5 %all-to-all-start.1 = ((bf16[16,64,128]{2,1,0:T(8,128)(2,1)}), bf16[16,64,128]{2,1,0:T(8,128)(2,1)S(1)}, u32[]{:S(2)}, u32[]{:S(2)}) async-start(bf16[16,64,128]{2,1,0:T(8,128)(2,1)} %shard_map.106.refs_4_), calls=%async_computation.1 | async-start | bytes 524288 | tf_op jit(solution)/shard_map/all_to_all | solution.py:57
  89.9 35.8 %copy-start.1 = (f32[256,256]{1,0:T(8,128)S(1)}, f32[256,256]{1,0:T(8,128)}, u32[]{:S(2)}) copy-start(f32[256,256]{1,0:T(8,128)} %refs_2_.1) | copy-start | bytes 786436
  89.9 35.8 %copy-start.7 = (f32[256]{0:T(256)S(1)}, f32[256]{0:T(256)}, u32[]{:S(2)}) copy-start(f32[256]{0:T(256)} %param.17) | copy-start | bytes 3076
  90.8 21.4 %all-to-all-start.3 = ((bf16[32,64,128]{2,1,0:T(8,128)(2,1)}), bf16[32,64,128]{2,1,0:T(8,128)(2,1)S(1)}, u32[]{:S(2)}, u32[]{:S(2)}) async-start(bf16[32,64,128]{2,1,0:T(8,128)(2,1)} %shard_map.109), calls=%async_computation.3 | async-start | bytes 1048576 | tf_op jit(solution)/shard_map/all_to_all | solution.py:57
  112.2 0.8 copy-start.10
  125.8 0.9 copy-start.4
Sparse Core Ops, SparseCore 0:
  29.6 73.8 all-gather.2

commit v6 on v5

--- a/solution.py
+++ b/solution.py
@@ -85,11 +85,10 @@
         pick = iota((432, 128), 0) == 4 * iota((432, 128), 1) + r
         block = jnp.dot(panel[...], jnp.where(pick, 1.0, 0.0).astype(BF16), preferred_element_type=F32)
         block = jnp.concatenate([block, jnp.zeros((10, 128), F32)], axis=0)
-        if r == 0:
-            at = iota((64, 128), 1)
-            block = jnp.where(at == 108, first, block)
-            block = jnp.where(at == 109, second, block)
-            block = jnp.where(at == 110, third, block)
+        at = iota((64, 128), 1)
+        block = jnp.where(at == 108, first, block)
+        block = jnp.where(at == 109, second, block)
+        block = jnp.where(at == 110, third, block)
         out_ref[r] = block.astype(BF16)
 
 
@@ -141,7 +140,7 @@
             send_ref[to, 128:] = delta[:, 128 * c : 128 * c + 128]
 
 
-def weight_grad_body(got_ref, out_ref, moved, deltas, whole):
+def weight_grad_body(got_ref, basis_ref, out_ref, moved, deltas, whole):
     pieces = []
     for plane, at in [(0, 64)] + [(e, 0) for e in range(8)] + [(7, 64)]:
         pieces.append(got_ref[plane, at : at + 32].astype(F32))
@@ -169,13 +168,16 @@
             for e in range(2):
                 parts.append(whole[pl.ds(8 * y_to + 4 * e + z_to, 27, stride=32), :])
                 parts.append(none)
-            out_ref[4 * y_to + z_to] = jnp.concatenate(parts, axis=0).astype(BF16)
-
-
-def over_y_zl_body(got_ref, out_ref):
-    total = sum(got_ref[i].astype(F32) for i in range(16)) * (1.0 / CELLS)
+            out_ref[4 * y_to + z_to, :64] = jnp.concatenate(parts, axis=0).astype(BF16)
+            out_ref[4 * y_to + z_to, 64:] = basis_ref[z_to]
+
+
+def over_y_zl_body(place_ref, got_ref, out_ref, basis_ref):
+    total = sum(got_ref[i, :64].astype(F32) for i in range(16)) * (1.0 / CELLS)
     for to in range(4):
         out_ref[to] = total.astype(BF16)
+    for y in range(4):
+        basis_ref[y] = got_ref[4 * y + place_ref[0], 64:]
 
 
 def over_zh_zg_body(got_ref, out_ref):
@@ -184,20 +186,10 @@
         out_ref[to] = total
 
 
-def slot_of(owner):
-    return owner & 1, owner >> 1
-
-
-def rotate_body(owner_ref, place_ref, got_ref, basis_any, out_ref, panels_ref, basis, grads, ordered, sems):
-    zg, zl = place_ref[0], place_ref[1]
-    copies = []
-    for j in range(8):
-        zh, z = slot_of(owner_ref[j])
-        copies.append(pltpu.make_async_copy(basis_any.at[zh, zg, z, zl], basis.at[j], sems.at[j]))
-    for g in range(2):
-        zh, z = slot_of(owner_ref[zl + 4 * g])
-        copies.append(pltpu.make_async_copy(basis_any.at[zh, zg, z], panels_ref.at[g], sems.at[8 + g]))
-    started(copies)
+def rotate_body(owner_ref, place_ref, got_ref, own_ref, other_ref, out_ref, basis, grads, ordered):
+    basis[0] = own_ref[...]
+    basis[1] = other_ref[...]
+    slots = [(place_ref[1] ^ (owner_ref[j] & 1), owner_ref[j] >> 1) for j in range(8)]
     for y in range(4):
         for x in range(4):
             at = 32 * (8 * x + 2 * y)
@@ -210,31 +202,33 @@
     inside = iota((64, 128), 1) < 108
     total = jnp.zeros((64, 256), F32)
     for j in range(8):
-        copies[j].wait()
-        block = jnp.where(inside, basis[j].astype(F32), 0.0).astype(BF16)
+        block = jnp.where(inside, basis[slots[j]].astype(F32), 0.0).astype(BF16)
         rows = ordered[108 * j : 108 * j + 128, :].astype(BF16)
         total = total + jnp.dot(block, rows, preferred_element_type=F32)
+    total = jnp.concatenate([total[:56, :128], total[:56, 128:]], axis=0)
+    high = total.astype(BF16)
+    rest = (total - high.astype(F32)).astype(BF16)
     for to in range(4):
-        out_ref[to] = total[:56]
-    for copy in copies[8:]:
-        copy.wait()
-
-
-def update_body(
-    got_ref, basis, out_basis_any, out_eigen_any, out_ref, out_basis, out_eigen, ordered, sems
-):
+        out_ref[to, :112] = high
+        out_ref[to, 112:224] = rest
+        for g in range(2):
+            out_ref[to, 224 + 64 * g : 288 + 64 * g] = basis[slots[to + 4 * g]]
+
+
+def update_body(got_ref, out_basis_any, out_eigen_any, out_ref, out_basis, out_eigen, ordered, sems):
     copies = [
         pltpu.make_async_copy(out_basis_any, out_basis, sems.at[0]),
         pltpu.make_async_copy(out_eigen_any, out_eigen, sems.at[1]),
     ]
     started(copies)
     highest = lax.Precision.HIGHEST
-    rotated = (got_ref[0] + got_ref[1]) + (got_ref[2] + got_ref[3])
+    total = sum(got_ref[i, :112].astype(F32) + got_ref[i, 112:224].astype(F32) for i in range(4))
+    rotated = jnp.concatenate([total[:56], total[56:]], axis=1)
     rotated = jnp.concatenate([rotated, jnp.zeros((8, 256), F32)], axis=0)
     for copy in copies:
         copy.wait()
     rotated = jnp.dot(rotated, out_basis[...], precision=highest, preferred_element_type=F32)
-    terms = basis[0, 0].astype(F32)
+    terms = got_ref[0, 224:288].astype(F32)
     eigen = (terms[:, 108:109] + terms[:, 109:110]) + terms[:, 110:111]
     scaled = rotated / (eigen * out_eigen[...] + DAMPING)
     scaled = jnp.where(iota((64, 256), 0) < 54, scaled, 0.0)
@@ -245,7 +239,7 @@
     rest = (turned - high.astype(F32)).astype(BF16)
     for g in range(2):
         for r in range(4):
-            block = basis[g, r].astype(F32).T.astype(BF16)
+            block = got_ref[r, 224 + 64 * g : 288 + 64 * g].astype(F32).T.astype(BF16)
             rows = jnp.dot(block, high, preferred_element_type=F32) + jnp.dot(block, rest, preferred_element_type=F32)
             for c in range(2):
                 ordered[g, c, pl.ds(r, 108, stride=4), :] = rows[:108, 128 * c : 128 * c + 128]
@@ -307,10 +301,6 @@
     return lax.ppermute(block, SPACE, up), lax.ppermute(block, SPACE, down)
 
 
-def turned(block):
-    return lax.ppermute(block, ("y", "zl"), [(4 * y + z, 4 * z + y) for y in range(4) for z in range(4)])
-
-
 def per_device(
     activations,
     conv_weight,
@@ -323,29 +313,17 @@
     output_eigen,
 ):
     dma = pltpu.SemaphoreType.DMA
-    place = jnp.stack([lax.axis_index("zg"), lax.axis_index("zl")]).astype(jnp.int32)
+    place = jnp.stack([lax.axis_index("y"), lax.axis_index("zh")]).astype(jnp.int32)
     inner = lax.axis_index(XC).astype(jnp.int32).reshape(1)
     plane = activations.reshape(256, 128)
     low, high = neighbours(plane)
 
-    stored = call(
-        basis_body,
-        shape((4, 64, 128), BF16),
-        arrays=(basis_panels[0].T,),
-        remote=(input_eigen.reshape(1, 54),),
-        scratch=[pltpu.VMEM((1, 54), F32), dma],
-        flops=4_000_000_000,
-    )
-
-    stored = turned(stored)
-    basis = lax.all_gather(stored, ("zh", "zg", "zl")).reshape(2, 2, 4, 4, 64, 128)
     delta, send = call(
         forward_body,
         [shape((256, 256), BF16), shape((8, 384, 128), BF16)],
         (inner,),
         (low, high),
         (plane, conv_weight, conv_bias.reshape(1, 256), cotangent.reshape(256, 256)),
-        (stored,),
         scratch=[
             pltpu.VMEM((256, 3456), BF16),
             pltpu.VMEM((256, 128), BF16),
@@ -358,10 +336,18 @@
     )
     delta_low, delta_high = neighbours(delta)
     got = exchange(send, XC)
+    stored = call(
+        basis_body,
+        shape((4, 64, 128), BF16),
+        arrays=(basis_panels[0].T,),
+        remote=(input_eigen.reshape(1, 54),),
+        after=(delta,),
+        scratch=[pltpu.VMEM((1, 54), F32), dma],
+    )
     part = call(
         weight_grad_body,
-        shape((16, 64, 128), BF16),
-        arrays=(got,),
+        shape((16, 128, 128), BF16),
+        arrays=(got, stored),
         after=(delta_low, delta_high),
         scratch=[pltpu.VMEM((288, 2560), BF16), pltpu.VMEM((2048, 128), BF16), pltpu.VMEM((864, 128), F32)],
         flops=2 * 864 * 2048 * 128,
@@ -375,29 +361,32 @@
         scratch=[pltpu.VMEM((3456, 256), BF16), dma],
         flops=2 * 256 * 3456 * 256,
     )
-    part = call(over_y_zl_body, shape((4, 64, 128), BF16), arrays=(exchange(part, ("y", "zl")),), after=(token,))
+    part, own = call(
+        over_y_zl_body,
+        [shape((4, 64, 128), BF16), shape((4, 64, 128), BF16)],
+        (place,),
+        (exchange(part, ("y", "zl")),),
+        after=(token,),
+    )
+    other = lax.ppermute(own, "zh", [(0, 1), (1, 0)])
     part = call(over_zh_zg_body, shape((32, 64, 128), BF16), arrays=(exchange(part, ("zh", "zg")),))
     grads = exchange(part, YXC)
-    rotated, panels = call(
+    rotated = call(
         rotate_body,
-        [shape((4, 56, 256), F32), shape((2, 4, 64, 128), BF16)],
+        shape((4, 352, 128), BF16),
         (panel_owner, place),
-        (grads,),
-        (basis,),
+        (grads, own, other),
         scratch=[
-            pltpu.VMEM((8, 64, 128), BF16),
+            pltpu.VMEM((2, 4, 64, 128), BF16),
             pltpu.VMEM((2, 1024, 128), F32),
             pltpu.VMEM((896, 256), F32),
-            dma((10,)),
         ],
-        limit=LIMIT + 15_000_000,
     )
     part = call(
         update_body,
         shape((8, 112, 256), BF16),
-        (),
-        (exchange(rotated, "zl"), panels),
-        (output_basis, output_eigen.reshape(1, 256)),
+        arrays=(exchange(rotated, "zl"),),
+        remote=(output_basis, output_eigen.reshape(1, 256)),
         scratch=[
             pltpu.VMEM((256, 256), F32),
             pltpu.VMEM((1, 256), F32),

time: 176 us -> 168 us (0.955)
  between operations: 14.2 us -> 0.8 us
  waiting for transfers between devices: 26.9 us -> 34.6 us
  starting transfers between devices: 44.6 us -> 39 us
  blocking collectives: 71.6 us -> 76.5 us
    ppermute x1, waiting for transfers between devices: 0.01 us -> 12.4 us  [per_device(): other = lax.ppermute(own, 'zh', [(0, 1), (1, 0)])]
    all_to_all x3, starting transfers between devices: 28.3 us -> 19.8 us  [exchange(): return lax.all_to_all(x, axes, 0, 0)]
    all_to_all x4, blocking collectives: 71.6 us -> 76.5 us  [exchange(): return lax.all_to_all(x, axes, 0, 0)]
    all_to_all x3, waiting for transfers between devices: 17.6 us -> 13.5 us  [exchange(): return lax.all_to_all(x, axes, 0, 0)]
    ppermute x4, waiting for transfers between devices: 6.47 us -> 8.69 us  [neighbours(): return (lax.ppermute(block, SPACE, up), lax.ppermute(block, SPACE, down))]
    all_gather x1 -> x0, waiting for transfers between devices: 2.17 us -> none  [per_device(): lax.all_gather(stored, ('zh', 'zg', 'zl')).reshape(2, 2, 4, 4, 64, 128)]
    ppermute x1, starting transfers between devices: 0.8 us -> 2.66 us  [per_device(): other = lax.ppermute(own, 'zh', [(0, 1), (1, 0)])]
    unnamed x22 -> x20, local copies, waits for them, and re-layouts: 3.49 us -> 3.93 us
  transfers between devices with their start and end apart: 9 -> 8, of which waited for: 5 -> 4; matrix products, arithmetic and copies ran while one was open for 0% -> 0% of each run, Pallas kernels for 3% -> 1%
where the time goes in v6:
time: 168 us; the launch traced here: 167 us
  blocking collectives  76.5 us (46%)
  starting transfers between devices  39 us (23%)
  waiting for transfers between devices  34.6 us (21%)
  Pallas kernels  12.1 us (7%)
  local copies, waits for them, and re-layouts  3.93 us (2%)
    all_to_all x4, blocking collectives, exchange(): return lax.all_to_all(x, axes, 0, 0)  76.5 us
    all_to_all x3, starting transfers between devices, exchange(): return lax.all_to_all(x, axes, 0, 0)  19.8 us
    ppermute x4, starting transfers between devices, neighbours(): return (lax.ppermute(block, SPACE, up), lax.ppermute(block, SPACE, down))  16.5 us
    all_to_all x3, waiting for transfers between devices, exchange(): return lax.all_to_all(x, axes, 0, 0)  13.5 us
    ppermute x1, waiting for transfers between devices, per_device(): other = lax.ppermute(own, 'zh', [(0, 1), (1, 0)])  12.4 us
    pallas_call x10, Pallas kernels, call(): pl.pallas_call(kernel, out_shape=out_shape, in_specs=[SMEM] * len(scalars...  12.1 us
    ppermute x4, waiting for transfers between devices, neighbours(): return (lax.ppermute(block, SPACE, up), lax.ppermute(block, SPACE, down))  8.69 us
    unnamed x20, local copies, waits for them, and re-layouts  3.93 us
  transfers between devices with their start and end apart: 8, of which 4 were waited for; matrix products, arithmetic and copies ran while one was open for 0% of the time, Pallas kernels for 1%

profile of v6, /device:TPU:1, one launch (start us, length us, event | category | flops | bytes accessed | tf_op | source)
XLA Modules:
  0.0 167.0 jit_solution(14718147162970926967)
XLA Ops:
  0.6 8.8 %collective-permute-start.1 = (bf16[256,128]{1,0:T(8,128)(2,1)}, bf16[256,128]{1,0:T(8,128)(2,1)S(1)}, u32[]{:S(2)}, u32[]{:S(2)}) collective-permute-start(bf16[256,128]{1,0:T(8,128)(2,1)} %bitcast.13), channel_id=1, source_target_pairs={{1,0},{2,1},{3,2},{4,3},{5,4},{6,5},{7,6},{8,7},{9,8},{10,9},{11,1... | collective-permute-start | bytes 196616 | tf_op jit(solution)/shard_map/ppermute | solution.py:301
  9.4 1.9 %collective-permute-start = (bf16[256,128]{1,0:T(8,128)(2,1)}, bf16[256,128]{1,0:T(8,128)(2,1)S(1)}, u32[]{:S(2)}, u32[]{:S(2)}) collective-permute-start(bf16[256,128]{1,0:T(8,128)(2,1)} %bitcast.14), channel_id=1, source_target_pairs={{0,1},{1,2},{2,3},{3,4},{4,5},{5,6},{6,7},{7,8},{8,9},{9,10},{10,1... | collective-permute-start | bytes 196616 | tf_op jit(solution)/shard_map/ppermute | solution.py:301
  11.4 1.6 collective-permute-done.refs_1_
  13.0 1.5 copy-done
  14.5 0.9 copy-done.3
  15.4 0.8 copy-done.4
  16.2 0.7 copy-done.6
  16.9 2.5 %shard_map.104 = (bf16[256,256]{1,0:T(8,128)(2,1)S(1)}, bf16[8,384,128]{2,1,0:T(8,128)(2,1)}) custom-call(s32[1]{0:T(128)} %bitcast.refs_0_, bf16[256,128]{1,0:T(8,128)(2,1)S(1)} %collective-permute-done.refs_1_, bf16[256,128]{1,0:T(8,128)(2,1)S(1)} %collective-permute-done.1.refs_2_, bf16[256,128]{1,0:T(8,128)(2,1)S(1)} %bitcast.15, ...), custom_call_target="tpu_custom_call" | custom-call | flops 452984832 | bytes 2098180 | tf_op jit(solution)/shard_map/pallas_call | solution.py:33
  19.4 3.9 %all-to-all-start = ((bf16[8,384,128]{2,1,0:T(8,128)(2,1)}), bf16[8,384,128]{2,1,0:T(8,128)(2,1)S(1)}, u32[]{:S(2)}, u32[]{:S(2)}) async-start(bf16[8,384,128]{2,1,0:T(8,128)(2,1)} %get-tuple-element.9), calls=%async_computation | async-start | bytes 1572864 | tf_op jit(solution)/shard_map/all_to_all | solution.py:57
  23.4 2.0 %collective-permute-start.3 = (bf16[256,256]{1,0:T(8,128)(2,1)S(1)}, bf16[256,256]{1,0:T(8,128)(2,1)S(1)}, u32[]{:S(2)}, u32[]{:S(2)}) collective-permute-start(bf16[256,256]{1,0:T(8,128)(2,1)S(1)} %get-tuple-element.8.refs_2_), channel_id=1, source_target_pairs={{1,0},{2,1},{3,2},{4,3},{5,4},{6,5},{7,6},{8,7},{9,8},{10,9},{11,1... | collective-permute-start | bytes 393224 | tf_op jit(solution)/shard_map/ppermute | solution.py:301
  25.4 3.8 %collective-permute-start.2 = (bf16[256,256]{1,0:T(8,128)(2,1)S(1)}, bf16[256,256]{1,0:T(8,128)(2,1)S(1)}, u32[]{:S(2)}, u32[]{:S(2)}) collective-permute-start(bf16[256,256]{1,0:T(8,128)(2,1)S(1)} %get-tuple-element.8.refs_2_), channel_id=1, source_target_pairs={{0,1},{1,2},{2,3},{3,4},{4,5},{5,6},{6,7},{7,8},{8,9},{9,10},{10,1... | collective-permute-start | bytes 393224 | tf_op jit(solution)/shard_map/ppermute | solution.py:301
  29.2 0.3 shard_map.105.refs_1_
  29.5 7.1 %collective-permute-done.3.refs_3_.refs_1_ = bf16[256,256]{1,0:T(8,128)(2,1)S(1)} collective-permute-done((bf16[256,256]{1,0:T(8,128)(2,1)S(1)}, bf16[256,256]{1,0:T(8,128)(2,1)S(1)}, u32[]{:S(2)}, u32[]{:S(2)}) %collective-permute-start.3) | collective-permute-done | bytes 131104 | tf_op jit(solution)/shard_map/ppermute | solution.py:301
  36.6 2.3 %shard_map.106.refs_4_ = bf16[16,128,128]{2,1,0:T(8,128)(2,1)} custom-call(bf16[8,384,128]{2,1,0:T(8,128)(2,1)S(1)} %all-to-all-done.refs_0_, bf16[4,64,128]{2,1,0:T(8,128)(2,1)S(1)} %shard_map.105.refs_1_, bf16[256,256]{1,0:T(8,128)(2,1)S(1)} %collective-permute-done.2.refs_2_.refs_0_, bf16[256,256]{1,0:T(8,128)(2,1)S(1)} %collective-permute-done.3.refs_3_.refs_1_), custom_call_target="tpu_custom_call" | custom-call | flops 452984832 | bytes 1114112 | tf_op jit(solution)/shard_map/pallas_call | solution.py:33
  38.9 9.1 %all-to-all-start.1 = ((bf16[16,128,128]{2,1,0:T(8,128)(2,1)}), bf16[16,128,128]{2,1,0:T(8,128)(2,1)S(1)}, u32[]{:S(2)}, u32[]{:S(2)}) async-start(bf16[16,128,128]{2,1,0:T(8,128)(2,1)} %shard_map.106.refs_4_), calls=%async_computation.1 | async-start | bytes 1048576 | tf_op jit(solution)/shard_map/all_to_all | solution.py:57
  48.0 0.1 pad_add_fusion.refs_0_.refs_1_
  48.1 2.1 %shard_map.107 = (bf16[256,128]{1,0:T(8,128)(2,1)}, f32[8,128]{1,0:T(8,128)S(1)}) custom-call(bf16[256,256]{1,0:T(8,128)(2,1)S(1)} %collective-permute-done.2.refs_2_.refs_0_, bf16[256,256]{1,0:T(8,128)(2,1)S(1)} %collective-permute-done.3.refs_3_.refs_1_, bf16[256,256]{1,0:T(8,128)(2,1)S(1)} %get-tuple-element.8.refs_2_, bf16[3456,256]{1,0:T(8,128)(2,1)S(1)} %copy-done.1, ...), custom_call_target="tpu_custom_call" | custom-call | flops 452984832 | bytes 2686976 | tf_op jit(solution)/shard_map/pallas_call | solution.py:33
  50.2 0.0 copy-start.9
  50.2 13.5 %all-to-all-done.1.refs_1_ = bf16[16,128,128]{2,1,0:T(8,128)(2,1)S(1)} async-done(((bf16[16,128,128]{2,1,0:T(8,128)(2,1)}), bf16[16,128,128]{2,1,0:T(8,128)(2,1)S(1)}, u32[]{:S(2)}, u32[]{:S(2)}) %all-to-all-start.1) | async-done | bytes 524320 | tf_op jit(solution)/shard_map/all_to_all | solution.py:57
  63.7 0.6 shard_map.108
  64.3 24.8 %all_to_all.35.refs_0_ = bf16[4,64,128]{2,1,0:T(8,128)(2,1)S(1)} all-to-all(bf16[4,64,128]{2,1,0:T(8,128)(2,1)S(1)} %get-tuple-element.12), channel_id=1, replica_groups=mesh['y'=4,'zh'=2,'zg'=2,'zl'=4,'x'=4,'c'=2] {'zh','zg'}, dimensions={0} | all-to-all | bytes 131072 | tf_op jit(solution)/shard_map/all_to_all | solution.py:57
  89.1 0.9 shard_map.109
  90.0 6.8 %all-to-all-start.3 = ((bf16[32,64,128]{2,1,0:T(8,128)(2,1)}), bf16[32,64,128]{2,1,0:T(8,128)(2,1)S(1)}, u32[]{:S(2)}, u32[]{:S(2)}) async-start(bf16[32,64,128]{2,1,0:T(8,128)(2,1)} %shard_map.109), calls=%async_computation.3 | async-start | bytes 1048576 | tf_op jit(solution)/shard_map/all_to_all | solution.py:57
  96.7 2.7 %collective-permute-start.4 = (bf16[4,64,128]{2,1,0:T(8,128)(2,1)S(1)}, bf16[4,64,128]{2,1,0:T(8,128)(2,1)S(1)}, u32[]{:S(2)}, u32[]{:S(2)}) collective-permute-start(bf16[4,64,128]{2,1,0:T(8,128)(2,1)S(1)} %get-tuple-element.13.refs_3_), channel_id=1, source_target_pairs={{0,64},{64,0},{1,65},{65,1},{2,66},{66,2},{3,67},{67,3},{4,68},{68... | collective-permute-start | bytes 196616 | tf_op jit(solution)/shard_map/ppermute | solution.py:371
  99.4 12.4 %collective-permute-done.4.refs_4_ = bf16[4,64,128]{2,1,0:T(8,128)(2,1)S(1)} collective-permute-done((bf16[4,64,128]{2,1,0:T(8,128)(2,1)S(1)}, bf16[4,64,128]{2,1,0:T(8,128)(2,1)S(1)}, u32[]{:S(2)}, u32[]{:S(2)}) %collective-permute-start.4) | collective-permute-done | bytes 65568 | tf_op jit(solution)/shard_map/ppermute | solution.py:371
  111.8 1.3 shard_map.110
  113.1 9.8 %all_to_all.36.refs_0_ = bf16[4,352,128]{2,1,0:T(8,128)(2,1)S(1)} all-to-all(bf16[4,352,128]{2,1,0:T(8,128)(2,1)S(1)} %shard_map.110), channel_id=1, replica_groups=mesh['y'=4,'zh'=2,'zg'=2,'zl'=4,'x'=4,'c'=2] {'zl'}, dimensions={0} | all-to-all | bytes 720896 | tf_op jit(solution)/shard_map/all_to_all | solution.py:57
  122.9 1.4 shard_map.111
  124.3 18.0 %all_to_all.37.refs_0_ = bf16[8,112,256]{2,1,0:T(8,128)(2,1)S(1)} all-to-all(bf16[8,112,256]{2,1,0:T(8,128)(2,1)S(1)} %shard_map.111), channel_id=1, replica_groups=mesh['y'=4,'zh'=2,'zg'=2,'zl'=4,'x'=4,'c'=2] {'x','c'}, dimensions={0} | all-to-all | bytes 917504 | tf_op jit(solution)/shard_map/all_to_all | solution.py:57
  142.3 0.1 shard_map.112
  142.4 23.9 %all_to_all.38.refs_0_ = bf16[8,112,128]{2,1,0:T(8,128)(2,1)S(1)} all-to-all(bf16[8,112,128]{2,1,0:T(8,128)(2,1)S(1)} %shard_map.112), channel_id=1, replica_groups=mesh['y'=4,'zh'=2,'zg'=2,'zl'=4,'x'=4,'c'=2] {'zg','y'}, dimensions={0} | all-to-all | bytes 458752 | tf_op jit(solution)/shard_map/all_to_all | solution.py:57
  166.4 0.7 shard_map.113
  (19 shorter events, 0.0 us)
Async XLA Ops:
  0.6 10.7 %collective-permute-start.1 = (bf16[256,128]{1,0:T(8,128)(2,1)}, bf16[256,128]{1,0:T(8,128)(2,1)S(1)}, u32[]{:S(2)}, u32[]{:S(2)}) collective-permute-start(bf16[256,128]{1,0:T(8,128)(2,1)} %bitcast.13), channel_id=1, source_target_pairs={{1,0},{2,1},{3,2},{4,3},{5,4},{6,5},{7,6},{8,7},{9,8},{10,9},{11,1... | collective-permute-start | bytes 196616 | tf_op jit(solution)/shard_map/ppermute | solution.py:301
  9.4 3.6 %collective-permute-start = (bf16[256,128]{1,0:T(8,128)(2,1)}, bf16[256,128]{1,0:T(8,128)(2,1)S(1)}, u32[]{:S(2)}, u32[]{:S(2)}) collective-permute-start(bf16[256,128]{1,0:T(8,128)(2,1)} %bitcast.14), channel_id=1, source_target_pairs={{0,1},{1,2},{2,3},{3,4},{4,5},{5,6},{6,7},{7,8},{8,9},{9,10},{10,1... | collective-permute-start | bytes 196616 | tf_op jit(solution)/shard_map/ppermute | solution.py:301
  13.0 1.5 copy-start
  14.5 0.9 copy-start.3
  15.4 0.8 copy-start.4
  16.2 0.7 copy-start.6
  16.9 12.3 %copy-start.5 = (bf16[1,432,54]{1,2,0:T(8,128)(2,1)S(1)}, bf16[1,432,54]{1,2,0:T(8,128)(2,1)}, u32[]{:S(2)}) copy-start(bf16[1,432,54]{1,2,0:T(8,128)(2,1)} %param.13) | copy-start | bytes 139972
  16.9 12.3 %copy-start.8 = (f32[54]{0:T(128)S(1)}, f32[54]{0:T(128)}, u32[]{:S(2)}) copy-start(f32[54]{0:T(128)} %param.16) | copy-start | bytes 652
  19.4 17.2 %all-to-all-start = ((bf16[8,384,128]{2,1,0:T(8,128)(2,1)}), bf16[8,384,128]{2,1,0:T(8,128)(2,1)S(1)}, u32[]{:S(2)}, u32[]{:S(2)}) async-start(bf16[8,384,128]{2,1,0:T(8,128)(2,1)} %get-tuple-element.9), calls=%async_computation | async-start | bytes 1572864 | tf_op jit(solution)/shard_map/all_to_all | solution.py:57
  23.4 24.7 %copy-start.1 = (bf16[3456,256]{1,0:T(8,128)(2,1)S(1)}, bf16[3456,256]{1,0:T(8,128)(2,1)}, u32[]{:S(2)}) copy-start(bf16[3456,256]{1,0:T(8,128)(2,1)} %refs_3_.1) | copy-start | bytes 5308420
  23.4 13.2 %collective-permute-start.3 = (bf16[256,256]{1,0:T(8,128)(2,1)S(1)}, bf16[256,256]{1,0:T(8,128)(2,1)S(1)}, u32[]{:S(2)}, u32[]{:S(2)}) collective-permute-start(bf16[256,256]{1,0:T(8,128)(2,1)S(1)} %get-tuple-element.8.refs_2_), channel_id=1, source_target_pairs={{1,0},{2,1},{3,2},{4,3},{5,4},{6,5},{7,6},{8,7},{9,8},{10,9},{11,1... | collective-permute-start | bytes 393224 | tf_op jit(solution)/shard_map/ppermute | solution.py:301
  25.4 11.2 %collective-permute-start.2 = (bf16[256,256]{1,0:T(8,128)(2,1)S(1)}, bf16[256,256]{1,0:T(8,128)(2,1)S(1)}, u32[]{:S(2)}, u32[]{:S(2)}) collective-permute-start(bf16[256,256]{1,0:T(8,128)(2,1)S(1)} %get-tuple-element.8.refs_2_), channel_id=1, source_target_pairs={{0,1},{1,2},{2,3},{3,4},{4,5},{5,6},{6,7},{7,8},{8,9},{9,10},{10,1... | collective-permute-start | bytes 393224 | tf_op jit(solution)/shard_map/ppermute | solution.py:301
  38.9 24.8 %all-to-all-start.1 = ((bf16[16,128,128]{2,1,0:T(8,128)(2,1)}), bf16[16,128,128]{2,1,0:T(8,128)(2,1)S(1)}, u32[]{:S(2)}, u32[]{:S(2)}) async-start(bf16[16,128,128]{2,1,0:T(8,128)(2,1)} %shard_map.106.refs_4_), calls=%async_computation.1 | async-start | bytes 1048576 | tf_op jit(solution)/shard_map/all_to_all | solution.py:57
  50.2 61.6 %copy-start.9 = (s32[8]{0:T(128)S(1)}, s32[8]{0:T(128)}, u32[]{:S(2)}) copy-start(s32[8]{0:T(128)} %refs_0_.1) | copy-start | bytes 100
  64.3 58.6 %copy-start.2 = (f32[256,256]{1,0:T(8,128)S(1)}, f32[256,256]{1,0:T(8,128)}, u32[]{:S(2)}) copy-start(f32[256,256]{1,0:T(8,128)} %refs_1_.1) | copy-start | bytes 786436
  64.3 58.6 %copy-start.7 = (f32[256]{0:T(256)S(1)}, f32[256]{0:T(256)}, u32[]{:S(2)}) copy-start(f32[256]{0:T(256)} %param.17) | copy-start | bytes 3076
  90.0 21.8 %all-to-all-start.3 = ((bf16[32,64,128]{2,1,0:T(8,128)(2,1)}), bf16[32,64,128]{2,1,0:T(8,128)(2,1)S(1)}, u32[]{:S(2)}, u32[]{:S(2)}) async-start(bf16[32,64,128]{2,1,0:T(8,128)(2,1)} %shard_map.109), calls=%async_computation.3 | async-start | bytes 1048576 | tf_op jit(solution)/shard_map/all_to_all | solution.py:57
  96.7 15.0 %collective-permute-start.4 = (bf16[4,64,128]{2,1,0:T(8,128)(2,1)S(1)}, bf16[4,64,128]{2,1,0:T(8,128)(2,1)S(1)}, u32[]{:S(2)}, u32[]{:S(2)}) collective-permute-start(bf16[4,64,128]{2,1,0:T(8,128)(2,1)S(1)} %get-tuple-element.13.refs_3_), channel_id=1, source_target_pairs={{0,64},{64,0},{1,65},{65,1},{2,66},{66,2},{3,67},{67,3},{4,68},{68... | collective-permute-start | bytes 196616 | tf_op jit(solution)/shard_map/ppermute | solution.py:371

commit v7 on v6

--- a/solution.py
+++ b/solution.py
@@ -93,21 +93,13 @@
 
 
 def forward_body(
-    place_ref, low_ref, high_ref, mine_any, weight_any, bias_any, cot_any,
-    delta_ref, send_ref, patches, mine, weight, bias, cot, sems,
+    place_ref, low_ref, high_ref, mine, weight, bias, cot, basis_ref, delta_ref, send_ref, slices_ref, patches
 ):
-    copies = started(
-        [
-            pltpu.make_async_copy(source, target, sems.at[i])
-            for i, (source, target) in enumerate(
-                [(mine_any, mine), (weight_any, weight), (bias_any, bias), (cot_any, cot)]
-            )
-        ]
-    )
+    for y in range(4):
+        for r in range(4):
+            slices_ref[4 * y + r] = basis_ref[r]
     none = jnp.zeros((16, 128), BF16)
-    for a in (0, 2, 1):
-        if a == 1:
-            copies[0].wait()
+    for a in range(3):
         wide = (low_ref, mine, high_ref)[a][...].astype(F32)
         for c in range(3):
             moved = x_shifted(wide, c - 1).astype(BF16)
@@ -120,8 +112,6 @@
                 else:
                     shifted = moved
                 patches[:, at : at + 128] = shifted
-    for copy in copies[1:]:
-        copy.wait()
     pre = jnp.dot(patches[...], weight[...], preferred_element_type=F32) + bias[...]
     logistic = 1.0 / (1.0 + jnp.exp(-pre))
     delta = (cot[...].astype(F32) * logistic * (1.0 + pre * (1.0 - logistic))).astype(BF16)
@@ -140,7 +130,7 @@
             send_ref[to, 128:] = delta[:, 128 * c : 128 * c + 128]
 
 
-def weight_grad_body(got_ref, basis_ref, out_ref, moved, deltas, whole):
+def weight_grad_body(got_ref, out_ref, moved, deltas, whole):
     pieces = []
     for plane, at in [(0, 64)] + [(e, 0) for e in range(8)] + [(7, 64)]:
         pieces.append(got_ref[plane, at : at + 32].astype(F32))
@@ -168,28 +158,31 @@
             for e in range(2):
                 parts.append(whole[pl.ds(8 * y_to + 4 * e + z_to, 27, stride=32), :])
                 parts.append(none)
-            out_ref[4 * y_to + z_to, :64] = jnp.concatenate(parts, axis=0).astype(BF16)
-            out_ref[4 * y_to + z_to, 64:] = basis_ref[z_to]
-
-
-def over_y_zl_body(place_ref, got_ref, out_ref, basis_ref):
-    total = sum(got_ref[i, :64].astype(F32) for i in range(16)) * (1.0 / CELLS)
+            out_ref[4 * y_to + z_to] = jnp.concatenate(parts, axis=0).astype(BF16)
+
+
+def over_y_zl_body(place_ref, got_ref, basis_ref, out_ref):
+    total = (sum(got_ref[i].astype(F32) for i in range(16)) * (1.0 / CELLS)).astype(BF16)
     for to in range(4):
-        out_ref[to] = total.astype(BF16)
+        out_ref[to, :64] = total
     for y in range(4):
-        basis_ref[y] = got_ref[4 * y + place_ref[0], 64:]
-
-
-def over_zh_zg_body(got_ref, out_ref):
-    total = ((got_ref[0].astype(F32) + got_ref[1].astype(F32)) + (got_ref[2].astype(F32) + got_ref[3].astype(F32))).astype(BF16)
+        block = basis_ref[4 * y + place_ref[0]]
+        for to in range(4):
+            out_ref[to, 64 + 64 * y : 128 + 64 * y] = block
+
+
+def over_zh_zg_body(got_ref, out_ref, basis_ref):
+    total = sum(got_ref[i, :64].astype(F32) for i in range(4)).astype(BF16)
     for to in range(32):
         out_ref[to] = total
-
-
-def rotate_body(owner_ref, place_ref, got_ref, own_ref, other_ref, out_ref, basis, grads, ordered):
-    basis[0] = own_ref[...]
-    basis[1] = other_ref[...]
-    slots = [(place_ref[1] ^ (owner_ref[j] & 1), owner_ref[j] >> 1) for j in range(8)]
+    for zh in range(2):
+        for y in range(4):
+            for zg in range(2):
+                block = got_ref[2 * zh + zg, 64 + 64 * y : 128 + 64 * y]
+                basis_ref[2 * y + zh, 64 * zg : 64 * zg + 64] = block
+
+
+def rotate_body(owner_ref, place_ref, got_ref, basis_ref, out_ref, grads, ordered):
     for y in range(4):
         for x in range(4):
             at = 32 * (8 * x + 2 * y)
@@ -199,20 +192,18 @@
         for c in range(2):
             ordered[32 * tap : 32 * tap + 32, 128 * c : 128 * c + 128] = grads[c, pl.ds(tap, 32, stride=32), :]
     ordered[864:, :] = jnp.zeros((32, 256), F32)
-    inside = iota((64, 128), 1) < 108
-    total = jnp.zeros((64, 256), F32)
+    inside = iota((128, 128), 1) < 108
+    total = jnp.zeros((128, 256), F32)
     for j in range(8):
-        block = jnp.where(inside, basis[slots[j]].astype(F32), 0.0).astype(BF16)
+        block = jnp.where(inside, basis_ref[owner_ref[j]].astype(F32), 0.0).astype(BF16)
         rows = ordered[108 * j : 108 * j + 128, :].astype(BF16)
         total = total + jnp.dot(block, rows, preferred_element_type=F32)
-    total = jnp.concatenate([total[:56, :128], total[:56, 128:]], axis=0)
-    high = total.astype(BF16)
-    rest = (total - high.astype(F32)).astype(BF16)
+    total = jnp.concatenate(
+        [total[64 * zg : 64 * zg + 56, 128 * c : 128 * c + 128] for zg in range(2) for c in range(2)], axis=0
+    ).astype(BF16)
     for to in range(4):
-        out_ref[to, :112] = high
-        out_ref[to, 112:224] = rest
-        for g in range(2):
-            out_ref[to, 224 + 64 * g : 288 + 64 * g] = basis[slots[to + 4 * g]]
+        out_ref[to, :224] = total
+        out_ref[to, 224:] = basis_ref[owner_ref[4 * place_ref[1] + to]]
 
 
 def update_body(got_ref, out_basis_any, out_eigen_any, out_ref, out_basis, out_eigen, ordered, sems):
@@ -222,46 +213,46 @@
     ]
     started(copies)
     highest = lax.Precision.HIGHEST
-    total = sum(got_ref[i, :112].astype(F32) + got_ref[i, 112:224].astype(F32) for i in range(4))
-    rotated = jnp.concatenate([total[:56], total[56:]], axis=1)
-    rotated = jnp.concatenate([rotated, jnp.zeros((8, 256), F32)], axis=0)
+    total = sum(got_ref[i, :224].astype(F32) for i in range(4))
+    none = jnp.zeros((8, 256), F32)
+    parts = []
+    for zg in range(2):
+        at = 112 * zg
+        parts.append(jnp.concatenate([total[at : at + 56], total[at + 56 : at + 112]], axis=1))
+        parts.append(none)
+    rotated = jnp.concatenate(parts, axis=0)
     for copy in copies:
         copy.wait()
     rotated = jnp.dot(rotated, out_basis[...], precision=highest, preferred_element_type=F32)
-    terms = got_ref[0, 224:288].astype(F32)
+    terms = got_ref[0, 224:].astype(F32)
     eigen = (terms[:, 108:109] + terms[:, 109:110]) + terms[:, 110:111]
     scaled = rotated / (eigen * out_eigen[...] + DAMPING)
-    scaled = jnp.where(iota((64, 256), 0) < 54, scaled, 0.0)
+    scaled = jnp.where((iota((128, 256), 0) & 63) < 54, scaled, 0.0)
     turned = lax.dot_general(
         scaled, out_basis[...], (((1,), (1,)), ((), ())), precision=highest, preferred_element_type=F32
     )
     high = turned.astype(BF16)
     rest = (turned - high.astype(F32)).astype(BF16)
-    for g in range(2):
-        for r in range(4):
-            block = got_ref[r, 224 + 64 * g : 288 + 64 * g].astype(F32).T.astype(BF16)
-            rows = jnp.dot(block, high, preferred_element_type=F32) + jnp.dot(block, rest, preferred_element_type=F32)
-            for c in range(2):
-                ordered[g, c, pl.ds(r, 108, stride=4), :] = rows[:108, 128 * c : 128 * c + 128]
+    for r in range(4):
+        block = got_ref[r, 224:].astype(F32).T.astype(BF16)
+        rows = jnp.dot(block, high, preferred_element_type=F32) + jnp.dot(block, rest, preferred_element_type=F32)
         for c in range(2):
-            ordered[g, c, 432:, :] = jnp.zeros((8, 128), F32)
+            ordered[c, pl.ds(r, 108, stride=4), :] = rows[:108, 128 * c : 128 * c + 128]
     for c in range(2):
-        for to in range(8):
-            rows = [ordered[g, c, 54 * to : 54 * to + 56, :] for g in range(2)]
-            out_ref[to, :, 128 * c : 128 * c + 128] = jnp.concatenate(rows, axis=0).astype(BF16)
+        ordered[c, 432:, :] = jnp.zeros((8, 128), F32)
+    for to in range(8):
+        rows = [ordered[c, 54 * to : 54 * to + 56, :] for c in range(2)]
+        out_ref[to] = jnp.concatenate(rows, axis=0).astype(BF16)
 
 
 def over_xc_body(got_ref, out_ref):
     total = sum(got_ref[i].astype(F32) for i in range(8))
-    for g in range(2):
-        rows = total[56 * g : 56 * g + 56]
-        rows = jnp.concatenate([rows[:, :128], rows[:, 128:]], axis=0).astype(BF16)
-        for y in range(4):
-            out_ref[4 * g + y] = rows
+    for to in range(4):
+        out_ref[to] = total
 
 
 def last_body(got_ref, out_ref):
-    total = sum(got_ref[i].astype(F32) for i in range(8))
+    total = (got_ref[0] + got_ref[1]) + (got_ref[2] + got_ref[3])
     out_ref[...] = jnp.concatenate([total[:54], total[56:110]], axis=1)
 
 
@@ -313,44 +304,43 @@
     output_eigen,
 ):
     dma = pltpu.SemaphoreType.DMA
-    place = jnp.stack([lax.axis_index("y"), lax.axis_index("zh")]).astype(jnp.int32)
+    place = jnp.stack([lax.axis_index("y"), lax.axis_index("zg")]).astype(jnp.int32)
     inner = lax.axis_index(XC).astype(jnp.int32).reshape(1)
     plane = activations.reshape(256, 128)
     low, high = neighbours(plane)
 
-    delta, send = call(
-        forward_body,
-        [shape((256, 256), BF16), shape((8, 384, 128), BF16)],
-        (inner,),
-        (low, high),
-        (plane, conv_weight, conv_bias.reshape(1, 256), cotangent.reshape(256, 256)),
-        scratch=[
-            pltpu.VMEM((256, 3456), BF16),
-            pltpu.VMEM((256, 128), BF16),
-            pltpu.VMEM((3456, 256), BF16),
-            pltpu.VMEM((1, 256), F32),
-            pltpu.VMEM((256, 256), BF16),
-            dma((4,)),
-        ],
-        flops=2 * 256 * 3456 * 256,
-    )
-    delta_low, delta_high = neighbours(delta)
-    got = exchange(send, XC)
     stored = call(
         basis_body,
         shape((4, 64, 128), BF16),
         arrays=(basis_panels[0].T,),
         remote=(input_eigen.reshape(1, 54),),
-        after=(delta,),
         scratch=[pltpu.VMEM((1, 54), F32), dma],
-    )
+        flops=4_000_000_000,
+    )
+    delta, send, slices = call(
+        forward_body,
+        [shape((256, 256), BF16), shape((8, 384, 128), BF16), shape((16, 64, 128), BF16)],
+        (inner,),
+        (low, high, plane, conv_weight, conv_bias.reshape(1, 256), cotangent.reshape(256, 256), stored),
+        scratch=[pltpu.VMEM((256, 3456), BF16)],
+        flops=2 * 256 * 3456 * 256,
+    )
+    slices = exchange(slices, ("y", "zl"))
     part = call(
         weight_grad_body,
-        shape((16, 128, 128), BF16),
-        arrays=(got, stored),
-        after=(delta_low, delta_high),
+        shape((16, 64, 128), BF16),
+        arrays=(exchange(send, XC),),
+        after=(slices,),
         scratch=[pltpu.VMEM((288, 2560), BF16), pltpu.VMEM((2048, 128), BF16), pltpu.VMEM((864, 128), F32)],
         flops=2 * 864 * 2048 * 128,
+    )
+    delta_low, delta_high = neighbours(delta)
+    part = call(
+        over_y_zl_body,
+        shape((4, 320, 128), BF16),
+        (place,),
+        (exchange(part, ("y", "zl")), slices),
+        after=(delta_low, delta_high),
     )
     data, token = call(
         data_grad_body,
@@ -361,41 +351,33 @@
         scratch=[pltpu.VMEM((3456, 256), BF16), dma],
         flops=2 * 256 * 3456 * 256,
     )
-    part, own = call(
-        over_y_zl_body,
-        [shape((4, 64, 128), BF16), shape((4, 64, 128), BF16)],
-        (place,),
-        (exchange(part, ("y", "zl")),),
+    part, basis = call(
+        over_zh_zg_body,
+        [shape((32, 64, 128), BF16), shape((8, 128, 128), BF16)],
+        arrays=(exchange(part, ("zh", "zg")),),
         after=(token,),
     )
-    other = lax.ppermute(own, "zh", [(0, 1), (1, 0)])
-    part = call(over_zh_zg_body, shape((32, 64, 128), BF16), arrays=(exchange(part, ("zh", "zg")),))
-    grads = exchange(part, YXC)
     rotated = call(
         rotate_body,
         shape((4, 352, 128), BF16),
         (panel_owner, place),
-        (grads, own, other),
-        scratch=[
-            pltpu.VMEM((2, 4, 64, 128), BF16),
-            pltpu.VMEM((2, 1024, 128), F32),
-            pltpu.VMEM((896, 256), F32),
-        ],
+        (exchange(part, YXC), basis),
+        scratch=[pltpu.VMEM((2, 1024, 128), F32), pltpu.VMEM((896, 256), F32)],
     )
     part = call(
         update_body,
-        shape((8, 112, 256), BF16),
+        shape((8, 112, 128), BF16),
         arrays=(exchange(rotated, "zl"),),
         remote=(output_basis, output_eigen.reshape(1, 256)),
         scratch=[
             pltpu.VMEM((256, 256), F32),
             pltpu.VMEM((1, 256), F32),
-            pltpu.VMEM((2, 2, 440, 128), F32),
+            pltpu.VMEM((2, 440, 128), F32),
             dma((2,)),
         ],
     )
-    part = call(over_xc_body, shape((8, 112, 128), BF16), arrays=(exchange(part, XC),))
-    update = call(last_body, shape((54, 256), F32), arrays=(exchange(part, ("zg", "y")),))
+    part = call(over_xc_body, shape((4, 112, 128), F32), arrays=(exchange(part, XC),))
+    update = call(last_body, shape((54, 256), F32), arrays=(exchange(part, "y"),))
     return (data.reshape(1, 1, 16, 16, 128), update)
 
 

time: 168 us -> 155 us (0.923)
  waiting for transfers between devices: 34.6 us -> 14 us
  blocking collectives: 76.5 us -> 94 us
  starting transfers between devices: 39 us -> 32.6 us
  Pallas kernels: 12.1 us -> 10 us
    all_to_all x4 -> x6, blocking collectives: 76.5 us -> 94 us  [exchange(): return lax.all_to_all(x, axes, 0, 0)]
    ppermute x1 -> x0, waiting for transfers between devices: 12.4 us -> none  [per_device(): other = lax.ppermute(own, 'zh', [(0, 1), (1, 0)])]
    ppermute x4, waiting for transfers between devices: 8.69 us -> 1.85 us  [neighbours(): return (lax.ppermute(block, SPACE, up), lax.ppermute(block, SPACE, down))]
    all_to_all x3 -> x2, starting transfers between devices: 19.8 us -> 16 us  [exchange(): return lax.all_to_all(x, axes, 0, 0)]
    ppermute x1 -> x0, starting transfers between devices: 2.66 us -> none  [per_device(): other = lax.ppermute(own, 'zh', [(0, 1), (1, 0)])]
    pallas_call x10, Pallas kernels: 12.1 us -> 10 us  [call(): pl.pallas_call(kernel, out_shape=out_shape, in_specs=[SMEM] * len(scalars...]
    all_to_all x3 -> x2, waiting for transfers between devices: 13.5 us -> 12.1 us  [exchange(): return lax.all_to_all(x, axes, 0, 0)]
    unnamed x20 -> x18, local copies, waits for them, and re-layouts: 3.93 us -> 2.62 us
  transfers between devices with their start and end apart: 8 -> 6, of which waited for: 4 -> 4; matrix products, arithmetic and copies ran while one was open for 0% -> 0% of each run, Pallas kernels for 1% -> 2%
where the time goes in v7:
time: 155 us; the launch traced here: 154 us
  blocking collectives  94 us (61%)
  starting transfers between devices  32.6 us (21%)
  waiting for transfers between devices  14 us (9%)
  Pallas kernels  10 us (6%)
  local copies, waits for them, and re-layouts  2.62 us (2%)
    all_to_all x6, blocking collectives, exchange(): return lax.all_to_all(x, axes, 0, 0)  94 us
    ppermute x4, starting transfers between devices, neighbours(): return (lax.ppermute(block, SPACE, up), lax.ppermute(block, SPACE, down))  16.5 us
    all_to_all x2, starting transfers between devices, exchange(): return lax.all_to_all(x, axes, 0, 0)  16 us
    all_to_all x2, waiting for transfers between devices, exchange(): return lax.all_to_all(x, axes, 0, 0)  12.1 us
    pallas_call x10, Pallas kernels, call(): pl.pallas_call(kernel, out_shape=out_shape, in_specs=[SMEM] * len(scalars...  10 us
  transfers between devices with their start and end apart: 6, of which 4 were waited for; matrix products, arithmetic and copies ran while one was open for 0% of the time, Pallas kernels for 2%

profile of v7, /device:TPU:1, one launch (start us, length us, event | category | flops | bytes accessed | tf_op | source)
XLA Modules:
  0.0 154.1 jit_solution(5644090222775648132)
XLA Ops:
  0.6 8.8 %collective-permute-start.1 = (bf16[256,128]{1,0:T(8,128)(2,1)}, bf16[256,128]{1,0:T(8,128)(2,1)S(1)}, u32[]{:S(2)}, u32[]{:S(2)}) collective-permute-start(bf16[256,128]{1,0:T(8,128)(2,1)} %bitcast.13), channel_id=1, source_target_pairs={{1,0},{2,1},{3,2},{4,3},{5,4},{6,5},{7,6},{8,7},{9,8},{10,9},{11,1... | collective-permute-start | bytes 196616 | tf_op jit(solution)/shard_map/ppermute | solution.py:292
  9.4 1.9 %collective-permute-start = (bf16[256,128]{1,0:T(8,128)(2,1)}, bf16[256,128]{1,0:T(8,128)(2,1)S(1)}, u32[]{:S(2)}, u32[]{:S(2)}) collective-permute-start(bf16[256,128]{1,0:T(8,128)(2,1)} %bitcast.14), channel_id=1, source_target_pairs={{0,1},{1,2},{2,3},{3,4},{4,5},{5,6},{6,7},{7,8},{8,9},{9,10},{10,1... | collective-permute-start | bytes 196616 | tf_op jit(solution)/shard_map/ppermute | solution.py:292
  11.4 0.8 copy-done.7
  12.2 0.7 copy-done.8
  12.8 0.3 shard_map.104.refs_7_
  13.2 0.0 collective-permute-done.refs_1_
  13.2 1.1 copy-done
  14.3 0.8 shard_map.105
  15.2 15.1 %all_to_all.40.refs_0_ = bf16[8,384,128]{2,1,0:T(8,128)(2,1)S(1)} all-to-all(bf16[8,384,128]{2,1,0:T(8,128)(2,1)S(1)} %get-tuple-element.10), channel_id=1, replica_groups=mesh['y'=4,'zh'=2,'zg'=2,'zl'=4,'x'=4,'c'=2] {'x','c'}, dimensions={0} | all-to-all | bytes 1572864 | tf_op jit(solution)/shard_map/all_to_all | solution.py:57
  30.3 17.8 %all_to_all.41.refs_1_.refs_2_ = bf16[16,64,128]{2,1,0:T(8,128)(2,1)S(1)} all-to-all(bf16[16,64,128]{2,1,0:T(8,128)(2,1)S(1)} %get-tuple-element.11), channel_id=1, replica_groups=mesh['y'=4,'zh'=2,'zg'=2,'zl'=4,'x'=4,'c'=2] {'y','zl'}, dimensions={0} | all-to-all | bytes 524288 | tf_op jit(solution)/shard_map/all_to_all | solution.py:57
  48.1 2.2 %shard_map.106 = bf16[16,64,128]{2,1,0:T(8,128)(2,1)} custom-call(bf16[8,384,128]{2,1,0:T(8,128)(2,1)S(1)} %all_to_all.40.refs_0_, bf16[16,64,128]{2,1,0:T(8,128)(2,1)S(1)} %all_to_all.41.refs_1_.refs_2_), custom_call_target="tpu_custom_call" | custom-call | flops 452984832 | bytes 1048576 | tf_op jit(solution)/shard_map/pallas_call | solution.py:33
  50.2 3.9 %all-to-all-start.2 = ((bf16[16,64,128]{2,1,0:T(8,128)(2,1)}), bf16[16,64,128]{2,1,0:T(8,128)(2,1)S(1)}, u32[]{:S(2)}, u32[]{:S(2)}) async-start(bf16[16,64,128]{2,1,0:T(8,128)(2,1)} %shard_map.106), calls=%async_computation.2 | async-start | bytes 524288 | tf_op jit(solution)/shard_map/all_to_all | solution.py:57
  54.2 3.7 %collective-permute-start.3 = (bf16[256,256]{1,0:T(8,128)(2,1)S(1)}, bf16[256,256]{1,0:T(8,128)(2,1)S(1)}, u32[]{:S(2)}, u32[]{:S(2)}) collective-permute-start(bf16[256,256]{1,0:T(8,128)(2,1)S(1)} %get-tuple-element.9.refs_2_), channel_id=1, source_target_pairs={{1,0},{2,1},{3,2},{4,3},{5,4},{6,5},{7,6},{8,7},{9,8},{10,9},{11,1... | collective-permute-start | bytes 393224 | tf_op jit(solution)/shard_map/ppermute | solution.py:292
  57.9 2.1 %collective-permute-start.2 = (bf16[256,256]{1,0:T(8,128)(2,1)S(1)}, bf16[256,256]{1,0:T(8,128)(2,1)S(1)}, u32[]{:S(2)}, u32[]{:S(2)}) collective-permute-start(bf16[256,256]{1,0:T(8,128)(2,1)S(1)} %get-tuple-element.9.refs_2_), channel_id=1, source_target_pairs={{0,1},{1,2},{2,3},{3,4},{4,5},{5,6},{6,7},{7,8},{8,9},{9,10},{10,1... | collective-permute-start | bytes 393224 | tf_op jit(solution)/shard_map/ppermute | solution.py:292
  60.0 0.1 pad_add_fusion.refs_0_.refs_1_
  60.1 0.9 collective-permute-done.3.refs_4_.refs_1_
  61.0 0.9 collective-permute-done.2.refs_3_.refs_0_
  61.9 0.8 all-to-all-done.2.refs_1_
  62.7 1.3 shard_map.107.refs_4_
  64.0 12.1 %all-to-all-start.3 = ((bf16[4,320,128]{2,1,0:T(8,128)(2,1)}), bf16[4,320,128]{2,1,0:T(8,128)(2,1)S(1)}, u32[]{:S(2)}, u32[]{:S(2)}) async-start(bf16[4,320,128]{2,1,0:T(8,128)(2,1)} %shard_map.107.refs_4_), calls=%async_computation.3 | async-start | bytes 655360 | tf_op jit(solution)/shard_map/all_to_all | solution.py:57
  76.1 2.1 %shard_map.108 = (bf16[256,128]{1,0:T(8,128)(2,1)}, f32[8,128]{1,0:T(8,128)S(1)}) custom-call(bf16[256,256]{1,0:T(8,128)(2,1)S(1)} %collective-permute-done.2.refs_3_.refs_0_, bf16[256,256]{1,0:T(8,128)(2,1)S(1)} %collective-permute-done.3.refs_4_.refs_1_, bf16[256,256]{1,0:T(8,128)(2,1)S(1)} %get-tuple-element.9.refs_2_, bf16[3456,256]{1,0:T(8,128)(2,1)S(1)} %copy-done, ...), custom_call_target="tpu_custom_call" | custom-call | flops 452984832 | bytes 2490368 | tf_op jit(solution)/shard_map/pallas_call | solution.py:33
  78.2 0.0 copy-start.1
  78.3 0.0 copy-start.5
  78.3 11.4 %all-to-all-done.3.refs_0_ = bf16[4,320,128]{2,1,0:T(8,128)(2,1)S(1)} async-done(((bf16[4,320,128]{2,1,0:T(8,128)(2,1)}), bf16[4,320,128]{2,1,0:T(8,128)(2,1)S(1)}, u32[]{:S(2)}, u32[]{:S(2)}) %all-to-all-start.3) | async-done | bytes 327712 | tf_op jit(solution)/shard_map/all_to_all | solution.py:57
  89.6 0.1 shard_map.109
  89.7 26.3 %all_to_all.42.refs_2_ = bf16[32,64,128]{2,1,0:T(8,128)(2,1)S(1)} all-to-all(bf16[32,64,128]{2,1,0:T(8,128)(2,1)S(1)} %get-tuple-element.14), channel_id=1, replica_groups=mesh['y'=4,'zh'=2,'zg'=2,'zl'=4,'x'=4,'c'=2] {'y','x','c'}, dimensions={0} | all-to-all | bytes 1048576 | tf_op jit(solution)/shard_map/all_to_all | solution.py:57
  116.0 1.3 shard_map.110
  117.3 16.4 %all_to_all.43.refs_0_ = bf16[4,352,128]{2,1,0:T(8,128)(2,1)S(1)} all-to-all(bf16[4,352,128]{2,1,0:T(8,128)(2,1)S(1)} %shard_map.110), channel_id=1, replica_groups=mesh['y'=4,'zh'=2,'zg'=2,'zl'=4,'x'=4,'c'=2] {'zl'}, dimensions={0} | all-to-all | bytes 720896 | tf_op jit(solution)/shard_map/all_to_all | solution.py:57
  133.8 1.3 shard_map.111
  135.0 10.6 %all_to_all.44.refs_0_ = bf16[8,112,128]{2,1,0:T(8,128)(2,1)S(1)} all-to-all(bf16[8,112,128]{2,1,0:T(8,128)(2,1)S(1)} %shard_map.111), channel_id=1, replica_groups=mesh['y'=4,'zh'=2,'zg'=2,'zl'=4,'x'=4,'c'=2] {'x','c'}, dimensions={0} | all-to-all | bytes 458752 | tf_op jit(solution)/shard_map/all_to_all | solution.py:57
  145.7 7.7 %all_to_all.45.refs_0_ = f32[4,112,128]{2,1,0:T(8,128)S(1)} all-to-all(f32[4,112,128]{2,1,0:T(8,128)S(1)} %shard_map.112), channel_id=1, replica_groups=mesh['y'=4,'zh'=2,'zg'=2,'zl'=4,'x'=4,'c'=2] {'y'}, dimensions={0} | all-to-all | bytes 458752 | tf_op jit(solution)/shard_map/all_to_all | solution.py:57
  153.4 0.6 shard_map.113
  (15 shorter events, 0.1 us)
Async XLA Ops:
  0.6 12.5 %collective-permute-start.1 = (bf16[256,128]{1,0:T(8,128)(2,1)}, bf16[256,128]{1,0:T(8,128)(2,1)S(1)}, u32[]{:S(2)}, u32[]{:S(2)}) collective-permute-start(bf16[256,128]{1,0:T(8,128)(2,1)} %bitcast.13), channel_id=1, source_target_pairs={{1,0},{2,1},{3,2},{4,3},{5,4},{6,5},{7,6},{8,7},{9,8},{10,9},{11,1... | collective-permute-start | bytes 196616 | tf_op jit(solution)/shard_map/ppermute | solution.py:292
  9.4 3.8 %collective-permute-start = (bf16[256,128]{1,0:T(8,128)(2,1)}, bf16[256,128]{1,0:T(8,128)(2,1)S(1)}, u32[]{:S(2)}, u32[]{:S(2)}) collective-permute-start(bf16[256,128]{1,0:T(8,128)(2,1)} %bitcast.14), channel_id=1, source_target_pairs={{0,1},{1,2},{2,3},{3,4},{4,5},{5,6},{6,7},{7,8},{8,9},{9,10},{10,1... | collective-permute-start | bytes 196616 | tf_op jit(solution)/shard_map/ppermute | solution.py:292
  11.4 0.8 copy-start.7
  12.2 0.7 copy-start.8
  12.8 1.5 copy-start
  12.8 1.5 copy-start.2
  12.8 1.5 copy-start.3
  12.8 1.5 copy-start.4
  50.2 12.5 %all-to-all-start.2 = ((bf16[16,64,128]{2,1,0:T(8,128)(2,1)}), bf16[16,64,128]{2,1,0:T(8,128)(2,1)S(1)}, u32[]{:S(2)}, u32[]{:S(2)}) async-start(bf16[16,64,128]{2,1,0:T(8,128)(2,1)} %shard_map.106), calls=%async_computation.2 | async-start | bytes 524288 | tf_op jit(solution)/shard_map/all_to_all | solution.py:57
  54.2 6.9 %collective-permute-start.3 = (bf16[256,256]{1,0:T(8,128)(2,1)S(1)}, bf16[256,256]{1,0:T(8,128)(2,1)S(1)}, u32[]{:S(2)}, u32[]{:S(2)}) collective-permute-start(bf16[256,256]{1,0:T(8,128)(2,1)S(1)} %get-tuple-element.9.refs_2_), channel_id=1, source_target_pairs={{1,0},{2,1},{3,2},{4,3},{5,4},{6,5},{7,6},{8,7},{9,8},{10,9},{11,1... | collective-permute-start | bytes 393224 | tf_op jit(solution)/shard_map/ppermute | solution.py:292
  57.9 4.0 %collective-permute-start.2 = (bf16[256,256]{1,0:T(8,128)(2,1)S(1)}, bf16[256,256]{1,0:T(8,128)(2,1)S(1)}, u32[]{:S(2)}, u32[]{:S(2)}) collective-permute-start(bf16[256,256]{1,0:T(8,128)(2,1)S(1)} %get-tuple-element.9.refs_2_), channel_id=1, source_target_pairs={{0,1},{1,2},{2,3},{3,4},{4,5},{5,6},{6,7},{7,8},{8,9},{9,10},{10,1... | collective-permute-start | bytes 393224 | tf_op jit(solution)/shard_map/ppermute | solution.py:292
  64.0 25.6 %all-to-all-start.3 = ((bf16[4,320,128]{2,1,0:T(8,128)(2,1)}), bf16[4,320,128]{2,1,0:T(8,128)(2,1)S(1)}, u32[]{:S(2)}, u32[]{:S(2)}) async-start(bf16[4,320,128]{2,1,0:T(8,128)(2,1)} %shard_map.107.refs_4_), calls=%async_computation.3 | async-start | bytes 655360 | tf_op jit(solution)/shard_map/all_to_all | solution.py:57
  76.1 39.9 %copy-start.6 = (s32[8]{0:T(128)S(1)}, s32[8]{0:T(128)}, u32[]{:S(2)}) copy-start(s32[8]{0:T(128)} %refs_0_.1) | copy-start | bytes 100
  78.2 55.5 %copy-start.1 = (f32[256,256]{1,0:T(8,128)S(1)}, f32[256,256]{1,0:T(8,128)}, u32[]{:S(2)}) copy-start(f32[256,256]{1,0:T(8,128)} %refs_1_.1) | copy-start | bytes 786436
  78.3 55.5 %copy-start.5 = (f32[256]{0:T(256)S(1)}, f32[256]{0:T(256)}, u32[]{:S(2)}) copy-start(f32[256]{0:T(256)} %param.17) | copy-start | bytes 3076

commit v8 on v7

--- a/solution.py
+++ b/solution.py
@@ -92,15 +92,21 @@
         out_ref[r] = block.astype(BF16)
 
 
+def by_side(place_ref, inside, outside):
+    first = place_ref[3] == 0
+    inside, outside = inside[...].astype(F32), outside[...].astype(F32)
+    return jnp.where(first, outside, inside), jnp.where(first, inside, outside)
+
+
 def forward_body(
-    place_ref, low_ref, high_ref, mine, weight, bias, cot, basis_ref, delta_ref, send_ref, slices_ref, patches
+    place_ref, inside_ref, outside_ref, mine, weight, bias, cot, basis_ref, delta_ref, send_ref, same_ref, patches
 ):
-    for y in range(4):
-        for r in range(4):
-            slices_ref[4 * y + r] = basis_ref[r]
+    same_ref[...] = basis_ref[...]
+    low, high = by_side(place_ref, inside_ref, outside_ref)
+    planes = (low, mine[...].astype(F32), high)
     none = jnp.zeros((16, 128), BF16)
     for a in range(3):
-        wide = (low_ref, mine, high_ref)[a][...].astype(F32)
+        wide = planes[a]
         for c in range(3):
             moved = x_shifted(wide, c - 1).astype(BF16)
             for b in range(3):
@@ -116,9 +122,8 @@
     logistic = 1.0 / (1.0 + jnp.exp(-pre))
     delta = (cot[...].astype(F32) * logistic * (1.0 + pre * (1.0 - logistic))).astype(BF16)
     delta_ref[...] = delta
-    rim = jnp.where(place_ref[0] < 4, low_ref[...].astype(F32), high_ref[...].astype(F32))
-    act_t = mine[...].astype(F32).T.astype(BF16)
-    rim_t = rim.T.astype(BF16)
+    act_t = planes[1].T.astype(BF16)
+    rim_t = jnp.where(place_ref[4] < 4, low, high).T.astype(BF16)
     for x in range(4):
         for c in range(2):
             to = 2 * x + c
@@ -130,7 +135,7 @@
             send_ref[to, 128:] = delta[:, 128 * c : 128 * c + 128]
 
 
-def weight_grad_body(got_ref, out_ref, moved, deltas, whole):
+def weight_grad_body(place_ref, got_ref, basis_ref, out_ref, own_ref, one_ref, two_ref, three_ref, moved, deltas, whole):
     pieces = []
     for plane, at in [(0, 64)] + [(e, 0) for e in range(8)] + [(7, 64)]:
         pieces.append(got_ref[plane, at : at + 32].astype(F32))
@@ -151,6 +156,8 @@
         whole[288 * a : 288 * a + 288, :] = jnp.dot(
             moved[:, 256 * a : 256 * a + 2048], deltas[...], preferred_element_type=F32
         )
+    for k, ref in enumerate((own_ref, one_ref, two_ref, three_ref)):
+        ref[...] = basis_ref[place_ref[2] ^ k]
     none = jnp.zeros((5, 128), F32)
     for y_to in range(4):
         for z_to in range(4):
@@ -161,17 +168,17 @@
             out_ref[4 * y_to + z_to] = jnp.concatenate(parts, axis=0).astype(BF16)
 
 
-def over_y_zl_body(place_ref, got_ref, basis_ref, out_ref):
+def over_y_zl_body(place_ref, got_ref, own_ref, one_ref, two_ref, three_ref, out_ref):
     total = (sum(got_ref[i].astype(F32) for i in range(16)) * (1.0 / CELLS)).astype(BF16)
     for to in range(4):
         out_ref[to, :64] = total
-    for y in range(4):
-        block = basis_ref[4 * y + place_ref[0]]
+    for k, ref in enumerate((own_ref, one_ref, two_ref, three_ref)):
+        at = pl.multiple_of(64 + 64 * (place_ref[2] ^ k), 64)
         for to in range(4):
-            out_ref[to, 64 + 64 * y : 128 + 64 * y] = block
-
-
-def over_zh_zg_body(got_ref, out_ref, basis_ref):
+            out_ref[to, pl.ds(at, 64)] = ref[...]
+
+
+def over_zh_zg_body(owner_ref, place_ref, got_ref, out_ref, basis_ref, own_ref, one_ref, two_ref, three_ref):
     total = sum(got_ref[i, :64].astype(F32) for i in range(4)).astype(BF16)
     for to in range(32):
         out_ref[to] = total
@@ -180,9 +187,11 @@
             for zg in range(2):
                 block = got_ref[2 * zh + zg, 64 + 64 * y : 128 + 64 * y]
                 basis_ref[2 * y + zh, 64 * zg : 64 * zg + 64] = block
-
-
-def rotate_body(owner_ref, place_ref, got_ref, basis_ref, out_ref, grads, ordered):
+    for k, ref in enumerate((own_ref, one_ref, two_ref, three_ref)):
+        ref[...] = basis_ref[owner_ref[4 * place_ref[1] + (place_ref[2] ^ k)]]
+
+
+def rotate_body(owner_ref, got_ref, basis_ref, out_ref, grads, ordered):
     for y in range(4):
         for x in range(4):
             at = 32 * (8 * x + 2 * y)
@@ -202,18 +211,22 @@
         [total[64 * zg : 64 * zg + 56, 128 * c : 128 * c + 128] for zg in range(2) for c in range(2)], axis=0
     ).astype(BF16)
     for to in range(4):
-        out_ref[to, :224] = total
-        out_ref[to, 224:] = basis_ref[owner_ref[4 * place_ref[1] + to]]
-
-
-def update_body(got_ref, out_basis_any, out_eigen_any, out_ref, out_basis, out_eigen, ordered, sems):
+        out_ref[to] = total
+
+
+def update_body(
+    place_ref, got_ref, own_ref, one_ref, two_ref, three_ref, out_basis_any, out_eigen_any,
+    out_ref, panel, out_basis, out_eigen, ordered, sems,
+):
+    for k, ref in enumerate((own_ref, one_ref, two_ref, three_ref)):
+        panel[place_ref[2] ^ k] = ref[...]
     copies = [
         pltpu.make_async_copy(out_basis_any, out_basis, sems.at[0]),
         pltpu.make_async_copy(out_eigen_any, out_eigen, sems.at[1]),
     ]
     started(copies)
     highest = lax.Precision.HIGHEST
-    total = sum(got_ref[i, :224].astype(F32) for i in range(4))
+    total = sum(got_ref[i].astype(F32) for i in range(4))
     none = jnp.zeros((8, 256), F32)
     parts = []
     for zg in range(2):
@@ -224,7 +237,7 @@
     for copy in copies:
         copy.wait()
     rotated = jnp.dot(rotated, out_basis[...], precision=highest, preferred_element_type=F32)
-    terms = got_ref[0, 224:].astype(F32)
+    terms = own_ref[...].astype(F32)
     eigen = (terms[:, 108:109] + terms[:, 109:110]) + terms[:, 110:111]
     scaled = rotated / (eigen * out_eigen[...] + DAMPING)
     scaled = jnp.where((iota((128, 256), 0) & 63) < 54, scaled, 0.0)
@@ -234,7 +247,7 @@
     high = turned.astype(BF16)
     rest = (turned - high.astype(F32)).astype(BF16)
     for r in range(4):
-        block = got_ref[r, 224:].astype(F32).T.astype(BF16)
+        block = panel[r].astype(F32).T.astype(BF16)
         rows = jnp.dot(block, high, preferred_element_type=F32) + jnp.dot(block, rest, preferred_element_type=F32)
         for c in range(2):
             ordered[c, pl.ds(r, 108, stride=4), :] = rows[:108, 128 * c : 128 * c + 128]
@@ -256,13 +269,15 @@
     out_ref[...] = jnp.concatenate([total[:54], total[56:110]], axis=1)
 
 
-def data_grad_body(low_ref, high_ref, mine_ref, weight_any, out_ref, token_ref, weight, sem):
+def data_grad_body(place_ref, inside_ref, outside_ref, mine_ref, weight_any, out_ref, token_ref, weight, sem):
     copy = pltpu.make_async_copy(weight_any, weight, sem)
     copy.start()
+    low, high = by_side(place_ref, inside_ref, outside_ref)
+    planes = (high, mine_ref[...].astype(F32), low)
     none = jnp.zeros((16, 256), BF16)
     total = jnp.zeros((256, 128), F32)
     for a in range(3):
-        wide = (high_ref, mine_ref, low_ref)[a][...].astype(F32)
+        wide = planes[a]
         if a == 0:
             copy.wait()
         for c in range(3):
@@ -286,10 +301,13 @@
 
 
 def neighbours(block):
-    count = 64
-    up = [(i, i + 1) for i in range(count - 1)]
-    down = [(i + 1, i) for i in range(count - 1)]
-    return lax.ppermute(block, SPACE, up), lax.ppermute(block, SPACE, down)
+    inside = lax.ppermute(block, "c", [(0, 1), (1, 0)])
+    pairs = [(i, i + 1) for i in range(1, 63, 2)]
+    return inside, lax.ppermute(block, SPACE, pairs + [(j, i) for i, j in pairs])
+
+
+def among_zl(blocks):
+    return [blocks[0]] + [lax.ppermute(blocks[k], "zl", [(i, i ^ k) for i in range(4)]) for k in (1, 2, 3)]
 
 
 def per_device(
@@ -304,10 +322,9 @@
     output_eigen,
 ):
     dma = pltpu.SemaphoreType.DMA
-    place = jnp.stack([lax.axis_index("y"), lax.axis_index("zg")]).astype(jnp.int32)
-    inner = lax.axis_index(XC).astype(jnp.int32).reshape(1)
+    place = jnp.stack([lax.axis_index(a) for a in ("y", "zg", "zl", "c", XC)]).astype(jnp.int32)
     plane = activations.reshape(256, 128)
-    low, high = neighbours(plane)
+    inside, outside = neighbours(plane)
 
     stored = call(
         basis_body,
@@ -317,59 +334,64 @@
         scratch=[pltpu.VMEM((1, 54), F32), dma],
         flops=4_000_000_000,
     )
-    delta, send, slices = call(
+    delta, send, stored = call(
         forward_body,
-        [shape((256, 256), BF16), shape((8, 384, 128), BF16), shape((16, 64, 128), BF16)],
-        (inner,),
-        (low, high, plane, conv_weight, conv_bias.reshape(1, 256), cotangent.reshape(256, 256), stored),
+        [shape((256, 256), BF16), shape((8, 384, 128), BF16), shape((4, 64, 128), BF16)],
+        (place,),
+        (inside, outside, plane, conv_weight, conv_bias.reshape(1, 256), cotangent.reshape(256, 256), stored),
         scratch=[pltpu.VMEM((256, 3456), BF16)],
         flops=2 * 256 * 3456 * 256,
     )
-    slices = exchange(slices, ("y", "zl"))
-    part = call(
+    stored = lax.ppermute(stored, ("y", "zl"), [(4 * y + z, 4 * z + y) for y in range(4) for z in range(4)])
+    part, *slices = call(
         weight_grad_body,
-        shape((16, 64, 128), BF16),
-        arrays=(exchange(send, XC),),
-        after=(slices,),
+        [shape((16, 64, 128), BF16)] + [shape((64, 128), BF16)] * 4,
+        (place,),
+        (exchange(send, XC), stored),
         scratch=[pltpu.VMEM((288, 2560), BF16), pltpu.VMEM((2048, 128), BF16), pltpu.VMEM((864, 128), F32)],
         flops=2 * 864 * 2048 * 128,
     )
-    delta_low, delta_high = neighbours(delta)
     part = call(
         over_y_zl_body,
         shape((4, 320, 128), BF16),
         (place,),
-        (exchange(part, ("y", "zl")), slices),
-        after=(delta_low, delta_high),
-    )
+        (exchange(part, ("y", "zl")), *among_zl(slices)),
+    )
+    inside, outside = neighbours(delta)
     data, token = call(
         data_grad_body,
         [shape((256, 128), BF16), shape((8, 128), F32)],
-        arrays=(delta_low, delta_high, delta),
-        remote=(conv_weight,),
+        (place,),
+        (inside, outside, delta),
+        (conv_weight,),
         after=(part,),
         scratch=[pltpu.VMEM((3456, 256), BF16), dma],
         flops=2 * 256 * 3456 * 256,
     )
-    part, basis = call(
+    part, basis, *slices = call(
         over_zh_zg_body,
-        [shape((32, 64, 128), BF16), shape((8, 128, 128), BF16)],
-        arrays=(exchange(part, ("zh", "zg")),),
+        [shape((32, 64, 128), BF16), shape((8, 128, 128), BF16)] + [shape((128, 128), BF16)] * 4,
+        (panel_owner, place),
+        (exchange(part, ("zh", "zg")),),
         after=(token,),
     )
+    slices = among_zl(slices)
     rotated = call(
         rotate_body,
-        shape((4, 352, 128), BF16),
-        (panel_owner, place),
+        shape((4, 224, 128), BF16),
+        (panel_owner,),
         (exchange(part, YXC), basis),
+        after=slices[1:],
         scratch=[pltpu.VMEM((2, 1024, 128), F32), pltpu.VMEM((896, 256), F32)],
     )
     part = call(
         update_body,
         shape((8, 112, 128), BF16),
-        arrays=(exchange(rotated, "zl"),),
-        remote=(output_basis, output_eigen.reshape(1, 256)),
+        (place,),
+        (exchange(rotated, "zl"), *slices),
+        (output_basis, output_eigen.reshape(1, 256)),
         scratch=[
+            pltpu.VMEM((4, 128, 128), BF16),
             pltpu.VMEM((256, 256), F32),
             pltpu.VMEM((1, 256), F32),
             pltpu.VMEM((2, 440, 128), F32),

time: 155 us -> 147 us (0.948)
  blocking collectives: 94 us -> 32.2 us
  starting transfers between devices: 32.6 us -> 71 us
  waiting for transfers between devices: 14 us -> 24.5 us
  Pallas kernels: 10 us -> 14.5 us
    all_to_all x6 -> x3, blocking collectives: 94 us -> 32.2 us  [exchange(): return lax.all_to_all(x, axes, 0, 0)]
    ppermute x4 -> x11, starting transfers between devices: 16.5 us -> 36.1 us  [the longest x6 18.5 us: among_zl(): lax.ppermute(blocks[k], 'zl', [(i, i ^ k) for i in range(4)])]
    all_to_all x2 -> x4, starting transfers between devices: 16 us -> 34.9 us  [exchange(): return lax.all_to_all(x, axes, 0, 0)]
    ppermute x4 -> x11, waiting for transfers between devices: 1.85 us -> 7.14 us  [the longest x6 5.82 us: among_zl(): lax.ppermute(blocks[k], 'zl', [(i, i ^ k) for i in range(4)])]
    all_to_all x2 -> x4, waiting for transfers between devices: 12.1 us -> 17.4 us  [exchange(): return lax.all_to_all(x, axes, 0, 0)]
    pallas_call x10, Pallas kernels: 10 us -> 14.5 us  [call(): pl.pallas_call(kernel, out_shape=out_shape, in_specs=[SMEM] * len(scalars...]
  transfers between devices with their start and end apart: 6 -> 15, of which waited for: 4 -> 8; matrix products, arithmetic and copies ran while one was open for 0% -> 0% of each run, Pallas kernels for 2% -> 2%
where the time goes in v8:
time: 147 us; the launch traced here: 146 us
  starting transfers between devices  71 us (48%)
  blocking collectives  32.2 us (22%)
  waiting for transfers between devices  24.5 us (17%)
  Pallas kernels  14.5 us (10%)
  local copies, waits for them, and re-layouts  2.63 us (2%)
    all_to_all x4, starting transfers between devices, exchange(): return lax.all_to_all(x, axes, 0, 0)  34.9 us
    all_to_all x3, blocking collectives, exchange(): return lax.all_to_all(x, axes, 0, 0)  32.2 us
    ppermute x6, starting transfers between devices, among_zl(): lax.ppermute(blocks[k], 'zl', [(i, i ^ k) for i in range(4)])  18.5 us
    all_to_all x4, waiting for transfers between devices, exchange(): return lax.all_to_all(x, axes, 0, 0)  17.4 us
    pallas_call x10, Pallas kernels, call(): pl.pallas_call(kernel, out_shape=out_shape, in_specs=[SMEM] * len(scalars...  14.5 us
    ppermute x2, starting transfers between devices, neighbours(): lax.ppermute(block, SPACE, pairs + [(j, i) for i, j in pairs])  10 us
    ppermute x2, starting transfers between devices, neighbours(): inside = lax.ppermute(block, 'c', [(0, 1), (1, 0)])  6.86 us
    ppermute x6, waiting for transfers between devices, among_zl(): lax.ppermute(blocks[k], 'zl', [(i, i ^ k) for i in range(4)])  5.82 us
  transfers between devices with their start and end apart: 15, of which 8 were waited for; matrix products, arithmetic and copies ran while one was open for 0% of the time, Pallas kernels for 2%

profile of v8, /device:TPU:1, one launch (start us, length us, event | category | flops | bytes accessed | tf_op | source)
XLA Modules:
  0.0 145.7 jit_solution(14662042948461849062)
XLA Ops:
  0.6 4.5 %collective-permute-start.1 = (bf16[256,128]{1,0:T(8,128)(2,1)}, bf16[256,128]{1,0:T(8,128)(2,1)S(1)}, u32[]{:S(2)}, u32[]{:S(2)}) collective-permute-start(bf16[256,128]{1,0:T(8,128)(2,1)} %bitcast.15), channel_id=1, source_target_pairs={{1,2},{3,4},{5,6},{7,8},{9,10},{11,12},{13,14},{15,16},{17,18},{19... | collective-permute-start | bytes 196616 | tf_op jit(solution)/shard_map/ppermute | solution.py:306
  5.1 4.9 %collective-permute-start = (bf16[256,128]{1,0:T(8,128)(2,1)}, bf16[256,128]{1,0:T(8,128)(2,1)S(1)}, u32[]{:S(2)}, u32[]{:S(2)}) collective-permute-start(bf16[256,128]{1,0:T(8,128)(2,1)} %bitcast.16), channel_id=1, source_target_pairs={{0,1},{1,0},{2,3},{3,2},{4,5},{5,4},{6,7},{7,6},{8,9},{9,8},{10,11... | collective-permute-start | bytes 196616 | tf_op jit(solution)/shard_map/ppermute | solution.py:304
  10.1 0.8 copy-done.7
  12.0 1.0 copy-done
  13.1 2.3 %shard_map.105 = (bf16[256,256]{1,0:T(8,128)(2,1)S(1)}, bf16[8,384,128]{2,1,0:T(8,128)(2,1)}, bf16[4,64,128]{2,1,0:T(8,128)(2,1)S(1)}) custom-call(s32[5]{0:T(128)S(1)} %stack.23.refs_0_.refs_1_, bf16[256,128]{1,0:T(8,128)(2,1)S(1)} %collective-permute-done.refs_1_, bf16[256,128]{1,0:T(8,128)(2,1)S(1)} %collective-permute-done.1.refs_2_, ...), custom_call_target="tpu_custom_call" | custom-call | flops 452984832 | bytes 2163732 | tf_op jit(solution)/shard_map/pallas_call | solution.py:33
  15.3 3.5 %all-to-all-start = ((bf16[8,384,128]{2,1,0:T(8,128)(2,1)}), bf16[8,384,128]{2,1,0:T(8,128)(2,1)S(1)}, u32[]{:S(2)}, u32[]{:S(2)}) async-start(bf16[8,384,128]{2,1,0:T(8,128)(2,1)} %get-tuple-element.19), calls=%async_computation | async-start | bytes 1572864 | tf_op jit(solution)/shard_map/all_to_all | solution.py:57
  18.8 0.7 collective-permute-start.4
  19.5 11.6 %all-to-all-done.refs_1_ = bf16[8,384,128]{2,1,0:T(8,128)(2,1)S(1)} async-done(((bf16[8,384,128]{2,1,0:T(8,128)(2,1)}), bf16[8,384,128]{2,1,0:T(8,128)(2,1)S(1)}, u32[]{:S(2)}, u32[]{:S(2)}) %all-to-all-start) | async-done | bytes 786464 | tf_op jit(solution)/shard_map/all_to_all | solution.py:57
  31.1 2.7 %shard_map.106 = (bf16[16,64,128]{2,1,0:T(8,128)(2,1)}, bf16[64,128]{1,0:T(8,128)(2,1)S(1)}, bf16[64,128]{1,0:T(8,128)(2,1)S(1)}, bf16[64,128]{1,0:T(8,128)(2,1)S(1)}, bf16[64,128]{1,0:T(8,128)(2,1)S(1)}) custom-call(s32[5]{0:T(128)S(1)} %stack.23.refs_0_.refs_1_, bf16[8,384,128]{2,1,0:T(8,128)(2,1)S(1)} %all-to-all-done.refs_1_, ...), custom_call_target="tpu_custom_call" | custom-call | flops 452984832 | bytes 851988 | tf_op jit(solution)/shard_map/pallas_call | solution.py:33
  33.8 7.9 %all-to-all-start.1 = ((bf16[16,64,128]{2,1,0:T(8,128)(2,1)}), bf16[16,64,128]{2,1,0:T(8,128)(2,1)S(1)}, u32[]{:S(2)}, u32[]{:S(2)}) async-start(bf16[16,64,128]{2,1,0:T(8,128)(2,1)} %get-tuple-element.21), calls=%async_computation.1 | async-start | bytes 524288 | tf_op jit(solution)/shard_map/all_to_all | solution.py:57
  41.7 3.3 %collective-permute-start.5 = (bf16[64,128]{1,0:T(8,128)(2,1)S(1)}, bf16[64,128]{1,0:T(8,128)(2,1)S(1)}, u32[]{:S(2)}, u32[]{:S(2)}) collective-permute-start(bf16[64,128]{1,0:T(8,128)(2,1)S(1)} %get-tuple-element.23), channel_id=1, source_target_pairs={{0,8},{8,0},{16,24},{24,16},{1,9},{9,1},{17,25},{25,17},{2,10},{10... | collective-permute-start | bytes 49160 | tf_op jit(solution)/shard_map/ppermute | solution.py:310
  45.0 4.0 %collective-permute-start.6 = (bf16[64,128]{1,0:T(8,128)(2,1)S(1)}, bf16[64,128]{1,0:T(8,128)(2,1)S(1)}, u32[]{:S(2)}, u32[]{:S(2)}) collective-permute-start(bf16[64,128]{1,0:T(8,128)(2,1)S(1)} %get-tuple-element.24), channel_id=1, source_target_pairs={{0,16},{8,24},{16,0},{24,8},{1,17},{9,25},{17,1},{25,9},{2,18},{10... | collective-permute-start | bytes 49160 | tf_op jit(solution)/shard_map/ppermute | solution.py:310
  49.0 2.0 %collective-permute-start.7 = (bf16[64,128]{1,0:T(8,128)(2,1)S(1)}, bf16[64,128]{1,0:T(8,128)(2,1)S(1)}, u32[]{:S(2)}, u32[]{:S(2)}) collective-permute-start(bf16[64,128]{1,0:T(8,128)(2,1)S(1)} %get-tuple-element.25), channel_id=1, source_target_pairs={{0,24},{8,16},{16,8},{24,0},{1,25},{9,17},{17,9},{25,1},{2,26},{10... | collective-permute-start | bytes 49160 | tf_op jit(solution)/shard_map/ppermute | solution.py:310
  51.2 4.1 %collective-permute-done.7.refs_5_ = bf16[64,128]{1,0:T(8,128)(2,1)S(1)} collective-permute-done((bf16[64,128]{1,0:T(8,128)(2,1)S(1)}, bf16[64,128]{1,0:T(8,128)(2,1)S(1)}, u32[]{:S(2)}, u32[]{:S(2)}) %collective-permute-start.7) | collective-permute-done | bytes 16416 | tf_op jit(solution)/shard_map/ppermute | solution.py:310
  55.3 1.3 shard_map.107.refs_5_
  56.6 11.0 %all-to-all-start.2 = ((bf16[4,320,128]{2,1,0:T(8,128)(2,1)}), bf16[4,320,128]{2,1,0:T(8,128)(2,1)S(1)}, u32[]{:S(2)}, u32[]{:S(2)}) async-start(bf16[4,320,128]{2,1,0:T(8,128)(2,1)} %shard_map.107.refs_5_), calls=%async_computation.2 | async-start | bytes 655360 | tf_op jit(solution)/shard_map/all_to_all | solution.py:57
  67.7 5.5 %collective-permute-start.3 = (bf16[256,256]{1,0:T(8,128)(2,1)S(1)}, bf16[256,256]{1,0:T(8,128)(2,1)S(1)}, u32[]{:S(2)}, u32[]{:S(2)}) collective-permute-start(bf16[256,256]{1,0:T(8,128)(2,1)S(1)} %get-tuple-element.18.refs_3_), channel_id=1, source_target_pairs={{1,2},{3,4},{5,6},{7,8},{9,10},{11,12},{13,14},{15,16},{17,18},{19... | collective-permute-start | bytes 393224 | tf_op jit(solution)/shard_map/ppermute | solution.py:306
  73.2 1.9 %collective-permute-start.2 = (bf16[256,256]{1,0:T(8,128)(2,1)S(1)}, bf16[256,256]{1,0:T(8,128)(2,1)S(1)}, u32[]{:S(2)}, u32[]{:S(2)}) collective-permute-start(bf16[256,256]{1,0:T(8,128)(2,1)S(1)} %get-tuple-element.18.refs_3_), channel_id=1, source_target_pairs={{0,1},{1,0},{2,3},{3,2},{4,5},{5,4},{6,7},{7,6},{8,9},{9,8},{10,11... | collective-permute-start | bytes 393224 | tf_op jit(solution)/shard_map/ppermute | solution.py:304
  75.1 0.7 collective-permute-done.3.refs_2_
  76.4 2.7 %shard_map.108 = (bf16[256,128]{1,0:T(8,128)(2,1)}, f32[8,128]{1,0:T(8,128)S(1)}) custom-call(s32[5]{0:T(128)S(1)} %stack.23.refs_0_.refs_1_, bf16[256,256]{1,0:T(8,128)(2,1)S(1)} %collective-permute-done.2.refs_1_, bf16[256,256]{1,0:T(8,128)(2,1)S(1)} %collective-permute-done.3.refs_2_, bf16[256,256]{1,0:T(8,128)(2,1)S(1)} %get-tuple-element.18.refs_3_, ...), custom_call_target="tpu_custom_call" | custom-call | flops 452984832 | bytes 2490388 | tf_op jit(solution)/shard_map/pallas_call | solution.py:33
  79.2 5.1 %all-to-all-done.2.refs_2_ = bf16[4,320,128]{2,1,0:T(8,128)(2,1)S(1)} async-done(((bf16[4,320,128]{2,1,0:T(8,128)(2,1)}), bf16[4,320,128]{2,1,0:T(8,128)(2,1)S(1)}, u32[]{:S(2)}, u32[]{:S(2)}) %all-to-all-start.2) | async-done | bytes 327712 | tf_op jit(solution)/shard_map/all_to_all | solution.py:57
  84.3 1.4 shard_map.109
  85.7 12.4 %all-to-all-start.3 = ((bf16[32,64,128]{2,1,0:T(8,128)(2,1)}), bf16[32,64,128]{2,1,0:T(8,128)(2,1)S(1)}, u32[]{:S(2)}, u32[]{:S(2)}) async-start(bf16[32,64,128]{2,1,0:T(8,128)(2,1)} %get-tuple-element.28), calls=%async_computation.3 | async-start | bytes 1048576 | tf_op jit(solution)/shard_map/all_to_all | solution.py:57
  98.1 1.9 %collective-permute-start.8 = (bf16[128,128]{1,0:T(8,128)(2,1)S(1)}, bf16[128,128]{1,0:T(8,128)(2,1)S(1)}, u32[]{:S(2)}, u32[]{:S(2)}) collective-permute-start(bf16[128,128]{1,0:T(8,128)(2,1)S(1)} %get-tuple-element.30), channel_id=1, source_target_pairs={{0,8},{8,0},{16,24},{24,16},{1,9},{9,1},{17,25},{25,17},{2,10},{10... | collective-permute-start | bytes 98312 | tf_op jit(solution)/shard_map/ppermute | solution.py:310
  100.1 2.2 %collective-permute-start.9 = (bf16[128,128]{1,0:T(8,128)(2,1)S(1)}, bf16[128,128]{1,0:T(8,128)(2,1)S(1)}, u32[]{:S(2)}, u32[]{:S(2)}) collective-permute-start(bf16[128,128]{1,0:T(8,128)(2,1)S(1)} %get-tuple-element.31), channel_id=1, source_target_pairs={{0,16},{8,24},{16,0},{24,8},{1,17},{9,25},{17,1},{25,9},{2,18},{10... | collective-permute-start | bytes 98312 | tf_op jit(solution)/shard_map/ppermute | solution.py:310
  102.3 5.2 %collective-permute-start.10 = (bf16[128,128]{1,0:T(8,128)(2,1)S(1)}, bf16[128,128]{1,0:T(8,128)(2,1)S(1)}, u32[]{:S(2)}, u32[]{:S(2)}) collective-permute-start(bf16[128,128]{1,0:T(8,128)(2,1)S(1)} %get-tuple-element.32), channel_id=1, source_target_pairs={{0,24},{8,16},{16,8},{24,0},{1,25},{9,17},{17,9},{25,1},{2,26},{10... | collective-permute-start | bytes 98312 | tf_op jit(solution)/shard_map/ppermute | solution.py:310
  107.5 1.6 %collective-permute-done.10.refs_5_ = bf16[128,128]{1,0:T(8,128)(2,1)S(1)} collective-permute-done((bf16[128,128]{1,0:T(8,128)(2,1)S(1)}, bf16[128,128]{1,0:T(8,128)(2,1)S(1)}, u32[]{:S(2)}, u32[]{:S(2)}) %collective-permute-start.10) | collective-permute-done | bytes 32800 | tf_op jit(solution)/shard_map/ppermute | solution.py:310
  109.7 1.3 shard_map.110
  111.0 9.2 %all_to_all.35.refs_1_ = bf16[4,224,128]{2,1,0:T(8,128)(2,1)S(1)} all-to-all(bf16[4,224,128]{2,1,0:T(8,128)(2,1)S(1)} %shard_map.110), channel_id=1, replica_groups=mesh['y'=4,'zh'=2,'zg'=2,'zl'=4,'x'=4,'c'=2] {'zl'}, dimensions={0} | all-to-all | bytes 458752 | tf_op jit(solution)/shard_map/all_to_all | solution.py:57
  120.2 1.8 %shard_map.111 = bf16[8,112,128]{2,1,0:T(8,128)(2,1)S(1)} custom-call(s32[5]{0:T(128)S(1)} %stack.23.refs_0_.refs_1_, bf16[4,224,128]{2,1,0:T(8,128)(2,1)S(1)} %all_to_all.35.refs_1_, bf16[128,128]{1,0:T(8,128)(2,1)S(1)} %get-tuple-element.33.refs_2_, bf16[128,128]{1,0:T(8,128)(2,1)S(1)} %collective-permute-done.8.refs_3_, ...), custom_call_target="tpu_custom_call" | custom-call | bytes 623636 | tf_op jit(solution)/shard_map/pallas_call | solution.py:33
  122.0 13.8 %all_to_all.36.refs_0_ = bf16[8,112,128]{2,1,0:T(8,128)(2,1)S(1)} all-to-all(bf16[8,112,128]{2,1,0:T(8,128)(2,1)S(1)} %shard_map.111), channel_id=1, replica_groups=mesh['y'=4,'zh'=2,'zg'=2,'zl'=4,'x'=4,'c'=2] {'x','c'}, dimensions={0} | all-to-all | bytes 458752 | tf_op jit(solution)/shard_map/all_to_all | solution.py:57
  135.9 9.1 %all_to_all.37.refs_0_ = f32[4,112,128]{2,1,0:T(8,128)S(1)} all-to-all(f32[4,112,128]{2,1,0:T(8,128)S(1)} %shard_map.112), channel_id=1, replica_groups=mesh['y'=4,'zh'=2,'zg'=2,'zl'=4,'x'=4,'c'=2] {'y'}, dimensions={0} | all-to-all | bytes 458752 | tf_op jit(solution)/shard_map/all_to_all | solution.py:57
  (30 shorter events, 3.2 us)
Async XLA Ops:
  0.6 11.4 %collective-permute-start.1 = (bf16[256,128]{1,0:T(8,128)(2,1)}, bf16[256,128]{1,0:T(8,128)(2,1)S(1)}, u32[]{:S(2)}, u32[]{:S(2)}) collective-permute-start(bf16[256,128]{1,0:T(8,128)(2,1)} %bitcast.15), channel_id=1, source_target_pairs={{1,2},{3,4},{5,6},{7,8},{9,10},{11,12},{13,14},{15,16},{17,18},{19... | collective-permute-start | bytes 196616 | tf_op jit(solution)/shard_map/ppermute | solution.py:306
  5.1 6.9 %collective-permute-start = (bf16[256,128]{1,0:T(8,128)(2,1)}, bf16[256,128]{1,0:T(8,128)(2,1)S(1)}, u32[]{:S(2)}, u32[]{:S(2)}) collective-permute-start(bf16[256,128]{1,0:T(8,128)(2,1)} %bitcast.16), channel_id=1, source_target_pairs={{0,1},{1,0},{2,3},{3,2},{4,5},{5,4},{6,7},{7,6},{8,9},{9,8},{10,11... | collective-permute-start | bytes 196616 | tf_op jit(solution)/shard_map/ppermute | solution.py:304
  10.1 0.8 copy-start.7
  10.9 0.7 copy-start.8
  11.6 1.5 %copy-start = (bf16[3456,256]{1,0:T(8,128)(2,1)S(1)}, bf16[3456,256]{1,0:T(8,128)(2,1)}, u32[]{:S(2)}) copy-start(bf16[3456,256]{1,0:T(8,128)(2,1)} %refs_4_.3) | copy-start | bytes 5308420
  11.6 1.5 %copy-start.2 = (bf16[1,1,16,16,256]{4,3,2,1,0:T(8,128)(2,1)S(1)}, bf16[1,1,16,16,256]{4,3,2,1,0:T(8,128)(2,1)}, u32[]{:S(2)}) copy-start(bf16[1,1,16,16,256]{4,3,2,1,0:T(8,128)(2,1)} %param.12) | copy-start | bytes 393220
  11.6 1.5 %copy-start.3 = (bf16[1,1,16,16,128]{4,3,2,1,0:T(8,128)(2,1)S(1)}, bf16[1,1,16,16,128]{4,3,2,1,0:T(8,128)(2,1)}, u32[]{:S(2)}) copy-start(bf16[1,1,16,16,128]{4,3,2,1,0:T(8,128)(2,1)} %param.9) | copy-start | bytes 196612
  11.6 1.5 %copy-start.5 = (f32[256]{0:T(256)S(1)}, f32[256]{0:T(256)}, u32[]{:S(2)}) copy-start(f32[256]{0:T(256)} %param.11) | copy-start | bytes 3076
  15.3 15.8 %all-to-all-start = ((bf16[8,384,128]{2,1,0:T(8,128)(2,1)}), bf16[8,384,128]{2,1,0:T(8,128)(2,1)S(1)}, u32[]{:S(2)}, u32[]{:S(2)}) async-start(bf16[8,384,128]{2,1,0:T(8,128)(2,1)} %get-tuple-element.19), calls=%async_computation | async-start | bytes 1572864 | tf_op jit(solution)/shard_map/all_to_all | solution.py:57
  18.8 0.7 collective-permute-start.4
  33.8 21.5 %all-to-all-start.1 = ((bf16[16,64,128]{2,1,0:T(8,128)(2,1)}), bf16[16,64,128]{2,1,0:T(8,128)(2,1)S(1)}, u32[]{:S(2)}, u32[]{:S(2)}) async-start(bf16[16,64,128]{2,1,0:T(8,128)(2,1)} %get-tuple-element.21), calls=%async_computation.1 | async-start | bytes 524288 | tf_op jit(solution)/shard_map/all_to_all | solution.py:57
  41.7 9.3 %collective-permute-start.5 = (bf16[64,128]{1,0:T(8,128)(2,1)S(1)}, bf16[64,128]{1,0:T(8,128)(2,1)S(1)}, u32[]{:S(2)}, u32[]{:S(2)}) collective-permute-start(bf16[64,128]{1,0:T(8,128)(2,1)S(1)} %get-tuple-element.23), channel_id=1, source_target_pairs={{0,8},{8,0},{16,24},{24,16},{1,9},{9,1},{17,25},{25,17},{2,10},{10... | collective-permute-start | bytes 49160 | tf_op jit(solution)/shard_map/ppermute | solution.py:310
  45.0 6.2 %collective-permute-start.6 = (bf16[64,128]{1,0:T(8,128)(2,1)S(1)}, bf16[64,128]{1,0:T(8,128)(2,1)S(1)}, u32[]{:S(2)}, u32[]{:S(2)}) collective-permute-start(bf16[64,128]{1,0:T(8,128)(2,1)S(1)} %get-tuple-element.24), channel_id=1, source_target_pairs={{0,16},{8,24},{16,0},{24,8},{1,17},{9,25},{17,1},{25,9},{2,18},{10... | collective-permute-start | bytes 49160 | tf_op jit(solution)/shard_map/ppermute | solution.py:310
  49.0 6.3 %collective-permute-start.7 = (bf16[64,128]{1,0:T(8,128)(2,1)S(1)}, bf16[64,128]{1,0:T(8,128)(2,1)S(1)}, u32[]{:S(2)}, u32[]{:S(2)}) collective-permute-start(bf16[64,128]{1,0:T(8,128)(2,1)S(1)} %get-tuple-element.25), channel_id=1, source_target_pairs={{0,24},{8,16},{16,8},{24,0},{1,25},{9,17},{17,9},{25,1},{2,26},{10... | collective-permute-start | bytes 49160 | tf_op jit(solution)/shard_map/ppermute | solution.py:310
  55.3 29.0 %copy-start.4 = (s32[8]{0:T(128)S(1)}, s32[8]{0:T(128)}, u32[]{:S(2)}) copy-start(s32[8]{0:T(128)} %refs_0_.3) | copy-start | bytes 100
  56.6 27.7 %all-to-all-start.2 = ((bf16[4,320,128]{2,1,0:T(8,128)(2,1)}), bf16[4,320,128]{2,1,0:T(8,128)(2,1)S(1)}, u32[]{:S(2)}, u32[]{:S(2)}) async-start(bf16[4,320,128]{2,1,0:T(8,128)(2,1)} %shard_map.107.refs_5_), calls=%async_computation.2 | async-start | bytes 655360 | tf_op jit(solution)/shard_map/all_to_all | solution.py:57
  67.7 8.1 %collective-permute-start.3 = (bf16[256,256]{1,0:T(8,128)(2,1)S(1)}, bf16[256,256]{1,0:T(8,128)(2,1)S(1)}, u32[]{:S(2)}, u32[]{:S(2)}) collective-permute-start(bf16[256,256]{1,0:T(8,128)(2,1)S(1)} %get-tuple-element.18.refs_3_), channel_id=1, source_target_pairs={{1,2},{3,4},{5,6},{7,8},{9,10},{11,12},{13,14},{15,16},{17,18},{19... | collective-permute-start | bytes 393224 | tf_op jit(solution)/shard_map/ppermute | solution.py:306
  73.2 3.2 %collective-permute-start.2 = (bf16[256,256]{1,0:T(8,128)(2,1)S(1)}, bf16[256,256]{1,0:T(8,128)(2,1)S(1)}, u32[]{:S(2)}, u32[]{:S(2)}) collective-permute-start(bf16[256,256]{1,0:T(8,128)(2,1)S(1)} %get-tuple-element.18.refs_3_), channel_id=1, source_target_pairs={{0,1},{1,0},{2,3},{3,2},{4,5},{5,4},{6,7},{7,6},{8,9},{9,8},{10,11... | collective-permute-start | bytes 393224 | tf_op jit(solution)/shard_map/ppermute | solution.py:304
  79.2 41.0 %copy-start.1 = (f32[256,256]{1,0:T(8,128)S(1)}, f32[256,256]{1,0:T(8,128)}, u32[]{:S(2)}) copy-start(f32[256,256]{1,0:T(8,128)} %refs_6_.1) | copy-start | bytes 786436
  79.2 41.0 %copy-start.6 = (f32[256]{0:T(256)S(1)}, f32[256]{0:T(256)}, u32[]{:S(2)}) copy-start(f32[256]{0:T(256)} %param.17) | copy-start | bytes 3076
  85.7 24.0 %all-to-all-start.3 = ((bf16[32,64,128]{2,1,0:T(8,128)(2,1)}), bf16[32,64,128]{2,1,0:T(8,128)(2,1)S(1)}, u32[]{:S(2)}, u32[]{:S(2)}) async-start(bf16[32,64,128]{2,1,0:T(8,128)(2,1)} %get-tuple-element.28), calls=%async_computation.3 | async-start | bytes 1048576 | tf_op jit(solution)/shard_map/all_to_all | solution.py:57
  98.1 9.3 %collective-permute-start.8 = (bf16[128,128]{1,0:T(8,128)(2,1)S(1)}, bf16[128,128]{1,0:T(8,128)(2,1)S(1)}, u32[]{:S(2)}, u32[]{:S(2)}) collective-permute-start(bf16[128,128]{1,0:T(8,128)(2,1)S(1)} %get-tuple-element.30), channel_id=1, source_target_pairs={{0,8},{8,0},{16,24},{24,16},{1,9},{9,1},{17,25},{25,17},{2,10},{10... | collective-permute-start | bytes 98312 | tf_op jit(solution)/shard_map/ppermute | solution.py:310
  100.1 7.4 %collective-permute-start.9 = (bf16[128,128]{1,0:T(8,128)(2,1)S(1)}, bf16[128,128]{1,0:T(8,128)(2,1)S(1)}, u32[]{:S(2)}, u32[]{:S(2)}) collective-permute-start(bf16[128,128]{1,0:T(8,128)(2,1)S(1)} %get-tuple-element.31), channel_id=1, source_target_pairs={{0,16},{8,24},{16,0},{24,8},{1,17},{9,25},{17,1},{25,9},{2,18},{10... | collective-permute-start | bytes 98312 | tf_op jit(solution)/shard_map/ppermute | solution.py:310
  102.3 6.8 %collective-permute-start.10 = (bf16[128,128]{1,0:T(8,128)(2,1)S(1)}, bf16[128,128]{1,0:T(8,128)(2,1)S(1)}, u32[]{:S(2)}, u32[]{:S(2)}) collective-permute-start(bf16[128,128]{1,0:T(8,128)(2,1)S(1)} %get-tuple-element.32), channel_id=1, source_target_pairs={{0,24},{8,16},{16,8},{24,0},{1,25},{9,17},{17,9},{25,1},{2,26},{10... | collective-permute-start | bytes 98312 | tf_op jit(solution)/shard_map/ppermute | solution.py:310

commit v9 on v8

--- a/solution.py
+++ b/solution.py
@@ -92,21 +92,23 @@
         out_ref[r] = block.astype(BF16)
 
 
-def by_side(place_ref, inside, outside):
-    first = place_ref[3] == 0
-    inside, outside = inside[...].astype(F32), outside[...].astype(F32)
-    return jnp.where(first, outside, inside), jnp.where(first, inside, outside)
+def by_side(place_ref, inside_ref, outside_ref, planes):
+    second = place_ref[3]
+    planes[2 - 2 * second] = inside_ref[...]
+    planes[2 * second] = outside_ref[...]
 
 
 def forward_body(
-    place_ref, inside_ref, outside_ref, mine, weight, bias, cot, basis_ref, delta_ref, send_ref, same_ref, patches
+    place_ref, inside_ref, outside_ref, mine, weight, bias, cot, basis_ref,
+    delta_ref, send_ref, own_ref, one_ref, two_ref, three_ref, patches, planes,
 ):
-    same_ref[...] = basis_ref[...]
-    low, high = by_side(place_ref, inside_ref, outside_ref)
-    planes = (low, mine[...].astype(F32), high)
+    for k, ref in enumerate((own_ref, one_ref, two_ref, three_ref)):
+        ref[...] = basis_ref[place_ref[0] ^ k]
+    by_side(place_ref, inside_ref, outside_ref, planes)
+    planes[1] = mine[...]
     none = jnp.zeros((16, 128), BF16)
     for a in range(3):
-        wide = planes[a]
+        wide = planes[a].astype(F32)
         for c in range(3):
             moved = x_shifted(wide, c - 1).astype(BF16)
             for b in range(3):
@@ -122,8 +124,8 @@
     logistic = 1.0 / (1.0 + jnp.exp(-pre))
     delta = (cot[...].astype(F32) * logistic * (1.0 + pre * (1.0 - logistic))).astype(BF16)
     delta_ref[...] = delta
-    act_t = planes[1].T.astype(BF16)
-    rim_t = jnp.where(place_ref[4] < 4, low, high).T.astype(BF16)
+    act_t = mine[...].astype(F32).T.astype(BF16)
+    rim_t = planes[2 * (place_ref[4] >> 2)].astype(F32).T.astype(BF16)
     for x in range(4):
         for c in range(2):
             to = 2 * x + c
@@ -135,7 +137,7 @@
             send_ref[to, 128:] = delta[:, 128 * c : 128 * c + 128]
 
 
-def weight_grad_body(place_ref, got_ref, basis_ref, out_ref, own_ref, one_ref, two_ref, three_ref, moved, deltas, whole):
+def weight_grad_body(got_ref, out_ref, moved, deltas, whole):
     pieces = []
     for plane, at in [(0, 64)] + [(e, 0) for e in range(8)] + [(7, 64)]:
         pieces.append(got_ref[plane, at : at + 32].astype(F32))
@@ -156,8 +158,6 @@
         whole[288 * a : 288 * a + 288, :] = jnp.dot(
             moved[:, 256 * a : 256 * a + 2048], deltas[...], preferred_element_type=F32
         )
-    for k, ref in enumerate((own_ref, one_ref, two_ref, three_ref)):
-        ref[...] = basis_ref[place_ref[2] ^ k]
     none = jnp.zeros((5, 128), F32)
     for y_to in range(4):
         for z_to in range(4):
@@ -269,15 +269,15 @@
     out_ref[...] = jnp.concatenate([total[:54], total[56:110]], axis=1)
 
 
-def data_grad_body(place_ref, inside_ref, outside_ref, mine_ref, weight_any, out_ref, token_ref, weight, sem):
+def data_grad_body(place_ref, inside_ref, outside_ref, mine_ref, weight_any, out_ref, token_ref, weight, planes, sem):
     copy = pltpu.make_async_copy(weight_any, weight, sem)
     copy.start()
-    low, high = by_side(place_ref, inside_ref, outside_ref)
-    planes = (high, mine_ref[...].astype(F32), low)
+    by_side(place_ref, inside_ref, outside_ref, planes)
+    planes[1] = mine_ref[...]
     none = jnp.zeros((16, 256), BF16)
     total = jnp.zeros((256, 128), F32)
     for a in range(3):
-        wide = planes[a]
+        wide = planes[2 - a].astype(F32)
         if a == 0:
             copy.wait()
         for c in range(3):
@@ -306,6 +306,13 @@
     return inside, lax.ppermute(block, SPACE, pairs + [(j, i) for i, j in pairs])
 
 
+def turned(blocks):
+    return [
+        lax.ppermute(block, ("y", "zl"), [(4 * y + z, 4 * z + (y ^ k)) for y in range(4) for z in range(4)])
+        for k, block in enumerate(blocks)
+    ]
+
+
 def among_zl(blocks):
     return [blocks[0]] + [lax.ppermute(blocks[k], "zl", [(i, i ^ k) for i in range(4)]) for k in (1, 2, 3)]
 
@@ -334,20 +341,20 @@
         scratch=[pltpu.VMEM((1, 54), F32), dma],
         flops=4_000_000_000,
     )
-    delta, send, stored = call(
+    delta, send, *slices = call(
         forward_body,
-        [shape((256, 256), BF16), shape((8, 384, 128), BF16), shape((4, 64, 128), BF16)],
+        [shape((256, 256), BF16), shape((8, 384, 128), BF16)] + [shape((64, 128), BF16)] * 4,
         (place,),
         (inside, outside, plane, conv_weight, conv_bias.reshape(1, 256), cotangent.reshape(256, 256), stored),
-        scratch=[pltpu.VMEM((256, 3456), BF16)],
+        scratch=[pltpu.VMEM((256, 3456), BF16), pltpu.VMEM((3, 256, 128), BF16)],
         flops=2 * 256 * 3456 * 256,
     )
-    stored = lax.ppermute(stored, ("y", "zl"), [(4 * y + z, 4 * z + y) for y in range(4) for z in range(4)])
-    part, *slices = call(
+    slices = turned(slices)
+    part = call(
         weight_grad_body,
-        [shape((16, 64, 128), BF16)] + [shape((64, 128), BF16)] * 4,
-        (place,),
-        (exchange(send, XC), stored),
+        shape((16, 64, 128), BF16),
+        arrays=(exchange(send, XC),),
+        after=slices[:2],
         scratch=[pltpu.VMEM((288, 2560), BF16), pltpu.VMEM((2048, 128), BF16), pltpu.VMEM((864, 128), F32)],
         flops=2 * 864 * 2048 * 128,
     )
@@ -355,25 +362,13 @@
         over_y_zl_body,
         shape((4, 320, 128), BF16),
         (place,),
-        (exchange(part, ("y", "zl")), *among_zl(slices)),
-    )
-    inside, outside = neighbours(delta)
-    data, token = call(
-        data_grad_body,
-        [shape((256, 128), BF16), shape((8, 128), F32)],
-        (place,),
-        (inside, outside, delta),
-        (conv_weight,),
-        after=(part,),
-        scratch=[pltpu.VMEM((3456, 256), BF16), dma],
-        flops=2 * 256 * 3456 * 256,
+        (exchange(part, ("y", "zl")), *slices),
     )
     part, basis, *slices = call(
         over_zh_zg_body,
         [shape((32, 64, 128), BF16), shape((8, 128, 128), BF16)] + [shape((128, 128), BF16)] * 4,
         (panel_owner, place),
         (exchange(part, ("zh", "zg")),),
-        after=(token,),
     )
     slices = among_zl(slices)
     rotated = call(
@@ -381,7 +376,7 @@
         shape((4, 224, 128), BF16),
         (panel_owner,),
         (exchange(part, YXC), basis),
-        after=slices[1:],
+        after=slices[1:2],
         scratch=[pltpu.VMEM((2, 1024, 128), F32), pltpu.VMEM((896, 256), F32)],
     )
     part = call(
@@ -398,8 +393,21 @@
             dma((2,)),
         ],
     )
-    part = call(over_xc_body, shape((4, 112, 128), F32), arrays=(exchange(part, XC),))
-    update = call(last_body, shape((54, 256), F32), arrays=(exchange(part, "y"),))
+    inside, outside = neighbours(delta)
+    part = call(
+        over_xc_body, shape((4, 112, 128), F32), arrays=(exchange(part, XC),), after=(inside, outside)
+    )
+    data, token = call(
+        data_grad_body,
+        [shape((256, 128), BF16), shape((8, 128), F32)],
+        (place,),
+        (inside, outside, delta),
+        (conv_weight,),
+        after=(part,),
+        scratch=[pltpu.VMEM((3456, 256), BF16), pltpu.VMEM((3, 256, 256), BF16), dma],
+        flops=2 * 256 * 3456 * 256,
+    )
+    update = call(last_body, shape((54, 256), F32), arrays=(exchange(part, "y"),), after=(token,))
     return (data.reshape(1, 1, 16, 16, 128), update)
 
 

time: 147 us -> 153 us (1.041)
  starting transfers between devices: 71 us -> 79.1 us
  blocking collectives: 32.2 us -> 27 us
  waiting for transfers between devices: 24.5 us -> 27.4 us
    ppermute x1 -> x4, starting transfers between devices: 0.66 us -> 13.1 us  [turned(): lax.ppermute(block, ('y', 'zl'), [(4 * y + z, 4 * z + (y ^ k)) for y in r...]
    ppermute x6 -> x3, starting transfers between devices: 18.5 us -> 11 us  [among_zl(): lax.ppermute(blocks[k], 'zl', [(i, i ^ k) for i in range(4)])]
    all_to_all x3 -> x1, blocking collectives: 32.2 us -> 27 us  [exchange(): return lax.all_to_all(x, axes, 0, 0)]
    ppermute x2, starting transfers between devices: 10 us -> 5.5 us  [neighbours(): lax.ppermute(block, SPACE, pairs + [(j, i) for i, j in pairs])]
    ppermute x2, waiting for transfers between devices: 0.71 us -> 4.65 us  [neighbours(): lax.ppermute(block, SPACE, pairs + [(j, i) for i, j in pairs])]
    ppermute x2, starting transfers between devices: 6.86 us -> 10.8 us  [neighbours(): inside = lax.ppermute(block, 'c', [(0, 1), (1, 0)])]
    all_to_all x4 -> x6, starting transfers between devices: 34.9 us -> 38.7 us  [exchange(): return lax.all_to_all(x, axes, 0, 0)]
    ppermute x1 -> x4, waiting for transfers between devices: 0.01 us -> 2.58 us  [turned(): lax.ppermute(block, ('y', 'zl'), [(4 * y + z, 4 * z + (y ^ k)) for y in r...]
  transfers between devices with their start and end apart: 15 -> 17, of which waited for: 8 -> 10; matrix products, arithmetic and copies ran while one was open for 0% -> 0% of each run, Pallas kernels for 2% -> 2%
where the time goes in v9:
time: 153 us; the launch traced here: 151 us
  starting transfers between devices  79.1 us (52%)
  waiting for transfers between devices  27.4 us (18%)
  blocking collectives  27 us (18%)
  Pallas kernels  15.3 us (10%)
  local copies, waits for them, and re-layouts  1.59 us (1%)
    all_to_all x6, starting transfers between devices, exchange(): return lax.all_to_all(x, axes, 0, 0)  38.7 us
    all_to_all x1, blocking collectives, exchange(): return lax.all_to_all(x, axes, 0, 0)  27 us
    pallas_call x10, Pallas kernels, call(): pl.pallas_call(kernel, out_shape=out_shape, in_specs=[SMEM] * len(scalars...  15.3 us
    all_to_all x6, waiting for transfers between devices, exchange(): return lax.all_to_all(x, axes, 0, 0)  15 us
    ppermute x4, starting transfers between devices, turned(): lax.ppermute(block, ('y', 'zl'), [(4 * y + z, 4 * z + (y ^ k)) for y in r...  13.1 us
    ppermute x3, starting transfers between devices, among_zl(): lax.ppermute(blocks[k], 'zl', [(i, i ^ k) for i in range(4)])  11 us
    ppermute x2, starting transfers between devices, neighbours(): inside = lax.ppermute(block, 'c', [(0, 1), (1, 0)])  10.8 us
    ppermute x2, starting transfers between devices, neighbours(): lax.ppermute(block, SPACE, pairs + [(j, i) for i, j in pairs])  5.5 us
  transfers between devices with their start and end apart: 17, of which 10 were waited for; matrix products, arithmetic and copies ran while one was open for 0% of the time, Pallas kernels for 2%

profile of v9, /device:TPU:1, one launch (start us, length us, event | category | flops | bytes accessed | tf_op | source)
XLA Modules:
  0.0 151.3 jit_solution(12340621983936651996)
XLA Ops:
  0.6 8.8 %collective-permute-start = (bf16[256,128]{1,0:T(8,128)(2,1)}, bf16[256,128]{1,0:T(8,128)(2,1)S(1)}, u32[]{:S(2)}, u32[]{:S(2)}) collective-permute-start(bf16[256,128]{1,0:T(8,128)(2,1)} %bitcast.15), channel_id=1, source_target_pairs={{0,1},{1,0},{2,3},{3,2},{4,5},{5,4},{6,7},{7,6},{8,9},{9,8},{10,11... | collective-permute-start | bytes 196616 | tf_op jit(solution)/shard_map/ppermute | solution.py:304
  9.4 1.9 %collective-permute-start.1 = (bf16[256,128]{1,0:T(8,128)(2,1)}, bf16[256,128]{1,0:T(8,128)(2,1)S(1)}, u32[]{:S(2)}, u32[]{:S(2)}) collective-permute-start(bf16[256,128]{1,0:T(8,128)(2,1)} %bitcast.16), channel_id=1, source_target_pairs={{1,2},{3,4},{5,6},{7,8},{9,10},{11,12},{13,14},{15,16},{17,18},{19... | collective-permute-start | bytes 196616 | tf_op jit(solution)/shard_map/ppermute | solution.py:306
  13.3 2.0 %collective-permute-done.1.refs_2_ = bf16[256,128]{1,0:T(8,128)(2,1)S(1)} collective-permute-done((bf16[256,128]{1,0:T(8,128)(2,1)}, bf16[256,128]{1,0:T(8,128)(2,1)S(1)}, u32[]{:S(2)}, u32[]{:S(2)}) %collective-permute-start.1) | collective-permute-done | bytes 65568 | tf_op jit(solution)/shard_map/ppermute | solution.py:306
  15.2 2.3 %shard_map.105 = (bf16[256,256]{1,0:T(8,128)(2,1)S(1)}, bf16[8,384,128]{2,1,0:T(8,128)(2,1)}, bf16[64,128]{1,0:T(8,128)(2,1)S(1)}, bf16[64,128]{1,0:T(8,128)(2,1...) custom-call(s32[5]{0:T(128)S(1)} %stack.23.refs_0_.refs_1_, ...), custom_call_target="tpu_custom_call" | custom-call | flops 452984832 | bytes 2163732 | tf_op jit(solution)/shard_map/pallas_call | solution.py:33
  17.5 3.5 %all-to-all-start = ((bf16[8,384,128]{2,1,0:T(8,128)(2,1)}), bf16[8,384,128]{2,1,0:T(8,128)(2,1)S(1)}, u32[]{:S(2)}, u32[]{:S(2)}) async-start(bf16[8,384,128]{2,1,0:T(8,128)(2,1)} %get-tuple-element.17), calls=%async_computation | async-start | bytes 1572864 | tf_op jit(solution)/shard_map/all_to_all | solution.py:57
  21.7 3.1 %collective-permute-start.5 = (bf16[64,128]{1,0:T(8,128)(2,1)S(1)}, bf16[64,128]{1,0:T(8,128)(2,1)S(1)}, u32[]{:S(2)}, u32[]{:S(2)}) collective-permute-start(bf16[64,128]{1,0:T(8,128)(2,1)S(1)} %get-tuple-element.19), channel_id=1, source_target_pairs={{0,8},{8,136},{16,264},{24,392},{128,0},{136,128},{144,256},{152,3... | collective-permute-start | bytes 49160 | tf_op jit(solution)/shard_map/ppermute | solution.py:311
  24.8 1.7 %collective-permute-done.5.refs_2_.refs_3_ = bf16[64,128]{1,0:T(8,128)(2,1)S(1)} collective-permute-done((bf16[64,128]{1,0:T(8,128)(2,1)S(1)}, bf16[64,128]{1,0:T(8,128)(2,1)S(1)}, u32[]{:S(2)}, u32[]{:S(2)}) %collective-permute-start.5) | collective-permute-done | bytes 16416 | tf_op jit(solution)/shard_map/ppermute | solution.py:311
  26.6 5.7 %all-to-all-done.refs_0_ = bf16[8,384,128]{2,1,0:T(8,128)(2,1)S(1)} async-done(((bf16[8,384,128]{2,1,0:T(8,128)(2,1)}), bf16[8,384,128]{2,1,0:T(8,128)(2,1)S(1)}, u32[]{:S(2)}, u32[]{:S(2)}) %all-to-all-start) | async-done | bytes 786464 | tf_op jit(solution)/shard_map/all_to_all | solution.py:57
  32.3 2.2 %shard_map.106 = bf16[16,64,128]{2,1,0:T(8,128)(2,1)} custom-call(bf16[8,384,128]{2,1,0:T(8,128)(2,1)S(1)} %all-to-all-done.refs_0_, bf16[64,128]{1,0:T(8,128)(2,1)S(1)} %collective-permute-done.4.refs_1_.refs_2_, bf16[64,128]{1,0:T(8,128)(2,1)S(1)} %collective-permute-done.5.refs_2_.refs_3_), custom_call_target="tpu_custom_call" | custom-call | flops 452984832 | bytes 819200 | tf_op jit(solution)/shard_map/pallas_call | solution.py:33
  34.4 8.0 %all-to-all-start.1 = ((bf16[16,64,128]{2,1,0:T(8,128)(2,1)}), bf16[16,64,128]{2,1,0:T(8,128)(2,1)S(1)}, u32[]{:S(2)}, u32[]{:S(2)}) async-start(bf16[16,64,128]{2,1,0:T(8,128)(2,1)} %shard_map.106), calls=%async_computation.1 | async-start | bytes 524288 | tf_op jit(solution)/shard_map/all_to_all | solution.py:57
  42.4 4.2 %collective-permute-start.6 = (bf16[64,128]{1,0:T(8,128)(2,1)S(1)}, bf16[64,128]{1,0:T(8,128)(2,1)S(1)}, u32[]{:S(2)}, u32[]{:S(2)}) collective-permute-start(bf16[64,128]{1,0:T(8,128)(2,1)S(1)} %get-tuple-element.20), channel_id=1, source_target_pairs={{0,16},{8,144},{16,272},{24,400},{128,24},{136,152},{144,280},{152... | collective-permute-start | bytes 49160 | tf_op jit(solution)/shard_map/ppermute | solution.py:311
  46.6 5.2 %collective-permute-start.7 = (bf16[64,128]{1,0:T(8,128)(2,1)S(1)}, bf16[64,128]{1,0:T(8,128)(2,1)S(1)}, u32[]{:S(2)}, u32[]{:S(2)}) collective-permute-start(bf16[64,128]{1,0:T(8,128)(2,1)S(1)} %get-tuple-element.21), channel_id=1, source_target_pairs={{0,24},{8,152},{16,280},{24,408},{128,16},{136,144},{144,272},{152... | collective-permute-start | bytes 49160 | tf_op jit(solution)/shard_map/ppermute | solution.py:311
  51.8 0.8 collective-permute-done.7.refs_5_
  53.3 27.0 %all_to_all.35.refs_2_ = bf16[4,320,128]{2,1,0:T(8,128)(2,1)S(1)} all-to-all(bf16[4,320,128]{2,1,0:T(8,128)(2,1)S(1)} %shard_map.107), channel_id=1, replica_groups=mesh['y'=4,'zh'=2,'zg'=2,'zl'=4,'x'=4,'c'=2] {'zh','zg'}, dimensions={0} | all-to-all | bytes 655360 | tf_op jit(solution)/shard_map/all_to_all | solution.py:57
  80.3 1.4 shard_map.108
  81.7 13.9 %all-to-all-start.3 = ((bf16[32,64,128]{2,1,0:T(8,128)(2,1)}), bf16[32,64,128]{2,1,0:T(8,128)(2,1)S(1)}, u32[]{:S(2)}, u32[]{:S(2)}) async-start(bf16[32,64,128]{2,1,0:T(8,128)(2,1)} %get-tuple-element.22), calls=%async_computation.3 | async-start | bytes 1048576 | tf_op jit(solution)/shard_map/all_to_all | solution.py:57
  95.6 3.9 %collective-permute-start.8 = (bf16[128,128]{1,0:T(8,128)(2,1)S(1)}, bf16[128,128]{1,0:T(8,128)(2,1)S(1)}, u32[]{:S(2)}, u32[]{:S(2)}) collective-permute-start(bf16[128,128]{1,0:T(8,128)(2,1)S(1)} %get-tuple-element.24), channel_id=1, source_target_pairs={{0,8},{8,0},{16,24},{24,16},{1,9},{9,1},{17,25},{25,17},{2,10},{10... | collective-permute-start | bytes 98312 | tf_op jit(solution)/shard_map/ppermute | solution.py:317
  99.5 1.6 %collective-permute-done.8.refs_3_ = bf16[128,128]{1,0:T(8,128)(2,1)S(1)} collective-permute-done((bf16[128,128]{1,0:T(8,128)(2,1)S(1)}, bf16[128,128]{1,0:T(8,128)(2,1)S(1)}, u32[]{:S(2)}, u32[]{:S(2)}) %collective-permute-start.8) | collective-permute-done | bytes 32800 | tf_op jit(solution)/shard_map/ppermute | solution.py:317
  101.1 6.1 %all-to-all-done.3.refs_1_ = bf16[32,64,128]{2,1,0:T(8,128)(2,1)S(1)} async-done(((bf16[32,64,128]{2,1,0:T(8,128)(2,1)}), bf16[32,64,128]{2,1,0:T(8,128)(2,1)S(1)}, u32[]{:S(2)}, u32[]{:S(2)}) %all-to-all-start.3) | async-done | bytes 524320 | tf_op jit(solution)/shard_map/all_to_all | solution.py:57
  107.2 2.0 %shard_map.109 = bf16[4,224,128]{2,1,0:T(8,128)(2,1)} custom-call(s32[8]{0:T(128)S(1)} %copy-done.4, bf16[32,64,128]{2,1,0:T(8,128)(2,1)S(1)} %all-to-all-done.3.refs_1_, bf16[8,128,128]{2,1,0:T(8,128)(2,1)S(1)} %get-tuple-element.23.refs_2_, bf16[128,128]{1,0:T(8,128)(2,1)S(1)} %collective-permute-done.8.refs_3_), custom_call_target="tpu_custom_call" | custom-call | bytes 819232 | tf_op jit(solution)/shard_map/pallas_call | solution.py:33
  109.1 4.2 %all-to-all-start.4 = ((bf16[4,224,128]{2,1,0:T(8,128)(2,1)}), bf16[4,224,128]{2,1,0:T(8,128)(2,1)S(1)}, u32[]{:S(2)}, u32[]{:S(2)}) async-start(bf16[4,224,128]{2,1,0:T(8,128)(2,1)} %shard_map.109), calls=%async_computation.4 | async-start | bytes 458752 | tf_op jit(solution)/shard_map/all_to_all | solution.py:57
  113.3 5.2 %collective-permute-start.10 = (bf16[128,128]{1,0:T(8,128)(2,1)S(1)}, bf16[128,128]{1,0:T(8,128)(2,1)S(1)}, u32[]{:S(2)}, u32[]{:S(2)}) collective-permute-start(bf16[128,128]{1,0:T(8,128)(2,1)S(1)} %get-tuple-element.27), channel_id=1, source_target_pairs={{0,24},{8,16},{16,8},{24,0},{1,25},{9,17},{17,9},{25,1},{2,26},{10... | collective-permute-start | bytes 98312 | tf_op jit(solution)/shard_map/ppermute | solution.py:317
  118.4 1.9 %collective-permute-start.9 = (bf16[128,128]{1,0:T(8,128)(2,1)S(1)}, bf16[128,128]{1,0:T(8,128)(2,1)S(1)}, u32[]{:S(2)}, u32[]{:S(2)}) collective-permute-start(bf16[128,128]{1,0:T(8,128)(2,1)S(1)} %get-tuple-element.26), channel_id=1, source_target_pairs={{0,16},{8,24},{16,0},{24,8},{1,17},{9,25},{17,1},{25,9},{2,18},{10... | collective-permute-start | bytes 98312 | tf_op jit(solution)/shard_map/ppermute | solution.py:317
  120.9 3.1 %collective-permute-done.9.refs_4_ = bf16[128,128]{1,0:T(8,128)(2,1)S(1)} collective-permute-done((bf16[128,128]{1,0:T(8,128)(2,1)S(1)}, bf16[128,128]{1,0:T(8,128)(2,1)S(1)}, u32[]{:S(2)}, u32[]{:S(2)}) %collective-permute-start.9) | collective-permute-done | bytes 32800 | tf_op jit(solution)/shard_map/ppermute | solution.py:317
  124.0 2.5 %shard_map.110 = bf16[8,112,128]{2,1,0:T(8,128)(2,1)} custom-call(s32[5]{0:T(128)S(1)} %stack.23.refs_0_.refs_1_, bf16[4,224,128]{2,1,0:T(8,128)(2,1)S(1)} %all-to-all-done.4.refs_1_, bf16[128,128]{1,0:T(8,128)(2,1)S(1)} %get-tuple-element.25.refs_2_, bf16[128,128]{1,0:T(8,128)(2,1)S(1)} %collective-permute-done.8.refs_3_, ...), custom_call_target="tpu_custom_call" | custom-call | bytes 623636 | tf_op jit(solution)/shard_map/pallas_call | solution.py:33
  126.5 5.8 %all-to-all-start.5 = ((bf16[8,112,128]{2,1,0:T(8,128)(2,1)}), bf16[8,112,128]{2,1,0:T(8,128)(2,1)S(1)}, u32[]{:S(2)}, u32[]{:S(2)}) async-start(bf16[8,112,128]{2,1,0:T(8,128)(2,1)} %shard_map.110), calls=%async_computation.5 | async-start | bytes 458752 | tf_op jit(solution)/shard_map/all_to_all | solution.py:57
  132.3 2.0 %collective-permute-start.2 = (bf16[256,256]{1,0:T(8,128)(2,1)S(1)}, bf16[256,256]{1,0:T(8,128)(2,1)S(1)}, u32[]{:S(2)}, u32[]{:S(2)}) collective-permute-start(bf16[256,256]{1,0:T(8,128)(2,1)S(1)} %get-tuple-element.16.refs_3_), channel_id=1, source_target_pairs={{0,1},{1,0},{2,3},{3,2},{4,5},{5,4},{6,7},{7,6},{8,9},{9,8},{10,11... | collective-permute-start | bytes 393224 | tf_op jit(solution)/shard_map/ppermute | solution.py:304
  134.3 3.6 %collective-permute-start.3 = (bf16[256,256]{1,0:T(8,128)(2,1)S(1)}, bf16[256,256]{1,0:T(8,128)(2,1)S(1)}, u32[]{:S(2)}, u32[]{:S(2)}) collective-permute-start(bf16[256,256]{1,0:T(8,128)(2,1)S(1)} %get-tuple-element.16.refs_3_), channel_id=1, source_target_pairs={{1,2},{3,4},{5,6},{7,8},{9,10},{11,12},{13,14},{15,16},{17,18},{19... | collective-permute-start | bytes 393224 | tf_op jit(solution)/shard_map/ppermute | solution.py:306
  137.9 2.7 %collective-permute-done.3.refs_2_ = bf16[256,256]{1,0:T(8,128)(2,1)S(1)} collective-permute-done((bf16[256,256]{1,0:T(8,128)(2,1)S(1)}, bf16[256,256]{1,0:T(8,128)(2,1)S(1)}, u32[]{:S(2)}, u32[]{:S(2)}) %collective-permute-start.3) | collective-permute-done | bytes 131104 | tf_op jit(solution)/shard_map/ppermute | solution.py:306
  141.3 3.4 %all-to-all-start.6 = ((f32[4,112,128]{2,1,0:T(8,128)}), f32[4,112,128]{2,1,0:T(8,128)S(1)}, u32[]{:S(2)}, u32[]{:S(2)}) async-start(f32[4,112,128]{2,1,0:T(8,128)} %shard_map.111.refs_5_), calls=%async_computation.6 | async-start | bytes 458752 | tf_op jit(solution)/shard_map/all_to_all | solution.py:57
  144.7 2.7 %shard_map.112 = (bf16[256,128]{1,0:T(8,128)(2,1)}, f32[8,128]{1,0:T(8,128)S(1)}) custom-call(s32[5]{0:T(128)S(1)} %stack.23.refs_0_.refs_1_, bf16[256,256]{1,0:T(8,128)(2,1)S(1)} %collective-permute-done.2.refs_1_, bf16[256,256]{1,0:T(8,128)(2,1)S(1)} %collective-permute-done.3.refs_2_, bf16[256,256]{1,0:T(8,128)(2,1)S(1)} %get-tuple-element.16.refs_3_, ...), custom_call_target="tpu_custom_call" | custom-call | flops 452984832 | bytes 2392084 | tf_op jit(solution)/shard_map/pallas_call | solution.py:33
  147.4 3.2 %all-to-all-done.6.refs_0_ = f32[4,112,128]{2,1,0:T(8,128)S(1)} async-done(((f32[4,112,128]{2,1,0:T(8,128)}), f32[4,112,128]{2,1,0:T(8,128)S(1)}, u32[]{:S(2)}, u32[]{:S(2)}) %all-to-all-start.6) | async-done | bytes 229408 | tf_op jit(solution)/shard_map/all_to_all | solution.py:57
  (32 shorter events, 5.1 us)
Async XLA Ops:
  0.6 12.6 %collective-permute-start = (bf16[256,128]{1,0:T(8,128)(2,1)}, bf16[256,128]{1,0:T(8,128)(2,1)S(1)}, u32[]{:S(2)}, u32[]{:S(2)}) collective-permute-start(bf16[256,128]{1,0:T(8,128)(2,1)} %bitcast.15), channel_id=1, source_target_pairs={{0,1},{1,0},{2,3},{3,2},{4,5},{5,4},{6,7},{7,6},{8,9},{9,8},{10,11... | collective-permute-start | bytes 196616 | tf_op jit(solution)/shard_map/ppermute | solution.py:304
  9.4 5.8 %collective-permute-start.1 = (bf16[256,128]{1,0:T(8,128)(2,1)}, bf16[256,128]{1,0:T(8,128)(2,1)S(1)}, u32[]{:S(2)}, u32[]{:S(2)}) collective-permute-start(bf16[256,128]{1,0:T(8,128)(2,1)} %bitcast.16), channel_id=1, source_target_pairs={{1,2},{3,4},{5,6},{7,8},{9,10},{11,12},{13,14},{15,16},{17,18},{19... | collective-permute-start | bytes 196616 | tf_op jit(solution)/shard_map/ppermute | solution.py:306
  11.4 0.8 copy-start.7
  12.2 0.7 copy-start.8
  12.8 2.4 %copy-start = (bf16[3456,256]{1,0:T(8,128)(2,1)S(1)}, bf16[3456,256]{1,0:T(8,128)(2,1)}, u32[]{:S(2)}) copy-start(bf16[3456,256]{1,0:T(8,128)(2,1)} %refs_4_.3) | copy-start | bytes 5308420
  12.8 2.4 %copy-start.2 = (bf16[1,1,16,16,256]{4,3,2,1,0:T(8,128)(2,1)S(1)}, bf16[1,1,16,16,256]{4,3,2,1,0:T(8,128)(2,1)}, u32[]{:S(2)}) copy-start(bf16[1,1,16,16,256]{4,3,2,1,0:T(8,128)(2,1)} %param.12) | copy-start | bytes 393220
  12.8 2.4 %copy-start.3 = (bf16[1,1,16,16,128]{4,3,2,1,0:T(8,128)(2,1)S(1)}, bf16[1,1,16,16,128]{4,3,2,1,0:T(8,128)(2,1)}, u32[]{:S(2)}) copy-start(bf16[1,1,16,16,128]{4,3,2,1,0:T(8,128)(2,1)} %param.9) | copy-start | bytes 196612
  12.8 2.4 %copy-start.5 = (f32[256]{0:T(256)S(1)}, f32[256]{0:T(256)}, u32[]{:S(2)}) copy-start(f32[256]{0:T(256)} %param.11) | copy-start | bytes 3076
  17.5 14.8 %all-to-all-start = ((bf16[8,384,128]{2,1,0:T(8,128)(2,1)}), bf16[8,384,128]{2,1,0:T(8,128)(2,1)S(1)}, u32[]{:S(2)}, u32[]{:S(2)}) async-start(bf16[8,384,128]{2,1,0:T(8,128)(2,1)} %get-tuple-element.17), calls=%async_computation | async-start | bytes 1572864 | tf_op jit(solution)/shard_map/all_to_all | solution.py:57
  21.0 59.3 %copy-start.4 = (s32[8]{0:T(128)S(1)}, s32[8]{0:T(128)}, u32[]{:S(2)}) copy-start(s32[8]{0:T(128)} %refs_0_.3) | copy-start | bytes 100
  21.0 3.8 %collective-permute-start.4 = (bf16[64,128]{1,0:T(8,128)(2,1)S(1)}, bf16[64,128]{1,0:T(8,128)(2,1)S(1)}, u32[]{:S(2)}, u32[]{:S(2)}) collective-permute-start(bf16[64,128]{1,0:T(8,128)(2,1)S(1)} %get-tuple-element.18), channel_id=1, source_target_pairs={{0,0},{8,128},{16,256},{24,384},{128,8},{136,136},{144,264},{152,3... | collective-permute-start | bytes 49160 | tf_op jit(solution)/shard_map/ppermute | solution.py:311
  21.7 4.9 %collective-permute-start.5 = (bf16[64,128]{1,0:T(8,128)(2,1)S(1)}, bf16[64,128]{1,0:T(8,128)(2,1)S(1)}, u32[]{:S(2)}, u32[]{:S(2)}) collective-permute-start(bf16[64,128]{1,0:T(8,128)(2,1)S(1)} %get-tuple-element.19), channel_id=1, source_target_pairs={{0,8},{8,136},{16,264},{24,392},{128,0},{136,128},{144,256},{152,3... | collective-permute-start | bytes 49160 | tf_op jit(solution)/shard_map/ppermute | solution.py:311
  34.4 18.2 %all-to-all-start.1 = ((bf16[16,64,128]{2,1,0:T(8,128)(2,1)}), bf16[16,64,128]{2,1,0:T(8,128)(2,1)S(1)}, u32[]{:S(2)}, u32[]{:S(2)}) async-start(bf16[16,64,128]{2,1,0:T(8,128)(2,1)} %shard_map.106), calls=%async_computation.1 | async-start | bytes 524288 | tf_op jit(solution)/shard_map/all_to_all | solution.py:57
  42.4 9.4 %collective-permute-start.6 = (bf16[64,128]{1,0:T(8,128)(2,1)S(1)}, bf16[64,128]{1,0:T(8,128)(2,1)S(1)}, u32[]{:S(2)}, u32[]{:S(2)}) collective-permute-start(bf16[64,128]{1,0:T(8,128)(2,1)S(1)} %get-tuple-element.20), channel_id=1, source_target_pairs={{0,16},{8,144},{16,272},{24,400},{128,24},{136,152},{144,280},{152... | collective-permute-start | bytes 49160 | tf_op jit(solution)/shard_map/ppermute | solution.py:311
  46.6 6.1 %collective-permute-start.7 = (bf16[64,128]{1,0:T(8,128)(2,1)S(1)}, bf16[64,128]{1,0:T(8,128)(2,1)S(1)}, u32[]{:S(2)}, u32[]{:S(2)}) collective-permute-start(bf16[64,128]{1,0:T(8,128)(2,1)S(1)} %get-tuple-element.21), channel_id=1, source_target_pairs={{0,24},{8,152},{16,280},{24,408},{128,16},{136,144},{144,272},{152... | collective-permute-start | bytes 49160 | tf_op jit(solution)/shard_map/ppermute | solution.py:311
  53.3 70.7 %copy-start.1 = (f32[256,256]{1,0:T(8,128)S(1)}, f32[256,256]{1,0:T(8,128)}, u32[]{:S(2)}) copy-start(f32[256,256]{1,0:T(8,128)} %refs_6_.1) | copy-start | bytes 786436
  53.3 70.7 %copy-start.6 = (f32[256]{0:T(256)S(1)}, f32[256]{0:T(256)}, u32[]{:S(2)}) copy-start(f32[256]{0:T(256)} %param.17) | copy-start | bytes 3076
  81.7 25.5 %all-to-all-start.3 = ((bf16[32,64,128]{2,1,0:T(8,128)(2,1)}), bf16[32,64,128]{2,1,0:T(8,128)(2,1)S(1)}, u32[]{:S(2)}, u32[]{:S(2)}) async-start(bf16[32,64,128]{2,1,0:T(8,128)(2,1)} %get-tuple-element.22), calls=%async_computation.3 | async-start | bytes 1048576 | tf_op jit(solution)/shard_map/all_to_all | solution.py:57
  95.6 5.5 %collective-permute-start.8 = (bf16[128,128]{1,0:T(8,128)(2,1)S(1)}, bf16[128,128]{1,0:T(8,128)(2,1)S(1)}, u32[]{:S(2)}, u32[]{:S(2)}) collective-permute-start(bf16[128,128]{1,0:T(8,128)(2,1)S(1)} %get-tuple-element.24), channel_id=1, source_target_pairs={{0,8},{8,0},{16,24},{24,16},{1,9},{9,1},{17,25},{25,17},{2,10},{10... | collective-permute-start | bytes 98312 | tf_op jit(solution)/shard_map/ppermute | solution.py:317
  109.1 14.9 %all-to-all-start.4 = ((bf16[4,224,128]{2,1,0:T(8,128)(2,1)}), bf16[4,224,128]{2,1,0:T(8,128)(2,1)S(1)}, u32[]{:S(2)}, u32[]{:S(2)}) async-start(bf16[4,224,128]{2,1,0:T(8,128)(2,1)} %shard_map.109), calls=%async_computation.4 | async-start | bytes 458752 | tf_op jit(solution)/shard_map/all_to_all | solution.py:57
  113.3 7.6 %collective-permute-start.10 = (bf16[128,128]{1,0:T(8,128)(2,1)S(1)}, bf16[128,128]{1,0:T(8,128)(2,1)S(1)}, u32[]{:S(2)}, u32[]{:S(2)}) collective-permute-start(bf16[128,128]{1,0:T(8,128)(2,1)S(1)} %get-tuple-element.27), channel_id=1, source_target_pairs={{0,24},{8,16},{16,8},{24,0},{1,25},{9,17},{17,9},{25,1},{2,26},{10... | collective-permute-start | bytes 98312 | tf_op jit(solution)/shard_map/ppermute | solution.py:317
  118.4 5.6 %collective-permute-start.9 = (bf16[128,128]{1,0:T(8,128)(2,1)S(1)}, bf16[128,128]{1,0:T(8,128)(2,1)S(1)}, u32[]{:S(2)}, u32[]{:S(2)}) collective-permute-start(bf16[128,128]{1,0:T(8,128)(2,1)S(1)} %get-tuple-element.26), channel_id=1, source_target_pairs={{0,16},{8,24},{16,0},{24,8},{1,17},{9,25},{17,1},{25,9},{2,18},{10... | collective-permute-start | bytes 98312 | tf_op jit(solution)/shard_map/ppermute | solution.py:317
  126.5 14.1 %all-to-all-start.5 = ((bf16[8,112,128]{2,1,0:T(8,128)(2,1)}), bf16[8,112,128]{2,1,0:T(8,128)(2,1)S(1)}, u32[]{:S(2)}, u32[]{:S(2)}) async-start(bf16[8,112,128]{2,1,0:T(8,128)(2,1)} %shard_map.110), calls=%async_computation.5 | async-start | bytes 458752 | tf_op jit(solution)/shard_map/all_to_all | solution.py:57
  132.3 5.6 %collective-permute-start.2 = (bf16[256,256]{1,0:T(8,128)(2,1)S(1)}, bf16[256,256]{1,0:T(8,128)(2,1)S(1)}, u32[]{:S(2)}, u32[]{:S(2)}) collective-permute-start(bf16[256,256]{1,0:T(8,128)(2,1)S(1)} %get-tuple-element.16.refs_3_), channel_id=1, source_target_pairs={{0,1},{1,0},{2,3},{3,2},{4,5},{5,4},{6,7},{7,6},{8,9},{9,8},{10,11... | collective-permute-start | bytes 393224 | tf_op jit(solution)/shard_map/ppermute | solution.py:304
  134.3 6.3 %collective-permute-start.3 = (bf16[256,256]{1,0:T(8,128)(2,1)S(1)}, bf16[256,256]{1,0:T(8,128)(2,1)S(1)}, u32[]{:S(2)}, u32[]{:S(2)}) collective-permute-start(bf16[256,256]{1,0:T(8,128)(2,1)S(1)} %get-tuple-element.16.refs_3_), channel_id=1, source_target_pairs={{1,2},{3,4},{5,6},{7,8},{9,10},{11,12},{13,14},{15,16},{17,18},{19... | collective-permute-start | bytes 393224 | tf_op jit(solution)/shard_map/ppermute | solution.py:306
  141.3 9.3 %all-to-all-start.6 = ((f32[4,112,128]{2,1,0:T(8,128)}), f32[4,112,128]{2,1,0:T(8,128)S(1)}, u32[]{:S(2)}, u32[]{:S(2)}) async-start(f32[4,112,128]{2,1,0:T(8,128)} %shard_map.111.refs_5_), calls=%async_computation.6 | async-start | bytes 458752 | tf_op jit(solution)/shard_map/all_to_all | solution.py:57

commit v10 on v9

--- a/solution.py
+++ b/solution.py
@@ -92,19 +92,20 @@
         out_ref[r] = block.astype(BF16)
 
 
-def by_side(place_ref, inside_ref, outside_ref, planes):
-    second = place_ref[3]
+def by_side(core_ref, inside_ref, outside_ref, planes):
+    second = core_ref[0]
     planes[2 - 2 * second] = inside_ref[...]
     planes[2 * second] = outside_ref[...]
 
 
 def forward_body(
-    place_ref, inside_ref, outside_ref, mine, weight, bias, cot, basis_ref,
-    delta_ref, send_ref, own_ref, one_ref, two_ref, three_ref, patches, planes,
+    y_ref, core_ref, inner_ref, inside_ref, outside_ref, mine, weight, bias, cot, basis_ref,
+    delta_ref, send_ref, even_ref, odd_ref, patches, planes,
 ):
-    for k, ref in enumerate((own_ref, one_ref, two_ref, three_ref)):
-        ref[...] = basis_ref[place_ref[0] ^ k]
-    by_side(place_ref, inside_ref, outside_ref, planes)
+    for k, ref in enumerate((even_ref, odd_ref)):
+        ref[0] = basis_ref[y_ref[0] ^ k]
+        ref[1] = basis_ref[y_ref[0] ^ k ^ 2]
+    by_side(core_ref, inside_ref, outside_ref, planes)
     planes[1] = mine[...]
     none = jnp.zeros((16, 128), BF16)
     for a in range(3):
@@ -125,7 +126,7 @@
     delta = (cot[...].astype(F32) * logistic * (1.0 + pre * (1.0 - logistic))).astype(BF16)
     delta_ref[...] = delta
     act_t = mine[...].astype(F32).T.astype(BF16)
-    rim_t = planes[2 * (place_ref[4] >> 2)].astype(F32).T.astype(BF16)
+    rim_t = planes[2 * (inner_ref[0] >> 2)].astype(F32).T.astype(BF16)
     for x in range(4):
         for c in range(2):
             to = 2 * x + c
@@ -137,7 +138,7 @@
             send_ref[to, 128:] = delta[:, 128 * c : 128 * c + 128]
 
 
-def weight_grad_body(got_ref, out_ref, moved, deltas, whole):
+def weight_grad_body(got_ref, even_ref, odd_ref, out_ref, pair_ref, moved, deltas, whole):
     pieces = []
     for plane, at in [(0, 64)] + [(e, 0) for e in range(8)] + [(7, 64)]:
         pieces.append(got_ref[plane, at : at + 32].astype(F32))
@@ -158,6 +159,8 @@
         whole[288 * a : 288 * a + 288, :] = jnp.dot(
             moved[:, 256 * a : 256 * a + 2048], deltas[...], preferred_element_type=F32
         )
+    pair_ref[0] = even_ref[1]
+    pair_ref[1] = odd_ref[1]
     none = jnp.zeros((5, 128), F32)
     for y_to in range(4):
         for z_to in range(4):
@@ -168,30 +171,32 @@
             out_ref[4 * y_to + z_to] = jnp.concatenate(parts, axis=0).astype(BF16)
 
 
-def over_y_zl_body(place_ref, got_ref, own_ref, one_ref, two_ref, three_ref, out_ref):
+def over_y_zl_body(zl_ref, got_ref, even_ref, odd_ref, pair_ref, out_ref):
     total = (sum(got_ref[i].astype(F32) for i in range(16)) * (1.0 / CELLS)).astype(BF16)
     for to in range(4):
         out_ref[to, :64] = total
-    for k, ref in enumerate((own_ref, one_ref, two_ref, three_ref)):
-        at = pl.multiple_of(64 + 64 * (place_ref[2] ^ k), 64)
+    for k, ref in enumerate((even_ref.at[0], odd_ref.at[0], pair_ref.at[0], pair_ref.at[1])):
+        at = pl.multiple_of(64 + 64 * (zl_ref[0] ^ k), 64)
         for to in range(4):
             out_ref[to, pl.ds(at, 64)] = ref[...]
 
 
-def over_zh_zg_body(owner_ref, place_ref, got_ref, out_ref, basis_ref, own_ref, one_ref, two_ref, three_ref):
+def over_zh_zg_body(owner_ref, zg_ref, zl_ref, got_ref, out_ref, basis_ref, here_ref, next_ref):
     total = sum(got_ref[i, :64].astype(F32) for i in range(4)).astype(BF16)
     for to in range(32):
         out_ref[to] = total
-    for zh in range(2):
-        for y in range(4):
-            for zg in range(2):
-                block = got_ref[2 * zh + zg, 64 + 64 * y : 128 + 64 * y]
-                basis_ref[2 * y + zh, 64 * zg : 64 * zg + 64] = block
-    for k, ref in enumerate((own_ref, one_ref, two_ref, three_ref)):
-        ref[...] = basis_ref[owner_ref[4 * place_ref[1] + (place_ref[2] ^ k)]]
-
-
-def rotate_body(owner_ref, got_ref, basis_ref, out_ref, grads, ordered):
+    for j in range(8):
+        at = pl.multiple_of(64 + 64 * (owner_ref[j] >> 1), 64)
+        for zg in range(2):
+            basis_ref[j, 64 * zg : 64 * zg + 64] = got_ref[2 * (owner_ref[j] & 1) + zg, pl.ds(at, 64)]
+    for k, ref in enumerate((here_ref, next_ref)):
+        ref[0] = basis_ref[4 * zg_ref[0] + (zl_ref[0] ^ k)]
+        ref[1] = basis_ref[4 * zg_ref[0] + (zl_ref[0] ^ k ^ 2)]
+
+
+def rotate_body(got_ref, basis_ref, here_ref, next_ref, out_ref, pair_ref, grads, ordered):
+    pair_ref[0] = here_ref[1]
+    pair_ref[1] = next_ref[1]
     for y in range(4):
         for x in range(4):
             at = 32 * (8 * x + 2 * y)
@@ -204,7 +209,7 @@
     inside = iota((128, 128), 1) < 108
     total = jnp.zeros((128, 256), F32)
     for j in range(8):
-        block = jnp.where(inside, basis_ref[owner_ref[j]].astype(F32), 0.0).astype(BF16)
+        block = jnp.where(inside, basis_ref[j].astype(F32), 0.0).astype(BF16)
         rows = ordered[108 * j : 108 * j + 128, :].astype(BF16)
         total = total + jnp.dot(block, rows, preferred_element_type=F32)
     total = jnp.concatenate(
@@ -215,11 +220,11 @@
 
 
 def update_body(
-    place_ref, got_ref, own_ref, one_ref, two_ref, three_ref, out_basis_any, out_eigen_any,
+    zl_ref, got_ref, here_ref, next_ref, pair_ref, out_basis_any, out_eigen_any,
     out_ref, panel, out_basis, out_eigen, ordered, sems,
 ):
-    for k, ref in enumerate((own_ref, one_ref, two_ref, three_ref)):
-        panel[place_ref[2] ^ k] = ref[...]
+    for k, ref in enumerate((here_ref.at[0], next_ref.at[0], pair_ref.at[0], pair_ref.at[1])):
+        panel[zl_ref[0] ^ k] = ref[...]
     copies = [
         pltpu.make_async_copy(out_basis_any, out_basis, sems.at[0]),
         pltpu.make_async_copy(out_eigen_any, out_eigen, sems.at[1]),
@@ -237,7 +242,7 @@
     for copy in copies:
         copy.wait()
     rotated = jnp.dot(rotated, out_basis[...], precision=highest, preferred_element_type=F32)
-    terms = own_ref[...].astype(F32)
+    terms = here_ref[0].astype(F32)
     eigen = (terms[:, 108:109] + terms[:, 109:110]) + terms[:, 110:111]
     scaled = rotated / (eigen * out_eigen[...] + DAMPING)
     scaled = jnp.where((iota((128, 256), 0) & 63) < 54, scaled, 0.0)
@@ -269,10 +274,10 @@
     out_ref[...] = jnp.concatenate([total[:54], total[56:110]], axis=1)
 
 
-def data_grad_body(place_ref, inside_ref, outside_ref, mine_ref, weight_any, out_ref, token_ref, weight, planes, sem):
+def data_grad_body(core_ref, inside_ref, outside_ref, mine_ref, weight_any, out_ref, token_ref, weight, planes, sem):
     copy = pltpu.make_async_copy(weight_any, weight, sem)
     copy.start()
-    by_side(place_ref, inside_ref, outside_ref, planes)
+    by_side(core_ref, inside_ref, outside_ref, planes)
     planes[1] = mine_ref[...]
     none = jnp.zeros((16, 256), BF16)
     total = jnp.zeros((256, 128), F32)
@@ -306,15 +311,13 @@
     return inside, lax.ppermute(block, SPACE, pairs + [(j, i) for i, j in pairs])
 
 
-def turned(blocks):
-    return [
-        lax.ppermute(block, ("y", "zl"), [(4 * y + z, 4 * z + (y ^ k)) for y in range(4) for z in range(4)])
-        for k, block in enumerate(blocks)
-    ]
-
-
-def among_zl(blocks):
-    return [blocks[0]] + [lax.ppermute(blocks[k], "zl", [(i, i ^ k) for i in range(4)]) for k in (1, 2, 3)]
+def turned(block, k):
+    pairs = [(4 * y + z, 4 * z + (y ^ k)) for y in range(4) for z in range(4)]
+    return lax.ppermute(block, ("y", "zl"), pairs)
+
+
+def across(block, k):
+    return lax.ppermute(block, "zl", [(i, i ^ k) for i in range(4)])
 
 
 def per_device(
@@ -329,7 +332,7 @@
     output_eigen,
 ):
     dma = pltpu.SemaphoreType.DMA
-    place = jnp.stack([lax.axis_index(a) for a in ("y", "zg", "zl", "c", XC)]).astype(jnp.int32)
+    y, zg, zl, core, inner = (lax.axis_index(a).astype(jnp.int32).reshape(1) for a in ("y", "zg", "zl", "c", XC))
     plane = activations.reshape(256, 128)
     inside, outside = neighbours(plane)
 
@@ -341,49 +344,48 @@
         scratch=[pltpu.VMEM((1, 54), F32), dma],
         flops=4_000_000_000,
     )
-    delta, send, *slices = call(
+    delta, send, even, odd = call(
         forward_body,
-        [shape((256, 256), BF16), shape((8, 384, 128), BF16)] + [shape((64, 128), BF16)] * 4,
-        (place,),
+        [shape((256, 256), BF16), shape((8, 384, 128), BF16)] + [shape((2, 64, 128), BF16)] * 2,
+        (y, core, inner),
         (inside, outside, plane, conv_weight, conv_bias.reshape(1, 256), cotangent.reshape(256, 256), stored),
         scratch=[pltpu.VMEM((256, 3456), BF16), pltpu.VMEM((3, 256, 128), BF16)],
         flops=2 * 256 * 3456 * 256,
     )
-    slices = turned(slices)
-    part = call(
+    even, odd = turned(even, 0), turned(odd, 1)
+    part, pair = call(
         weight_grad_body,
-        shape((16, 64, 128), BF16),
-        arrays=(exchange(send, XC),),
-        after=slices[:2],
+        [shape((16, 64, 128), BF16), shape((2, 64, 128), BF16)],
+        arrays=(exchange(send, XC), even, odd),
         scratch=[pltpu.VMEM((288, 2560), BF16), pltpu.VMEM((2048, 128), BF16), pltpu.VMEM((864, 128), F32)],
         flops=2 * 864 * 2048 * 128,
     )
     part = call(
         over_y_zl_body,
         shape((4, 320, 128), BF16),
-        (place,),
-        (exchange(part, ("y", "zl")), *slices),
-    )
-    part, basis, *slices = call(
+        (zl,),
+        (exchange(part, ("y", "zl")), even, odd, across(pair, 2)),
+    )
+    inside, outside = neighbours(delta)
+    part, basis, here, there = call(
         over_zh_zg_body,
-        [shape((32, 64, 128), BF16), shape((8, 128, 128), BF16)] + [shape((128, 128), BF16)] * 4,
-        (panel_owner, place),
+        [shape((32, 64, 128), BF16), shape((8, 128, 128), BF16)] + [shape((2, 128, 128), BF16)] * 2,
+        (panel_owner, zg, zl),
         (exchange(part, ("zh", "zg")),),
-    )
-    slices = among_zl(slices)
-    rotated = call(
+        after=(inside, outside),
+    )
+    there = across(there, 1)
+    rotated, pair = call(
         rotate_body,
-        shape((4, 224, 128), BF16),
-        (panel_owner,),
-        (exchange(part, YXC), basis),
-        after=slices[1:2],
+        [shape((4, 224, 128), BF16), shape((2, 128, 128), BF16)],
+        arrays=(exchange(part, YXC), basis, here, there),
         scratch=[pltpu.VMEM((2, 1024, 128), F32), pltpu.VMEM((896, 256), F32)],
     )
     part = call(
         update_body,
         shape((8, 112, 128), BF16),
-        (place,),
-        (exchange(rotated, "zl"), *slices),
+        (zl,),
+        (exchange(rotated, "zl"), here, there, across(pair, 2)),
         (output_basis, output_eigen.reshape(1, 256)),
         scratch=[
             pltpu.VMEM((4, 128, 128), BF16),
@@ -393,14 +395,11 @@
             dma((2,)),
         ],
     )
-    inside, outside = neighbours(delta)
-    part = call(
-        over_xc_body, shape((4, 112, 128), F32), arrays=(exchange(part, XC),), after=(inside, outside)
-    )
+    part = call(over_xc_body, shape((4, 112, 128), F32), arrays=(exchange(part, XC),))
     data, token = call(
         data_grad_body,
         [shape((256, 128), BF16), shape((8, 128), F32)],
-        (place,),
+        (core,),
         (inside, outside, delta),
         (conv_weight,),
         after=(part,),

time: 153 us -> 143 us (0.935)
  blocking collectives: 27 us -> 9.99 us
  waiting for transfers between devices: 27.4 us -> 43.4 us
  starting transfers between devices: 79.1 us -> 73 us
  Pallas kernels: 15.3 us -> 12.6 us
    all_to_all x1, blocking collectives: 27 us -> 9.99 us  [exchange(): return lax.all_to_all(x, axes, 0, 0)]
    all_to_all x6, waiting for transfers between devices: 15 us -> 24.9 us  [exchange(): return lax.all_to_all(x, axes, 0, 0)]
    ppermute x7 -> x5, waiting for transfers between devices: 7.79 us -> 17.2 us  [the longest x3 15.3 us: across(): return lax.ppermute(block, 'zl', [(i, i ^ k) for i in range(4)])]
    ppermute x7 -> x5, starting transfers between devices: 24.1 us -> 14.9 us  [the longest x3 10.3 us: across(): return lax.ppermute(block, 'zl', [(i, i ^ k) for i in range(4)])]
    ppermute x2, starting transfers between devices: 5.5 us -> 10.2 us  [neighbours(): lax.ppermute(block, SPACE, pairs + [(j, i) for i, j in pairs])]
    ppermute x2, waiting for transfers between devices: 4.65 us -> 0.71 us  [neighbours(): lax.ppermute(block, SPACE, pairs + [(j, i) for i, j in pairs])]
    ppermute x2, starting transfers between devices: 10.8 us -> 6.86 us  [neighbours(): inside = lax.ppermute(block, 'c', [(0, 1), (1, 0)])]
    pallas_call x10, Pallas kernels: 15.3 us -> 12.6 us  [call(): pl.pallas_call(kernel, out_shape=out_shape, in_specs=[SMEM] * len(scalars...]
  transfers between devices with their start and end apart: 17 -> 15, of which waited for: 10 -> 11; matrix products, arithmetic and copies ran while one was open for 0% -> 0% of each run, Pallas kernels for 2% -> 2%
where the time goes in v10:
time: 143 us; the launch traced here: 142 us
  starting transfers between devices  73 us (51%)
  waiting for transfers between devices  43.4 us (30%)
  Pallas kernels  12.6 us (9%)
  blocking collectives  9.99 us (7%)
  local copies, waits for them, and re-layouts  2.61 us (2%)
    all_to_all x6, starting transfers between devices, exchange(): return lax.all_to_all(x, axes, 0, 0)  41 us
    all_to_all x6, waiting for transfers between devices, exchange(): return lax.all_to_all(x, axes, 0, 0)  24.9 us
    ppermute x3, waiting for transfers between devices, across(): return lax.ppermute(block, 'zl', [(i, i ^ k) for i in range(4)])  15.3 us
    pallas_call x10, Pallas kernels, call(): pl.pallas_call(kernel, out_shape=out_shape, in_specs=[SMEM] * len(scalars...  12.6 us
    ppermute x3, starting transfers between devices, across(): return lax.ppermute(block, 'zl', [(i, i ^ k) for i in range(4)])  10.3 us
    ppermute x2, starting transfers between devices, neighbours(): lax.ppermute(block, SPACE, pairs + [(j, i) for i, j in pairs])  10.2 us
    all_to_all x1, blocking collectives, exchange(): return lax.all_to_all(x, axes, 0, 0)  9.99 us
    ppermute x2, starting transfers between devices, neighbours(): inside = lax.ppermute(block, 'c', [(0, 1), (1, 0)])  6.86 us
  transfers between devices with their start and end apart: 15, of which 11 were waited for; matrix products, arithmetic and copies ran while one was open for 0% of the time, Pallas kernels for 2%

profile of v10, /device:TPU:1, one launch (start us, length us, event | category | flops | bytes accessed | tf_op | source)
XLA Modules:
  0.0 142.5 jit_solution(14863490850848567040)
XLA Ops:
  0.6 4.5 %collective-permute-start.1 = (bf16[256,128]{1,0:T(8,128)(2,1)}, bf16[256,128]{1,0:T(8,128)(2,1)S(1)}, u32[]{:S(2)}, u32[]{:S(2)}) collective-permute-start(bf16[256,128]{1,0:T(8,128)(2,1)} %bitcast.15), channel_id=1, source_target_pairs={{1,2},{3,4},{5,6},{7,8},{9,10},{11,12},{13,14},{15,16},{17,18},{19... | collective-permute-start | bytes 196616 | tf_op jit(solution)/shard_map/ppermute | solution.py:311
  5.1 4.9 %collective-permute-start = (bf16[256,128]{1,0:T(8,128)(2,1)}, bf16[256,128]{1,0:T(8,128)(2,1)S(1)}, u32[]{:S(2)}, u32[]{:S(2)}) collective-permute-start(bf16[256,128]{1,0:T(8,128)(2,1)} %bitcast.16), channel_id=1, source_target_pairs={{0,1},{1,0},{2,3},{3,2},{4,5},{5,4},{6,7},{7,6},{8,9},{9,8},{10,11... | collective-permute-start | bytes 196616 | tf_op jit(solution)/shard_map/ppermute | solution.py:309
  10.1 0.8 copy-done.7
  11.9 1.1 copy-done
  13.1 1.7 %shard_map.105 = (bf16[256,256]{1,0:T(8,128)(2,1)S(1)}, bf16[8,384,128]{2,1,0:T(8,128)(2,1)}, bf16[2,64,128]{2,1,0:T(8,128)(2,1)S(1)}, bf16[2,64,128]{2,1,0:T(8,128)(2,1)S(1)}) custom-call(s32[1]{0:T(128)} %bitcast.1.refs_0_, s32[1]{0:T(128)} %bitcast.refs_1_.refs_0_, s32[1]{0:T(128)} %bitcast.2.refs_2_, bf16[256,128]{1,0:T(8,128)(2,1)S(1)} %collective-permute-done.refs_3_, ...), custom_call_target="tpu_custom_call" | custom-call | flops 452984832 | bytes 2163724 | tf_op jit(solution)/shard_map/pallas_call | solution.py:33
  14.8 3.5 %all-to-all-start = ((bf16[8,384,128]{2,1,0:T(8,128)(2,1)}), bf16[8,384,128]{2,1,0:T(8,128)(2,1)S(1)}, u32[]{:S(2)}, u32[]{:S(2)}) async-start(bf16[8,384,128]{2,1,0:T(8,128)(2,1)} %get-tuple-element.17), calls=%async_computation | async-start | bytes 1572864 | tf_op jit(solution)/shard_map/all_to_all | solution.py:57
  19.0 4.0 %collective-permute-start.5 = (bf16[2,64,128]{2,1,0:T(8,128)(2,1)S(1)}, bf16[2,64,128]{2,1,0:T(8,128)(2,1)S(1)}, u32[]{:S(2)}, u32[]{:S(2)}) collective-permute-start(bf16[2,64,128]{2,1,0:T(8,128)(2,1)S(1)} %get-tuple-element.19), channel_id=1, source_target_pairs={{0,8},{8,136},{16,264},{24,392},{128,0},{136,128},{144,256},{152,3... | collective-permute-start | bytes 98312 | tf_op jit(solution)/shard_map/ppermute | solution.py:316
  23.0 1.9 %collective-permute-done.5.refs_2_.refs_3_ = bf16[2,64,128]{2,1,0:T(8,128)(2,1)S(1)} collective-permute-done((bf16[2,64,128]{2,1,0:T(8,128)(2,1)S(1)}, bf16[2,64,128]{2,1,0:T(8,128)(2,1)S(1)}, u32[]{:S(2)}, u32[]{:S(2)}) %collective-permute-start.5) | collective-permute-done | bytes 32800 | tf_op jit(solution)/shard_map/ppermute | solution.py:316
  24.9 5.7 %all-to-all-done.refs_0_ = bf16[8,384,128]{2,1,0:T(8,128)(2,1)S(1)} async-done(((bf16[8,384,128]{2,1,0:T(8,128)(2,1)}), bf16[8,384,128]{2,1,0:T(8,128)(2,1)S(1)}, u32[]{:S(2)}, u32[]{:S(2)}) %all-to-all-start) | async-done | bytes 786464 | tf_op jit(solution)/shard_map/all_to_all | solution.py:57
  30.6 2.2 %shard_map.106 = (bf16[16,64,128]{2,1,0:T(8,128)(2,1)}, bf16[2,64,128]{2,1,0:T(8,128)(2,1)S(1)}) custom-call(bf16[8,384,128]{2,1,0:T(8,128)(2,1)S(1)} %all-to-all-done.refs_0_, bf16[2,64,128]{2,1,0:T(8,128)(2,1)S(1)} %collective-permute-done.4.refs_1_.refs_2_, bf16[2,64,128]{2,1,0:T(8,128)(2,1)S(1)} %collective-permute-done.5.refs_2_.refs_3_), custom_call_target="tpu_custom_call" | custom-call | flops 452984832 | bytes 851968 | tf_op jit(solution)/shard_map/pallas_call | solution.py:33
  32.7 7.9 %all-to-all-start.1 = ((bf16[16,64,128]{2,1,0:T(8,128)(2,1)}), bf16[16,64,128]{2,1,0:T(8,128)(2,1)S(1)}, u32[]{:S(2)}, u32[]{:S(2)}) async-start(bf16[16,64,128]{2,1,0:T(8,128)(2,1)} %get-tuple-element.20), calls=%async_computation.1 | async-start | bytes 524288 | tf_op jit(solution)/shard_map/all_to_all | solution.py:57
  40.7 4.2 %collective-permute-start.6 = (bf16[2,64,128]{2,1,0:T(8,128)(2,1)S(1)}, bf16[2,64,128]{2,1,0:T(8,128)(2,1)S(1)}, u32[]{:S(2)}, u32[]{:S(2)}) collective-permute-start(bf16[2,64,128]{2,1,0:T(8,128)(2,1)S(1)} %get-tuple-element.21), channel_id=1, source_target_pairs={{0,16},{8,24},{16,0},{24,8},{1,17},{9,25},{17,1},{25,9},{2,18},{10... | collective-permute-start | bytes 98312 | tf_op jit(solution)/shard_map/ppermute | solution.py:320
  44.9 5.5 %collective-permute-done.6.refs_4_ = bf16[2,64,128]{2,1,0:T(8,128)(2,1)S(1)} collective-permute-done((bf16[2,64,128]{2,1,0:T(8,128)(2,1)S(1)}, bf16[2,64,128]{2,1,0:T(8,128)(2,1)S(1)}, u32[]{:S(2)}, u32[]{:S(2)}) %collective-permute-start.6) | collective-permute-done | bytes 32800 | tf_op jit(solution)/shard_map/ppermute | solution.py:320
  50.7 0.8 shard_map.107
  51.5 11.2 %all-to-all-start.2 = ((bf16[4,320,128]{2,1,0:T(8,128)(2,1)}), bf16[4,320,128]{2,1,0:T(8,128)(2,1)S(1)}, u32[]{:S(2)}, u32[]{:S(2)}) async-start(bf16[4,320,128]{2,1,0:T(8,128)(2,1)} %shard_map.107), calls=%async_computation.2 | async-start | bytes 655360 | tf_op jit(solution)/shard_map/all_to_all | solution.py:57
  62.7 5.7 %collective-permute-start.3 = (bf16[256,256]{1,0:T(8,128)(2,1)S(1)}, bf16[256,256]{1,0:T(8,128)(2,1)S(1)}, u32[]{:S(2)}, u32[]{:S(2)}) collective-permute-start(bf16[256,256]{1,0:T(8,128)(2,1)S(1)} %get-tuple-element.16.refs_3_), channel_id=1, source_target_pairs={{1,2},{3,4},{5,6},{7,8},{9,10},{11,12},{13,14},{15,16},{17,18},{19... | collective-permute-start | bytes 393224 | tf_op jit(solution)/shard_map/ppermute | solution.py:311
  68.4 1.9 %collective-permute-start.2 = (bf16[256,256]{1,0:T(8,128)(2,1)S(1)}, bf16[256,256]{1,0:T(8,128)(2,1)S(1)}, u32[]{:S(2)}, u32[]{:S(2)}) collective-permute-start(bf16[256,256]{1,0:T(8,128)(2,1)S(1)} %get-tuple-element.16.refs_3_), channel_id=1, source_target_pairs={{0,1},{1,0},{2,3},{3,2},{4,5},{5,4},{6,7},{7,6},{8,9},{9,8},{10,11... | collective-permute-start | bytes 393224 | tf_op jit(solution)/shard_map/ppermute | solution.py:309
  71.7 9.4 %all-to-all-done.2.refs_3_ = bf16[4,320,128]{2,1,0:T(8,128)(2,1)S(1)} async-done(((bf16[4,320,128]{2,1,0:T(8,128)(2,1)}), bf16[4,320,128]{2,1,0:T(8,128)(2,1)S(1)}, u32[]{:S(2)}, u32[]{:S(2)}) %all-to-all-start.2) | async-done | bytes 327712 | tf_op jit(solution)/shard_map/all_to_all | solution.py:57
  81.1 1.4 shard_map.108
  82.5 11.6 %all-to-all-start.3 = ((bf16[32,64,128]{2,1,0:T(8,128)(2,1)}), bf16[32,64,128]{2,1,0:T(8,128)(2,1)S(1)}, u32[]{:S(2)}, u32[]{:S(2)}) async-start(bf16[32,64,128]{2,1,0:T(8,128)(2,1)} %get-tuple-element.22), calls=%async_computation.3 | async-start | bytes 1048576 | tf_op jit(solution)/shard_map/all_to_all | solution.py:57
  94.1 1.9 %collective-permute-start.7 = (bf16[2,128,128]{2,1,0:T(8,128)(2,1)S(1)}, bf16[2,128,128]{2,1,0:T(8,128)(2,1)S(1)}, u32[]{:S(2)}, u32[]{:S(2)}) collective-permute-start(bf16[2,128,128]{2,1,0:T(8,128)(2,1)S(1)} %get-tuple-element.25), channel_id=1, source_target_pairs={{0,8},{8,0},{16,24},{24,16},{1,9},{9,1},{17,25},{25,17},{2,10},{10... | collective-permute-start | bytes 196616 | tf_op jit(solution)/shard_map/ppermute | solution.py:320
  96.1 3.4 %collective-permute-done.7.refs_3_ = bf16[2,128,128]{2,1,0:T(8,128)(2,1)S(1)} collective-permute-done((bf16[2,128,128]{2,1,0:T(8,128)(2,1)S(1)}, bf16[2,128,128]{2,1,0:T(8,128)(2,1)S(1)}, u32[]{:S(2)}, u32[]{:S(2)}) %collective-permute-start.7) | collective-permute-done | bytes 65568 | tf_op jit(solution)/shard_map/ppermute | solution.py:320
  99.5 6.2 %all-to-all-done.3.refs_0_ = bf16[32,64,128]{2,1,0:T(8,128)(2,1)S(1)} async-done(((bf16[32,64,128]{2,1,0:T(8,128)(2,1)}), bf16[32,64,128]{2,1,0:T(8,128)(2,1)S(1)}, u32[]{:S(2)}, u32[]{:S(2)}) %all-to-all-start.3) | async-done | bytes 524320 | tf_op jit(solution)/shard_map/all_to_all | solution.py:57
  105.7 1.4 shard_map.109
  107.1 3.4 %all-to-all-start.4 = ((bf16[4,224,128]{2,1,0:T(8,128)(2,1)}), bf16[4,224,128]{2,1,0:T(8,128)(2,1)S(1)}, u32[]{:S(2)}, u32[]{:S(2)}) async-start(bf16[4,224,128]{2,1,0:T(8,128)(2,1)} %get-tuple-element.26), calls=%async_computation.4 | async-start | bytes 458752 | tf_op jit(solution)/shard_map/all_to_all | solution.py:57
  110.5 4.2 %collective-permute-start.8 = (bf16[2,128,128]{2,1,0:T(8,128)(2,1)S(1)}, bf16[2,128,128]{2,1,0:T(8,128)(2,1)S(1)}, u32[]{:S(2)}, u32[]{:S(2)}) collective-permute-start(bf16[2,128,128]{2,1,0:T(8,128)(2,1)S(1)} %get-tuple-element.27), channel_id=1, source_target_pairs={{0,16},{8,24},{16,0},{24,8},{1,17},{9,25},{17,1},{25,9},{2,18},{10... | collective-permute-start | bytes 196616 | tf_op jit(solution)/shard_map/ppermute | solution.py:320
  114.7 6.4 %collective-permute-done.8.refs_4_ = bf16[2,128,128]{2,1,0:T(8,128)(2,1)S(1)} collective-permute-done((bf16[2,128,128]{2,1,0:T(8,128)(2,1)S(1)}, bf16[2,128,128]{2,1,0:T(8,128)(2,1)S(1)}, u32[]{:S(2)}, u32[]{:S(2)}) %collective-permute-start.8) | collective-permute-done | bytes 65568 | tf_op jit(solution)/shard_map/ppermute | solution.py:320
  121.1 1.3 shard_map.110
  122.4 10.0 %all_to_all.35.refs_0_ = bf16[8,112,128]{2,1,0:T(8,128)(2,1)S(1)} all-to-all(bf16[8,112,128]{2,1,0:T(8,128)(2,1)S(1)} %shard_map.110), channel_id=1, replica_groups=mesh['y'=4,'zh'=2,'zg'=2,'zl'=4,'x'=4,'c'=2] {'x','c'}, dimensions={0} | all-to-all | bytes 458752 | tf_op jit(solution)/shard_map/all_to_all | solution.py:57
  133.1 3.4 %all-to-all-start.6 = ((f32[4,112,128]{2,1,0:T(8,128)}), f32[4,112,128]{2,1,0:T(8,128)S(1)}, u32[]{:S(2)}, u32[]{:S(2)}) async-start(f32[4,112,128]{2,1,0:T(8,128)} %shard_map.111.refs_5_), calls=%async_computation.6 | async-start | bytes 458752 | tf_op jit(solution)/shard_map/all_to_all | solution.py:57
  136.5 2.1 %shard_map.112 = (bf16[256,128]{1,0:T(8,128)(2,1)}, f32[8,128]{1,0:T(8,128)S(1)}) custom-call(s32[1]{0:T(128)} %bitcast.refs_1_.refs_0_, bf16[256,256]{1,0:T(8,128)(2,1)S(1)} %collective-permute-done.2.refs_4_.refs_1_, bf16[256,256]{1,0:T(8,128)(2,1)S(1)} %collective-permute-done.3.refs_5_.refs_2_, bf16[256,256]{1,0:T(8,128)(2,1)S(1)} %get-tuple-element.16.refs_3_, ...), custom_call_target="tpu_custom_call" | custom-call | flops 452984832 | bytes 2392068 | tf_op jit(solution)/shard_map/pallas_call | solution.py:33
  138.7 3.2 %all-to-all-done.6.refs_0_ = f32[4,112,128]{2,1,0:T(8,128)S(1)} async-done(((f32[4,112,128]{2,1,0:T(8,128)}), f32[4,112,128]{2,1,0:T(8,128)S(1)}, u32[]{:S(2)}, u32[]{:S(2)}) %all-to-all-start.6) | async-done | bytes 229408 | tf_op jit(solution)/shard_map/all_to_all | solution.py:57
  (27 shorter events, 4.7 us)
Async XLA Ops:
  0.6 11.3 %collective-permute-start.1 = (bf16[256,128]{1,0:T(8,128)(2,1)}, bf16[256,128]{1,0:T(8,128)(2,1)S(1)}, u32[]{:S(2)}, u32[]{:S(2)}) collective-permute-start(bf16[256,128]{1,0:T(8,128)(2,1)} %bitcast.15), channel_id=1, source_target_pairs={{1,2},{3,4},{5,6},{7,8},{9,10},{11,12},{13,14},{15,16},{17,18},{19... | collective-permute-start | bytes 196616 | tf_op jit(solution)/shard_map/ppermute | solution.py:311
  5.1 6.8 %collective-permute-start = (bf16[256,128]{1,0:T(8,128)(2,1)}, bf16[256,128]{1,0:T(8,128)(2,1)S(1)}, u32[]{:S(2)}, u32[]{:S(2)}) collective-permute-start(bf16[256,128]{1,0:T(8,128)(2,1)} %bitcast.16), channel_id=1, source_target_pairs={{0,1},{1,0},{2,3},{3,2},{4,5},{5,4},{6,7},{7,6},{8,9},{9,8},{10,11... | collective-permute-start | bytes 196616 | tf_op jit(solution)/shard_map/ppermute | solution.py:309
  10.1 0.8 copy-start.7
  10.9 0.7 copy-start.8
  11.6 1.5 %copy-start = (bf16[3456,256]{1,0:T(8,128)(2,1)S(1)}, bf16[3456,256]{1,0:T(8,128)(2,1)}, u32[]{:S(2)}) copy-start(bf16[3456,256]{1,0:T(8,128)(2,1)} %refs_4_.1) | copy-start | bytes 5308420
  11.6 1.5 %copy-start.2 = (bf16[1,1,16,16,256]{4,3,2,1,0:T(8,128)(2,1)S(1)}, bf16[1,1,16,16,256]{4,3,2,1,0:T(8,128)(2,1)}, u32[]{:S(2)}) copy-start(bf16[1,1,16,16,256]{4,3,2,1,0:T(8,128)(2,1)} %param.12) | copy-start | bytes 393220
  11.6 1.5 %copy-start.3 = (bf16[1,1,16,16,128]{4,3,2,1,0:T(8,128)(2,1)S(1)}, bf16[1,1,16,16,128]{4,3,2,1,0:T(8,128)(2,1)}, u32[]{:S(2)}) copy-start(bf16[1,1,16,16,128]{4,3,2,1,0:T(8,128)(2,1)} %param.9) | copy-start | bytes 196612
  11.6 1.5 %copy-start.4 = (f32[256]{0:T(256)S(1)}, f32[256]{0:T(256)}, u32[]{:S(2)}) copy-start(f32[256]{0:T(256)} %param.11) | copy-start | bytes 3076
  14.8 15.8 %all-to-all-start = ((bf16[8,384,128]{2,1,0:T(8,128)(2,1)}), bf16[8,384,128]{2,1,0:T(8,128)(2,1)S(1)}, u32[]{:S(2)}, u32[]{:S(2)}) async-start(bf16[8,384,128]{2,1,0:T(8,128)(2,1)} %get-tuple-element.17), calls=%async_computation | async-start | bytes 1572864 | tf_op jit(solution)/shard_map/all_to_all | solution.py:57
  18.3 4.7 %collective-permute-start.4 = (bf16[2,64,128]{2,1,0:T(8,128)(2,1)S(1)}, bf16[2,64,128]{2,1,0:T(8,128)(2,1)S(1)}, u32[]{:S(2)}, u32[]{:S(2)}) collective-permute-start(bf16[2,64,128]{2,1,0:T(8,128)(2,1)S(1)} %get-tuple-element.18), channel_id=1, source_target_pairs={{0,0},{8,128},{16,256},{24,384},{128,8},{136,136},{144,264},{152,3... | collective-permute-start | bytes 98312 | tf_op jit(solution)/shard_map/ppermute | solution.py:316
  19.0 62.1 %copy-start.6 = (s32[8]{0:T(128)S(1)}, s32[8]{0:T(128)}, u32[]{:S(2)}) copy-start(s32[8]{0:T(128)} %refs_0_.1) | copy-start | bytes 100
  19.0 5.9 %collective-permute-start.5 = (bf16[2,64,128]{2,1,0:T(8,128)(2,1)S(1)}, bf16[2,64,128]{2,1,0:T(8,128)(2,1)S(1)}, u32[]{:S(2)}, u32[]{:S(2)}) collective-permute-start(bf16[2,64,128]{2,1,0:T(8,128)(2,1)S(1)} %get-tuple-element.19), channel_id=1, source_target_pairs={{0,8},{8,136},{16,264},{24,392},{128,0},{136,128},{144,256},{152,3... | collective-permute-start | bytes 98312 | tf_op jit(solution)/shard_map/ppermute | solution.py:316
  32.7 18.0 %all-to-all-start.1 = ((bf16[16,64,128]{2,1,0:T(8,128)(2,1)}), bf16[16,64,128]{2,1,0:T(8,128)(2,1)S(1)}, u32[]{:S(2)}, u32[]{:S(2)}) async-start(bf16[16,64,128]{2,1,0:T(8,128)(2,1)} %get-tuple-element.20), calls=%async_computation.1 | async-start | bytes 524288 | tf_op jit(solution)/shard_map/all_to_all | solution.py:57
  40.7 9.7 %collective-permute-start.6 = (bf16[2,64,128]{2,1,0:T(8,128)(2,1)S(1)}, bf16[2,64,128]{2,1,0:T(8,128)(2,1)S(1)}, u32[]{:S(2)}, u32[]{:S(2)}) collective-permute-start(bf16[2,64,128]{2,1,0:T(8,128)(2,1)S(1)} %get-tuple-element.21), channel_id=1, source_target_pairs={{0,16},{8,24},{16,0},{24,8},{1,17},{9,25},{17,1},{25,9},{2,18},{10... | collective-permute-start | bytes 98312 | tf_op jit(solution)/shard_map/ppermute | solution.py:320
  51.5 69.6 %copy-start.1 = (f32[256,256]{1,0:T(8,128)S(1)}, f32[256,256]{1,0:T(8,128)}, u32[]{:S(2)}) copy-start(f32[256,256]{1,0:T(8,128)} %refs_5_.1) | copy-start | bytes 786436
  51.5 69.6 %copy-start.5 = (f32[256]{0:T(256)S(1)}, f32[256]{0:T(256)}, u32[]{:S(2)}) copy-start(f32[256]{0:T(256)} %param.17) | copy-start | bytes 3076
  51.5 29.6 %all-to-all-start.2 = ((bf16[4,320,128]{2,1,0:T(8,128)(2,1)}), bf16[4,320,128]{2,1,0:T(8,128)(2,1)S(1)}, u32[]{:S(2)}, u32[]{:S(2)}) async-start(bf16[4,320,128]{2,1,0:T(8,128)(2,1)} %shard_map.107), calls=%async_computation.2 | async-start | bytes 655360 | tf_op jit(solution)/shard_map/all_to_all | solution.py:57
  62.7 8.4 %collective-permute-start.3 = (bf16[256,256]{1,0:T(8,128)(2,1)S(1)}, bf16[256,256]{1,0:T(8,128)(2,1)S(1)}, u32[]{:S(2)}, u32[]{:S(2)}) collective-permute-start(bf16[256,256]{1,0:T(8,128)(2,1)S(1)} %get-tuple-element.16.refs_3_), channel_id=1, source_target_pairs={{1,2},{3,4},{5,6},{7,8},{9,10},{11,12},{13,14},{15,16},{17,18},{19... | collective-permute-start | bytes 393224 | tf_op jit(solution)/shard_map/ppermute | solution.py:311
  68.4 3.2 %collective-permute-start.2 = (bf16[256,256]{1,0:T(8,128)(2,1)S(1)}, bf16[256,256]{1,0:T(8,128)(2,1)S(1)}, u32[]{:S(2)}, u32[]{:S(2)}) collective-permute-start(bf16[256,256]{1,0:T(8,128)(2,1)S(1)} %get-tuple-element.16.refs_3_), channel_id=1, source_target_pairs={{0,1},{1,0},{2,3},{3,2},{4,5},{5,4},{6,7},{7,6},{8,9},{9,8},{10,11... | collective-permute-start | bytes 393224 | tf_op jit(solution)/shard_map/ppermute | solution.py:309
  82.5 23.2 %all-to-all-start.3 = ((bf16[32,64,128]{2,1,0:T(8,128)(2,1)}), bf16[32,64,128]{2,1,0:T(8,128)(2,1)S(1)}, u32[]{:S(2)}, u32[]{:S(2)}) async-start(bf16[32,64,128]{2,1,0:T(8,128)(2,1)} %get-tuple-element.22), calls=%async_computation.3 | async-start | bytes 1048576 | tf_op jit(solution)/shard_map/all_to_all | solution.py:57
  94.1 5.4 %collective-permute-start.7 = (bf16[2,128,128]{2,1,0:T(8,128)(2,1)S(1)}, bf16[2,128,128]{2,1,0:T(8,128)(2,1)S(1)}, u32[]{:S(2)}, u32[]{:S(2)}) collective-permute-start(bf16[2,128,128]{2,1,0:T(8,128)(2,1)S(1)} %get-tuple-element.25), channel_id=1, source_target_pairs={{0,8},{8,0},{16,24},{24,16},{1,9},{9,1},{17,25},{25,17},{2,10},{10... | collective-permute-start | bytes 196616 | tf_op jit(solution)/shard_map/ppermute | solution.py:320
  107.1 14.0 %all-to-all-start.4 = ((bf16[4,224,128]{2,1,0:T(8,128)(2,1)}), bf16[4,224,128]{2,1,0:T(8,128)(2,1)S(1)}, u32[]{:S(2)}, u32[]{:S(2)}) async-start(bf16[4,224,128]{2,1,0:T(8,128)(2,1)} %get-tuple-element.26), calls=%async_computation.4 | async-start | bytes 458752 | tf_op jit(solution)/shard_map/all_to_all | solution.py:57
  110.5 10.6 %collective-permute-start.8 = (bf16[2,128,128]{2,1,0:T(8,128)(2,1)S(1)}, bf16[2,128,128]{2,1,0:T(8,128)(2,1)S(1)}, u32[]{:S(2)}, u32[]{:S(2)}) collective-permute-start(bf16[2,128,128]{2,1,0:T(8,128)(2,1)S(1)} %get-tuple-element.27), channel_id=1, source_target_pairs={{0,16},{8,24},{16,0},{24,8},{1,17},{9,25},{17,1},{25,9},{2,18},{10... | collective-permute-start | bytes 196616 | tf_op jit(solution)/shard_map/ppermute | solution.py:320
  133.1 8.7 %all-to-all-start.6 = ((f32[4,112,128]{2,1,0:T(8,128)}), f32[4,112,128]{2,1,0:T(8,128)S(1)}, u32[]{:S(2)}, u32[]{:S(2)}) async-start(f32[4,112,128]{2,1,0:T(8,128)} %shard_map.111.refs_5_), calls=%async_computation.6 | async-start | bytes 458752 | tf_op jit(solution)/shard_map/all_to_all | solution.py:57

commit v11 on v10

--- a/solution.py
+++ b/solution.py
@@ -92,20 +92,21 @@
         out_ref[r] = block.astype(BF16)
 
 
-def by_side(core_ref, inside_ref, outside_ref, planes):
-    second = core_ref[0]
+def by_side(inside_ref, outside_ref, planes):
+    second = lax.axis_index("c")
     planes[2 - 2 * second] = inside_ref[...]
     planes[2 * second] = outside_ref[...]
 
 
 def forward_body(
-    y_ref, core_ref, inner_ref, inside_ref, outside_ref, mine, weight, bias, cot, basis_ref,
+    inside_ref, outside_ref, mine, weight, bias, cot, basis_ref,
     delta_ref, send_ref, even_ref, odd_ref, patches, planes,
 ):
-    for k, ref in enumerate((even_ref, odd_ref)):
-        ref[0] = basis_ref[y_ref[0] ^ k]
-        ref[1] = basis_ref[y_ref[0] ^ k ^ 2]
-    by_side(core_ref, inside_ref, outside_ref, planes)
+    y = lax.axis_index("y")
+    for k, ref in ((0, even_ref), (2, odd_ref)):
+        ref[0] = basis_ref[y ^ k]
+        ref[1] = basis_ref[y ^ k ^ 1]
+    by_side(inside_ref, outside_ref, planes)
     planes[1] = mine[...]
     none = jnp.zeros((16, 128), BF16)
     for a in range(3):
@@ -126,7 +127,7 @@
     delta = (cot[...].astype(F32) * logistic * (1.0 + pre * (1.0 - logistic))).astype(BF16)
     delta_ref[...] = delta
     act_t = mine[...].astype(F32).T.astype(BF16)
-    rim_t = planes[2 * (inner_ref[0] >> 2)].astype(F32).T.astype(BF16)
+    rim_t = planes[2 * (lax.axis_index("x") >> 1)].astype(F32).T.astype(BF16)
     for x in range(4):
         for c in range(2):
             to = 2 * x + c
@@ -138,7 +139,7 @@
             send_ref[to, 128:] = delta[:, 128 * c : 128 * c + 128]
 
 
-def weight_grad_body(got_ref, even_ref, odd_ref, out_ref, pair_ref, moved, deltas, whole):
+def weight_grad_body(got_ref, out_ref, moved, deltas, whole):
     pieces = []
     for plane, at in [(0, 64)] + [(e, 0) for e in range(8)] + [(7, 64)]:
         pieces.append(got_ref[plane, at : at + 32].astype(F32))
@@ -159,8 +160,6 @@
         whole[288 * a : 288 * a + 288, :] = jnp.dot(
             moved[:, 256 * a : 256 * a + 2048], deltas[...], preferred_element_type=F32
         )
-    pair_ref[0] = even_ref[1]
-    pair_ref[1] = odd_ref[1]
     none = jnp.zeros((5, 128), F32)
     for y_to in range(4):
         for z_to in range(4):
@@ -171,27 +170,43 @@
             out_ref[4 * y_to + z_to] = jnp.concatenate(parts, axis=0).astype(BF16)
 
 
-def over_y_zl_body(zl_ref, got_ref, even_ref, odd_ref, pair_ref, out_ref):
-    total = (sum(got_ref[i].astype(F32) for i in range(16)) * (1.0 / CELLS)).astype(BF16)
+def pair_body(even_ref, odd_ref, out_ref):
+    out_ref[0] = even_ref[1]
+    out_ref[1] = odd_ref[1]
+
+
+def over_y_zl_body(got_ref, even_ref, odd_ref, pair_ref, out_ref, slices, rows):
+    total = sum(got_ref[i].astype(F32) for i in range(16)) * (1.0 / CELLS)
+    zl = lax.axis_index("zl")
+    for k, block in ((0, even_ref[0]), (2, odd_ref[0]), (1, pair_ref[0]), (3, pair_ref[1])):
+        slices[zl ^ k] = block
+    rows[:27, :] = total[:27]
+    rows[27:54, :] = total[32:59]
+    for y in range(4):
+        rows[54 + 54 * y : 108 + 54 * y, :] = slices[y].astype(F32)[:54]
+    rows[270:, :] = jnp.zeros((2, 128), F32)
     for to in range(4):
-        out_ref[to, :64] = total
-    for k, ref in enumerate((even_ref.at[0], odd_ref.at[0], pair_ref.at[0], pair_ref.at[1])):
-        at = pl.multiple_of(64 + 64 * (zl_ref[0] ^ k), 64)
-        for to in range(4):
-            out_ref[to, pl.ds(at, 64)] = ref[...]
-
-
-def over_zh_zg_body(owner_ref, zg_ref, zl_ref, got_ref, out_ref, basis_ref, here_ref, next_ref):
-    total = sum(got_ref[i, :64].astype(F32) for i in range(4)).astype(BF16)
+        out_ref[to] = rows[...].astype(BF16)
+
+
+def over_zh_zg_body(owner_ref, got_ref, out_ref, basis_ref, here_ref, next_ref, rows, slices):
+    for i in range(4):
+        rows[i, :272, :] = got_ref[i].astype(F32)
+        rows[i, 272:, :] = jnp.zeros((8, 128), F32)
+        for y in range(4):
+            slices[i, y] = rows[i, 54 + 54 * y : 118 + 54 * y, :].astype(BF16)
+    total = (rows[0, :54, :] + rows[1, :54, :]) + (rows[2, :54, :] + rows[3, :54, :])
+    none = jnp.zeros((5, 128), F32)
+    total = jnp.concatenate([total[:27], none, total[27:], none], axis=0).astype(BF16)
     for to in range(32):
         out_ref[to] = total
     for j in range(8):
-        at = pl.multiple_of(64 + 64 * (owner_ref[j] >> 1), 64)
         for zg in range(2):
-            basis_ref[j, 64 * zg : 64 * zg + 64] = got_ref[2 * (owner_ref[j] & 1) + zg, pl.ds(at, 64)]
-    for k, ref in enumerate((here_ref, next_ref)):
-        ref[0] = basis_ref[4 * zg_ref[0] + (zl_ref[0] ^ k)]
-        ref[1] = basis_ref[4 * zg_ref[0] + (zl_ref[0] ^ k ^ 2)]
+            basis_ref[j, 64 * zg : 64 * zg + 64] = slices[2 * (owner_ref[j] & 1) + zg, owner_ref[j] >> 1]
+    zg, zl = lax.axis_index("zg"), lax.axis_index("zl")
+    for k, ref in ((0, here_ref), (2, next_ref)):
+        ref[0] = basis_ref[4 * zg + (zl ^ k)]
+        ref[1] = basis_ref[4 * zg + (zl ^ k ^ 1)]
 
 
 def rotate_body(got_ref, basis_ref, here_ref, next_ref, out_ref, pair_ref, grads, ordered):
@@ -220,11 +235,12 @@
 
 
 def update_body(
-    zl_ref, got_ref, here_ref, next_ref, pair_ref, out_basis_any, out_eigen_any,
+    got_ref, here_ref, next_ref, pair_ref, out_basis_any, out_eigen_any,
     out_ref, panel, out_basis, out_eigen, ordered, sems,
 ):
-    for k, ref in enumerate((here_ref.at[0], next_ref.at[0], pair_ref.at[0], pair_ref.at[1])):
-        panel[zl_ref[0] ^ k] = ref[...]
+    zl = lax.axis_index("zl")
+    for k, block in ((0, here_ref[0]), (2, next_ref[0]), (1, pair_ref[0]), (3, pair_ref[1])):
+        panel[zl ^ k] = block
     copies = [
         pltpu.make_async_copy(out_basis_any, out_basis, sems.at[0]),
         pltpu.make_async_copy(out_eigen_any, out_eigen, sems.at[1]),
@@ -274,10 +290,10 @@
     out_ref[...] = jnp.concatenate([total[:54], total[56:110]], axis=1)
 
 
-def data_grad_body(core_ref, inside_ref, outside_ref, mine_ref, weight_any, out_ref, token_ref, weight, planes, sem):
+def data_grad_body(inside_ref, outside_ref, mine_ref, weight_any, out_ref, token_ref, weight, planes, sem):
     copy = pltpu.make_async_copy(weight_any, weight, sem)
     copy.start()
-    by_side(core_ref, inside_ref, outside_ref, planes)
+    by_side(inside_ref, outside_ref, planes)
     planes[1] = mine_ref[...]
     none = jnp.zeros((16, 256), BF16)
     total = jnp.zeros((256, 128), F32)
@@ -332,7 +348,6 @@
     output_eigen,
 ):
     dma = pltpu.SemaphoreType.DMA
-    y, zg, zl, core, inner = (lax.axis_index(a).astype(jnp.int32).reshape(1) for a in ("y", "zg", "zl", "c", XC))
     plane = activations.reshape(256, 128)
     inside, outside = neighbours(plane)
 
@@ -347,34 +362,37 @@
     delta, send, even, odd = call(
         forward_body,
         [shape((256, 256), BF16), shape((8, 384, 128), BF16)] + [shape((2, 64, 128), BF16)] * 2,
-        (y, core, inner),
+        (),
         (inside, outside, plane, conv_weight, conv_bias.reshape(1, 256), cotangent.reshape(256, 256), stored),
         scratch=[pltpu.VMEM((256, 3456), BF16), pltpu.VMEM((3, 256, 128), BF16)],
         flops=2 * 256 * 3456 * 256,
     )
-    even, odd = turned(even, 0), turned(odd, 1)
-    part, pair = call(
+    even, odd = turned(even, 0), turned(odd, 2)
+    part = call(
         weight_grad_body,
-        [shape((16, 64, 128), BF16), shape((2, 64, 128), BF16)],
-        arrays=(exchange(send, XC), even, odd),
+        shape((16, 64, 128), BF16),
+        arrays=(exchange(send, XC),),
+        after=(even,),
         scratch=[pltpu.VMEM((288, 2560), BF16), pltpu.VMEM((2048, 128), BF16), pltpu.VMEM((864, 128), F32)],
         flops=2 * 864 * 2048 * 128,
     )
+    pair = call(pair_body, shape((2, 64, 128), BF16), arrays=(even, odd), after=(part,))
     part = call(
         over_y_zl_body,
-        shape((4, 320, 128), BF16),
-        (zl,),
-        (exchange(part, ("y", "zl")), even, odd, across(pair, 2)),
+        shape((4, 272, 128), BF16),
+        arrays=(exchange(part, ("y", "zl")), even, odd, across(pair, 1)),
+        scratch=[pltpu.VMEM((4, 64, 128), BF16), pltpu.VMEM((272, 128), F32)],
     )
     inside, outside = neighbours(delta)
     part, basis, here, there = call(
         over_zh_zg_body,
         [shape((32, 64, 128), BF16), shape((8, 128, 128), BF16)] + [shape((2, 128, 128), BF16)] * 2,
-        (panel_owner, zg, zl),
+        (panel_owner,),
         (exchange(part, ("zh", "zg")),),
         after=(inside, outside),
-    )
-    there = across(there, 1)
+        scratch=[pltpu.VMEM((4, 280, 128), F32), pltpu.VMEM((4, 4, 64, 128), BF16)],
+    )
+    there = across(there, 2)
     rotated, pair = call(
         rotate_body,
         [shape((4, 224, 128), BF16), shape((2, 128, 128), BF16)],
@@ -384,8 +402,8 @@
     part = call(
         update_body,
         shape((8, 112, 128), BF16),
-        (zl,),
-        (exchange(rotated, "zl"), here, there, across(pair, 2)),
+        (),
+        (exchange(rotated, "zl"), here, there, across(pair, 1)),
         (output_basis, output_eigen.reshape(1, 256)),
         scratch=[
             pltpu.VMEM((4, 128, 128), BF16),
@@ -399,7 +417,7 @@
     data, token = call(
         data_grad_body,
         [shape((256, 128), BF16), shape((8, 128), F32)],
-        (core,),
+        (),
         (inside, outside, delta),
         (conv_weight,),
         after=(part,),

time: 143 us -> 141 us (0.986)
  waiting for transfers between devices: 43.4 us -> 37.7 us
  starting transfers between devices: 73 us -> 76.8 us
    ppermute x3, waiting for transfers between devices: 15.3 us -> 9.63 us  [across(): return lax.ppermute(block, 'zl', [(i, i ^ k) for i in range(4)])]
    all_to_all x6, starting transfers between devices: 41 us -> 44.3 us  [exchange(): return lax.all_to_all(x, axes, 0, 0)]
    pallas_call x10 -> x11, Pallas kernels: 12.6 us -> 12.7 us  [call(): pl.pallas_call(kernel, out_shape=out_shape, in_specs=[SMEM] * len(scalars...]
  transfers between devices with their start and end apart: 15 -> 15, of which waited for: 11 -> 10; matrix products, arithmetic and copies ran while one was open for 0% -> 0% of each run, Pallas kernels for 2% -> 2%
where the time goes in v11:
time: 141 us; the launch traced here: 140 us
  starting transfers between devices  76.8 us (54%)
  waiting for transfers between devices  37.7 us (27%)
  Pallas kernels  12.7 us (9%)
  blocking collectives  9.64 us (7%)
  local copies, waits for them, and re-layouts  2.62 us (2%)
    all_to_all x6, starting transfers between devices, exchange(): return lax.all_to_all(x, axes, 0, 0)  44.3 us
    all_to_all x6, waiting for transfers between devices, exchange(): return lax.all_to_all(x, axes, 0, 0)  24.1 us
    pallas_call x11, Pallas kernels, call(): pl.pallas_call(kernel, out_shape=out_shape, in_specs=[SMEM] * len(scalars...  12.7 us
    ppermute x3, starting transfers between devices, across(): return lax.ppermute(block, 'zl', [(i, i ^ k) for i in range(4)])  11.4 us
    all_to_all x1, blocking collectives, exchange(): return lax.all_to_all(x, axes, 0, 0)  9.64 us
    ppermute x3, waiting for transfers between devices, across(): return lax.ppermute(block, 'zl', [(i, i ^ k) for i in range(4)])  9.63 us
    ppermute x2, starting transfers between devices, neighbours(): lax.ppermute(block, SPACE, pairs + [(j, i) for i, j in pairs])  9.36 us
    ppermute x2, starting transfers between devices, neighbours(): inside = lax.ppermute(block, 'c', [(0, 1), (1, 0)])  6.86 us
  transfers between devices with their start and end apart: 15, of which 10 were waited for; matrix products, arithmetic and copies ran while one was open for 0% of the time, Pallas kernels for 2%

profile of v11, /device:TPU:1, one launch (start us, length us, event | category | flops | bytes accessed | tf_op | source)
XLA Modules:
  0.0 140.2 jit_solution(13718395985391319078)
XLA Ops:
  0.6 4.5 %collective-permute-start.1 = (bf16[256,128]{1,0:T(8,128)(2,1)}, bf16[256,128]{1,0:T(8,128)(2,1)S(1)}, u32[]{:S(2)}, u32[]{:S(2)}) collective-permute-start(bf16[256,128]{1,0:T(8,128)(2,1)} %bitcast.10), channel_id=1, source_target_pairs={{1,2},{3,4},{5,6},{7,8},{9,10},{11,12},{13,14},{15,16},{17,18},{19... | collective-permute-start | bytes 196616 | tf_op jit(solution)/shard_map/ppermute | solution.py:327
  5.1 4.9 %collective-permute-start = (bf16[256,128]{1,0:T(8,128)(2,1)}, bf16[256,128]{1,0:T(8,128)(2,1)S(1)}, u32[]{:S(2)}, u32[]{:S(2)}) collective-permute-start(bf16[256,128]{1,0:T(8,128)(2,1)} %bitcast.11), channel_id=1, source_target_pairs={{0,1},{1,0},{2,3},{3,2},{4,5},{5,4},{6,7},{7,6},{8,9},{9,8},{10,11... | collective-permute-start | bytes 196616 | tf_op jit(solution)/shard_map/ppermute | solution.py:325
  10.1 0.8 copy-done.7
  11.9 1.1 copy-done
  13.1 1.7 %shard_map.105 = (bf16[256,256]{1,0:T(8,128)(2,1)S(1)}, bf16[8,384,128]{2,1,0:T(8,128)(2,1)}, bf16[2,64,128]{2,1,0:T(8,128)(2,1)S(1)}, bf16[2,64,128]{2,1,0:T(8,128)(2,1)S(1)}) custom-call(bf16[256,128]{1,0:T(8,128)(2,1)S(1)} %collective-permute-done.refs_0_, bf16[256,128]{1,0:T(8,128)(2,1)S(1)} %collective-permute-done.1.refs_1_, ...), custom_call_target="tpu_custom_call" | custom-call | flops 452984832 | bytes 2163712 | tf_op jit(solution)/shard_map/pallas_call | solution.py:33
  14.8 3.5 %all-to-all-start = ((bf16[8,384,128]{2,1,0:T(8,128)(2,1)}), bf16[8,384,128]{2,1,0:T(8,128)(2,1)S(1)}, u32[]{:S(2)}, u32[]{:S(2)}) async-start(bf16[8,384,128]{2,1,0:T(8,128)(2,1)} %get-tuple-element.15), calls=%async_computation | async-start | bytes 1572864 | tf_op jit(solution)/shard_map/all_to_all | solution.py:57
  19.0 11.6 %all-to-all-done.refs_0_ = bf16[8,384,128]{2,1,0:T(8,128)(2,1)S(1)} async-done(((bf16[8,384,128]{2,1,0:T(8,128)(2,1)}), bf16[8,384,128]{2,1,0:T(8,128)(2,1)S(1)}, u32[]{:S(2)}, u32[]{:S(2)}) %all-to-all-start) | async-done | bytes 786464 | tf_op jit(solution)/shard_map/all_to_all | solution.py:57
  30.6 2.2 %shard_map.106.refs_2_ = bf16[16,64,128]{2,1,0:T(8,128)(2,1)} custom-call(bf16[8,384,128]{2,1,0:T(8,128)(2,1)S(1)} %all-to-all-done.refs_0_, bf16[2,64,128]{2,1,0:T(8,128)(2,1)S(1)} %collective-permute-done.4.refs_1_.refs_0_), custom_call_target="tpu_custom_call" | custom-call | flops 452984832 | bytes 819200 | tf_op jit(solution)/shard_map/pallas_call | solution.py:33
  32.7 7.9 %all-to-all-start.1 = ((bf16[16,64,128]{2,1,0:T(8,128)(2,1)}), bf16[16,64,128]{2,1,0:T(8,128)(2,1)S(1)}, u32[]{:S(2)}, u32[]{:S(2)}) async-start(bf16[16,64,128]{2,1,0:T(8,128)(2,1)} %shard_map.106.refs_2_), calls=%async_computation.1 | async-start | bytes 524288 | tf_op jit(solution)/shard_map/all_to_all | solution.py:57
  40.7 4.2 %collective-permute-start.5 = (bf16[2,64,128]{2,1,0:T(8,128)(2,1)S(1)}, bf16[2,64,128]{2,1,0:T(8,128)(2,1)S(1)}, u32[]{:S(2)}, u32[]{:S(2)}) collective-permute-start(bf16[2,64,128]{2,1,0:T(8,128)(2,1)S(1)} %get-tuple-element.17), channel_id=1, source_target_pairs={{0,16},{8,144},{16,272},{24,400},{128,24},{136,152},{144,280},{152... | collective-permute-start | bytes 98312 | tf_op jit(solution)/shard_map/ppermute | solution.py:332
  44.8 2.6 %collective-permute-done.5.refs_1_.refs_2_ = bf16[2,64,128]{2,1,0:T(8,128)(2,1)S(1)} collective-permute-done((bf16[2,64,128]{2,1,0:T(8,128)(2,1)S(1)}, bf16[2,64,128]{2,1,0:T(8,128)(2,1)S(1)}, u32[]{:S(2)}, u32[]{:S(2)}) %collective-permute-start.5) | collective-permute-done | bytes 32800 | tf_op jit(solution)/shard_map/ppermute | solution.py:332
  47.5 3.9 %collective-permute-start.6 = (bf16[2,64,128]{2,1,0:T(8,128)(2,1)S(1)}, bf16[2,64,128]{2,1,0:T(8,128)(2,1)S(1)}, u32[]{:S(2)}, u32[]{:S(2)}) collective-permute-start(bf16[2,64,128]{2,1,0:T(8,128)(2,1)S(1)} %shard_map.107), channel_id=1, source_target_pairs={{0,8},{8,0},{16,24},{24,16},{1,9},{9,1},{17,25},{25,17},{2,10},{10... | collective-permute-start | bytes 98312 | tf_op jit(solution)/shard_map/ppermute | solution.py:336
  51.4 1.6 %collective-permute-done.6.refs_3_ = bf16[2,64,128]{2,1,0:T(8,128)(2,1)S(1)} collective-permute-done((bf16[2,64,128]{2,1,0:T(8,128)(2,1)S(1)}, bf16[2,64,128]{2,1,0:T(8,128)(2,1)S(1)}, u32[]{:S(2)}, u32[]{:S(2)}) %collective-permute-start.6) | collective-permute-done | bytes 32800 | tf_op jit(solution)/shard_map/ppermute | solution.py:336
  53.0 0.8 shard_map.108
  53.7 11.2 %all-to-all-start.2 = ((bf16[4,272,128]{2,1,0:T(8,128)(2,1)}), bf16[4,272,128]{2,1,0:T(8,128)(2,1)S(1)}, u32[]{:S(2)}, u32[]{:S(2)}) async-start(bf16[4,272,128]{2,1,0:T(8,128)(2,1)} %shard_map.108), calls=%async_computation.2 | async-start | bytes 557056 | tf_op jit(solution)/shard_map/all_to_all | solution.py:57
  64.9 4.9 %collective-permute-start.3 = (bf16[256,256]{1,0:T(8,128)(2,1)S(1)}, bf16[256,256]{1,0:T(8,128)(2,1)S(1)}, u32[]{:S(2)}, u32[]{:S(2)}) collective-permute-start(bf16[256,256]{1,0:T(8,128)(2,1)S(1)} %get-tuple-element.14.refs_2_), channel_id=1, source_target_pairs={{1,2},{3,4},{5,6},{7,8},{9,10},{11,12},{13,14},{15,16},{17,18},{19... | collective-permute-start | bytes 393224 | tf_op jit(solution)/shard_map/ppermute | solution.py:327
  69.8 1.9 %collective-permute-start.2 = (bf16[256,256]{1,0:T(8,128)(2,1)S(1)}, bf16[256,256]{1,0:T(8,128)(2,1)S(1)}, u32[]{:S(2)}, u32[]{:S(2)}) collective-permute-start(bf16[256,256]{1,0:T(8,128)(2,1)S(1)} %get-tuple-element.14.refs_2_), channel_id=1, source_target_pairs={{0,1},{1,0},{2,3},{3,2},{4,5},{5,4},{6,7},{7,6},{8,9},{9,8},{10,11... | collective-permute-start | bytes 393224 | tf_op jit(solution)/shard_map/ppermute | solution.py:325
  73.0 5.1 %all-to-all-done.2.refs_1_ = bf16[4,272,128]{2,1,0:T(8,128)(2,1)S(1)} async-done(((bf16[4,272,128]{2,1,0:T(8,128)(2,1)}), bf16[4,272,128]{2,1,0:T(8,128)(2,1)S(1)}, u32[]{:S(2)}, u32[]{:S(2)}) %all-to-all-start.2) | async-done | bytes 278560 | tf_op jit(solution)/shard_map/all_to_all | solution.py:57
  78.1 1.5 %shard_map.109 = (bf16[32,64,128]{2,1,0:T(8,128)(2,1)}, bf16[8,128,128]{2,1,0:T(8,128)(2,1)S(1)}, bf16[2,128,128]{2,1,0:T(8,128)(2,1)S(1)}, bf16[2,128,128]{2,1,0:T(8,128)(2,1)S(1)}) custom-call(s32[8]{0:T(128)S(1)} %copy-done.6, bf16[4,272,128]{2,1,0:T(8,128)(2,1)S(1)} %all-to-all-done.2.refs_1_, ...), custom_call_target="tpu_custom_call" | custom-call | bytes 540704 | tf_op jit(solution)/shard_map/pallas_call | solution.py:33
  79.5 14.8 %all-to-all-start.3 = ((bf16[32,64,128]{2,1,0:T(8,128)(2,1)}), bf16[32,64,128]{2,1,0:T(8,128)(2,1)S(1)}, u32[]{:S(2)}, u32[]{:S(2)}) async-start(bf16[32,64,128]{2,1,0:T(8,128)(2,1)} %get-tuple-element.18), calls=%async_computation.3 | async-start | bytes 1048576 | tf_op jit(solution)/shard_map/all_to_all | solution.py:57
  94.4 4.2 %collective-permute-start.7 = (bf16[2,128,128]{2,1,0:T(8,128)(2,1)S(1)}, bf16[2,128,128]{2,1,0:T(8,128)(2,1)S(1)}, u32[]{:S(2)}, u32[]{:S(2)}) collective-permute-start(bf16[2,128,128]{2,1,0:T(8,128)(2,1)S(1)} %get-tuple-element.21), channel_id=1, source_target_pairs={{0,16},{8,24},{16,0},{24,8},{1,17},{9,25},{17,1},{25,9},{2,18},{10... | collective-permute-start | bytes 196616 | tf_op jit(solution)/shard_map/ppermute | solution.py:336
  98.5 3.1 %collective-permute-done.7.refs_3_.refs_2_ = bf16[2,128,128]{2,1,0:T(8,128)(2,1)S(1)} collective-permute-done((bf16[2,128,128]{2,1,0:T(8,128)(2,1)S(1)}, bf16[2,128,128]{2,1,0:T(8,128)(2,1)S(1)}, u32[]{:S(2)}, u32[]{:S(2)}) %collective-permute-start.7) | collective-permute-done | bytes 65568 | tf_op jit(solution)/shard_map/ppermute | solution.py:336
  101.6 4.3 %all-to-all-done.3.refs_0_ = bf16[32,64,128]{2,1,0:T(8,128)(2,1)S(1)} async-done(((bf16[32,64,128]{2,1,0:T(8,128)(2,1)}), bf16[32,64,128]{2,1,0:T(8,128)(2,1)S(1)}, u32[]{:S(2)}, u32[]{:S(2)}) %all-to-all-start.3) | async-done | bytes 524320 | tf_op jit(solution)/shard_map/all_to_all | solution.py:57
  105.9 1.4 %shard_map.110 = (bf16[4,224,128]{2,1,0:T(8,128)(2,1)}, bf16[2,128,128]{2,1,0:T(8,128)(2,1)S(1)}) custom-call(bf16[32,64,128]{2,1,0:T(8,128)(2,1)S(1)} %all-to-all-done.3.refs_0_, bf16[8,128,128]{2,1,0:T(8,128)(2,1)S(1)} %get-tuple-element.19.refs_1_, bf16[2,128,128]{2,1,0:T(8,128)(2,1)S(1)} %get-tuple-element.20.refs_2_.refs_1_, ...), custom_call_target="tpu_custom_call" | custom-call | bytes 917504 | tf_op jit(solution)/shard_map/pallas_call | solution.py:33
  107.3 3.5 %all-to-all-start.4 = ((bf16[4,224,128]{2,1,0:T(8,128)(2,1)}), bf16[4,224,128]{2,1,0:T(8,128)(2,1)S(1)}, u32[]{:S(2)}, u32[]{:S(2)}) async-start(bf16[4,224,128]{2,1,0:T(8,128)(2,1)} %get-tuple-element.22), calls=%async_computation.4 | async-start | bytes 458752 | tf_op jit(solution)/shard_map/all_to_all | solution.py:57
  110.8 3.4 %collective-permute-start.8 = (bf16[2,128,128]{2,1,0:T(8,128)(2,1)S(1)}, bf16[2,128,128]{2,1,0:T(8,128)(2,1)S(1)}, u32[]{:S(2)}, u32[]{:S(2)}) collective-permute-start(bf16[2,128,128]{2,1,0:T(8,128)(2,1)S(1)} %get-tuple-element.23), channel_id=1, source_target_pairs={{0,8},{8,0},{16,24},{24,16},{1,9},{9,1},{17,25},{25,17},{2,10},{10... | collective-permute-start | bytes 196616 | tf_op jit(solution)/shard_map/ppermute | solution.py:336
  114.2 4.9 %collective-permute-done.8.refs_3_ = bf16[2,128,128]{2,1,0:T(8,128)(2,1)S(1)} collective-permute-done((bf16[2,128,128]{2,1,0:T(8,128)(2,1)S(1)}, bf16[2,128,128]{2,1,0:T(8,128)(2,1)S(1)}, u32[]{:S(2)}, u32[]{:S(2)}) %collective-permute-start.8) | collective-permute-done | bytes 65568 | tf_op jit(solution)/shard_map/ppermute | solution.py:336
  119.2 1.3 shard_map.111
  120.5 9.6 %all_to_all.35.refs_0_ = bf16[8,112,128]{2,1,0:T(8,128)(2,1)S(1)} all-to-all(bf16[8,112,128]{2,1,0:T(8,128)(2,1)S(1)} %shard_map.111), channel_id=1, replica_groups=mesh['y'=4,'zh'=2,'zg'=2,'zl'=4,'x'=4,'c'=2] {'x','c'}, dimensions={0} | all-to-all | bytes 458752 | tf_op jit(solution)/shard_map/all_to_all | solution.py:57
  130.9 3.4 %all-to-all-start.6 = ((f32[4,112,128]{2,1,0:T(8,128)}), f32[4,112,128]{2,1,0:T(8,128)S(1)}, u32[]{:S(2)}, u32[]{:S(2)}) async-start(f32[4,112,128]{2,1,0:T(8,128)} %shard_map.112.refs_4_), calls=%async_computation.6 | async-start | bytes 458752 | tf_op jit(solution)/shard_map/all_to_all | solution.py:57
  134.2 2.1 %shard_map.113 = (bf16[256,128]{1,0:T(8,128)(2,1)}, f32[8,128]{1,0:T(8,128)S(1)}) custom-call(bf16[256,256]{1,0:T(8,128)(2,1)S(1)} %collective-permute-done.2.refs_2_.refs_0_, bf16[256,256]{1,0:T(8,128)(2,1)S(1)} %collective-permute-done.3.refs_3_.refs_1_, bf16[256,256]{1,0:T(8,128)(2,1)S(1)} %get-tuple-element.14.refs_2_, bf16[3456,256]{1,0:T(8,128)(2,1)S(1)} %copy-done, ...), custom_call_target="tpu_custom_call" | custom-call | flops 452984832 | bytes 2392064 | tf_op jit(solution)/shard_map/pallas_call | solution.py:33
  136.4 3.2 %all-to-all-done.6.refs_0_ = f32[4,112,128]{2,1,0:T(8,128)S(1)} async-done(((f32[4,112,128]{2,1,0:T(8,128)}), f32[4,112,128]{2,1,0:T(8,128)S(1)}, u32[]{:S(2)}, u32[]{:S(2)}) %all-to-all-start.6) | async-done | bytes 229408 | tf_op jit(solution)/shard_map/all_to_all | solution.py:57
  (28 shorter events, 4.3 us)
Async XLA Ops:
  0.6 11.3 %collective-permute-start.1 = (bf16[256,128]{1,0:T(8,128)(2,1)}, bf16[256,128]{1,0:T(8,128)(2,1)S(1)}, u32[]{:S(2)}, u32[]{:S(2)}) collective-permute-start(bf16[256,128]{1,0:T(8,128)(2,1)} %bitcast.10), channel_id=1, source_target_pairs={{1,2},{3,4},{5,6},{7,8},{9,10},{11,12},{13,14},{15,16},{17,18},{19... | collective-permute-start | bytes 196616 | tf_op jit(solution)/shard_map/ppermute | solution.py:327
  5.1 6.8 %collective-permute-start = (bf16[256,128]{1,0:T(8,128)(2,1)}, bf16[256,128]{1,0:T(8,128)(2,1)S(1)}, u32[]{:S(2)}, u32[]{:S(2)}) collective-permute-start(bf16[256,128]{1,0:T(8,128)(2,1)} %bitcast.11), channel_id=1, source_target_pairs={{0,1},{1,0},{2,3},{3,2},{4,5},{5,4},{6,7},{7,6},{8,9},{9,8},{10,11... | collective-permute-start | bytes 196616 | tf_op jit(solution)/shard_map/ppermute | solution.py:325
  10.1 0.8 copy-start.7
  10.9 0.7 copy-start.8
  11.6 1.5 %copy-start = (bf16[3456,256]{1,0:T(8,128)(2,1)S(1)}, bf16[3456,256]{1,0:T(8,128)(2,1)}, u32[]{:S(2)}) copy-start(bf16[3456,256]{1,0:T(8,128)(2,1)} %refs_3_.3) | copy-start | bytes 5308420
  11.6 1.5 %copy-start.2 = (bf16[1,1,16,16,256]{4,3,2,1,0:T(8,128)(2,1)S(1)}, bf16[1,1,16,16,256]{4,3,2,1,0:T(8,128)(2,1)}, u32[]{:S(2)}) copy-start(bf16[1,1,16,16,256]{4,3,2,1,0:T(8,128)(2,1)} %param.12) | copy-start | bytes 393220
  11.6 1.5 %copy-start.3 = (bf16[1,1,16,16,128]{4,3,2,1,0:T(8,128)(2,1)S(1)}, bf16[1,1,16,16,128]{4,3,2,1,0:T(8,128)(2,1)}, u32[]{:S(2)}) copy-start(bf16[1,1,16,16,128]{4,3,2,1,0:T(8,128)(2,1)} %param.9) | copy-start | bytes 196612
  11.6 1.5 %copy-start.4 = (f32[256]{0:T(256)S(1)}, f32[256]{0:T(256)}, u32[]{:S(2)}) copy-start(f32[256]{0:T(256)} %param.11) | copy-start | bytes 3076
  14.8 15.8 %all-to-all-start = ((bf16[8,384,128]{2,1,0:T(8,128)(2,1)}), bf16[8,384,128]{2,1,0:T(8,128)(2,1)S(1)}, u32[]{:S(2)}, u32[]{:S(2)}) async-start(bf16[8,384,128]{2,1,0:T(8,128)(2,1)} %get-tuple-element.15), calls=%async_computation | async-start | bytes 1572864 | tf_op jit(solution)/shard_map/all_to_all | solution.py:57
  18.3 59.8 %copy-start.6 = (s32[8]{0:T(128)S(1)}, s32[8]{0:T(128)}, u32[]{:S(2)}) copy-start(s32[8]{0:T(128)} %refs_0_.1) | copy-start | bytes 100
  18.3 0.7 collective-permute-start.4
  32.7 20.2 %all-to-all-start.1 = ((bf16[16,64,128]{2,1,0:T(8,128)(2,1)}), bf16[16,64,128]{2,1,0:T(8,128)(2,1)S(1)}, u32[]{:S(2)}, u32[]{:S(2)}) async-start(bf16[16,64,128]{2,1,0:T(8,128)(2,1)} %shard_map.106.refs_2_), calls=%async_computation.1 | async-start | bytes 524288 | tf_op jit(solution)/shard_map/all_to_all | solution.py:57
  40.7 6.8 %collective-permute-start.5 = (bf16[2,64,128]{2,1,0:T(8,128)(2,1)S(1)}, bf16[2,64,128]{2,1,0:T(8,128)(2,1)S(1)}, u32[]{:S(2)}, u32[]{:S(2)}) collective-permute-start(bf16[2,64,128]{2,1,0:T(8,128)(2,1)S(1)} %get-tuple-element.17), channel_id=1, source_target_pairs={{0,16},{8,144},{16,272},{24,400},{128,24},{136,152},{144,280},{152... | collective-permute-start | bytes 98312 | tf_op jit(solution)/shard_map/ppermute | solution.py:332
  47.5 5.5 %collective-permute-start.6 = (bf16[2,64,128]{2,1,0:T(8,128)(2,1)S(1)}, bf16[2,64,128]{2,1,0:T(8,128)(2,1)S(1)}, u32[]{:S(2)}, u32[]{:S(2)}) collective-permute-start(bf16[2,64,128]{2,1,0:T(8,128)(2,1)S(1)} %shard_map.107), channel_id=1, source_target_pairs={{0,8},{8,0},{16,24},{24,16},{1,9},{9,1},{17,25},{25,17},{2,10},{10... | collective-permute-start | bytes 98312 | tf_op jit(solution)/shard_map/ppermute | solution.py:336
  53.7 65.4 %copy-start.1 = (f32[256,256]{1,0:T(8,128)S(1)}, f32[256,256]{1,0:T(8,128)}, u32[]{:S(2)}) copy-start(f32[256,256]{1,0:T(8,128)} %refs_4_.1) | copy-start | bytes 786436
  53.7 65.4 %copy-start.5 = (f32[256]{0:T(256)S(1)}, f32[256]{0:T(256)}, u32[]{:S(2)}) copy-start(f32[256]{0:T(256)} %param.17) | copy-start | bytes 3076
  53.7 24.3 %all-to-all-start.2 = ((bf16[4,272,128]{2,1,0:T(8,128)(2,1)}), bf16[4,272,128]{2,1,0:T(8,128)(2,1)S(1)}, u32[]{:S(2)}, u32[]{:S(2)}) async-start(bf16[4,272,128]{2,1,0:T(8,128)(2,1)} %shard_map.108), calls=%async_computation.2 | async-start | bytes 557056 | tf_op jit(solution)/shard_map/all_to_all | solution.py:57
  64.9 7.5 %collective-permute-start.3 = (bf16[256,256]{1,0:T(8,128)(2,1)S(1)}, bf16[256,256]{1,0:T(8,128)(2,1)S(1)}, u32[]{:S(2)}, u32[]{:S(2)}) collective-permute-start(bf16[256,256]{1,0:T(8,128)(2,1)S(1)} %get-tuple-element.14.refs_2_), channel_id=1, source_target_pairs={{1,2},{3,4},{5,6},{7,8},{9,10},{11,12},{13,14},{15,16},{17,18},{19... | collective-permute-start | bytes 393224 | tf_op jit(solution)/shard_map/ppermute | solution.py:327
  69.8 3.2 %collective-permute-start.2 = (bf16[256,256]{1,0:T(8,128)(2,1)S(1)}, bf16[256,256]{1,0:T(8,128)(2,1)S(1)}, u32[]{:S(2)}, u32[]{:S(2)}) collective-permute-start(bf16[256,256]{1,0:T(8,128)(2,1)S(1)} %get-tuple-element.14.refs_2_), channel_id=1, source_target_pairs={{0,1},{1,0},{2,3},{3,2},{4,5},{5,4},{6,7},{7,6},{8,9},{9,8},{10,11... | collective-permute-start | bytes 393224 | tf_op jit(solution)/shard_map/ppermute | solution.py:325
  79.5 26.4 %all-to-all-start.3 = ((bf16[32,64,128]{2,1,0:T(8,128)(2,1)}), bf16[32,64,128]{2,1,0:T(8,128)(2,1)S(1)}, u32[]{:S(2)}, u32[]{:S(2)}) async-start(bf16[32,64,128]{2,1,0:T(8,128)(2,1)} %get-tuple-element.18), calls=%async_computation.3 | async-start | bytes 1048576 | tf_op jit(solution)/shard_map/all_to_all | solution.py:57
  94.4 7.3 %collective-permute-start.7 = (bf16[2,128,128]{2,1,0:T(8,128)(2,1)S(1)}, bf16[2,128,128]{2,1,0:T(8,128)(2,1)S(1)}, u32[]{:S(2)}, u32[]{:S(2)}) collective-permute-start(bf16[2,128,128]{2,1,0:T(8,128)(2,1)S(1)} %get-tuple-element.21), channel_id=1, source_target_pairs={{0,16},{8,24},{16,0},{24,8},{1,17},{9,25},{17,1},{25,9},{2,18},{10... | collective-permute-start | bytes 196616 | tf_op jit(solution)/shard_map/ppermute | solution.py:336
  107.3 11.8 %all-to-all-start.4 = ((bf16[4,224,128]{2,1,0:T(8,128)(2,1)}), bf16[4,224,128]{2,1,0:T(8,128)(2,1)S(1)}, u32[]{:S(2)}, u32[]{:S(2)}) async-start(bf16[4,224,128]{2,1,0:T(8,128)(2,1)} %get-tuple-element.22), calls=%async_computation.4 | async-start | bytes 458752 | tf_op jit(solution)/shard_map/all_to_all | solution.py:57
  110.8 8.3 %collective-permute-start.8 = (bf16[2,128,128]{2,1,0:T(8,128)(2,1)S(1)}, bf16[2,128,128]{2,1,0:T(8,128)(2,1)S(1)}, u32[]{:S(2)}, u32[]{:S(2)}) collective-permute-start(bf16[2,128,128]{2,1,0:T(8,128)(2,1)S(1)} %get-tuple-element.23), channel_id=1, source_target_pairs={{0,8},{8,0},{16,24},{24,16},{1,9},{9,1},{17,25},{25,17},{2,10},{10... | collective-permute-start | bytes 196616 | tf_op jit(solution)/shard_map/ppermute | solution.py:336
  130.9 8.7 %all-to-all-start.6 = ((f32[4,112,128]{2,1,0:T(8,128)}), f32[4,112,128]{2,1,0:T(8,128)S(1)}, u32[]{:S(2)}, u32[]{:S(2)}) async-start(f32[4,112,128]{2,1,0:T(8,128)} %shard_map.112.refs_4_), calls=%async_computation.6 | async-start | bytes 458752 | tf_op jit(solution)/shard_map/all_to_all | solution.py:57

commit v12 on v11

--- a/solution.py
+++ b/solution.py
@@ -96,6 +96,10 @@
     second = lax.axis_index("c")
     planes[2 - 2 * second] = inside_ref[...]
     planes[2 * second] = outside_ref[...]
+
+
+def first_body(out_ref):
+    out_ref[...] = jnp.zeros((8, 128), F32)
 
 
 def forward_body(
@@ -139,7 +143,7 @@
             send_ref[to, 128:] = delta[:, 128 * c : 128 * c + 128]
 
 
-def weight_grad_body(got_ref, out_ref, moved, deltas, whole):
+def weight_grad_body(got_ref, even_ref, odd_ref, out_ref, pair_ref, moved, deltas, whole):
     pieces = []
     for plane, at in [(0, 64)] + [(e, 0) for e in range(8)] + [(7, 64)]:
         pieces.append(got_ref[plane, at : at + 32].astype(F32))
@@ -160,7 +164,9 @@
         whole[288 * a : 288 * a + 288, :] = jnp.dot(
             moved[:, 256 * a : 256 * a + 2048], deltas[...], preferred_element_type=F32
         )
-    none = jnp.zeros((5, 128), F32)
+    pair_ref[0] = even_ref[1]
+    pair_ref[1] = odd_ref[1]
+    none = jnp.zeros((1, 128), F32)
     for y_to in range(4):
         for z_to in range(4):
             parts = []
@@ -170,18 +176,13 @@
             out_ref[4 * y_to + z_to] = jnp.concatenate(parts, axis=0).astype(BF16)
 
 
-def pair_body(even_ref, odd_ref, out_ref):
-    out_ref[0] = even_ref[1]
-    out_ref[1] = odd_ref[1]
-
-
 def over_y_zl_body(got_ref, even_ref, odd_ref, pair_ref, out_ref, slices, rows):
     total = sum(got_ref[i].astype(F32) for i in range(16)) * (1.0 / CELLS)
     zl = lax.axis_index("zl")
     for k, block in ((0, even_ref[0]), (2, odd_ref[0]), (1, pair_ref[0]), (3, pair_ref[1])):
         slices[zl ^ k] = block
     rows[:27, :] = total[:27]
-    rows[27:54, :] = total[32:59]
+    rows[27:54, :] = total[28:55]
     for y in range(4):
         rows[54 + 54 * y : 108 + 54 * y, :] = slices[y].astype(F32)[:54]
     rows[270:, :] = jnp.zeros((2, 128), F32)
@@ -196,7 +197,7 @@
         for y in range(4):
             slices[i, y] = rows[i, 54 + 54 * y : 118 + 54 * y, :].astype(BF16)
     total = (rows[0, :54, :] + rows[1, :54, :]) + (rows[2, :54, :] + rows[3, :54, :])
-    none = jnp.zeros((5, 128), F32)
+    none = jnp.zeros((1, 128), F32)
     total = jnp.concatenate([total[:27], none, total[27:], none], axis=0).astype(BF16)
     for to in range(32):
         out_ref[to] = total
@@ -214,12 +215,12 @@
     pair_ref[1] = next_ref[1]
     for y in range(4):
         for x in range(4):
-            at = 32 * (8 * x + 2 * y)
+            at = 28 * (8 * x + 2 * y)
             for c in range(2):
-                grads[c, at : at + 64, :] = got_ref[8 * y + 2 * x + c].astype(F32)
+                grads[c, at : at + 56, :] = got_ref[8 * y + 2 * x + c].astype(F32)
     for tap in range(27):
         for c in range(2):
-            ordered[32 * tap : 32 * tap + 32, 128 * c : 128 * c + 128] = grads[c, pl.ds(tap, 32, stride=32), :]
+            ordered[32 * tap : 32 * tap + 32, 128 * c : 128 * c + 128] = grads[c, pl.ds(tap, 32, stride=28), :]
     ordered[864:, :] = jnp.zeros((32, 256), F32)
     inside = iota((128, 128), 1) < 108
     total = jnp.zeros((128, 256), F32)
@@ -351,13 +352,14 @@
     plane = activations.reshape(256, 128)
     inside, outside = neighbours(plane)
 
+    first = call(first_body, shape((8, 128), F32), flops=4_000_000_000)
     stored = call(
         basis_body,
         shape((4, 64, 128), BF16),
         arrays=(basis_panels[0].T,),
         remote=(input_eigen.reshape(1, 54),),
+        after=(first,),
         scratch=[pltpu.VMEM((1, 54), F32), dma],
-        flops=4_000_000_000,
     )
     delta, send, even, odd = call(
         forward_body,
@@ -368,15 +370,13 @@
         flops=2 * 256 * 3456 * 256,
     )
     even, odd = turned(even, 0), turned(odd, 2)
-    part = call(
+    part, pair = call(
         weight_grad_body,
-        shape((16, 64, 128), BF16),
-        arrays=(exchange(send, XC),),
-        after=(even,),
+        [shape((16, 56, 128), BF16), shape((2, 64, 128), BF16)],
+        arrays=(exchange(send, XC), even, odd),
         scratch=[pltpu.VMEM((288, 2560), BF16), pltpu.VMEM((2048, 128), BF16), pltpu.VMEM((864, 128), F32)],
         flops=2 * 864 * 2048 * 128,
     )
-    pair = call(pair_body, shape((2, 64, 128), BF16), arrays=(even, odd), after=(part,))
     part = call(
         over_y_zl_body,
         shape((4, 272, 128), BF16),
@@ -386,7 +386,7 @@
     inside, outside = neighbours(delta)
     part, basis, here, there = call(
         over_zh_zg_body,
-        [shape((32, 64, 128), BF16), shape((8, 128, 128), BF16)] + [shape((2, 128, 128), BF16)] * 2,
+        [shape((32, 56, 128), BF16), shape((8, 128, 128), BF16)] + [shape((2, 128, 128), BF16)] * 2,
         (panel_owner,),
         (exchange(part, ("zh", "zg")),),
         after=(inside, outside),
@@ -397,7 +397,7 @@
         rotate_body,
         [shape((4, 224, 128), BF16), shape((2, 128, 128), BF16)],
         arrays=(exchange(part, YXC), basis, here, there),
-        scratch=[pltpu.VMEM((2, 1024, 128), F32), pltpu.VMEM((896, 256), F32)],
+        scratch=[pltpu.VMEM((2, 896, 128), F32), pltpu.VMEM((896, 256), F32)],
     )
     part = call(
         update_body,

time: 141 us -> 134 us (0.950)
  waiting for transfers between devices: 37.7 us -> 34.3 us
  local copies, waits for them, and re-layouts: 2.62 us -> 0.04 us
    all_to_all x6, waiting for transfers between devices: 24.1 us -> 19 us  [exchange(): return lax.all_to_all(x, axes, 0, 0)]
    all_to_all x6, starting transfers between devices: 44.3 us -> 41.6 us  [exchange(): return lax.all_to_all(x, axes, 0, 0)]
    ppermute x2, starting transfers between devices: 4.82 us -> 7.46 us  [turned(): return lax.ppermute(block, ('y', 'zl'), pairs)]
    unnamed x18, local copies, waits for them, and re-layouts: 2.62 us -> 0.04 us
    ppermute x3, waiting for transfers between devices: 9.63 us -> 11.2 us  [across(): return lax.ppermute(block, 'zl', [(i, i ^ k) for i in range(4)])]
  transfers between devices with their start and end apart: 15 -> 15, of which waited for: 10 -> 12; matrix products, arithmetic and copies ran while one was open for 0% -> 0% of each run, Pallas kernels for 2% -> 2%
where the time goes in v12:
time: 134 us
  starting transfers between devices  76.6 us (57%)
  waiting for transfers between devices  34.3 us (26%)
  Pallas kernels  12.2 us (9%)
  blocking collectives  9.64 us (7%)
    all_to_all x6, starting transfers between devices, exchange(): return lax.all_to_all(x, axes, 0, 0)  41.6 us
    all_to_all x6, waiting for transfers between devices, exchange(): return lax.all_to_all(x, axes, 0, 0)  19 us
    pallas_call x11, Pallas kernels, call(): pl.pallas_call(kernel, out_shape=out_shape, in_specs=[SMEM] * len(scalars...  12.2 us
    ppermute x3, waiting for transfers between devices, across(): return lax.ppermute(block, 'zl', [(i, i ^ k) for i in range(4)])  11.2 us
    ppermute x3, starting transfers between devices, across(): return lax.ppermute(block, 'zl', [(i, i ^ k) for i in range(4)])  11 us
    ppermute x2, starting transfers between devices, neighbours(): lax.ppermute(block, SPACE, pairs + [(j, i) for i, j in pairs])  9.68 us
    all_to_all x1, blocking collectives, exchange(): return lax.all_to_all(x, axes, 0, 0)  9.64 us
    ppermute x2, starting transfers between devices, turned(): return lax.ppermute(block, ('y', 'zl'), pairs)  7.46 us
  transfers between devices with their start and end apart: 15, of which 12 were waited for; matrix products, arithmetic and copies ran while one was open for 0% of the time, Pallas kernels for 2%

profile of v12, /device:TPU:1, one launch (start us, length us, event | category | flops | bytes accessed | tf_op | source)
XLA Modules:
  0.0 133.6 jit_solution(1214085337315145976)
XLA Ops:
  0.7 4.6 %collective-permute-start.1 = (bf16[256,128]{1,0:T(8,128)(2,1)}, bf16[256,128]{1,0:T(8,128)(2,1)S(1)}, u32[]{:S(2)}, u32[]{:S(2)}) collective-permute-start(bf16[256,128]{1,0:T(8,128)(2,1)} %bitcast.10), channel_id=1, source_target_pairs={{1,2},{3,4},{5,6},{7,8},{9,10},{11,12},{13,14},{15,16},{17,18},{19... | collective-permute-start | bytes 196616 | tf_op jit(solution)/shard_map/ppermute | solution.py:328
  5.3 4.9 %collective-permute-start = (bf16[256,128]{1,0:T(8,128)(2,1)}, bf16[256,128]{1,0:T(8,128)(2,1)S(1)}, u32[]{:S(2)}, u32[]{:S(2)}) collective-permute-start(bf16[256,128]{1,0:T(8,128)(2,1)} %bitcast.11), channel_id=1, source_target_pairs={{0,1},{1,0},{2,3},{3,2},{4,5},{5,4},{6,7},{7,6},{8,9},{9,8},{10,11... | collective-permute-start | bytes 196616 | tf_op jit(solution)/shard_map/ppermute | solution.py:326
  11.4 1.7 %shard_map.106 = (bf16[256,256]{1,0:T(8,128)(2,1)S(1)}, bf16[8,384,128]{2,1,0:T(8,128)(2,1)}, bf16[2,64,128]{2,1,0:T(8,128)(2,1)S(1)}, bf16[2,64,128]{2,1,0:T(8,128)(2,1)S(1)}) custom-call(bf16[256,128]{1,0:T(8,128)(2,1)S(1)} %collective-permute-done.refs_0_, bf16[256,128]{1,0:T(8,128)(2,1)S(1)} %collective-permute-done.1.refs_1_, ...), custom_call_target="tpu_custom_call" | custom-call | flops 452984832 | bytes 2163712 | tf_op jit(solution)/shard_map/pallas_call | solution.py:33
  13.1 3.8 %all-to-all-start = ((bf16[8,384,128]{2,1,0:T(8,128)(2,1)}), bf16[8,384,128]{2,1,0:T(8,128)(2,1)S(1)}, u32[]{:S(2)}, u32[]{:S(2)}) async-start(bf16[8,384,128]{2,1,0:T(8,128)(2,1)} %get-tuple-element.17), calls=%async_computation | async-start | bytes 1572864 | tf_op jit(solution)/shard_map/all_to_all | solution.py:57
  16.9 0.8 collective-permute-start.4
  17.7 6.7 %collective-permute-start.5 = (bf16[2,64,128]{2,1,0:T(8,128)(2,1)S(1)}, bf16[2,64,128]{2,1,0:T(8,128)(2,1)S(1)}, u32[]{:S(2)}, u32[]{:S(2)}) collective-permute-start(bf16[2,64,128]{2,1,0:T(8,128)(2,1)S(1)} %get-tuple-element.19), channel_id=1, source_target_pairs={{0,16},{8,144},{16,272},{24,400},{128,24},{136,152},{144,280},{152... | collective-permute-start | bytes 98312 | tf_op jit(solution)/shard_map/ppermute | solution.py:333
  24.4 2.0 %collective-permute-done.5.refs_2_ = bf16[2,64,128]{2,1,0:T(8,128)(2,1)S(1)} collective-permute-done((bf16[2,64,128]{2,1,0:T(8,128)(2,1)S(1)}, bf16[2,64,128]{2,1,0:T(8,128)(2,1)S(1)}, u32[]{:S(2)}, u32[]{:S(2)}) %collective-permute-start.5) | collective-permute-done | bytes 32800 | tf_op jit(solution)/shard_map/ppermute | solution.py:333
  26.4 2.9 %all-to-all-done.refs_0_ = bf16[8,384,128]{2,1,0:T(8,128)(2,1)S(1)} async-done(((bf16[8,384,128]{2,1,0:T(8,128)(2,1)}), bf16[8,384,128]{2,1,0:T(8,128)(2,1)S(1)}, u32[]{:S(2)}, u32[]{:S(2)}) %all-to-all-start) | async-done | bytes 786464 | tf_op jit(solution)/shard_map/all_to_all | solution.py:57
  29.3 2.1 %shard_map.107 = (bf16[16,56,128]{2,1,0:T(8,128)(2,1)}, bf16[2,64,128]{2,1,0:T(8,128)(2,1)S(1)}) custom-call(bf16[8,384,128]{2,1,0:T(8,128)(2,1)S(1)} %all-to-all-done.refs_0_, bf16[2,64,128]{2,1,0:T(8,128)(2,1)S(1)} %collective-permute-done.4.refs_1_, bf16[2,64,128]{2,1,0:T(8,128)(2,1)S(1)} %collective-permute-done.5.refs_2_), custom_call_target="tpu_custom_call" | custom-call | flops 452984832 | bytes 851968 | tf_op jit(solution)/shard_map/pallas_call | solution.py:33
  31.4 8.1 %all-to-all-start.1 = ((bf16[16,56,128]{2,1,0:T(8,128)(2,1)}), bf16[16,56,128]{2,1,0:T(8,128)(2,1)S(1)}, u32[]{:S(2)}, u32[]{:S(2)}) async-start(bf16[16,56,128]{2,1,0:T(8,128)(2,1)} %get-tuple-element.20), calls=%async_computation.1 | async-start | bytes 458752 | tf_op jit(solution)/shard_map/all_to_all | solution.py:57
  39.5 3.3 %collective-permute-start.6 = (bf16[2,64,128]{2,1,0:T(8,128)(2,1)S(1)}, bf16[2,64,128]{2,1,0:T(8,128)(2,1)S(1)}, u32[]{:S(2)}, u32[]{:S(2)}) collective-permute-start(bf16[2,64,128]{2,1,0:T(8,128)(2,1)S(1)} %get-tuple-element.21), channel_id=1, source_target_pairs={{0,8},{8,0},{16,24},{24,16},{1,9},{9,1},{17,25},{25,17},{2,10},{10... | collective-permute-start | bytes 98312 | tf_op jit(solution)/shard_map/ppermute | solution.py:337
  42.7 2.5 %collective-permute-done.6.refs_3_ = bf16[2,64,128]{2,1,0:T(8,128)(2,1)S(1)} collective-permute-done((bf16[2,64,128]{2,1,0:T(8,128)(2,1)S(1)}, bf16[2,64,128]{2,1,0:T(8,128)(2,1)S(1)}, u32[]{:S(2)}, u32[]{:S(2)}) %collective-permute-start.6) | collective-permute-done | bytes 32800 | tf_op jit(solution)/shard_map/ppermute | solution.py:337
  45.2 2.5 %all-to-all-done.1.refs_0_ = bf16[16,56,128]{2,1,0:T(8,128)(2,1)S(1)} async-done(((bf16[16,56,128]{2,1,0:T(8,128)(2,1)}), bf16[16,56,128]{2,1,0:T(8,128)(2,1)S(1)}, u32[]{:S(2)}, u32[]{:S(2)}) %all-to-all-start.1) | async-done | bytes 229408 | tf_op jit(solution)/shard_map/all_to_all | solution.py:57
  47.8 0.8 shard_map.108
  48.5 12.2 %all-to-all-start.2 = ((bf16[4,272,128]{2,1,0:T(8,128)(2,1)}), bf16[4,272,128]{2,1,0:T(8,128)(2,1)S(1)}, u32[]{:S(2)}, u32[]{:S(2)}) async-start(bf16[4,272,128]{2,1,0:T(8,128)(2,1)} %shard_map.108), calls=%async_computation.2 | async-start | bytes 557056 | tf_op jit(solution)/shard_map/all_to_all | solution.py:57
  60.8 5.0 %collective-permute-start.3 = (bf16[256,256]{1,0:T(8,128)(2,1)S(1)}, bf16[256,256]{1,0:T(8,128)(2,1)S(1)}, u32[]{:S(2)}, u32[]{:S(2)}) collective-permute-start(bf16[256,256]{1,0:T(8,128)(2,1)S(1)} %get-tuple-element.16.refs_2_), channel_id=1, source_target_pairs={{1,2},{3,4},{5,6},{7,8},{9,10},{11,12},{13,14},{15,16},{17,18},{19... | collective-permute-start | bytes 393224 | tf_op jit(solution)/shard_map/ppermute | solution.py:328
  65.8 1.9 %collective-permute-start.2 = (bf16[256,256]{1,0:T(8,128)(2,1)S(1)}, bf16[256,256]{1,0:T(8,128)(2,1)S(1)}, u32[]{:S(2)}, u32[]{:S(2)}) collective-permute-start(bf16[256,256]{1,0:T(8,128)(2,1)S(1)} %get-tuple-element.16.refs_2_), channel_id=1, source_target_pairs={{0,1},{1,0},{2,3},{3,2},{4,5},{5,4},{6,7},{7,6},{8,9},{9,8},{10,11... | collective-permute-start | bytes 393224 | tf_op jit(solution)/shard_map/ppermute | solution.py:326
  69.0 7.8 %all-to-all-done.2.refs_1_ = bf16[4,272,128]{2,1,0:T(8,128)(2,1)S(1)} async-done(((bf16[4,272,128]{2,1,0:T(8,128)(2,1)}), bf16[4,272,128]{2,1,0:T(8,128)(2,1)S(1)}, u32[]{:S(2)}, u32[]{:S(2)}) %all-to-all-start.2) | async-done | bytes 278560 | tf_op jit(solution)/shard_map/all_to_all | solution.py:57
  76.8 1.4 %shard_map.109 = (bf16[32,56,128]{2,1,0:T(8,128)(2,1)}, bf16[8,128,128]{2,1,0:T(8,128)(2,1)S(1)}, bf16[2,128,128]{2,1,0:T(8,128)(2,1)S(1)}, bf16[2,128,128]{2,1,0:T(8,128)(2,1)S(1)}) custom-call(s32[8]{0:T(128)S(1)} %copy-done.8, bf16[4,272,128]{2,1,0:T(8,128)(2,1)S(1)} %all-to-all-done.2.refs_1_, ...), custom_call_target="tpu_custom_call" | custom-call | bytes 540704 | tf_op jit(solution)/shard_map/pallas_call | solution.py:33
  78.3 10.3 %all-to-all-start.3 = ((bf16[32,56,128]{2,1,0:T(8,128)(2,1)}), bf16[32,56,128]{2,1,0:T(8,128)(2,1)S(1)}, u32[]{:S(2)}, u32[]{:S(2)}) async-start(bf16[32,56,128]{2,1,0:T(8,128)(2,1)} %get-tuple-element.22), calls=%async_computation.3 | async-start | bytes 917504 | tf_op jit(solution)/shard_map/all_to_all | solution.py:57
  88.6 4.4 %collective-permute-start.7 = (bf16[2,128,128]{2,1,0:T(8,128)(2,1)S(1)}, bf16[2,128,128]{2,1,0:T(8,128)(2,1)S(1)}, u32[]{:S(2)}, u32[]{:S(2)}) collective-permute-start(bf16[2,128,128]{2,1,0:T(8,128)(2,1)S(1)} %get-tuple-element.25), channel_id=1, source_target_pairs={{0,16},{8,24},{16,0},{24,8},{1,17},{9,25},{17,1},{25,9},{2,18},{10... | collective-permute-start | bytes 196616 | tf_op jit(solution)/shard_map/ppermute | solution.py:337
  93.0 3.8 %collective-permute-done.7.refs_3_.refs_2_ = bf16[2,128,128]{2,1,0:T(8,128)(2,1)S(1)} collective-permute-done((bf16[2,128,128]{2,1,0:T(8,128)(2,1)S(1)}, bf16[2,128,128]{2,1,0:T(8,128)(2,1)S(1)}, u32[]{:S(2)}, u32[]{:S(2)}) %collective-permute-start.7) | collective-permute-done | bytes 65568 | tf_op jit(solution)/shard_map/ppermute | solution.py:337
  96.8 2.7 %all-to-all-done.3.refs_0_ = bf16[32,56,128]{2,1,0:T(8,128)(2,1)S(1)} async-done(((bf16[32,56,128]{2,1,0:T(8,128)(2,1)}), bf16[32,56,128]{2,1,0:T(8,128)(2,1)S(1)}, u32[]{:S(2)}, u32[]{:S(2)}) %all-to-all-start.3) | async-done | bytes 458784 | tf_op jit(solution)/shard_map/all_to_all | solution.py:57
  99.4 1.1 shard_map.110
  100.5 3.8 %all-to-all-start.4 = ((bf16[4,224,128]{2,1,0:T(8,128)(2,1)}), bf16[4,224,128]{2,1,0:T(8,128)(2,1)S(1)}, u32[]{:S(2)}, u32[]{:S(2)}) async-start(bf16[4,224,128]{2,1,0:T(8,128)(2,1)} %get-tuple-element.26), calls=%async_computation.4 | async-start | bytes 458752 | tf_op jit(solution)/shard_map/all_to_all | solution.py:57
  104.2 3.4 %collective-permute-start.8 = (bf16[2,128,128]{2,1,0:T(8,128)(2,1)S(1)}, bf16[2,128,128]{2,1,0:T(8,128)(2,1)S(1)}, u32[]{:S(2)}, u32[]{:S(2)}) collective-permute-start(bf16[2,128,128]{2,1,0:T(8,128)(2,1)S(1)} %get-tuple-element.27), channel_id=1, source_target_pairs={{0,8},{8,0},{16,24},{24,16},{1,9},{9,1},{17,25},{25,17},{2,10},{10... | collective-permute-start | bytes 196616 | tf_op jit(solution)/shard_map/ppermute | solution.py:337
  107.6 5.0 %collective-permute-done.8.refs_3_ = bf16[2,128,128]{2,1,0:T(8,128)(2,1)S(1)} collective-permute-done((bf16[2,128,128]{2,1,0:T(8,128)(2,1)S(1)}, bf16[2,128,128]{2,1,0:T(8,128)(2,1)S(1)}, u32[]{:S(2)}, u32[]{:S(2)}) %collective-permute-start.8) | collective-permute-done | bytes 65568 | tf_op jit(solution)/shard_map/ppermute | solution.py:337
  112.6 1.3 shard_map.111
  113.9 9.6 %all_to_all.35.refs_0_ = bf16[8,112,128]{2,1,0:T(8,128)(2,1)S(1)} all-to-all(bf16[8,112,128]{2,1,0:T(8,128)(2,1)S(1)} %shard_map.111), channel_id=1, replica_groups=mesh['y'=4,'zh'=2,'zg'=2,'zl'=4,'x'=4,'c'=2] {'x','c'}, dimensions={0} | all-to-all | bytes 458752 | tf_op jit(solution)/shard_map/all_to_all | solution.py:57
  124.3 3.4 %all-to-all-start.6 = ((f32[4,112,128]{2,1,0:T(8,128)}), f32[4,112,128]{2,1,0:T(8,128)S(1)}, u32[]{:S(2)}, u32[]{:S(2)}) async-start(f32[4,112,128]{2,1,0:T(8,128)} %shard_map.112.refs_4_), calls=%async_computation.6 | async-start | bytes 458752 | tf_op jit(solution)/shard_map/all_to_all | solution.py:57
  127.6 2.1 %shard_map.113 = (bf16[256,128]{1,0:T(8,128)(2,1)}, f32[8,128]{1,0:T(8,128)S(1)}) custom-call(bf16[256,256]{1,0:T(8,128)(2,1)S(1)} %collective-permute-done.2.refs_2_.refs_0_, bf16[256,256]{1,0:T(8,128)(2,1)S(1)} %collective-permute-done.3.refs_3_.refs_1_, bf16[256,256]{1,0:T(8,128)(2,1)S(1)} %get-tuple-element.16.refs_2_, bf16[3456,256]{1,0:T(8,128)(2,1)S(1)} %copy-done, ...), custom_call_target="tpu_custom_call" | custom-call | flops 452984832 | bytes 2392064 | tf_op jit(solution)/shard_map/pallas_call | solution.py:33
  129.8 3.2 %all-to-all-done.6.refs_0_ = f32[4,112,128]{2,1,0:T(8,128)S(1)} async-done(((f32[4,112,128]{2,1,0:T(8,128)}), f32[4,112,128]{2,1,0:T(8,128)S(1)}, u32[]{:S(2)}, u32[]{:S(2)}) %all-to-all-start.6) | async-done | bytes 229408 | tf_op jit(solution)/shard_map/all_to_all | solution.py:57
  (28 shorter events, 3.8 us)
Async XLA Ops:
  0.6 9.7 %copy-start.4 = (bf16[1,432,54]{1,2,0:T(8,128)(2,1)S(1)}, bf16[1,432,54]{1,2,0:T(8,128)(2,1)}, u32[]{:S(2)}) copy-start(bf16[1,432,54]{1,2,0:T(8,128)(2,1)} %param.13) | copy-start | bytes 139972
  0.6 9.7 %copy-start.7 = (f32[54]{0:T(128)S(1)}, f32[54]{0:T(128)}, u32[]{:S(2)}) copy-start(f32[54]{0:T(128)} %param.16) | copy-start | bytes 652
  0.7 10.7 %copy-start = (bf16[3456,256]{1,0:T(8,128)(2,1)S(1)}, bf16[3456,256]{1,0:T(8,128)(2,1)}, u32[]{:S(2)}) copy-start(bf16[3456,256]{1,0:T(8,128)(2,1)} %refs_3_.3) | copy-start | bytes 5308420
  0.7 10.7 %copy-start.2 = (bf16[1,1,16,16,256]{4,3,2,1,0:T(8,128)(2,1)S(1)}, bf16[1,1,16,16,256]{4,3,2,1,0:T(8,128)(2,1)}, u32[]{:S(2)}) copy-start(bf16[1,1,16,16,256]{4,3,2,1,0:T(8,128)(2,1)} %param.12) | copy-start | bytes 393220
  0.7 10.7 %copy-start.3 = (bf16[1,1,16,16,128]{4,3,2,1,0:T(8,128)(2,1)S(1)}, bf16[1,1,16,16,128]{4,3,2,1,0:T(8,128)(2,1)}, u32[]{:S(2)}) copy-start(bf16[1,1,16,16,128]{4,3,2,1,0:T(8,128)(2,1)} %param.9) | copy-start | bytes 196612
  0.7 10.7 %copy-start.5 = (f32[256]{0:T(256)S(1)}, f32[256]{0:T(256)}, u32[]{:S(2)}) copy-start(f32[256]{0:T(256)} %param.11) | copy-start | bytes 3076
  0.7 10.0 %collective-permute-start.1 = (bf16[256,128]{1,0:T(8,128)(2,1)}, bf16[256,128]{1,0:T(8,128)(2,1)S(1)}, u32[]{:S(2)}, u32[]{:S(2)}) collective-permute-start(bf16[256,128]{1,0:T(8,128)(2,1)} %bitcast.10), channel_id=1, source_target_pairs={{1,2},{3,4},{5,6},{7,8},{9,10},{11,12},{13,14},{15,16},{17,18},{19... | collective-permute-start | bytes 196616 | tf_op jit(solution)/shard_map/ppermute | solution.py:328
  5.3 6.0 %collective-permute-start = (bf16[256,128]{1,0:T(8,128)(2,1)}, bf16[256,128]{1,0:T(8,128)(2,1)S(1)}, u32[]{:S(2)}, u32[]{:S(2)}) collective-permute-start(bf16[256,128]{1,0:T(8,128)(2,1)} %bitcast.11), channel_id=1, source_target_pairs={{0,1},{1,0},{2,3},{3,2},{4,5},{5,4},{6,7},{7,6},{8,9},{9,8},{10,11... | collective-permute-start | bytes 196616 | tf_op jit(solution)/shard_map/ppermute | solution.py:326
  13.1 16.1 %all-to-all-start = ((bf16[8,384,128]{2,1,0:T(8,128)(2,1)}), bf16[8,384,128]{2,1,0:T(8,128)(2,1)S(1)}, u32[]{:S(2)}, u32[]{:S(2)}) async-start(bf16[8,384,128]{2,1,0:T(8,128)(2,1)} %get-tuple-element.17), calls=%async_computation | async-start | bytes 1572864 | tf_op jit(solution)/shard_map/all_to_all | solution.py:57
  16.9 59.9 %copy-start.8 = (s32[8]{0:T(128)S(1)}, s32[8]{0:T(128)}, u32[]{:S(2)}) copy-start(s32[8]{0:T(128)} %refs_0_.1) | copy-start | bytes 100
  16.9 7.5 %collective-permute-start.4 = (bf16[2,64,128]{2,1,0:T(8,128)(2,1)S(1)}, bf16[2,64,128]{2,1,0:T(8,128)(2,1)S(1)}, u32[]{:S(2)}, u32[]{:S(2)}) collective-permute-start(bf16[2,64,128]{2,1,0:T(8,128)(2,1)S(1)} %get-tuple-element.18), channel_id=1, source_target_pairs={{0,0},{8,128},{16,256},{24,384},{128,8},{136,136},{144,264},{152,3... | collective-permute-start | bytes 98312 | tf_op jit(solution)/shard_map/ppermute | solution.py:333
  17.7 8.7 %collective-permute-start.5 = (bf16[2,64,128]{2,1,0:T(8,128)(2,1)S(1)}, bf16[2,64,128]{2,1,0:T(8,128)(2,1)S(1)}, u32[]{:S(2)}, u32[]{:S(2)}) collective-permute-start(bf16[2,64,128]{2,1,0:T(8,128)(2,1)S(1)} %get-tuple-element.19), channel_id=1, source_target_pairs={{0,16},{8,144},{16,272},{24,400},{128,24},{136,152},{144,280},{152... | collective-permute-start | bytes 98312 | tf_op jit(solution)/shard_map/ppermute | solution.py:333
  31.4 16.4 %all-to-all-start.1 = ((bf16[16,56,128]{2,1,0:T(8,128)(2,1)}), bf16[16,56,128]{2,1,0:T(8,128)(2,1)S(1)}, u32[]{:S(2)}, u32[]{:S(2)}) async-start(bf16[16,56,128]{2,1,0:T(8,128)(2,1)} %get-tuple-element.20), calls=%async_computation.1 | async-start | bytes 458752 | tf_op jit(solution)/shard_map/all_to_all | solution.py:57
  39.5 5.8 %collective-permute-start.6 = (bf16[2,64,128]{2,1,0:T(8,128)(2,1)S(1)}, bf16[2,64,128]{2,1,0:T(8,128)(2,1)S(1)}, u32[]{:S(2)}, u32[]{:S(2)}) collective-permute-start(bf16[2,64,128]{2,1,0:T(8,128)(2,1)S(1)} %get-tuple-element.21), channel_id=1, source_target_pairs={{0,8},{8,0},{16,24},{24,16},{1,9},{9,1},{17,25},{25,17},{2,10},{10... | collective-permute-start | bytes 98312 | tf_op jit(solution)/shard_map/ppermute | solution.py:337
  48.5 64.1 %copy-start.1 = (f32[256,256]{1,0:T(8,128)S(1)}, f32[256,256]{1,0:T(8,128)}, u32[]{:S(2)}) copy-start(f32[256,256]{1,0:T(8,128)} %refs_4_.1) | copy-start | bytes 786436
  48.5 64.1 %copy-start.6 = (f32[256]{0:T(256)S(1)}, f32[256]{0:T(256)}, u32[]{:S(2)}) copy-start(f32[256]{0:T(256)} %param.17) | copy-start | bytes 3076
  48.5 28.3 %all-to-all-start.2 = ((bf16[4,272,128]{2,1,0:T(8,128)(2,1)}), bf16[4,272,128]{2,1,0:T(8,128)(2,1)S(1)}, u32[]{:S(2)}, u32[]{:S(2)}) async-start(bf16[4,272,128]{2,1,0:T(8,128)(2,1)} %shard_map.108), calls=%async_computation.2 | async-start | bytes 557056 | tf_op jit(solution)/shard_map/all_to_all | solution.py:57
  60.8 7.7 %collective-permute-start.3 = (bf16[256,256]{1,0:T(8,128)(2,1)S(1)}, bf16[256,256]{1,0:T(8,128)(2,1)S(1)}, u32[]{:S(2)}, u32[]{:S(2)}) collective-permute-start(bf16[256,256]{1,0:T(8,128)(2,1)S(1)} %get-tuple-element.16.refs_2_), channel_id=1, source_target_pairs={{1,2},{3,4},{5,6},{7,8},{9,10},{11,12},{13,14},{15,16},{17,18},{19... | collective-permute-start | bytes 393224 | tf_op jit(solution)/shard_map/ppermute | solution.py:328
  65.8 3.2 %collective-permute-start.2 = (bf16[256,256]{1,0:T(8,128)(2,1)S(1)}, bf16[256,256]{1,0:T(8,128)(2,1)S(1)}, u32[]{:S(2)}, u32[]{:S(2)}) collective-permute-start(bf16[256,256]{1,0:T(8,128)(2,1)S(1)} %get-tuple-element.16.refs_2_), channel_id=1, source_target_pairs={{0,1},{1,0},{2,3},{3,2},{4,5},{5,4},{6,7},{7,6},{8,9},{9,8},{10,11... | collective-permute-start | bytes 393224 | tf_op jit(solution)/shard_map/ppermute | solution.py:326
  78.3 21.2 %all-to-all-start.3 = ((bf16[32,56,128]{2,1,0:T(8,128)(2,1)}), bf16[32,56,128]{2,1,0:T(8,128)(2,1)S(1)}, u32[]{:S(2)}, u32[]{:S(2)}) async-start(bf16[32,56,128]{2,1,0:T(8,128)(2,1)} %get-tuple-element.22), calls=%async_computation.3 | async-start | bytes 917504 | tf_op jit(solution)/shard_map/all_to_all | solution.py:57
  88.6 8.2 %collective-permute-start.7 = (bf16[2,128,128]{2,1,0:T(8,128)(2,1)S(1)}, bf16[2,128,128]{2,1,0:T(8,128)(2,1)S(1)}, u32[]{:S(2)}, u32[]{:S(2)}) collective-permute-start(bf16[2,128,128]{2,1,0:T(8,128)(2,1)S(1)} %get-tuple-element.25), channel_id=1, source_target_pairs={{0,16},{8,24},{16,0},{24,8},{1,17},{9,25},{17,1},{25,9},{2,18},{10... | collective-permute-start | bytes 196616 | tf_op jit(solution)/shard_map/ppermute | solution.py:337
  100.5 12.1 %all-to-all-start.4 = ((bf16[4,224,128]{2,1,0:T(8,128)(2,1)}), bf16[4,224,128]{2,1,0:T(8,128)(2,1)S(1)}, u32[]{:S(2)}, u32[]{:S(2)}) async-start(bf16[4,224,128]{2,1,0:T(8,128)(2,1)} %get-tuple-element.26), calls=%async_computation.4 | async-start | bytes 458752 | tf_op jit(solution)/shard_map/all_to_all | solution.py:57
  104.2 8.3 %collective-permute-start.8 = (bf16[2,128,128]{2,1,0:T(8,128)(2,1)S(1)}, bf16[2,128,128]{2,1,0:T(8,128)(2,1)S(1)}, u32[]{:S(2)}, u32[]{:S(2)}) collective-permute-start(bf16[2,128,128]{2,1,0:T(8,128)(2,1)S(1)} %get-tuple-element.27), channel_id=1, source_target_pairs={{0,8},{8,0},{16,24},{24,16},{1,9},{9,1},{17,25},{25,17},{2,10},{10... | collective-permute-start | bytes 196616 | tf_op jit(solution)/shard_map/ppermute | solution.py:337
  124.3 8.7 %all-to-all-start.6 = ((f32[4,112,128]{2,1,0:T(8,128)}), f32[4,112,128]{2,1,0:T(8,128)S(1)}, u32[]{:S(2)}, u32[]{:S(2)}) async-start(f32[4,112,128]{2,1,0:T(8,128)} %shard_map.112.refs_4_), calls=%async_computation.6 | async-start | bytes 458752 | tf_op jit(solution)/shard_map/all_to_all | solution.py:57

commit v13 on v12

--- a/solution.py
+++ b/solution.py
@@ -149,7 +149,7 @@
         pieces.append(got_ref[plane, at : at + 32].astype(F32))
         pieces.append(got_ref[plane, at + 32 : at + 64].astype(F32))
     acts = jnp.concatenate(pieces, axis=1)
-    lane = iota((32, 2560), 1)
+    lane = iota((8, 2560), 1)
     x = lane & 15
     y = (lane >> 4) & 15
     for b in range(3):
@@ -157,7 +157,8 @@
             step = 16 * (b - 1) + (c - 1)
             turned = pltpu.roll(acts, (-step) % 2560, 1) if step else acts
             inside = (x + c >= 1) & (x + c < 17) & (y + b >= 1) & (y + b < 17)
-            moved[32 * (3 * b + c) : 32 * (3 * b + c) + 32, :] = jnp.where(inside, turned, 0.0).astype(BF16)
+            kept = jnp.where(inside[None], turned.reshape(4, 8, 2560), 0.0).reshape(32, 2560)
+            moved[32 * (3 * b + c) : 32 * (3 * b + c) + 32, :] = kept.astype(BF16)
     for e in range(8):
         deltas[256 * e : 256 * e + 256, :] = got_ref[e, 128:]
     for a in range(3):
@@ -283,11 +284,11 @@
 def over_xc_body(got_ref, out_ref):
     total = sum(got_ref[i].astype(F32) for i in range(8))
     for to in range(4):
-        out_ref[to] = total
+        out_ref[to] = total.astype(BF16)
 
 
 def last_body(got_ref, out_ref):
-    total = (got_ref[0] + got_ref[1]) + (got_ref[2] + got_ref[3])
+    total = sum(got_ref[i].astype(F32) for i in range(4))
     out_ref[...] = jnp.concatenate([total[:54], total[56:110]], axis=1)
 
 
@@ -399,12 +400,23 @@
         arrays=(exchange(part, YXC), basis, here, there),
         scratch=[pltpu.VMEM((2, 896, 128), F32), pltpu.VMEM((896, 256), F32)],
     )
+    data, token = call(
+        data_grad_body,
+        [shape((256, 128), BF16), shape((8, 128), F32)],
+        (),
+        (inside, outside, delta),
+        (conv_weight,),
+        after=(pair,),
+        scratch=[pltpu.VMEM((3456, 256), BF16), pltpu.VMEM((3, 256, 256), BF16), dma],
+        flops=2 * 256 * 3456 * 256,
+    )
     part = call(
         update_body,
         shape((8, 112, 128), BF16),
         (),
         (exchange(rotated, "zl"), here, there, across(pair, 1)),
         (output_basis, output_eigen.reshape(1, 256)),
+        after=(token,),
         scratch=[
             pltpu.VMEM((4, 128, 128), BF16),
             pltpu.VMEM((256, 256), F32),
@@ -413,18 +425,8 @@
             dma((2,)),
         ],
     )
-    part = call(over_xc_body, shape((4, 112, 128), F32), arrays=(exchange(part, XC),))
-    data, token = call(
-        data_grad_body,
-        [shape((256, 128), BF16), shape((8, 128), F32)],
-        (),
-        (inside, outside, delta),
-        (conv_weight,),
-        after=(part,),
-        scratch=[pltpu.VMEM((3456, 256), BF16), pltpu.VMEM((3, 256, 256), BF16), dma],
-        flops=2 * 256 * 3456 * 256,
-    )
-    update = call(last_body, shape((54, 256), F32), arrays=(exchange(part, "y"),), after=(token,))
+    part = call(over_xc_body, shape((4, 112, 128), BF16), arrays=(exchange(part, XC),))
+    update = call(last_body, shape((54, 256), F32), arrays=(exchange(part, "y"),))
     return (data.reshape(1, 1, 16, 16, 128), update)
 
 

time: 134 us -> 132 us (0.985)
  blocking collectives: 9.64 us -> 16.8 us
  waiting for transfers between devices: 34.3 us -> 28.9 us
  starting transfers between devices: 76.6 us -> 73.1 us
    all_to_all x1 -> x2, blocking collectives: 9.64 us -> 16.8 us  [exchange(): return lax.all_to_all(x, axes, 0, 0)]
    all_to_all x6 -> x5, waiting for transfers between devices: 19 us -> 15.3 us  [exchange(): return lax.all_to_all(x, axes, 0, 0)]
    all_to_all x6 -> x5, starting transfers between devices: 41.6 us -> 38.1 us  [exchange(): return lax.all_to_all(x, axes, 0, 0)]
    ppermute x3, waiting for transfers between devices: 11.2 us -> 9.66 us  [across(): return lax.ppermute(block, 'zl', [(i, i ^ k) for i in range(4)])]
  transfers between devices with their start and end apart: 15 -> 14, of which waited for: 12 -> 11; matrix products, arithmetic and copies ran while one was open for 0% -> 0% of each run, Pallas kernels for 2% -> 2%
where the time goes in v13:
time: 132 us; the launch traced here: 131 us
  starting transfers between devices  73.1 us (55%)
  waiting for transfers between devices  28.9 us (22%)
  blocking collectives  16.8 us (13%)
  Pallas kernels  11.5 us (9%)
    all_to_all x5, starting transfers between devices, exchange(): return lax.all_to_all(x, axes, 0, 0)  38.1 us
    all_to_all x2, blocking collectives, exchange(): return lax.all_to_all(x, axes, 0, 0)  16.8 us
    all_to_all x5, waiting for transfers between devices, exchange(): return lax.all_to_all(x, axes, 0, 0)  15.3 us
    pallas_call x11, Pallas kernels, call(): pl.pallas_call(kernel, out_shape=out_shape, in_specs=[SMEM] * len(scalars...  11.5 us
    ppermute x3, starting transfers between devices, across(): return lax.ppermute(block, 'zl', [(i, i ^ k) for i in range(4)])  11 us
    ppermute x2, starting transfers between devices, neighbours(): lax.ppermute(block, SPACE, pairs + [(j, i) for i, j in pairs])  9.68 us
    ppermute x3, waiting for transfers between devices, across(): return lax.ppermute(block, 'zl', [(i, i ^ k) for i in range(4)])  9.66 us
    ppermute x2, starting transfers between devices, turned(): return lax.ppermute(block, ('y', 'zl'), pairs)  7.46 us
  transfers between devices with their start and end apart: 14, of which 11 were waited for; matrix products, arithmetic and copies ran while one was open for 0% of the time, Pallas kernels for 2%

profile of v13, /device:TPU:1, one launch (start us, length us, event | category | flops | bytes accessed | tf_op | source)
XLA Modules:
  0.0 131.2 jit_solution(16135850709679889693)
XLA Ops:
  0.7 4.6 %collective-permute-start.1 = (bf16[256,128]{1,0:T(8,128)(2,1)}, bf16[256,128]{1,0:T(8,128)(2,1)S(1)}, u32[]{:S(2)}, u32[]{:S(2)}) collective-permute-start(bf16[256,128]{1,0:T(8,128)(2,1)} %bitcast.10), channel_id=1, source_target_pairs={{1,2},{3,4},{5,6},{7,8},{9,10},{11,12},{13,14},{15,16},{17,18},{19... | collective-permute-start | bytes 196616 | tf_op jit(solution)/shard_map/ppermute | solution.py:329
  5.3 4.9 %collective-permute-start = (bf16[256,128]{1,0:T(8,128)(2,1)}, bf16[256,128]{1,0:T(8,128)(2,1)S(1)}, u32[]{:S(2)}, u32[]{:S(2)}) collective-permute-start(bf16[256,128]{1,0:T(8,128)(2,1)} %bitcast.11), channel_id=1, source_target_pairs={{0,1},{1,0},{2,3},{3,2},{4,5},{5,4},{6,7},{7,6},{8,9},{9,8},{10,11... | collective-permute-start | bytes 196616 | tf_op jit(solution)/shard_map/ppermute | solution.py:327
  10.7 0.7 collective-permute-done.refs_0_
  11.4 1.7 %shard_map.106 = (bf16[256,256]{1,0:T(8,128)(2,1)S(1)}, bf16[8,384,128]{2,1,0:T(8,128)(2,1)}, bf16[2,64,128]{2,1,0:T(8,128)(2,1)S(1)}, bf16[2,64,128]{2,1,0:T(8,128)(2,1)S(1)}) custom-call(bf16[256,128]{1,0:T(8,128)(2,1)S(1)} %collective-permute-done.refs_0_, bf16[256,128]{1,0:T(8,128)(2,1)S(1)} %collective-permute-done.1.refs_1_, ...), custom_call_target="tpu_custom_call" | custom-call | flops 452984832 | bytes 2163712 | tf_op jit(solution)/shard_map/pallas_call | solution.py:33
  13.1 3.8 %all-to-all-start = ((bf16[8,384,128]{2,1,0:T(8,128)(2,1)}), bf16[8,384,128]{2,1,0:T(8,128)(2,1)S(1)}, u32[]{:S(2)}, u32[]{:S(2)}) async-start(bf16[8,384,128]{2,1,0:T(8,128)(2,1)} %get-tuple-element.17), calls=%async_computation | async-start | bytes 1572864 | tf_op jit(solution)/shard_map/all_to_all | solution.py:57
  16.9 0.8 collective-permute-start.4
  17.7 6.7 %collective-permute-start.5 = (bf16[2,64,128]{2,1,0:T(8,128)(2,1)S(1)}, bf16[2,64,128]{2,1,0:T(8,128)(2,1)S(1)}, u32[]{:S(2)}, u32[]{:S(2)}) collective-permute-start(bf16[2,64,128]{2,1,0:T(8,128)(2,1)S(1)} %get-tuple-element.19), channel_id=1, source_target_pairs={{0,16},{8,144},{16,272},{24,400},{128,24},{136,152},{144,280},{152... | collective-permute-start | bytes 98312 | tf_op jit(solution)/shard_map/ppermute | solution.py:334
  24.4 2.0 %collective-permute-done.5.refs_2_ = bf16[2,64,128]{2,1,0:T(8,128)(2,1)S(1)} collective-permute-done((bf16[2,64,128]{2,1,0:T(8,128)(2,1)S(1)}, bf16[2,64,128]{2,1,0:T(8,128)(2,1)S(1)}, u32[]{:S(2)}, u32[]{:S(2)}) %collective-permute-start.5) | collective-permute-done | bytes 32800 | tf_op jit(solution)/shard_map/ppermute | solution.py:334
  26.4 2.9 %all-to-all-done.refs_0_ = bf16[8,384,128]{2,1,0:T(8,128)(2,1)S(1)} async-done(((bf16[8,384,128]{2,1,0:T(8,128)(2,1)}), bf16[8,384,128]{2,1,0:T(8,128)(2,1)S(1)}, u32[]{:S(2)}, u32[]{:S(2)}) %all-to-all-start) | async-done | bytes 786464 | tf_op jit(solution)/shard_map/all_to_all | solution.py:57
  29.2 2.1 %shard_map.107 = (bf16[16,56,128]{2,1,0:T(8,128)(2,1)}, bf16[2,64,128]{2,1,0:T(8,128)(2,1)S(1)}) custom-call(bf16[8,384,128]{2,1,0:T(8,128)(2,1)S(1)} %all-to-all-done.refs_0_, bf16[2,64,128]{2,1,0:T(8,128)(2,1)S(1)} %collective-permute-done.4.refs_1_, bf16[2,64,128]{2,1,0:T(8,128)(2,1)S(1)} %collective-permute-done.5.refs_2_), custom_call_target="tpu_custom_call" | custom-call | flops 452984832 | bytes 851968 | tf_op jit(solution)/shard_map/pallas_call | solution.py:33
  31.4 8.1 %all-to-all-start.1 = ((bf16[16,56,128]{2,1,0:T(8,128)(2,1)}), bf16[16,56,128]{2,1,0:T(8,128)(2,1)S(1)}, u32[]{:S(2)}, u32[]{:S(2)}) async-start(bf16[16,56,128]{2,1,0:T(8,128)(2,1)} %get-tuple-element.20), calls=%async_computation.1 | async-start | bytes 458752 | tf_op jit(solution)/shard_map/all_to_all | solution.py:57
  39.5 3.3 %collective-permute-start.6 = (bf16[2,64,128]{2,1,0:T(8,128)(2,1)S(1)}, bf16[2,64,128]{2,1,0:T(8,128)(2,1)S(1)}, u32[]{:S(2)}, u32[]{:S(2)}) collective-permute-start(bf16[2,64,128]{2,1,0:T(8,128)(2,1)S(1)} %get-tuple-element.21), channel_id=1, source_target_pairs={{0,8},{8,0},{16,24},{24,16},{1,9},{9,1},{17,25},{25,17},{2,10},{10... | collective-permute-start | bytes 98312 | tf_op jit(solution)/shard_map/ppermute | solution.py:338
  42.7 3.1 %collective-permute-done.6.refs_3_ = bf16[2,64,128]{2,1,0:T(8,128)(2,1)S(1)} collective-permute-done((bf16[2,64,128]{2,1,0:T(8,128)(2,1)S(1)}, bf16[2,64,128]{2,1,0:T(8,128)(2,1)S(1)}, u32[]{:S(2)}, u32[]{:S(2)}) %collective-permute-start.6) | collective-permute-done | bytes 32800 | tf_op jit(solution)/shard_map/ppermute | solution.py:338
  45.8 1.9 %all-to-all-done.1.refs_0_ = bf16[16,56,128]{2,1,0:T(8,128)(2,1)S(1)} async-done(((bf16[16,56,128]{2,1,0:T(8,128)(2,1)}), bf16[16,56,128]{2,1,0:T(8,128)(2,1)S(1)}, u32[]{:S(2)}, u32[]{:S(2)}) %all-to-all-start.1) | async-done | bytes 229408 | tf_op jit(solution)/shard_map/all_to_all | solution.py:57
  47.7 0.8 shard_map.108
  48.5 12.1 %all-to-all-start.2 = ((bf16[4,272,128]{2,1,0:T(8,128)(2,1)}), bf16[4,272,128]{2,1,0:T(8,128)(2,1)S(1)}, u32[]{:S(2)}, u32[]{:S(2)}) async-start(bf16[4,272,128]{2,1,0:T(8,128)(2,1)} %shard_map.108), calls=%async_computation.2 | async-start | bytes 557056 | tf_op jit(solution)/shard_map/all_to_all | solution.py:57
  60.6 5.0 %collective-permute-start.3 = (bf16[256,256]{1,0:T(8,128)(2,1)S(1)}, bf16[256,256]{1,0:T(8,128)(2,1)S(1)}, u32[]{:S(2)}, u32[]{:S(2)}) collective-permute-start(bf16[256,256]{1,0:T(8,128)(2,1)S(1)} %get-tuple-element.16.refs_2_), channel_id=1, source_target_pairs={{1,2},{3,4},{5,6},{7,8},{9,10},{11,12},{13,14},{15,16},{17,18},{19... | collective-permute-start | bytes 393224 | tf_op jit(solution)/shard_map/ppermute | solution.py:329
  65.7 1.9 %collective-permute-start.2 = (bf16[256,256]{1,0:T(8,128)(2,1)S(1)}, bf16[256,256]{1,0:T(8,128)(2,1)S(1)}, u32[]{:S(2)}, u32[]{:S(2)}) collective-permute-start(bf16[256,256]{1,0:T(8,128)(2,1)S(1)} %get-tuple-element.16.refs_2_), channel_id=1, source_target_pairs={{0,1},{1,0},{2,3},{3,2},{4,5},{5,4},{6,7},{7,6},{8,9},{9,8},{10,11... | collective-permute-start | bytes 393224 | tf_op jit(solution)/shard_map/ppermute | solution.py:327
  68.9 7.8 %all-to-all-done.2.refs_1_ = bf16[4,272,128]{2,1,0:T(8,128)(2,1)S(1)} async-done(((bf16[4,272,128]{2,1,0:T(8,128)(2,1)}), bf16[4,272,128]{2,1,0:T(8,128)(2,1)S(1)}, u32[]{:S(2)}, u32[]{:S(2)}) %all-to-all-start.2) | async-done | bytes 278560 | tf_op jit(solution)/shard_map/all_to_all | solution.py:57
  76.7 1.4 %shard_map.109 = (bf16[32,56,128]{2,1,0:T(8,128)(2,1)}, bf16[8,128,128]{2,1,0:T(8,128)(2,1)S(1)}, bf16[2,128,128]{2,1,0:T(8,128)(2,1)S(1)}, bf16[2,128,128]{2,1,0:T(8,128)(2,1)S(1)}) custom-call(s32[8]{0:T(128)S(1)} %copy-done.8, bf16[4,272,128]{2,1,0:T(8,128)(2,1)S(1)} %all-to-all-done.2.refs_1_, ...), custom_call_target="tpu_custom_call" | custom-call | bytes 540704 | tf_op jit(solution)/shard_map/pallas_call | solution.py:33
  78.1 10.3 %all-to-all-start.3 = ((bf16[32,56,128]{2,1,0:T(8,128)(2,1)}), bf16[32,56,128]{2,1,0:T(8,128)(2,1)S(1)}, u32[]{:S(2)}, u32[]{:S(2)}) async-start(bf16[32,56,128]{2,1,0:T(8,128)(2,1)} %get-tuple-element.22), calls=%async_computation.3 | async-start | bytes 917504 | tf_op jit(solution)/shard_map/all_to_all | solution.py:57
  88.4 4.4 %collective-permute-start.7 = (bf16[2,128,128]{2,1,0:T(8,128)(2,1)S(1)}, bf16[2,128,128]{2,1,0:T(8,128)(2,1)S(1)}, u32[]{:S(2)}, u32[]{:S(2)}) collective-permute-start(bf16[2,128,128]{2,1,0:T(8,128)(2,1)S(1)} %get-tuple-element.25), channel_id=1, source_target_pairs={{0,16},{8,24},{16,0},{24,8},{1,17},{9,25},{17,1},{25,9},{2,18},{10... | collective-permute-start | bytes 196616 | tf_op jit(solution)/shard_map/ppermute | solution.py:338
  92.8 3.8 %collective-permute-done.7.refs_3_.refs_2_ = bf16[2,128,128]{2,1,0:T(8,128)(2,1)S(1)} collective-permute-done((bf16[2,128,128]{2,1,0:T(8,128)(2,1)S(1)}, bf16[2,128,128]{2,1,0:T(8,128)(2,1)S(1)}, u32[]{:S(2)}, u32[]{:S(2)}) %collective-permute-start.7) | collective-permute-done | bytes 65568 | tf_op jit(solution)/shard_map/ppermute | solution.py:338
  96.6 2.7 %all-to-all-done.3.refs_0_ = bf16[32,56,128]{2,1,0:T(8,128)(2,1)S(1)} async-done(((bf16[32,56,128]{2,1,0:T(8,128)(2,1)}), bf16[32,56,128]{2,1,0:T(8,128)(2,1)S(1)}, u32[]{:S(2)}, u32[]{:S(2)}) %all-to-all-start.3) | async-done | bytes 458784 | tf_op jit(solution)/shard_map/all_to_all | solution.py:57
  99.3 1.1 shard_map.110
  100.3 3.8 %all-to-all-start.4 = ((bf16[4,224,128]{2,1,0:T(8,128)(2,1)}), bf16[4,224,128]{2,1,0:T(8,128)(2,1)S(1)}, u32[]{:S(2)}, u32[]{:S(2)}) async-start(bf16[4,224,128]{2,1,0:T(8,128)(2,1)} %get-tuple-element.28), calls=%async_computation.4 | async-start | bytes 458752 | tf_op jit(solution)/shard_map/all_to_all | solution.py:57
  104.1 3.4 %collective-permute-start.8 = (bf16[2,128,128]{2,1,0:T(8,128)(2,1)S(1)}, bf16[2,128,128]{2,1,0:T(8,128)(2,1)S(1)}, u32[]{:S(2)}, u32[]{:S(2)}) collective-permute-start(bf16[2,128,128]{2,1,0:T(8,128)(2,1)S(1)} %get-tuple-element.26.refs_4_), channel_id=1, source_target_pairs={{0,8},{8,0},{16,24},{24,16},{1,9},{9,1},{17,25},{25,17},{2,10},{10... | collective-permute-start | bytes 196616 | tf_op jit(solution)/shard_map/ppermute | solution.py:338
  107.5 2.1 %shard_map.111 = (bf16[256,128]{1,0:T(8,128)(2,1)}, f32[8,128]{1,0:T(8,128)S(1)}) custom-call(bf16[256,256]{1,0:T(8,128)(2,1)S(1)} %collective-permute-done.2.refs_2_.refs_0_, bf16[256,256]{1,0:T(8,128)(2,1)S(1)} %collective-permute-done.3.refs_3_.refs_1_, bf16[256,256]{1,0:T(8,128)(2,1)S(1)} %get-tuple-element.16.refs_2_, bf16[3456,256]{1,0:T(8,128)(2,1)S(1)} %copy-done, ...), custom_call_target="tpu_custom_call" | custom-call | flops 452984832 | bytes 2228224 | tf_op jit(solution)/shard_map/pallas_call | solution.py:33
  109.6 2.8 %collective-permute-done.8.refs_3_ = bf16[2,128,128]{2,1,0:T(8,128)(2,1)S(1)} collective-permute-done((bf16[2,128,128]{2,1,0:T(8,128)(2,1)S(1)}, bf16[2,128,128]{2,1,0:T(8,128)(2,1)S(1)}, u32[]{:S(2)}, u32[]{:S(2)}) %collective-permute-start.8) | collective-permute-done | bytes 65568 | tf_op jit(solution)/shard_map/ppermute | solution.py:338
  112.4 1.3 shard_map.112
  113.8 9.6 %all_to_all.35.refs_0_ = bf16[8,112,128]{2,1,0:T(8,128)(2,1)S(1)} all-to-all(bf16[8,112,128]{2,1,0:T(8,128)(2,1)S(1)} %shard_map.112), channel_id=1, replica_groups=mesh['y'=4,'zh'=2,'zg'=2,'zl'=4,'x'=4,'c'=2] {'x','c'}, dimensions={0} | all-to-all | bytes 458752 | tf_op jit(solution)/shard_map/all_to_all | solution.py:57
  123.4 7.1 %all_to_all.36.refs_0_ = bf16[4,112,128]{2,1,0:T(8,128)(2,1)S(1)} all-to-all(bf16[4,112,128]{2,1,0:T(8,128)(2,1)S(1)} %shard_map.113), channel_id=1, replica_groups=mesh['y'=4,'zh'=2,'zg'=2,'zl'=4,'x'=4,'c'=2] {'y'}, dimensions={0} | all-to-all | bytes 229376 | tf_op jit(solution)/shard_map/all_to_all | solution.py:57
  (27 shorter events, 2.3 us)
Async XLA Ops:
  0.6 9.7 %copy-start.4 = (bf16[1,432,54]{1,2,0:T(8,128)(2,1)S(1)}, bf16[1,432,54]{1,2,0:T(8,128)(2,1)}, u32[]{:S(2)}) copy-start(bf16[1,432,54]{1,2,0:T(8,128)(2,1)} %param.13) | copy-start | bytes 139972
  0.6 9.7 %copy-start.7 = (f32[54]{0:T(128)S(1)}, f32[54]{0:T(128)}, u32[]{:S(2)}) copy-start(f32[54]{0:T(128)} %param.16) | copy-start | bytes 652
  0.7 10.7 %copy-start = (bf16[3456,256]{1,0:T(8,128)(2,1)S(1)}, bf16[3456,256]{1,0:T(8,128)(2,1)}, u32[]{:S(2)}) copy-start(bf16[3456,256]{1,0:T(8,128)(2,1)} %refs_3_.3) | copy-start | bytes 5308420
  0.7 10.7 %copy-start.2 = (bf16[1,1,16,16,256]{4,3,2,1,0:T(8,128)(2,1)S(1)}, bf16[1,1,16,16,256]{4,3,2,1,0:T(8,128)(2,1)}, u32[]{:S(2)}) copy-start(bf16[1,1,16,16,256]{4,3,2,1,0:T(8,128)(2,1)} %param.12) | copy-start | bytes 393220
  0.7 10.7 %copy-start.3 = (bf16[1,1,16,16,128]{4,3,2,1,0:T(8,128)(2,1)S(1)}, bf16[1,1,16,16,128]{4,3,2,1,0:T(8,128)(2,1)}, u32[]{:S(2)}) copy-start(bf16[1,1,16,16,128]{4,3,2,1,0:T(8,128)(2,1)} %param.9) | copy-start | bytes 196612
  0.7 10.7 %copy-start.5 = (f32[256]{0:T(256)S(1)}, f32[256]{0:T(256)}, u32[]{:S(2)}) copy-start(f32[256]{0:T(256)} %param.11) | copy-start | bytes 3076
  0.7 10.0 %collective-permute-start.1 = (bf16[256,128]{1,0:T(8,128)(2,1)}, bf16[256,128]{1,0:T(8,128)(2,1)S(1)}, u32[]{:S(2)}, u32[]{:S(2)}) collective-permute-start(bf16[256,128]{1,0:T(8,128)(2,1)} %bitcast.10), channel_id=1, source_target_pairs={{1,2},{3,4},{5,6},{7,8},{9,10},{11,12},{13,14},{15,16},{17,18},{19... | collective-permute-start | bytes 196616 | tf_op jit(solution)/shard_map/ppermute | solution.py:329
  5.3 6.0 %collective-permute-start = (bf16[256,128]{1,0:T(8,128)(2,1)}, bf16[256,128]{1,0:T(8,128)(2,1)S(1)}, u32[]{:S(2)}, u32[]{:S(2)}) collective-permute-start(bf16[256,128]{1,0:T(8,128)(2,1)} %bitcast.11), channel_id=1, source_target_pairs={{0,1},{1,0},{2,3},{3,2},{4,5},{5,4},{6,7},{7,6},{8,9},{9,8},{10,11... | collective-permute-start | bytes 196616 | tf_op jit(solution)/shard_map/ppermute | solution.py:327
  13.1 16.1 %all-to-all-start = ((bf16[8,384,128]{2,1,0:T(8,128)(2,1)}), bf16[8,384,128]{2,1,0:T(8,128)(2,1)S(1)}, u32[]{:S(2)}, u32[]{:S(2)}) async-start(bf16[8,384,128]{2,1,0:T(8,128)(2,1)} %get-tuple-element.17), calls=%async_computation | async-start | bytes 1572864 | tf_op jit(solution)/shard_map/all_to_all | solution.py:57
  16.9 59.7 %copy-start.8 = (s32[8]{0:T(128)S(1)}, s32[8]{0:T(128)}, u32[]{:S(2)}) copy-start(s32[8]{0:T(128)} %refs_0_.1) | copy-start | bytes 100
  16.9 7.5 %collective-permute-start.4 = (bf16[2,64,128]{2,1,0:T(8,128)(2,1)S(1)}, bf16[2,64,128]{2,1,0:T(8,128)(2,1)S(1)}, u32[]{:S(2)}, u32[]{:S(2)}) collective-permute-start(bf16[2,64,128]{2,1,0:T(8,128)(2,1)S(1)} %get-tuple-element.18), channel_id=1, source_target_pairs={{0,0},{8,128},{16,256},{24,384},{128,8},{136,136},{144,264},{152,3... | collective-permute-start | bytes 98312 | tf_op jit(solution)/shard_map/ppermute | solution.py:334
  17.7 8.7 %collective-permute-start.5 = (bf16[2,64,128]{2,1,0:T(8,128)(2,1)S(1)}, bf16[2,64,128]{2,1,0:T(8,128)(2,1)S(1)}, u32[]{:S(2)}, u32[]{:S(2)}) collective-permute-start(bf16[2,64,128]{2,1,0:T(8,128)(2,1)S(1)} %get-tuple-element.19), channel_id=1, source_target_pairs={{0,16},{8,144},{16,272},{24,400},{128,24},{136,152},{144,280},{152... | collective-permute-start | bytes 98312 | tf_op jit(solution)/shard_map/ppermute | solution.py:334
  31.4 16.4 %all-to-all-start.1 = ((bf16[16,56,128]{2,1,0:T(8,128)(2,1)}), bf16[16,56,128]{2,1,0:T(8,128)(2,1)S(1)}, u32[]{:S(2)}, u32[]{:S(2)}) async-start(bf16[16,56,128]{2,1,0:T(8,128)(2,1)} %get-tuple-element.20), calls=%async_computation.1 | async-start | bytes 458752 | tf_op jit(solution)/shard_map/all_to_all | solution.py:57
  39.5 6.3 %collective-permute-start.6 = (bf16[2,64,128]{2,1,0:T(8,128)(2,1)S(1)}, bf16[2,64,128]{2,1,0:T(8,128)(2,1)S(1)}, u32[]{:S(2)}, u32[]{:S(2)}) collective-permute-start(bf16[2,64,128]{2,1,0:T(8,128)(2,1)S(1)} %get-tuple-element.21), channel_id=1, source_target_pairs={{0,8},{8,0},{16,24},{24,16},{1,9},{9,1},{17,25},{25,17},{2,10},{10... | collective-permute-start | bytes 98312 | tf_op jit(solution)/shard_map/ppermute | solution.py:338
  48.5 28.2 %all-to-all-start.2 = ((bf16[4,272,128]{2,1,0:T(8,128)(2,1)}), bf16[4,272,128]{2,1,0:T(8,128)(2,1)S(1)}, u32[]{:S(2)}, u32[]{:S(2)}) async-start(bf16[4,272,128]{2,1,0:T(8,128)(2,1)} %shard_map.108), calls=%async_computation.2 | async-start | bytes 557056 | tf_op jit(solution)/shard_map/all_to_all | solution.py:57
  60.6 7.7 %collective-permute-start.3 = (bf16[256,256]{1,0:T(8,128)(2,1)S(1)}, bf16[256,256]{1,0:T(8,128)(2,1)S(1)}, u32[]{:S(2)}, u32[]{:S(2)}) collective-permute-start(bf16[256,256]{1,0:T(8,128)(2,1)S(1)} %get-tuple-element.16.refs_2_), channel_id=1, source_target_pairs={{1,2},{3,4},{5,6},{7,8},{9,10},{11,12},{13,14},{15,16},{17,18},{19... | collective-permute-start | bytes 393224 | tf_op jit(solution)/shard_map/ppermute | solution.py:329
  65.7 3.2 %collective-permute-start.2 = (bf16[256,256]{1,0:T(8,128)(2,1)S(1)}, bf16[256,256]{1,0:T(8,128)(2,1)S(1)}, u32[]{:S(2)}, u32[]{:S(2)}) collective-permute-start(bf16[256,256]{1,0:T(8,128)(2,1)S(1)} %get-tuple-element.16.refs_2_), channel_id=1, source_target_pairs={{0,1},{1,0},{2,3},{3,2},{4,5},{5,4},{6,7},{7,6},{8,9},{9,8},{10,11... | collective-permute-start | bytes 393224 | tf_op jit(solution)/shard_map/ppermute | solution.py:327
  78.1 21.2 %all-to-all-start.3 = ((bf16[32,56,128]{2,1,0:T(8,128)(2,1)}), bf16[32,56,128]{2,1,0:T(8,128)(2,1)S(1)}, u32[]{:S(2)}, u32[]{:S(2)}) async-start(bf16[32,56,128]{2,1,0:T(8,128)(2,1)} %get-tuple-element.22), calls=%async_computation.3 | async-start | bytes 917504 | tf_op jit(solution)/shard_map/all_to_all | solution.py:57
  88.4 8.2 %collective-permute-start.7 = (bf16[2,128,128]{2,1,0:T(8,128)(2,1)S(1)}, bf16[2,128,128]{2,1,0:T(8,128)(2,1)S(1)}, u32[]{:S(2)}, u32[]{:S(2)}) collective-permute-start(bf16[2,128,128]{2,1,0:T(8,128)(2,1)S(1)} %get-tuple-element.25), channel_id=1, source_target_pairs={{0,16},{8,24},{16,0},{24,8},{1,17},{9,25},{17,1},{25,9},{2,18},{10... | collective-permute-start | bytes 196616 | tf_op jit(solution)/shard_map/ppermute | solution.py:338
  99.3 13.1 %copy-start.1 = (f32[256,256]{1,0:T(8,128)S(1)}, f32[256,256]{1,0:T(8,128)}, u32[]{:S(2)}) copy-start(f32[256,256]{1,0:T(8,128)} %refs_4_.1) | copy-start | bytes 786436
  99.3 13.1 %copy-start.6 = (f32[256]{0:T(256)S(1)}, f32[256]{0:T(256)}, u32[]{:S(2)}) copy-start(f32[256]{0:T(256)} %param.17) | copy-start | bytes 3076
  100.3 12.1 %all-to-all-start.4 = ((bf16[4,224,128]{2,1,0:T(8,128)(2,1)}), bf16[4,224,128]{2,1,0:T(8,128)(2,1)S(1)}, u32[]{:S(2)}, u32[]{:S(2)}) async-start(bf16[4,224,128]{2,1,0:T(8,128)(2,1)} %get-tuple-element.28), calls=%async_computation.4 | async-start | bytes 458752 | tf_op jit(solution)/shard_map/all_to_all | solution.py:57
  104.1 8.3 %collective-permute-start.8 = (bf16[2,128,128]{2,1,0:T(8,128)(2,1)S(1)}, bf16[2,128,128]{2,1,0:T(8,128)(2,1)S(1)}, u32[]{:S(2)}, u32[]{:S(2)}) collective-permute-start(bf16[2,128,128]{2,1,0:T(8,128)(2,1)S(1)} %get-tuple-element.26.refs_4_), channel_id=1, source_target_pairs={{0,8},{8,0},{16,24},{24,16},{1,9},{9,1},{17,25},{25,17},{2,10},{10... | collective-permute-start | bytes 196616 | tf_op jit(solution)/shard_map/ppermute | solution.py:338

commit v14 on v12

--- a/solution.py
+++ b/solution.py
@@ -149,7 +149,7 @@
         pieces.append(got_ref[plane, at : at + 32].astype(F32))
         pieces.append(got_ref[plane, at + 32 : at + 64].astype(F32))
     acts = jnp.concatenate(pieces, axis=1)
-    lane = iota((32, 2560), 1)
+    lane = iota((8, 2560), 1)
     x = lane & 15
     y = (lane >> 4) & 15
     for b in range(3):
@@ -157,7 +157,8 @@
             step = 16 * (b - 1) + (c - 1)
             turned = pltpu.roll(acts, (-step) % 2560, 1) if step else acts
             inside = (x + c >= 1) & (x + c < 17) & (y + b >= 1) & (y + b < 17)
-            moved[32 * (3 * b + c) : 32 * (3 * b + c) + 32, :] = jnp.where(inside, turned, 0.0).astype(BF16)
+            kept = jnp.where(inside[None], turned.reshape(4, 8, 2560), 0.0).reshape(32, 2560)
+            moved[32 * (3 * b + c) : 32 * (3 * b + c) + 32, :] = kept.astype(BF16)
     for e in range(8):
         deltas[256 * e : 256 * e + 256, :] = got_ref[e, 128:]
     for a in range(3):
@@ -283,11 +284,11 @@
 def over_xc_body(got_ref, out_ref):
     total = sum(got_ref[i].astype(F32) for i in range(8))
     for to in range(4):
-        out_ref[to] = total
+        out_ref[to] = total.astype(BF16)
 
 
 def last_body(got_ref, out_ref):
-    total = (got_ref[0] + got_ref[1]) + (got_ref[2] + got_ref[3])
+    total = sum(got_ref[i].astype(F32) for i in range(4))
     out_ref[...] = jnp.concatenate([total[:54], total[56:110]], axis=1)
 
 
@@ -389,7 +390,7 @@
         [shape((32, 56, 128), BF16), shape((8, 128, 128), BF16)] + [shape((2, 128, 128), BF16)] * 2,
         (panel_owner,),
         (exchange(part, ("zh", "zg")),),
-        after=(inside, outside),
+        after=(outside,),
         scratch=[pltpu.VMEM((4, 280, 128), F32), pltpu.VMEM((4, 4, 64, 128), BF16)],
     )
     there = across(there, 2)
@@ -413,7 +414,7 @@
             dma((2,)),
         ],
     )
-    part = call(over_xc_body, shape((4, 112, 128), F32), arrays=(exchange(part, XC),))
+    part = call(over_xc_body, shape((4, 112, 128), BF16), arrays=(exchange(part, XC),), after=(inside,))
     data, token = call(
         data_grad_body,
         [shape((256, 128), BF16), shape((8, 128), F32)],

time: 134 us -> 135 us (level)
  blocking collectives: 9.64 us -> 0 us
  waiting for transfers between devices: 34.3 us -> 39.6 us
  starting transfers between devices: 76.6 us -> 80.5 us
    all_to_all x1 -> x0, blocking collectives: 9.64 us -> none  [exchange(): return lax.all_to_all(x, axes, 0, 0)]
    all_to_all x6 -> x7, starting transfers between devices: 41.6 us -> 45.3 us  [exchange(): return lax.all_to_all(x, axes, 0, 0)]
    all_to_all x6 -> x7, waiting for transfers between devices: 19 us -> 21.3 us  [exchange(): return lax.all_to_all(x, axes, 0, 0)]
    ppermute x2, waiting for transfers between devices: 0.71 us -> 2.64 us  [neighbours(): lax.ppermute(block, SPACE, pairs + [(j, i) for i, j in pairs])]
  transfers between devices with their start and end apart: 15 -> 16, of which waited for: 12 -> 13; matrix products, arithmetic and copies ran while one was open for 0% -> 0% of each run, Pallas kernels for 2% -> 2%
where the time goes in v14:
time: 135 us; the launch traced here: 134 us
  starting transfers between devices  80.5 us (60%)
  waiting for transfers between devices  39.6 us (29%)
  Pallas kernels  12.8 us (9%)
    all_to_all x7, starting transfers between devices, exchange(): return lax.all_to_all(x, axes, 0, 0)  45.3 us
    all_to_all x7, waiting for transfers between devices, exchange(): return lax.all_to_all(x, axes, 0, 0)  21.3 us
    pallas_call x11, Pallas kernels, call(): pl.pallas_call(kernel, out_shape=out_shape, in_specs=[SMEM] * len(scalars...  12.8 us
    ppermute x3, waiting for transfers between devices, across(): return lax.ppermute(block, 'zl', [(i, i ^ k) for i in range(4)])  11.8 us
    ppermute x3, starting transfers between devices, across(): return lax.ppermute(block, 'zl', [(i, i ^ k) for i in range(4)])  11.1 us
    ppermute x2, starting transfers between devices, neighbours(): lax.ppermute(block, SPACE, pairs + [(j, i) for i, j in pairs])  9.68 us
    ppermute x2, starting transfers between devices, turned(): return lax.ppermute(block, ('y', 'zl'), pairs)  7.46 us
    ppermute x2, starting transfers between devices, neighbours(): inside = lax.ppermute(block, 'c', [(0, 1), (1, 0)])  6.96 us
  transfers between devices with their start and end apart: 16, of which 13 were waited for; matrix products, arithmetic and copies ran while one was open for 0% of the time, Pallas kernels for 2%

profile of v14, /device:TPU:1, one launch (start us, length us, event | category | flops | bytes accessed | tf_op | source)
XLA Modules:
  0.0 133.9 jit_solution(12470384753860088975)
XLA Ops:
  0.7 4.6 %collective-permute-start.1 = (bf16[256,128]{1,0:T(8,128)(2,1)}, bf16[256,128]{1,0:T(8,128)(2,1)S(1)}, u32[]{:S(2)}, u32[]{:S(2)}) collective-permute-start(bf16[256,128]{1,0:T(8,128)(2,1)} %bitcast.10), channel_id=1, source_target_pairs={{1,2},{3,4},{5,6},{7,8},{9,10},{11,12},{13,14},{15,16},{17,18},{19... | collective-permute-start | bytes 196616 | tf_op jit(solution)/shard_map/ppermute | solution.py:329
  5.3 4.9 %collective-permute-start = (bf16[256,128]{1,0:T(8,128)(2,1)}, bf16[256,128]{1,0:T(8,128)(2,1)S(1)}, u32[]{:S(2)}, u32[]{:S(2)}) collective-permute-start(bf16[256,128]{1,0:T(8,128)(2,1)} %bitcast.11), channel_id=1, source_target_pairs={{0,1},{1,0},{2,3},{3,2},{4,5},{5,4},{6,7},{7,6},{8,9},{9,8},{10,11... | collective-permute-start | bytes 196616 | tf_op jit(solution)/shard_map/ppermute | solution.py:327
  11.4 1.7 %shard_map.106 = (bf16[256,256]{1,0:T(8,128)(2,1)S(1)}, bf16[8,384,128]{2,1,0:T(8,128)(2,1)}, bf16[2,64,128]{2,1,0:T(8,128)(2,1)S(1)}, bf16[2,64,128]{2,1,0:T(8,128)(2,1)S(1)}) custom-call(bf16[256,128]{1,0:T(8,128)(2,1)S(1)} %collective-permute-done.refs_0_, bf16[256,128]{1,0:T(8,128)(2,1)S(1)} %collective-permute-done.1.refs_1_, ...), custom_call_target="tpu_custom_call" | custom-call | flops 452984832 | bytes 2163712 | tf_op jit(solution)/shard_map/pallas_call | solution.py:33
  13.1 3.8 %all-to-all-start = ((bf16[8,384,128]{2,1,0:T(8,128)(2,1)}), bf16[8,384,128]{2,1,0:T(8,128)(2,1)S(1)}, u32[]{:S(2)}, u32[]{:S(2)}) async-start(bf16[8,384,128]{2,1,0:T(8,128)(2,1)} %get-tuple-element.17), calls=%async_computation | async-start | bytes 1572864 | tf_op jit(solution)/shard_map/all_to_all | solution.py:57
  17.7 6.7 %collective-permute-start.5 = (bf16[2,64,128]{2,1,0:T(8,128)(2,1)S(1)}, bf16[2,64,128]{2,1,0:T(8,128)(2,1)S(1)}, u32[]{:S(2)}, u32[]{:S(2)}) collective-permute-start(bf16[2,64,128]{2,1,0:T(8,128)(2,1)S(1)} %get-tuple-element.19), channel_id=1, source_target_pairs={{0,16},{8,144},{16,272},{24,400},{128,24},{136,152},{144,280},{152... | collective-permute-start | bytes 98312 | tf_op jit(solution)/shard_map/ppermute | solution.py:334
  24.4 2.0 %collective-permute-done.5.refs_2_ = bf16[2,64,128]{2,1,0:T(8,128)(2,1)S(1)} collective-permute-done((bf16[2,64,128]{2,1,0:T(8,128)(2,1)S(1)}, bf16[2,64,128]{2,1,0:T(8,128)(2,1)S(1)}, u32[]{:S(2)}, u32[]{:S(2)}) %collective-permute-start.5) | collective-permute-done | bytes 32800 | tf_op jit(solution)/shard_map/ppermute | solution.py:334
  26.4 2.9 %all-to-all-done.refs_0_ = bf16[8,384,128]{2,1,0:T(8,128)(2,1)S(1)} async-done(((bf16[8,384,128]{2,1,0:T(8,128)(2,1)}), bf16[8,384,128]{2,1,0:T(8,128)(2,1)S(1)}, u32[]{:S(2)}, u32[]{:S(2)}) %all-to-all-start) | async-done | bytes 786464 | tf_op jit(solution)/shard_map/all_to_all | solution.py:57
  29.2 2.1 %shard_map.107 = (bf16[16,56,128]{2,1,0:T(8,128)(2,1)}, bf16[2,64,128]{2,1,0:T(8,128)(2,1)S(1)}) custom-call(bf16[8,384,128]{2,1,0:T(8,128)(2,1)S(1)} %all-to-all-done.refs_0_, bf16[2,64,128]{2,1,0:T(8,128)(2,1)S(1)} %collective-permute-done.4.refs_1_, bf16[2,64,128]{2,1,0:T(8,128)(2,1)S(1)} %collective-permute-done.5.refs_2_), custom_call_target="tpu_custom_call" | custom-call | flops 452984832 | bytes 851968 | tf_op jit(solution)/shard_map/pallas_call | solution.py:33
  31.4 8.1 %all-to-all-start.1 = ((bf16[16,56,128]{2,1,0:T(8,128)(2,1)}), bf16[16,56,128]{2,1,0:T(8,128)(2,1)S(1)}, u32[]{:S(2)}, u32[]{:S(2)}) async-start(bf16[16,56,128]{2,1,0:T(8,128)(2,1)} %get-tuple-element.20), calls=%async_computation.1 | async-start | bytes 458752 | tf_op jit(solution)/shard_map/all_to_all | solution.py:57
  39.5 3.4 %collective-permute-start.6 = (bf16[2,64,128]{2,1,0:T(8,128)(2,1)S(1)}, bf16[2,64,128]{2,1,0:T(8,128)(2,1)S(1)}, u32[]{:S(2)}, u32[]{:S(2)}) collective-permute-start(bf16[2,64,128]{2,1,0:T(8,128)(2,1)S(1)} %get-tuple-element.21), channel_id=1, source_target_pairs={{0,8},{8,0},{16,24},{24,16},{1,9},{9,1},{17,25},{25,17},{2,10},{10... | collective-permute-start | bytes 98312 | tf_op jit(solution)/shard_map/ppermute | solution.py:338
  42.9 3.1 %collective-permute-done.6.refs_3_ = bf16[2,64,128]{2,1,0:T(8,128)(2,1)S(1)} collective-permute-done((bf16[2,64,128]{2,1,0:T(8,128)(2,1)S(1)}, bf16[2,64,128]{2,1,0:T(8,128)(2,1)S(1)}, u32[]{:S(2)}, u32[]{:S(2)}) %collective-permute-start.6) | collective-permute-done | bytes 32800 | tf_op jit(solution)/shard_map/ppermute | solution.py:338
  46.0 1.8 %all-to-all-done.1.refs_0_ = bf16[16,56,128]{2,1,0:T(8,128)(2,1)S(1)} async-done(((bf16[16,56,128]{2,1,0:T(8,128)(2,1)}), bf16[16,56,128]{2,1,0:T(8,128)(2,1)S(1)}, u32[]{:S(2)}, u32[]{:S(2)}) %all-to-all-start.1) | async-done | bytes 229408 | tf_op jit(solution)/shard_map/all_to_all | solution.py:57
  48.5 12.1 %all-to-all-start.2 = ((bf16[4,272,128]{2,1,0:T(8,128)(2,1)}), bf16[4,272,128]{2,1,0:T(8,128)(2,1)S(1)}, u32[]{:S(2)}, u32[]{:S(2)}) async-start(bf16[4,272,128]{2,1,0:T(8,128)(2,1)} %shard_map.108), calls=%async_computation.2 | async-start | bytes 557056 | tf_op jit(solution)/shard_map/all_to_all | solution.py:57
  60.6 5.0 %collective-permute-start.3 = (bf16[256,256]{1,0:T(8,128)(2,1)S(1)}, bf16[256,256]{1,0:T(8,128)(2,1)S(1)}, u32[]{:S(2)}, u32[]{:S(2)}) collective-permute-start(bf16[256,256]{1,0:T(8,128)(2,1)S(1)} %get-tuple-element.16.refs_2_), channel_id=1, source_target_pairs={{1,2},{3,4},{5,6},{7,8},{9,10},{11,12},{13,14},{15,16},{17,18},{19... | collective-permute-start | bytes 393224 | tf_op jit(solution)/shard_map/ppermute | solution.py:329
  65.7 2.6 %collective-permute-done.3.refs_2_.refs_1_ = bf16[256,256]{1,0:T(8,128)(2,1)S(1)} collective-permute-done((bf16[256,256]{1,0:T(8,128)(2,1)S(1)}, bf16[256,256]{1,0:T(8,128)(2,1)S(1)}, u32[]{:S(2)}, u32[]{:S(2)}) %collective-permute-start.3) | collective-permute-done | bytes 131104 | tf_op jit(solution)/shard_map/ppermute | solution.py:329
  68.3 8.4 %all-to-all-done.2.refs_1_ = bf16[4,272,128]{2,1,0:T(8,128)(2,1)S(1)} async-done(((bf16[4,272,128]{2,1,0:T(8,128)(2,1)}), bf16[4,272,128]{2,1,0:T(8,128)(2,1)S(1)}, u32[]{:S(2)}, u32[]{:S(2)}) %all-to-all-start.2) | async-done | bytes 278560 | tf_op jit(solution)/shard_map/all_to_all | solution.py:57
  76.7 1.4 %shard_map.109 = (bf16[32,56,128]{2,1,0:T(8,128)(2,1)}, bf16[8,128,128]{2,1,0:T(8,128)(2,1)S(1)}, bf16[2,128,128]{2,1,0:T(8,128)(2,1)S(1)}, bf16[2,128,128]{2,1,0:T(8,128)(2,1)S(1)}) custom-call(s32[8]{0:T(128)S(1)} %copy-done.8, bf16[4,272,128]{2,1,0:T(8,128)(2,1)S(1)} %all-to-all-done.2.refs_1_, bf16[256,256]{1,0:T(8,128)(2,1)S(1)} %collective-permute-done.3.refs_2_.refs_1_), custom_call_target="tpu_custom_call" | custom-call | bytes 409632 | tf_op jit(solution)/shard_map/pallas_call | solution.py:33
  78.1 10.3 %all-to-all-start.3 = ((bf16[32,56,128]{2,1,0:T(8,128)(2,1)}), bf16[32,56,128]{2,1,0:T(8,128)(2,1)S(1)}, u32[]{:S(2)}, u32[]{:S(2)}) async-start(bf16[32,56,128]{2,1,0:T(8,128)(2,1)} %get-tuple-element.22), calls=%async_computation.3 | async-start | bytes 917504 | tf_op jit(solution)/shard_map/all_to_all | solution.py:57
  88.5 4.4 %collective-permute-start.7 = (bf16[2,128,128]{2,1,0:T(8,128)(2,1)S(1)}, bf16[2,128,128]{2,1,0:T(8,128)(2,1)S(1)}, u32[]{:S(2)}, u32[]{:S(2)}) collective-permute-start(bf16[2,128,128]{2,1,0:T(8,128)(2,1)S(1)} %get-tuple-element.25), channel_id=1, source_target_pairs={{0,16},{8,24},{16,0},{24,8},{1,17},{9,25},{17,1},{25,9},{2,18},{10... | collective-permute-start | bytes 196616 | tf_op jit(solution)/shard_map/ppermute | solution.py:338
  92.8 3.7 %collective-permute-done.7.refs_3_.refs_2_ = bf16[2,128,128]{2,1,0:T(8,128)(2,1)S(1)} collective-permute-done((bf16[2,128,128]{2,1,0:T(8,128)(2,1)S(1)}, bf16[2,128,128]{2,1,0:T(8,128)(2,1)S(1)}, u32[]{:S(2)}, u32[]{:S(2)}) %collective-permute-start.7) | collective-permute-done | bytes 65568 | tf_op jit(solution)/shard_map/ppermute | solution.py:338
  96.6 2.7 %all-to-all-done.3.refs_0_ = bf16[32,56,128]{2,1,0:T(8,128)(2,1)S(1)} async-done(((bf16[32,56,128]{2,1,0:T(8,128)(2,1)}), bf16[32,56,128]{2,1,0:T(8,128)(2,1)S(1)}, u32[]{:S(2)}, u32[]{:S(2)}) %all-to-all-start.3) | async-done | bytes 458784 | tf_op jit(solution)/shard_map/all_to_all | solution.py:57
  100.4 3.7 %all-to-all-start.4 = ((bf16[4,224,128]{2,1,0:T(8,128)(2,1)}), bf16[4,224,128]{2,1,0:T(8,128)(2,1)S(1)}, u32[]{:S(2)}, u32[]{:S(2)}) async-start(bf16[4,224,128]{2,1,0:T(8,128)(2,1)} %get-tuple-element.26), calls=%async_computation.4 | async-start | bytes 458752 | tf_op jit(solution)/shard_map/all_to_all | solution.py:57
  104.1 3.4 %collective-permute-start.8 = (bf16[2,128,128]{2,1,0:T(8,128)(2,1)S(1)}, bf16[2,128,128]{2,1,0:T(8,128)(2,1)S(1)}, u32[]{:S(2)}, u32[]{:S(2)}) collective-permute-start(bf16[2,128,128]{2,1,0:T(8,128)(2,1)S(1)} %get-tuple-element.27), channel_id=1, source_target_pairs={{0,8},{8,0},{16,24},{24,16},{1,9},{9,1},{17,25},{25,17},{2,10},{10... | collective-permute-start | bytes 196616 | tf_op jit(solution)/shard_map/ppermute | solution.py:338
  107.5 5.0 %collective-permute-done.8.refs_3_ = bf16[2,128,128]{2,1,0:T(8,128)(2,1)S(1)} collective-permute-done((bf16[2,128,128]{2,1,0:T(8,128)(2,1)S(1)}, bf16[2,128,128]{2,1,0:T(8,128)(2,1)S(1)}, u32[]{:S(2)}, u32[]{:S(2)}) %collective-permute-start.8) | collective-permute-done | bytes 65568 | tf_op jit(solution)/shard_map/ppermute | solution.py:338
  112.4 2.0 %shard_map.111 = bf16[8,112,128]{2,1,0:T(8,128)(2,1)} custom-call(bf16[4,224,128]{2,1,0:T(8,128)(2,1)S(1)} %all-to-all-done.4.refs_0_, bf16[2,128,128]{2,1,0:T(8,128)(2,1)S(1)} %get-tuple-element.24.refs_2_.refs_1_, bf16[2,128,128]{2,1,0:T(8,128)(2,1)S(1)} %collective-permute-done.7.refs_3_.refs_2_, bf16[2,128,128]{2,1,0:T(8,128)(2,1)S(1)} %collective-permute-done.8.refs_3_, ...), custom_call_target="tpu_custom_call" | custom-call | bytes 689152 | tf_op jit(solution)/shard_map/pallas_call | solution.py:33
  114.4 3.9 %all-to-all-start.5 = ((bf16[8,112,128]{2,1,0:T(8,128)(2,1)}), bf16[8,112,128]{2,1,0:T(8,128)(2,1)S(1)}, u32[]{:S(2)}, u32[]{:S(2)}) async-start(bf16[8,112,128]{2,1,0:T(8,128)(2,1)} %shard_map.111), calls=%async_computation.5 | async-start | bytes 458752 | tf_op jit(solution)/shard_map/all_to_all | solution.py:57
  118.3 2.0 %collective-permute-start.2 = (bf16[256,256]{1,0:T(8,128)(2,1)S(1)}, bf16[256,256]{1,0:T(8,128)(2,1)S(1)}, u32[]{:S(2)}, u32[]{:S(2)}) collective-permute-start(bf16[256,256]{1,0:T(8,128)(2,1)S(1)} %get-tuple-element.16.refs_2_), channel_id=1, source_target_pairs={{0,1},{1,0},{2,3},{3,2},{4,5},{5,4},{6,7},{7,6},{8,9},{9,8},{10,11... | collective-permute-start | bytes 393224 | tf_op jit(solution)/shard_map/ppermute | solution.py:327
  120.4 1.2 collective-permute-done.2.refs_1_.refs_0_
  121.6 3.0 %all-to-all-done.5.refs_0_ = bf16[8,112,128]{2,1,0:T(8,128)(2,1)S(1)} async-done(((bf16[8,112,128]{2,1,0:T(8,128)(2,1)}), bf16[8,112,128]{2,1,0:T(8,128)(2,1)S(1)}, u32[]{:S(2)}, u32[]{:S(2)}) %all-to-all-start.5) | async-done | bytes 229408 | tf_op jit(solution)/shard_map/all_to_all | solution.py:57
  125.2 3.3 %all-to-all-start.6 = ((bf16[4,112,128]{2,1,0:T(8,128)(2,1)}), bf16[4,112,128]{2,1,0:T(8,128)(2,1)S(1)}, u32[]{:S(2)}, u32[]{:S(2)}) async-start(bf16[4,112,128]{2,1,0:T(8,128)(2,1)} %shard_map.112.refs_4_), calls=%async_computation.6 | async-start | bytes 229376 | tf_op jit(solution)/shard_map/all_to_all | solution.py:57
  128.6 2.1 %shard_map.113 = (bf16[256,128]{1,0:T(8,128)(2,1)}, f32[8,128]{1,0:T(8,128)S(1)}) custom-call(bf16[256,256]{1,0:T(8,128)(2,1)S(1)} %collective-permute-done.2.refs_1_.refs_0_, bf16[256,256]{1,0:T(8,128)(2,1)S(1)} %collective-permute-done.3.refs_2_.refs_1_, bf16[256,256]{1,0:T(8,128)(2,1)S(1)} %get-tuple-element.16.refs_2_, bf16[3456,256]{1,0:T(8,128)(2,1)S(1)} %copy-done, ...), custom_call_target="tpu_custom_call" | custom-call | flops 452984832 | bytes 2277376 | tf_op jit(solution)/shard_map/pallas_call | solution.py:33
  130.7 2.6 %all-to-all-done.6.refs_0_ = bf16[4,112,128]{2,1,0:T(8,128)(2,1)S(1)} async-done(((bf16[4,112,128]{2,1,0:T(8,128)(2,1)}), bf16[4,112,128]{2,1,0:T(8,128)(2,1)S(1)}, u32[]{:S(2)}, u32[]{:S(2)}) %all-to-all-start.6) | async-done | bytes 114720 | tf_op jit(solution)/shard_map/all_to_all | solution.py:57
  (29 shorter events, 5.0 us)
Async XLA Ops:
  0.6 9.7 %copy-start.4 = (bf16[1,432,54]{1,2,0:T(8,128)(2,1)S(1)}, bf16[1,432,54]{1,2,0:T(8,128)(2,1)}, u32[]{:S(2)}) copy-start(bf16[1,432,54]{1,2,0:T(8,128)(2,1)} %param.13) | copy-start | bytes 139972
  0.6 9.7 %copy-start.7 = (f32[54]{0:T(128)S(1)}, f32[54]{0:T(128)}, u32[]{:S(2)}) copy-start(f32[54]{0:T(128)} %param.16) | copy-start | bytes 652
  0.7 10.7 %copy-start = (bf16[3456,256]{1,0:T(8,128)(2,1)S(1)}, bf16[3456,256]{1,0:T(8,128)(2,1)}, u32[]{:S(2)}) copy-start(bf16[3456,256]{1,0:T(8,128)(2,1)} %refs_3_.3) | copy-start | bytes 5308420
  0.7 10.7 %copy-start.2 = (bf16[1,1,16,16,256]{4,3,2,1,0:T(8,128)(2,1)S(1)}, bf16[1,1,16,16,256]{4,3,2,1,0:T(8,128)(2,1)}, u32[]{:S(2)}) copy-start(bf16[1,1,16,16,256]{4,3,2,1,0:T(8,128)(2,1)} %param.12) | copy-start | bytes 393220
  0.7 10.7 %copy-start.3 = (bf16[1,1,16,16,128]{4,3,2,1,0:T(8,128)(2,1)S(1)}, bf16[1,1,16,16,128]{4,3,2,1,0:T(8,128)(2,1)}, u32[]{:S(2)}) copy-start(bf16[1,1,16,16,128]{4,3,2,1,0:T(8,128)(2,1)} %param.9) | copy-start | bytes 196612
  0.7 10.7 %copy-start.5 = (f32[256]{0:T(256)S(1)}, f32[256]{0:T(256)}, u32[]{:S(2)}) copy-start(f32[256]{0:T(256)} %param.11) | copy-start | bytes 3076
  0.7 10.0 %collective-permute-start.1 = (bf16[256,128]{1,0:T(8,128)(2,1)}, bf16[256,128]{1,0:T(8,128)(2,1)S(1)}, u32[]{:S(2)}, u32[]{:S(2)}) collective-permute-start(bf16[256,128]{1,0:T(8,128)(2,1)} %bitcast.10), channel_id=1, source_target_pairs={{1,2},{3,4},{5,6},{7,8},{9,10},{11,12},{13,14},{15,16},{17,18},{19... | collective-permute-start | bytes 196616 | tf_op jit(solution)/shard_map/ppermute | solution.py:329
  5.3 6.0 %collective-permute-start = (bf16[256,128]{1,0:T(8,128)(2,1)}, bf16[256,128]{1,0:T(8,128)(2,1)S(1)}, u32[]{:S(2)}, u32[]{:S(2)}) collective-permute-start(bf16[256,128]{1,0:T(8,128)(2,1)} %bitcast.11), channel_id=1, source_target_pairs={{0,1},{1,0},{2,3},{3,2},{4,5},{5,4},{6,7},{7,6},{8,9},{9,8},{10,11... | collective-permute-start | bytes 196616 | tf_op jit(solution)/shard_map/ppermute | solution.py:327
  13.1 16.1 %all-to-all-start = ((bf16[8,384,128]{2,1,0:T(8,128)(2,1)}), bf16[8,384,128]{2,1,0:T(8,128)(2,1)S(1)}, u32[]{:S(2)}, u32[]{:S(2)}) async-start(bf16[8,384,128]{2,1,0:T(8,128)(2,1)} %get-tuple-element.17), calls=%async_computation | async-start | bytes 1572864 | tf_op jit(solution)/shard_map/all_to_all | solution.py:57
  16.9 59.8 %copy-start.8 = (s32[8]{0:T(128)S(1)}, s32[8]{0:T(128)}, u32[]{:S(2)}) copy-start(s32[8]{0:T(128)} %refs_0_.1) | copy-start | bytes 100
  16.9 7.5 %collective-permute-start.4 = (bf16[2,64,128]{2,1,0:T(8,128)(2,1)S(1)}, bf16[2,64,128]{2,1,0:T(8,128)(2,1)S(1)}, u32[]{:S(2)}, u32[]{:S(2)}) collective-permute-start(bf16[2,64,128]{2,1,0:T(8,128)(2,1)S(1)} %get-tuple-element.18), channel_id=1, source_target_pairs={{0,0},{8,128},{16,256},{24,384},{128,8},{136,136},{144,264},{152,3... | collective-permute-start | bytes 98312 | tf_op jit(solution)/shard_map/ppermute | solution.py:334
  17.7 8.7 %collective-permute-start.5 = (bf16[2,64,128]{2,1,0:T(8,128)(2,1)S(1)}, bf16[2,64,128]{2,1,0:T(8,128)(2,1)S(1)}, u32[]{:S(2)}, u32[]{:S(2)}) collective-permute-start(bf16[2,64,128]{2,1,0:T(8,128)(2,1)S(1)} %get-tuple-element.19), channel_id=1, source_target_pairs={{0,16},{8,144},{16,272},{24,400},{128,24},{136,152},{144,280},{152... | collective-permute-start | bytes 98312 | tf_op jit(solution)/shard_map/ppermute | solution.py:334
  31.4 16.4 %all-to-all-start.1 = ((bf16[16,56,128]{2,1,0:T(8,128)(2,1)}), bf16[16,56,128]{2,1,0:T(8,128)(2,1)S(1)}, u32[]{:S(2)}, u32[]{:S(2)}) async-start(bf16[16,56,128]{2,1,0:T(8,128)(2,1)} %get-tuple-element.20), calls=%async_computation.1 | async-start | bytes 458752 | tf_op jit(solution)/shard_map/all_to_all | solution.py:57
  39.4 73.0 %copy-start.1 = (f32[256,256]{1,0:T(8,128)S(1)}, f32[256,256]{1,0:T(8,128)}, u32[]{:S(2)}) copy-start(f32[256,256]{1,0:T(8,128)} %refs_4_.1) | copy-start | bytes 786436
  39.5 73.0 %copy-start.6 = (f32[256]{0:T(256)S(1)}, f32[256]{0:T(256)}, u32[]{:S(2)}) copy-start(f32[256]{0:T(256)} %param.17) | copy-start | bytes 3076
  39.5 6.5 %collective-permute-start.6 = (bf16[2,64,128]{2,1,0:T(8,128)(2,1)S(1)}, bf16[2,64,128]{2,1,0:T(8,128)(2,1)S(1)}, u32[]{:S(2)}, u32[]{:S(2)}) collective-permute-start(bf16[2,64,128]{2,1,0:T(8,128)(2,1)S(1)} %get-tuple-element.21), channel_id=1, source_target_pairs={{0,8},{8,0},{16,24},{24,16},{1,9},{9,1},{17,25},{25,17},{2,10},{10... | collective-permute-start | bytes 98312 | tf_op jit(solution)/shard_map/ppermute | solution.py:338
  48.5 28.2 %all-to-all-start.2 = ((bf16[4,272,128]{2,1,0:T(8,128)(2,1)}), bf16[4,272,128]{2,1,0:T(8,128)(2,1)S(1)}, u32[]{:S(2)}, u32[]{:S(2)}) async-start(bf16[4,272,128]{2,1,0:T(8,128)(2,1)} %shard_map.108), calls=%async_computation.2 | async-start | bytes 557056 | tf_op jit(solution)/shard_map/all_to_all | solution.py:57
  60.6 7.7 %collective-permute-start.3 = (bf16[256,256]{1,0:T(8,128)(2,1)S(1)}, bf16[256,256]{1,0:T(8,128)(2,1)S(1)}, u32[]{:S(2)}, u32[]{:S(2)}) collective-permute-start(bf16[256,256]{1,0:T(8,128)(2,1)S(1)} %get-tuple-element.16.refs_2_), channel_id=1, source_target_pairs={{1,2},{3,4},{5,6},{7,8},{9,10},{11,12},{13,14},{15,16},{17,18},{19... | collective-permute-start | bytes 393224 | tf_op jit(solution)/shard_map/ppermute | solution.py:329
  78.1 21.2 %all-to-all-start.3 = ((bf16[32,56,128]{2,1,0:T(8,128)(2,1)}), bf16[32,56,128]{2,1,0:T(8,128)(2,1)S(1)}, u32[]{:S(2)}, u32[]{:S(2)}) async-start(bf16[32,56,128]{2,1,0:T(8,128)(2,1)} %get-tuple-element.22), calls=%async_computation.3 | async-start | bytes 917504 | tf_op jit(solution)/shard_map/all_to_all | solution.py:57
  88.5 8.1 %collective-permute-start.7 = (bf16[2,128,128]{2,1,0:T(8,128)(2,1)S(1)}, bf16[2,128,128]{2,1,0:T(8,128)(2,1)S(1)}, u32[]{:S(2)}, u32[]{:S(2)}) collective-permute-start(bf16[2,128,128]{2,1,0:T(8,128)(2,1)S(1)} %get-tuple-element.25), channel_id=1, source_target_pairs={{0,16},{8,24},{16,0},{24,8},{1,17},{9,25},{17,1},{25,9},{2,18},{10... | collective-permute-start | bytes 196616 | tf_op jit(solution)/shard_map/ppermute | solution.py:338
  100.4 12.1 %all-to-all-start.4 = ((bf16[4,224,128]{2,1,0:T(8,128)(2,1)}), bf16[4,224,128]{2,1,0:T(8,128)(2,1)S(1)}, u32[]{:S(2)}, u32[]{:S(2)}) async-start(bf16[4,224,128]{2,1,0:T(8,128)(2,1)} %get-tuple-element.26), calls=%async_computation.4 | async-start | bytes 458752 | tf_op jit(solution)/shard_map/all_to_all | solution.py:57
  104.1 8.3 %collective-permute-start.8 = (bf16[2,128,128]{2,1,0:T(8,128)(2,1)S(1)}, bf16[2,128,128]{2,1,0:T(8,128)(2,1)S(1)}, u32[]{:S(2)}, u32[]{:S(2)}) collective-permute-start(bf16[2,128,128]{2,1,0:T(8,128)(2,1)S(1)} %get-tuple-element.27), channel_id=1, source_target_pairs={{0,8},{8,0},{16,24},{24,16},{1,9},{9,1},{17,25},{25,17},{2,10},{10... | collective-permute-start | bytes 196616 | tf_op jit(solution)/shard_map/ppermute | solution.py:338
  114.4 10.1 %all-to-all-start.5 = ((bf16[8,112,128]{2,1,0:T(8,128)(2,1)}), bf16[8,112,128]{2,1,0:T(8,128)(2,1)S(1)}, u32[]{:S(2)}, u32[]{:S(2)}) async-start(bf16[8,112,128]{2,1,0:T(8,128)(2,1)} %shard_map.111), calls=%async_computation.5 | async-start | bytes 458752 | tf_op jit(solution)/shard_map/all_to_all | solution.py:57
  118.3 3.2 %collective-permute-start.2 = (bf16[256,256]{1,0:T(8,128)(2,1)S(1)}, bf16[256,256]{1,0:T(8,128)(2,1)S(1)}, u32[]{:S(2)}, u32[]{:S(2)}) collective-permute-start(bf16[256,256]{1,0:T(8,128)(2,1)S(1)} %get-tuple-element.16.refs_2_), channel_id=1, source_target_pairs={{0,1},{1,0},{2,3},{3,2},{4,5},{5,4},{6,7},{7,6},{8,9},{9,8},{10,11... | collective-permute-start | bytes 393224 | tf_op jit(solution)/shard_map/ppermute | solution.py:327
  125.2 8.0 %all-to-all-start.6 = ((bf16[4,112,128]{2,1,0:T(8,128)(2,1)}), bf16[4,112,128]{2,1,0:T(8,128)(2,1)S(1)}, u32[]{:S(2)}, u32[]{:S(2)}) async-start(bf16[4,112,128]{2,1,0:T(8,128)(2,1)} %shard_map.112.refs_4_), calls=%async_computation.6 | async-start | bytes 229376 | tf_op jit(solution)/shard_map/all_to_all | solution.py:57

commit v15 on v13

--- a/solution.py
+++ b/solution.py
@@ -17,8 +17,8 @@
 AXES = ("y", "zh", "zg", "zl", "x", "c")
 SIZES = (4, 2, 2, 4, 4, 2)
 SAMPLE = ("y", "zh")
-XC = ("x", "c")
-YXC = ("y", "x", "c")
+CX = ("c", "x")
+CXY = ("c", "x", "y")
 SPACE = ("zg", "zl", "x", "c")
 
 
@@ -134,7 +134,7 @@
     rim_t = planes[2 * (lax.axis_index("x") >> 1)].astype(F32).T.astype(BF16)
     for x in range(4):
         for c in range(2):
-            to = 2 * x + c
+            to = 4 * c + x
             for half in range(2):
                 lanes = slice(128 * half, 128 * half + 128)
                 rows = slice(32 * x, 32 * x + 32)
@@ -143,11 +143,15 @@
             send_ref[to, 128:] = delta[:, 128 * c : 128 * c + 128]
 
 
+def slot(e):
+    return 4 * (e % 2) + e // 2
+
+
 def weight_grad_body(got_ref, even_ref, odd_ref, out_ref, pair_ref, moved, deltas, whole):
     pieces = []
     for plane, at in [(0, 64)] + [(e, 0) for e in range(8)] + [(7, 64)]:
-        pieces.append(got_ref[plane, at : at + 32].astype(F32))
-        pieces.append(got_ref[plane, at + 32 : at + 64].astype(F32))
+        pieces.append(got_ref[slot(plane), at : at + 32].astype(F32))
+        pieces.append(got_ref[slot(plane), at + 32 : at + 64].astype(F32))
     acts = jnp.concatenate(pieces, axis=1)
     lane = iota((8, 2560), 1)
     x = lane & 15
@@ -160,7 +164,7 @@
             kept = jnp.where(inside[None], turned.reshape(4, 8, 2560), 0.0).reshape(32, 2560)
             moved[32 * (3 * b + c) : 32 * (3 * b + c) + 32, :] = kept.astype(BF16)
     for e in range(8):
-        deltas[256 * e : 256 * e + 256, :] = got_ref[e, 128:]
+        deltas[256 * e : 256 * e + 256, :] = got_ref[slot(e), 128:]
     for a in range(3):
         whole[288 * a : 288 * a + 288, :] = jnp.dot(
             moved[:, 256 * a : 256 * a + 2048], deltas[...], preferred_element_type=F32
@@ -174,7 +178,7 @@
             for e in range(2):
                 parts.append(whole[pl.ds(8 * y_to + 4 * e + z_to, 27, stride=32), :])
                 parts.append(none)
-            out_ref[4 * y_to + z_to] = jnp.concatenate(parts, axis=0).astype(BF16)
+            out_ref[4 * z_to + y_to] = jnp.concatenate(parts, axis=0).astype(BF16)
 
 
 def over_y_zl_body(got_ref, even_ref, odd_ref, pair_ref, out_ref, slices, rows):
@@ -204,7 +208,7 @@
         out_ref[to] = total
     for j in range(8):
         for zg in range(2):
-            basis_ref[j, 64 * zg : 64 * zg + 64] = slices[2 * (owner_ref[j] & 1) + zg, owner_ref[j] >> 1]
+            basis_ref[j, 64 * zg : 64 * zg + 64] = slices[2 * zg + (owner_ref[j] & 1), owner_ref[j] >> 1]
     zg, zl = lax.axis_index("zg"), lax.axis_index("zl")
     for k, ref in ((0, here_ref), (2, next_ref)):
         ref[0] = basis_ref[4 * zg + (zl ^ k)]
@@ -218,7 +222,7 @@
         for x in range(4):
             at = 28 * (8 * x + 2 * y)
             for c in range(2):
-                grads[c, at : at + 56, :] = got_ref[8 * y + 2 * x + c].astype(F32)
+                grads[c, at : at + 56, :] = got_ref[16 * c + 4 * x + y].astype(F32)
     for tap in range(27):
         for c in range(2):
             ordered[32 * tap : 32 * tap + 32, 128 * c : 128 * c + 128] = grads[c, pl.ds(tap, 32, stride=28), :]
@@ -278,7 +282,7 @@
         ordered[c, 432:, :] = jnp.zeros((8, 128), F32)
     for to in range(8):
         rows = [ordered[c, 54 * to : 54 * to + 56, :] for c in range(2)]
-        out_ref[to] = jnp.concatenate(rows, axis=0).astype(BF16)
+        out_ref[slot(to)] = jnp.concatenate(rows, axis=0).astype(BF16)
 
 
 def over_xc_body(got_ref, out_ref):
@@ -374,14 +378,14 @@
     part, pair = call(
         weight_grad_body,
         [shape((16, 56, 128), BF16), shape((2, 64, 128), BF16)],
-        arrays=(exchange(send, XC), even, odd),
+        arrays=(exchange(send, CX), even, odd),
         scratch=[pltpu.VMEM((288, 2560), BF16), pltpu.VMEM((2048, 128), BF16), pltpu.VMEM((864, 128), F32)],
         flops=2 * 864 * 2048 * 128,
     )
     part = call(
         over_y_zl_body,
         shape((4, 272, 128), BF16),
-        arrays=(exchange(part, ("y", "zl")), even, odd, across(pair, 1)),
+        arrays=(exchange(part, ("zl", "y")), even, odd, across(pair, 1)),
         scratch=[pltpu.VMEM((4, 64, 128), BF16), pltpu.VMEM((272, 128), F32)],
     )
     inside, outside = neighbours(delta)
@@ -389,7 +393,7 @@
         over_zh_zg_body,
         [shape((32, 56, 128), BF16), shape((8, 128, 128), BF16)] + [shape((2, 128, 128), BF16)] * 2,
         (panel_owner,),
-        (exchange(part, ("zh", "zg")),),
+        (exchange(part, ("zg", "zh")),),
         after=(inside, outside),
         scratch=[pltpu.VMEM((4, 280, 128), F32), pltpu.VMEM((4, 4, 64, 128), BF16)],
     )
@@ -397,7 +401,7 @@
     rotated, pair = call(
         rotate_body,
         [shape((4, 224, 128), BF16), shape((2, 128, 128), BF16)],
-        arrays=(exchange(part, YXC), basis, here, there),
+        arrays=(exchange(part, CXY), basis, here, there),
         scratch=[pltpu.VMEM((2, 896, 128), F32), pltpu.VMEM((896, 256), F32)],
     )
     data, token = call(
@@ -425,7 +429,7 @@
             dma((2,)),
         ],
     )
-    part = call(over_xc_body, shape((4, 112, 128), BF16), arrays=(exchange(part, XC),))
+    part = call(over_xc_body, shape((4, 112, 128), BF16), arrays=(exchange(part, CX),))
     update = call(last_body, shape((54, 256), F32), arrays=(exchange(part, "y"),))
     return (data.reshape(1, 1, 16, 16, 128), update)
 

time: 132 us -> 130 us (0.985)
  waiting for transfers between devices: 28.9 us -> 27 us
    ppermute x3, waiting for transfers between devices: 9.66 us -> 7.87 us  [across(): return lax.ppermute(block, 'zl', [(i, i ^ k) for i in range(4)])]
where the time goes in v15:
time: 130 us; the launch traced here: 129 us
  starting transfers between devices  73.4 us (56%)
  waiting for transfers between devices  27 us (21%)
  blocking collectives  16.7 us (13%)
  Pallas kernels  11.5 us (9%)
    all_to_all x5, starting transfers between devices, exchange(): return lax.all_to_all(x, axes, 0, 0)  37.9 us
    all_to_all x2, blocking collectives, exchange(): return lax.all_to_all(x, axes, 0, 0)  16.7 us
    all_to_all x5, waiting for transfers between devices, exchange(): return lax.all_to_all(x, axes, 0, 0)  15.1 us
    ppermute x3, starting transfers between devices, across(): return lax.ppermute(block, 'zl', [(i, i ^ k) for i in range(4)])  11.9 us
    pallas_call x11, Pallas kernels, call(): pl.pallas_call(kernel, out_shape=out_shape, in_specs=[SMEM] * len(scalars...  11.5 us
    ppermute x2, starting transfers between devices, neighbours(): lax.ppermute(block, SPACE, pairs + [(j, i) for i, j in pairs])  9.32 us
    ppermute x3, waiting for transfers between devices, across(): return lax.ppermute(block, 'zl', [(i, i ^ k) for i in range(4)])  7.87 us
    ppermute x2, starting transfers between devices, turned(): return lax.ppermute(block, ('y', 'zl'), pairs)  7.44 us
  transfers between devices with their start and end apart: 14, of which 11 were waited for; matrix products, arithmetic and copies ran while one was open for 0% of the time, Pallas kernels for 2%

profile of v15, /device:TPU:1, one launch (start us, length us, event | category | flops | bytes accessed | tf_op | source)
XLA Modules:
  0.0 129.5 jit_solution(2162938974624447455)
XLA Ops:
  0.7 4.6 %collective-permute-start.1 = (bf16[256,128]{1,0:T(8,128)(2,1)}, bf16[256,128]{1,0:T(8,128)(2,1)S(1)}, u32[]{:S(2)}, u32[]{:S(2)}) collective-permute-start(bf16[256,128]{1,0:T(8,128)(2,1)} %bitcast.10), channel_id=1, source_target_pairs={{1,2},{3,4},{5,6},{7,8},{9,10},{11,12},{13,14},{15,16},{17,18},{19... | collective-permute-start | bytes 196616 | tf_op jit(solution)/shard_map/ppermute | solution.py:333
  5.3 4.9 %collective-permute-start = (bf16[256,128]{1,0:T(8,128)(2,1)}, bf16[256,128]{1,0:T(8,128)(2,1)S(1)}, u32[]{:S(2)}, u32[]{:S(2)}) collective-permute-start(bf16[256,128]{1,0:T(8,128)(2,1)} %bitcast.11), channel_id=1, source_target_pairs={{0,1},{1,0},{2,3},{3,2},{4,5},{5,4},{6,7},{7,6},{8,9},{9,8},{10,11... | collective-permute-start | bytes 196616 | tf_op jit(solution)/shard_map/ppermute | solution.py:331
  10.7 0.7 collective-permute-done.refs_0_
  11.4 1.7 %shard_map.106 = (bf16[256,256]{1,0:T(8,128)(2,1)S(1)}, bf16[8,384,128]{2,1,0:T(8,128)(2,1)}, bf16[2,64,128]{2,1,0:T(8,128)(2,1)S(1)}, bf16[2,64,128]{2,1,0:T(8,128)(2,1)S(1)}) custom-call(bf16[256,128]{1,0:T(8,128)(2,1)S(1)} %collective-permute-done.refs_0_, bf16[256,128]{1,0:T(8,128)(2,1)S(1)} %collective-permute-done.1.refs_1_, ...), custom_call_target="tpu_custom_call" | custom-call | flops 452984832 | bytes 2163712 | tf_op jit(solution)/shard_map/pallas_call | solution.py:33
  13.1 3.8 %all-to-all-start = ((bf16[8,384,128]{2,1,0:T(8,128)(2,1)}), bf16[8,384,128]{2,1,0:T(8,128)(2,1)S(1)}, u32[]{:S(2)}, u32[]{:S(2)}) async-start(bf16[8,384,128]{2,1,0:T(8,128)(2,1)} %get-tuple-element.17), calls=%async_computation | async-start | bytes 1572864 | tf_op jit(solution)/shard_map/all_to_all | solution.py:57
  17.0 0.8 collective-permute-start.4
  17.8 6.7 %collective-permute-start.5 = (bf16[2,64,128]{2,1,0:T(8,128)(2,1)S(1)}, bf16[2,64,128]{2,1,0:T(8,128)(2,1)S(1)}, u32[]{:S(2)}, u32[]{:S(2)}) collective-permute-start(bf16[2,64,128]{2,1,0:T(8,128)(2,1)S(1)} %get-tuple-element.19), channel_id=1, source_target_pairs={{0,16},{8,144},{16,272},{24,400},{128,24},{136,152},{144,280},{152... | collective-permute-start | bytes 98312 | tf_op jit(solution)/shard_map/ppermute | solution.py:338
  24.4 2.0 %collective-permute-done.5.refs_2_ = bf16[2,64,128]{2,1,0:T(8,128)(2,1)S(1)} collective-permute-done((bf16[2,64,128]{2,1,0:T(8,128)(2,1)S(1)}, bf16[2,64,128]{2,1,0:T(8,128)(2,1)S(1)}, u32[]{:S(2)}, u32[]{:S(2)}) %collective-permute-start.5) | collective-permute-done | bytes 32800 | tf_op jit(solution)/shard_map/ppermute | solution.py:338
  26.4 2.7 %all-to-all-done.refs_0_ = bf16[8,384,128]{2,1,0:T(8,128)(2,1)S(1)} async-done(((bf16[8,384,128]{2,1,0:T(8,128)(2,1)}), bf16[8,384,128]{2,1,0:T(8,128)(2,1)S(1)}, u32[]{:S(2)}, u32[]{:S(2)}) %all-to-all-start) | async-done | bytes 786464 | tf_op jit(solution)/shard_map/all_to_all | solution.py:57
  29.1 2.1 %shard_map.107 = (bf16[16,56,128]{2,1,0:T(8,128)(2,1)}, bf16[2,64,128]{2,1,0:T(8,128)(2,1)S(1)}) custom-call(bf16[8,384,128]{2,1,0:T(8,128)(2,1)S(1)} %all-to-all-done.refs_0_, bf16[2,64,128]{2,1,0:T(8,128)(2,1)S(1)} %collective-permute-done.4.refs_1_, bf16[2,64,128]{2,1,0:T(8,128)(2,1)S(1)} %collective-permute-done.5.refs_2_), custom_call_target="tpu_custom_call" | custom-call | flops 452984832 | bytes 851968 | tf_op jit(solution)/shard_map/pallas_call | solution.py:33
  31.3 8.1 %all-to-all-start.1 = ((bf16[16,56,128]{2,1,0:T(8,128)(2,1)}), bf16[16,56,128]{2,1,0:T(8,128)(2,1)S(1)}, u32[]{:S(2)}, u32[]{:S(2)}) async-start(bf16[16,56,128]{2,1,0:T(8,128)(2,1)} %get-tuple-element.20), calls=%async_computation.1 | async-start | bytes 458752 | tf_op jit(solution)/shard_map/all_to_all | solution.py:57
  39.3 3.3 %collective-permute-start.6 = (bf16[2,64,128]{2,1,0:T(8,128)(2,1)S(1)}, bf16[2,64,128]{2,1,0:T(8,128)(2,1)S(1)}, u32[]{:S(2)}, u32[]{:S(2)}) collective-permute-start(bf16[2,64,128]{2,1,0:T(8,128)(2,1)S(1)} %get-tuple-element.21), channel_id=1, source_target_pairs={{0,8},{8,0},{16,24},{24,16},{1,9},{9,1},{17,25},{25,17},{2,10},{10... | collective-permute-start | bytes 98312 | tf_op jit(solution)/shard_map/ppermute | solution.py:342
  42.6 3.1 %collective-permute-done.6.refs_3_ = bf16[2,64,128]{2,1,0:T(8,128)(2,1)S(1)} collective-permute-done((bf16[2,64,128]{2,1,0:T(8,128)(2,1)S(1)}, bf16[2,64,128]{2,1,0:T(8,128)(2,1)S(1)}, u32[]{:S(2)}, u32[]{:S(2)}) %collective-permute-start.6) | collective-permute-done | bytes 32800 | tf_op jit(solution)/shard_map/ppermute | solution.py:342
  45.7 3.1 %all-to-all-done.1.refs_0_ = bf16[16,56,128]{2,1,0:T(8,128)(2,1)S(1)} async-done(((bf16[16,56,128]{2,1,0:T(8,128)(2,1)}), bf16[16,56,128]{2,1,0:T(8,128)(2,1)S(1)}, u32[]{:S(2)}, u32[]{:S(2)}) %all-to-all-start.1) | async-done | bytes 229408 | tf_op jit(solution)/shard_map/all_to_all | solution.py:57
  48.8 0.8 shard_map.108
  49.5 12.1 %all-to-all-start.2 = ((bf16[4,272,128]{2,1,0:T(8,128)(2,1)}), bf16[4,272,128]{2,1,0:T(8,128)(2,1)S(1)}, u32[]{:S(2)}, u32[]{:S(2)}) async-start(bf16[4,272,128]{2,1,0:T(8,128)(2,1)} %shard_map.108), calls=%async_computation.2 | async-start | bytes 557056 | tf_op jit(solution)/shard_map/all_to_all | solution.py:57
  61.6 4.7 %collective-permute-start.3 = (bf16[256,256]{1,0:T(8,128)(2,1)S(1)}, bf16[256,256]{1,0:T(8,128)(2,1)S(1)}, u32[]{:S(2)}, u32[]{:S(2)}) collective-permute-start(bf16[256,256]{1,0:T(8,128)(2,1)S(1)} %get-tuple-element.16.refs_2_), channel_id=1, source_target_pairs={{1,2},{3,4},{5,6},{7,8},{9,10},{11,12},{13,14},{15,16},{17,18},{19... | collective-permute-start | bytes 393224 | tf_op jit(solution)/shard_map/ppermute | solution.py:333
  66.3 1.9 %collective-permute-start.2 = (bf16[256,256]{1,0:T(8,128)(2,1)S(1)}, bf16[256,256]{1,0:T(8,128)(2,1)S(1)}, u32[]{:S(2)}, u32[]{:S(2)}) collective-permute-start(bf16[256,256]{1,0:T(8,128)(2,1)S(1)} %get-tuple-element.16.refs_2_), channel_id=1, source_target_pairs={{0,1},{1,0},{2,3},{3,2},{4,5},{5,4},{6,7},{7,6},{8,9},{9,8},{10,11... | collective-permute-start | bytes 393224 | tf_op jit(solution)/shard_map/ppermute | solution.py:331
  69.5 5.9 %all-to-all-done.2.refs_1_ = bf16[4,272,128]{2,1,0:T(8,128)(2,1)S(1)} async-done(((bf16[4,272,128]{2,1,0:T(8,128)(2,1)}), bf16[4,272,128]{2,1,0:T(8,128)(2,1)S(1)}, u32[]{:S(2)}, u32[]{:S(2)}) %all-to-all-start.2) | async-done | bytes 278560 | tf_op jit(solution)/shard_map/all_to_all | solution.py:57
  75.5 1.4 %shard_map.109 = (bf16[32,56,128]{2,1,0:T(8,128)(2,1)}, bf16[8,128,128]{2,1,0:T(8,128)(2,1)S(1)}, bf16[2,128,128]{2,1,0:T(8,128)(2,1)S(1)}, bf16[2,128,128]{2,1,0:T(8,128)(2,1)S(1)}) custom-call(s32[8]{0:T(128)S(1)} %copy-done.8, bf16[4,272,128]{2,1,0:T(8,128)(2,1)S(1)} %all-to-all-done.2.refs_1_, ...), custom_call_target="tpu_custom_call" | custom-call | bytes 540704 | tf_op jit(solution)/shard_map/pallas_call | solution.py:33
  76.9 9.6 %all-to-all-start.3 = ((bf16[32,56,128]{2,1,0:T(8,128)(2,1)}), bf16[32,56,128]{2,1,0:T(8,128)(2,1)S(1)}, u32[]{:S(2)}, u32[]{:S(2)}) async-start(bf16[32,56,128]{2,1,0:T(8,128)(2,1)} %get-tuple-element.22), calls=%async_computation.3 | async-start | bytes 917504 | tf_op jit(solution)/shard_map/all_to_all | solution.py:57
  86.5 4.9 %collective-permute-start.7 = (bf16[2,128,128]{2,1,0:T(8,128)(2,1)S(1)}, bf16[2,128,128]{2,1,0:T(8,128)(2,1)S(1)}, u32[]{:S(2)}, u32[]{:S(2)}) collective-permute-start(bf16[2,128,128]{2,1,0:T(8,128)(2,1)S(1)} %get-tuple-element.25), channel_id=1, source_target_pairs={{0,16},{8,24},{16,0},{24,8},{1,17},{9,25},{17,1},{25,9},{2,18},{10... | collective-permute-start | bytes 196616 | tf_op jit(solution)/shard_map/ppermute | solution.py:342
  91.4 2.3 %collective-permute-done.7.refs_3_.refs_2_ = bf16[2,128,128]{2,1,0:T(8,128)(2,1)S(1)} collective-permute-done((bf16[2,128,128]{2,1,0:T(8,128)(2,1)S(1)}, bf16[2,128,128]{2,1,0:T(8,128)(2,1)S(1)}, u32[]{:S(2)}, u32[]{:S(2)}) %collective-permute-start.7) | collective-permute-done | bytes 65568 | tf_op jit(solution)/shard_map/ppermute | solution.py:342
  93.7 3.4 %all-to-all-done.3.refs_0_ = bf16[32,56,128]{2,1,0:T(8,128)(2,1)S(1)} async-done(((bf16[32,56,128]{2,1,0:T(8,128)(2,1)}), bf16[32,56,128]{2,1,0:T(8,128)(2,1)S(1)}, u32[]{:S(2)}, u32[]{:S(2)}) %all-to-all-start.3) | async-done | bytes 458784 | tf_op jit(solution)/shard_map/all_to_all | solution.py:57
  97.1 1.1 shard_map.110
  98.1 4.3 %all-to-all-start.4 = ((bf16[4,224,128]{2,1,0:T(8,128)(2,1)}), bf16[4,224,128]{2,1,0:T(8,128)(2,1)S(1)}, u32[]{:S(2)}, u32[]{:S(2)}) async-start(bf16[4,224,128]{2,1,0:T(8,128)(2,1)} %get-tuple-element.28), calls=%async_computation.4 | async-start | bytes 458752 | tf_op jit(solution)/shard_map/all_to_all | solution.py:57
  102.4 3.7 %collective-permute-start.8 = (bf16[2,128,128]{2,1,0:T(8,128)(2,1)S(1)}, bf16[2,128,128]{2,1,0:T(8,128)(2,1)S(1)}, u32[]{:S(2)}, u32[]{:S(2)}) collective-permute-start(bf16[2,128,128]{2,1,0:T(8,128)(2,1)S(1)} %get-tuple-element.26.refs_4_), channel_id=1, source_target_pairs={{0,8},{8,0},{16,24},{24,16},{1,9},{9,1},{17,25},{25,17},{2,10},{10... | collective-permute-start | bytes 196616 | tf_op jit(solution)/shard_map/ppermute | solution.py:342
  106.1 2.1 %shard_map.111 = (bf16[256,128]{1,0:T(8,128)(2,1)}, f32[8,128]{1,0:T(8,128)S(1)}) custom-call(bf16[256,256]{1,0:T(8,128)(2,1)S(1)} %collective-permute-done.2.refs_2_.refs_0_, bf16[256,256]{1,0:T(8,128)(2,1)S(1)} %collective-permute-done.3.refs_3_.refs_1_, bf16[256,256]{1,0:T(8,128)(2,1)S(1)} %get-tuple-element.16.refs_2_, bf16[3456,256]{1,0:T(8,128)(2,1)S(1)} %copy-done, ...), custom_call_target="tpu_custom_call" | custom-call | flops 452984832 | bytes 2228224 | tf_op jit(solution)/shard_map/pallas_call | solution.py:33
  108.2 2.5 %collective-permute-done.8.refs_3_ = bf16[2,128,128]{2,1,0:T(8,128)(2,1)S(1)} collective-permute-done((bf16[2,128,128]{2,1,0:T(8,128)(2,1)S(1)}, bf16[2,128,128]{2,1,0:T(8,128)(2,1)S(1)}, u32[]{:S(2)}, u32[]{:S(2)}) %collective-permute-start.8) | collective-permute-done | bytes 65568 | tf_op jit(solution)/shard_map/ppermute | solution.py:342
  110.8 1.3 %shard_map.112 = bf16[8,112,128]{2,1,0:T(8,128)(2,1)S(1)} custom-call(bf16[4,224,128]{2,1,0:T(8,128)(2,1)S(1)} %all-to-all-done.4.refs_0_, bf16[2,128,128]{2,1,0:T(8,128)(2,1)S(1)} %get-tuple-element.24.refs_2_.refs_1_, bf16[2,128,128]{2,1,0:T(8,128)(2,1)S(1)} %collective-permute-done.7.refs_3_.refs_2_, ...), custom_call_target="tpu_custom_call" | custom-call | bytes 693248 | tf_op jit(solution)/shard_map/pallas_call | solution.py:33
  112.1 9.6 %all_to_all.35.refs_0_ = bf16[8,112,128]{2,1,0:T(8,128)(2,1)S(1)} all-to-all(bf16[8,112,128]{2,1,0:T(8,128)(2,1)S(1)} %shard_map.112), channel_id=1, replica_groups=mesh['y'=4,'zh'=2,'zg'=2,'zl'=4,'x'=4,'c'=2] {'c','x'}, dimensions={0} | all-to-all | bytes 458752 | tf_op jit(solution)/shard_map/all_to_all | solution.py:57
  121.7 7.1 %all_to_all.36.refs_0_ = bf16[4,112,128]{2,1,0:T(8,128)(2,1)S(1)} all-to-all(bf16[4,112,128]{2,1,0:T(8,128)(2,1)S(1)} %shard_map.113), channel_id=1, replica_groups=mesh['y'=4,'zh'=2,'zg'=2,'zl'=4,'x'=4,'c'=2] {'y'}, dimensions={0} | all-to-all | bytes 229376 | tf_op jit(solution)/shard_map/all_to_all | solution.py:57
  (27 shorter events, 2.3 us)
Async XLA Ops:
  0.6 9.7 %copy-start.4 = (bf16[1,432,54]{1,2,0:T(8,128)(2,1)S(1)}, bf16[1,432,54]{1,2,0:T(8,128)(2,1)}, u32[]{:S(2)}) copy-start(bf16[1,432,54]{1,2,0:T(8,128)(2,1)} %param.13) | copy-start | bytes 139972
  0.6 9.7 %copy-start.7 = (f32[54]{0:T(128)S(1)}, f32[54]{0:T(128)}, u32[]{:S(2)}) copy-start(f32[54]{0:T(128)} %param.16) | copy-start | bytes 652
  0.7 10.7 %copy-start = (bf16[3456,256]{1,0:T(8,128)(2,1)S(1)}, bf16[3456,256]{1,0:T(8,128)(2,1)}, u32[]{:S(2)}) copy-start(bf16[3456,256]{1,0:T(8,128)(2,1)} %refs_3_.3) | copy-start | bytes 5308420
  0.7 10.7 %copy-start.2 = (bf16[1,1,16,16,256]{4,3,2,1,0:T(8,128)(2,1)S(1)}, bf16[1,1,16,16,256]{4,3,2,1,0:T(8,128)(2,1)}, u32[]{:S(2)}) copy-start(bf16[1,1,16,16,256]{4,3,2,1,0:T(8,128)(2,1)} %param.12) | copy-start | bytes 393220
  0.7 10.7 %copy-start.3 = (bf16[1,1,16,16,128]{4,3,2,1,0:T(8,128)(2,1)S(1)}, bf16[1,1,16,16,128]{4,3,2,1,0:T(8,128)(2,1)}, u32[]{:S(2)}) copy-start(bf16[1,1,16,16,128]{4,3,2,1,0:T(8,128)(2,1)} %param.9) | copy-start | bytes 196612
  0.7 10.7 %copy-start.5 = (f32[256]{0:T(256)S(1)}, f32[256]{0:T(256)}, u32[]{:S(2)}) copy-start(f32[256]{0:T(256)} %param.11) | copy-start | bytes 3076
  0.7 10.0 %collective-permute-start.1 = (bf16[256,128]{1,0:T(8,128)(2,1)}, bf16[256,128]{1,0:T(8,128)(2,1)S(1)}, u32[]{:S(2)}, u32[]{:S(2)}) collective-permute-start(bf16[256,128]{1,0:T(8,128)(2,1)} %bitcast.10), channel_id=1, source_target_pairs={{1,2},{3,4},{5,6},{7,8},{9,10},{11,12},{13,14},{15,16},{17,18},{19... | collective-permute-start | bytes 196616 | tf_op jit(solution)/shard_map/ppermute | solution.py:333
  5.3 6.0 %collective-permute-start = (bf16[256,128]{1,0:T(8,128)(2,1)}, bf16[256,128]{1,0:T(8,128)(2,1)S(1)}, u32[]{:S(2)}, u32[]{:S(2)}) collective-permute-start(bf16[256,128]{1,0:T(8,128)(2,1)} %bitcast.11), channel_id=1, source_target_pairs={{0,1},{1,0},{2,3},{3,2},{4,5},{5,4},{6,7},{7,6},{8,9},{9,8},{10,11... | collective-permute-start | bytes 196616 | tf_op jit(solution)/shard_map/ppermute | solution.py:331
  13.1 16.0 %all-to-all-start = ((bf16[8,384,128]{2,1,0:T(8,128)(2,1)}), bf16[8,384,128]{2,1,0:T(8,128)(2,1)S(1)}, u32[]{:S(2)}, u32[]{:S(2)}) async-start(bf16[8,384,128]{2,1,0:T(8,128)(2,1)} %get-tuple-element.17), calls=%async_computation | async-start | bytes 1572864 | tf_op jit(solution)/shard_map/all_to_all | solution.py:57
  17.0 58.5 %copy-start.8 = (s32[8]{0:T(128)S(1)}, s32[8]{0:T(128)}, u32[]{:S(2)}) copy-start(s32[8]{0:T(128)} %refs_0_.1) | copy-start | bytes 100
  17.0 7.5 %collective-permute-start.4 = (bf16[2,64,128]{2,1,0:T(8,128)(2,1)S(1)}, bf16[2,64,128]{2,1,0:T(8,128)(2,1)S(1)}, u32[]{:S(2)}, u32[]{:S(2)}) collective-permute-start(bf16[2,64,128]{2,1,0:T(8,128)(2,1)S(1)} %get-tuple-element.18), channel_id=1, source_target_pairs={{0,0},{8,128},{16,256},{24,384},{128,8},{136,136},{144,264},{152,3... | collective-permute-start | bytes 98312 | tf_op jit(solution)/shard_map/ppermute | solution.py:338
  17.8 8.6 %collective-permute-start.5 = (bf16[2,64,128]{2,1,0:T(8,128)(2,1)S(1)}, bf16[2,64,128]{2,1,0:T(8,128)(2,1)S(1)}, u32[]{:S(2)}, u32[]{:S(2)}) collective-permute-start(bf16[2,64,128]{2,1,0:T(8,128)(2,1)S(1)} %get-tuple-element.19), channel_id=1, source_target_pairs={{0,16},{8,144},{16,272},{24,400},{128,24},{136,152},{144,280},{152... | collective-permute-start | bytes 98312 | tf_op jit(solution)/shard_map/ppermute | solution.py:338
  31.3 17.5 %all-to-all-start.1 = ((bf16[16,56,128]{2,1,0:T(8,128)(2,1)}), bf16[16,56,128]{2,1,0:T(8,128)(2,1)S(1)}, u32[]{:S(2)}, u32[]{:S(2)}) async-start(bf16[16,56,128]{2,1,0:T(8,128)(2,1)} %get-tuple-element.20), calls=%async_computation.1 | async-start | bytes 458752 | tf_op jit(solution)/shard_map/all_to_all | solution.py:57
  39.3 6.4 %collective-permute-start.6 = (bf16[2,64,128]{2,1,0:T(8,128)(2,1)S(1)}, bf16[2,64,128]{2,1,0:T(8,128)(2,1)S(1)}, u32[]{:S(2)}, u32[]{:S(2)}) collective-permute-start(bf16[2,64,128]{2,1,0:T(8,128)(2,1)S(1)} %get-tuple-element.21), channel_id=1, source_target_pairs={{0,8},{8,0},{16,24},{24,16},{1,9},{9,1},{17,25},{25,17},{2,10},{10... | collective-permute-start | bytes 98312 | tf_op jit(solution)/shard_map/ppermute | solution.py:342
  49.5 26.0 %all-to-all-start.2 = ((bf16[4,272,128]{2,1,0:T(8,128)(2,1)}), bf16[4,272,128]{2,1,0:T(8,128)(2,1)S(1)}, u32[]{:S(2)}, u32[]{:S(2)}) async-start(bf16[4,272,128]{2,1,0:T(8,128)(2,1)} %shard_map.108), calls=%async_computation.2 | async-start | bytes 557056 | tf_op jit(solution)/shard_map/all_to_all | solution.py:57
  61.6 7.3 %collective-permute-start.3 = (bf16[256,256]{1,0:T(8,128)(2,1)S(1)}, bf16[256,256]{1,0:T(8,128)(2,1)S(1)}, u32[]{:S(2)}, u32[]{:S(2)}) collective-permute-start(bf16[256,256]{1,0:T(8,128)(2,1)S(1)} %get-tuple-element.16.refs_2_), channel_id=1, source_target_pairs={{1,2},{3,4},{5,6},{7,8},{9,10},{11,12},{13,14},{15,16},{17,18},{19... | collective-permute-start | bytes 393224 | tf_op jit(solution)/shard_map/ppermute | solution.py:333
  66.3 3.2 %collective-permute-start.2 = (bf16[256,256]{1,0:T(8,128)(2,1)S(1)}, bf16[256,256]{1,0:T(8,128)(2,1)S(1)}, u32[]{:S(2)}, u32[]{:S(2)}) collective-permute-start(bf16[256,256]{1,0:T(8,128)(2,1)S(1)} %get-tuple-element.16.refs_2_), channel_id=1, source_target_pairs={{0,1},{1,0},{2,3},{3,2},{4,5},{5,4},{6,7},{7,6},{8,9},{9,8},{10,11... | collective-permute-start | bytes 393224 | tf_op jit(solution)/shard_map/ppermute | solution.py:331
  76.9 20.2 %all-to-all-start.3 = ((bf16[32,56,128]{2,1,0:T(8,128)(2,1)}), bf16[32,56,128]{2,1,0:T(8,128)(2,1)S(1)}, u32[]{:S(2)}, u32[]{:S(2)}) async-start(bf16[32,56,128]{2,1,0:T(8,128)(2,1)} %get-tuple-element.22), calls=%async_computation.3 | async-start | bytes 917504 | tf_op jit(solution)/shard_map/all_to_all | solution.py:57
  86.5 7.2 %collective-permute-start.7 = (bf16[2,128,128]{2,1,0:T(8,128)(2,1)S(1)}, bf16[2,128,128]{2,1,0:T(8,128)(2,1)S(1)}, u32[]{:S(2)}, u32[]{:S(2)}) collective-permute-start(bf16[2,128,128]{2,1,0:T(8,128)(2,1)S(1)} %get-tuple-element.25), channel_id=1, source_target_pairs={{0,16},{8,24},{16,0},{24,8},{1,17},{9,25},{17,1},{25,9},{2,18},{10... | collective-permute-start | bytes 196616 | tf_op jit(solution)/shard_map/ppermute | solution.py:342
  97.1 13.7 %copy-start.1 = (f32[256,256]{1,0:T(8,128)S(1)}, f32[256,256]{1,0:T(8,128)}, u32[]{:S(2)}) copy-start(f32[256,256]{1,0:T(8,128)} %refs_4_.1) | copy-start | bytes 786436
  97.1 13.7 %copy-start.6 = (f32[256]{0:T(256)S(1)}, f32[256]{0:T(256)}, u32[]{:S(2)}) copy-start(f32[256]{0:T(256)} %param.17) | copy-start | bytes 3076
  98.1 12.6 %all-to-all-start.4 = ((bf16[4,224,128]{2,1,0:T(8,128)(2,1)}), bf16[4,224,128]{2,1,0:T(8,128)(2,1)S(1)}, u32[]{:S(2)}, u32[]{:S(2)}) async-start(bf16[4,224,128]{2,1,0:T(8,128)(2,1)} %get-tuple-element.28), calls=%async_computation.4 | async-start | bytes 458752 | tf_op jit(solution)/shard_map/all_to_all | solution.py:57
  102.4 8.3 %collective-permute-start.8 = (bf16[2,128,128]{2,1,0:T(8,128)(2,1)S(1)}, bf16[2,128,128]{2,1,0:T(8,128)(2,1)S(1)}, u32[]{:S(2)}, u32[]{:S(2)}) collective-permute-start(bf16[2,128,128]{2,1,0:T(8,128)(2,1)S(1)} %get-tuple-element.26.refs_4_), channel_id=1, source_target_pairs={{0,8},{8,0},{16,24},{24,16},{1,9},{9,1},{17,25},{25,17},{2,10},{10... | collective-permute-start | bytes 196616 | tf_op jit(solution)/shard_map/ppermute | solution.py:342

commit v16 on v15

--- a/solution.py
+++ b/solution.py
@@ -198,7 +198,7 @@
 def over_zh_zg_body(owner_ref, got_ref, out_ref, basis_ref, here_ref, next_ref, rows, slices):
     for i in range(4):
         rows[i, :272, :] = got_ref[i].astype(F32)
-        rows[i, 272:, :] = jnp.zeros((8, 128), F32)
+        rows[i, 272:, :] = jnp.zeros((16, 128), F32)
         for y in range(4):
             slices[i, y] = rows[i, 54 + 54 * y : 118 + 54 * y, :].astype(BF16)
     total = (rows[0, :54, :] + rows[1, :54, :]) + (rows[2, :54, :] + rows[3, :54, :])
@@ -279,7 +279,7 @@
         for c in range(2):
             ordered[c, pl.ds(r, 108, stride=4), :] = rows[:108, 128 * c : 128 * c + 128]
     for c in range(2):
-        ordered[c, 432:, :] = jnp.zeros((8, 128), F32)
+        ordered[c, 432:, :] = jnp.zeros((16, 128), F32)
     for to in range(8):
         rows = [ordered[c, 54 * to : 54 * to + 56, :] for c in range(2)]
         out_ref[slot(to)] = jnp.concatenate(rows, axis=0).astype(BF16)
@@ -379,7 +379,7 @@
         weight_grad_body,
         [shape((16, 56, 128), BF16), shape((2, 64, 128), BF16)],
         arrays=(exchange(send, CX), even, odd),
-        scratch=[pltpu.VMEM((288, 2560), BF16), pltpu.VMEM((2048, 128), BF16), pltpu.VMEM((864, 128), F32)],
+        scratch=[pltpu.VMEM((288, 2560), BF16), pltpu.VMEM((2048, 128), BF16), pltpu.VMEM((1024, 128), F32)],
         flops=2 * 864 * 2048 * 128,
     )
     part = call(
@@ -395,7 +395,7 @@
         (panel_owner,),
         (exchange(part, ("zg", "zh")),),
         after=(inside, outside),
-        scratch=[pltpu.VMEM((4, 280, 128), F32), pltpu.VMEM((4, 4, 64, 128), BF16)],
+        scratch=[pltpu.VMEM((4, 288, 128), F32), pltpu.VMEM((4, 4, 64, 128), BF16)],
     )
     there = across(there, 2)
     rotated, pair = call(
@@ -425,7 +425,7 @@
             pltpu.VMEM((4, 128, 128), BF16),
             pltpu.VMEM((256, 256), F32),
             pltpu.VMEM((1, 256), F32),
-            pltpu.VMEM((2, 440, 128), F32),
+            pltpu.VMEM((2, 448, 128), F32),
             dma((2,)),
         ],
     )

time: 130 us -> 130 us (level)
  no operation moved by 1% of the time
where the time goes in v16:
time: 130 us; the launch traced here: 129 us
  starting transfers between devices  73.4 us (56%)
  waiting for transfers between devices  27 us (21%)
  blocking collectives  16.7 us (13%)
  Pallas kernels  11.5 us (9%)
    all_to_all x5, starting transfers between devices, exchange(): return lax.all_to_all(x, axes, 0, 0)  37.9 us
    all_to_all x2, blocking collectives, exchange(): return lax.all_to_all(x, axes, 0, 0)  16.7 us
    all_to_all x5, waiting for transfers between devices, exchange(): return lax.all_to_all(x, axes, 0, 0)  15.1 us
    ppermute x3, starting transfers between devices, across(): return lax.ppermute(block, 'zl', [(i, i ^ k) for i in range(4)])  11.9 us
    pallas_call x11, Pallas kernels, call(): pl.pallas_call(kernel, out_shape=out_shape, in_specs=[SMEM] * len(scalars...  11.5 us
    ppermute x2, starting transfers between devices, neighbours(): lax.ppermute(block, SPACE, pairs + [(j, i) for i, j in pairs])  9.32 us
    ppermute x3, waiting for transfers between devices, across(): return lax.ppermute(block, 'zl', [(i, i ^ k) for i in range(4)])  7.87 us
    ppermute x2, starting transfers between devices, turned(): return lax.ppermute(block, ('y', 'zl'), pairs)  7.44 us
  transfers between devices with their start and end apart: 14, of which 11 were waited for; matrix products, arithmetic and copies ran while one was open for 0% of the time, Pallas kernels for 2%

profile of v16, /device:TPU:1, one launch (start us, length us, event | category | flops | bytes accessed | tf_op | source)
XLA Modules:
  0.0 129.5 jit_solution(12250446057518307225)
XLA Ops:
  0.7 4.6 %collective-permute-start.1 = (bf16[256,128]{1,0:T(8,128)(2,1)}, bf16[256,128]{1,0:T(8,128)(2,1)S(1)}, u32[]{:S(2)}, u32[]{:S(2)}) collective-permute-start(bf16[256,128]{1,0:T(8,128)(2,1)} %bitcast.10), channel_id=1, source_target_pairs={{1,2},{3,4},{5,6},{7,8},{9,10},{11,12},{13,14},{15,16},{17,18},{19... | collective-permute-start | bytes 196616 | tf_op jit(solution)/shard_map/ppermute | solution.py:333
  5.3 4.9 %collective-permute-start = (bf16[256,128]{1,0:T(8,128)(2,1)}, bf16[256,128]{1,0:T(8,128)(2,1)S(1)}, u32[]{:S(2)}, u32[]{:S(2)}) collective-permute-start(bf16[256,128]{1,0:T(8,128)(2,1)} %bitcast.11), channel_id=1, source_target_pairs={{0,1},{1,0},{2,3},{3,2},{4,5},{5,4},{6,7},{7,6},{8,9},{9,8},{10,11... | collective-permute-start | bytes 196616 | tf_op jit(solution)/shard_map/ppermute | solution.py:331
  10.7 0.7 collective-permute-done.refs_0_
  11.4 1.7 %shard_map.106 = (bf16[256,256]{1,0:T(8,128)(2,1)S(1)}, bf16[8,384,128]{2,1,0:T(8,128)(2,1)}, bf16[2,64,128]{2,1,0:T(8,128)(2,1)S(1)}, bf16[2,64,128]{2,1,0:T(8,128)(2,1)S(1)}) custom-call(bf16[256,128]{1,0:T(8,128)(2,1)S(1)} %collective-permute-done.refs_0_, bf16[256,128]{1,0:T(8,128)(2,1)S(1)} %collective-permute-done.1.refs_1_, ...), custom_call_target="tpu_custom_call" | custom-call | flops 452984832 | bytes 2163712 | tf_op jit(solution)/shard_map/pallas_call | solution.py:33
  13.1 3.8 %all-to-all-start = ((bf16[8,384,128]{2,1,0:T(8,128)(2,1)}), bf16[8,384,128]{2,1,0:T(8,128)(2,1)S(1)}, u32[]{:S(2)}, u32[]{:S(2)}) async-start(bf16[8,384,128]{2,1,0:T(8,128)(2,1)} %get-tuple-element.17), calls=%async_computation | async-start | bytes 1572864 | tf_op jit(solution)/shard_map/all_to_all | solution.py:57
  17.0 0.8 collective-permute-start.4
  17.8 6.7 %collective-permute-start.5 = (bf16[2,64,128]{2,1,0:T(8,128)(2,1)S(1)}, bf16[2,64,128]{2,1,0:T(8,128)(2,1)S(1)}, u32[]{:S(2)}, u32[]{:S(2)}) collective-permute-start(bf16[2,64,128]{2,1,0:T(8,128)(2,1)S(1)} %get-tuple-element.19), channel_id=1, source_target_pairs={{0,16},{8,144},{16,272},{24,400},{128,24},{136,152},{144,280},{152... | collective-permute-start | bytes 98312 | tf_op jit(solution)/shard_map/ppermute | solution.py:338
  24.4 2.0 %collective-permute-done.5.refs_2_ = bf16[2,64,128]{2,1,0:T(8,128)(2,1)S(1)} collective-permute-done((bf16[2,64,128]{2,1,0:T(8,128)(2,1)S(1)}, bf16[2,64,128]{2,1,0:T(8,128)(2,1)S(1)}, u32[]{:S(2)}, u32[]{:S(2)}) %collective-permute-start.5) | collective-permute-done | bytes 32800 | tf_op jit(solution)/shard_map/ppermute | solution.py:338
  26.4 2.7 %all-to-all-done.refs_0_ = bf16[8,384,128]{2,1,0:T(8,128)(2,1)S(1)} async-done(((bf16[8,384,128]{2,1,0:T(8,128)(2,1)}), bf16[8,384,128]{2,1,0:T(8,128)(2,1)S(1)}, u32[]{:S(2)}, u32[]{:S(2)}) %all-to-all-start) | async-done | bytes 786464 | tf_op jit(solution)/shard_map/all_to_all | solution.py:57
  29.1 2.1 %shard_map.107 = (bf16[16,56,128]{2,1,0:T(8,128)(2,1)}, bf16[2,64,128]{2,1,0:T(8,128)(2,1)S(1)}) custom-call(bf16[8,384,128]{2,1,0:T(8,128)(2,1)S(1)} %all-to-all-done.refs_0_, bf16[2,64,128]{2,1,0:T(8,128)(2,1)S(1)} %collective-permute-done.4.refs_1_, bf16[2,64,128]{2,1,0:T(8,128)(2,1)S(1)} %collective-permute-done.5.refs_2_), custom_call_target="tpu_custom_call" | custom-call | flops 452984832 | bytes 851968 | tf_op jit(solution)/shard_map/pallas_call | solution.py:33
  31.3 8.1 %all-to-all-start.1 = ((bf16[16,56,128]{2,1,0:T(8,128)(2,1)}), bf16[16,56,128]{2,1,0:T(8,128)(2,1)S(1)}, u32[]{:S(2)}, u32[]{:S(2)}) async-start(bf16[16,56,128]{2,1,0:T(8,128)(2,1)} %get-tuple-element.20), calls=%async_computation.1 | async-start | bytes 458752 | tf_op jit(solution)/shard_map/all_to_all | solution.py:57
  39.3 3.3 %collective-permute-start.6 = (bf16[2,64,128]{2,1,0:T(8,128)(2,1)S(1)}, bf16[2,64,128]{2,1,0:T(8,128)(2,1)S(1)}, u32[]{:S(2)}, u32[]{:S(2)}) collective-permute-start(bf16[2,64,128]{2,1,0:T(8,128)(2,1)S(1)} %get-tuple-element.21), channel_id=1, source_target_pairs={{0,8},{8,0},{16,24},{24,16},{1,9},{9,1},{17,25},{25,17},{2,10},{10... | collective-permute-start | bytes 98312 | tf_op jit(solution)/shard_map/ppermute | solution.py:342
  42.6 3.1 %collective-permute-done.6.refs_3_ = bf16[2,64,128]{2,1,0:T(8,128)(2,1)S(1)} collective-permute-done((bf16[2,64,128]{2,1,0:T(8,128)(2,1)S(1)}, bf16[2,64,128]{2,1,0:T(8,128)(2,1)S(1)}, u32[]{:S(2)}, u32[]{:S(2)}) %collective-permute-start.6) | collective-permute-done | bytes 32800 | tf_op jit(solution)/shard_map/ppermute | solution.py:342
  45.7 3.1 %all-to-all-done.1.refs_0_ = bf16[16,56,128]{2,1,0:T(8,128)(2,1)S(1)} async-done(((bf16[16,56,128]{2,1,0:T(8,128)(2,1)}), bf16[16,56,128]{2,1,0:T(8,128)(2,1)S(1)}, u32[]{:S(2)}, u32[]{:S(2)}) %all-to-all-start.1) | async-done | bytes 229408 | tf_op jit(solution)/shard_map/all_to_all | solution.py:57
  48.8 0.8 shard_map.108
  49.5 12.1 %all-to-all-start.2 = ((bf16[4,272,128]{2,1,0:T(8,128)(2,1)}), bf16[4,272,128]{2,1,0:T(8,128)(2,1)S(1)}, u32[]{:S(2)}, u32[]{:S(2)}) async-start(bf16[4,272,128]{2,1,0:T(8,128)(2,1)} %shard_map.108), calls=%async_computation.2 | async-start | bytes 557056 | tf_op jit(solution)/shard_map/all_to_all | solution.py:57
  61.6 4.7 %collective-permute-start.3 = (bf16[256,256]{1,0:T(8,128)(2,1)S(1)}, bf16[256,256]{1,0:T(8,128)(2,1)S(1)}, u32[]{:S(2)}, u32[]{:S(2)}) collective-permute-start(bf16[256,256]{1,0:T(8,128)(2,1)S(1)} %get-tuple-element.16.refs_2_), channel_id=1, source_target_pairs={{1,2},{3,4},{5,6},{7,8},{9,10},{11,12},{13,14},{15,16},{17,18},{19... | collective-permute-start | bytes 393224 | tf_op jit(solution)/shard_map/ppermute | solution.py:333
  66.3 1.9 %collective-permute-start.2 = (bf16[256,256]{1,0:T(8,128)(2,1)S(1)}, bf16[256,256]{1,0:T(8,128)(2,1)S(1)}, u32[]{:S(2)}, u32[]{:S(2)}) collective-permute-start(bf16[256,256]{1,0:T(8,128)(2,1)S(1)} %get-tuple-element.16.refs_2_), channel_id=1, source_target_pairs={{0,1},{1,0},{2,3},{3,2},{4,5},{5,4},{6,7},{7,6},{8,9},{9,8},{10,11... | collective-permute-start | bytes 393224 | tf_op jit(solution)/shard_map/ppermute | solution.py:331
  69.5 5.9 %all-to-all-done.2.refs_1_ = bf16[4,272,128]{2,1,0:T(8,128)(2,1)S(1)} async-done(((bf16[4,272,128]{2,1,0:T(8,128)(2,1)}), bf16[4,272,128]{2,1,0:T(8,128)(2,1)S(1)}, u32[]{:S(2)}, u32[]{:S(2)}) %all-to-all-start.2) | async-done | bytes 278560 | tf_op jit(solution)/shard_map/all_to_all | solution.py:57
  75.5 1.4 %shard_map.109 = (bf16[32,56,128]{2,1,0:T(8,128)(2,1)}, bf16[8,128,128]{2,1,0:T(8,128)(2,1)S(1)}, bf16[2,128,128]{2,1,0:T(8,128)(2,1)S(1)}, bf16[2,128,128]{2,1,0:T(8,128)(2,1)S(1)}) custom-call(s32[8]{0:T(128)S(1)} %copy-done.8, bf16[4,272,128]{2,1,0:T(8,128)(2,1)S(1)} %all-to-all-done.2.refs_1_, ...), custom_call_target="tpu_custom_call" | custom-call | bytes 540704 | tf_op jit(solution)/shard_map/pallas_call | solution.py:33
  76.9 9.6 %all-to-all-start.3 = ((bf16[32,56,128]{2,1,0:T(8,128)(2,1)}), bf16[32,56,128]{2,1,0:T(8,128)(2,1)S(1)}, u32[]{:S(2)}, u32[]{:S(2)}) async-start(bf16[32,56,128]{2,1,0:T(8,128)(2,1)} %get-tuple-element.22), calls=%async_computation.3 | async-start | bytes 917504 | tf_op jit(solution)/shard_map/all_to_all | solution.py:57
  86.5 4.9 %collective-permute-start.7 = (bf16[2,128,128]{2,1,0:T(8,128)(2,1)S(1)}, bf16[2,128,128]{2,1,0:T(8,128)(2,1)S(1)}, u32[]{:S(2)}, u32[]{:S(2)}) collective-permute-start(bf16[2,128,128]{2,1,0:T(8,128)(2,1)S(1)} %get-tuple-element.25), channel_id=1, source_target_pairs={{0,16},{8,24},{16,0},{24,8},{1,17},{9,25},{17,1},{25,9},{2,18},{10... | collective-permute-start | bytes 196616 | tf_op jit(solution)/shard_map/ppermute | solution.py:342
  91.4 2.3 %collective-permute-done.7.refs_3_.refs_2_ = bf16[2,128,128]{2,1,0:T(8,128)(2,1)S(1)} collective-permute-done((bf16[2,128,128]{2,1,0:T(8,128)(2,1)S(1)}, bf16[2,128,128]{2,1,0:T(8,128)(2,1)S(1)}, u32[]{:S(2)}, u32[]{:S(2)}) %collective-permute-start.7) | collective-permute-done | bytes 65568 | tf_op jit(solution)/shard_map/ppermute | solution.py:342
  93.7 3.4 %all-to-all-done.3.refs_0_ = bf16[32,56,128]{2,1,0:T(8,128)(2,1)S(1)} async-done(((bf16[32,56,128]{2,1,0:T(8,128)(2,1)}), bf16[32,56,128]{2,1,0:T(8,128)(2,1)S(1)}, u32[]{:S(2)}, u32[]{:S(2)}) %all-to-all-start.3) | async-done | bytes 458784 | tf_op jit(solution)/shard_map/all_to_all | solution.py:57
  97.1 1.1 shard_map.110
  98.1 4.3 %all-to-all-start.4 = ((bf16[4,224,128]{2,1,0:T(8,128)(2,1)}), bf16[4,224,128]{2,1,0:T(8,128)(2,1)S(1)}, u32[]{:S(2)}, u32[]{:S(2)}) async-start(bf16[4,224,128]{2,1,0:T(8,128)(2,1)} %get-tuple-element.28), calls=%async_computation.4 | async-start | bytes 458752 | tf_op jit(solution)/shard_map/all_to_all | solution.py:57
  102.4 3.7 %collective-permute-start.8 = (bf16[2,128,128]{2,1,0:T(8,128)(2,1)S(1)}, bf16[2,128,128]{2,1,0:T(8,128)(2,1)S(1)}, u32[]{:S(2)}, u32[]{:S(2)}) collective-permute-start(bf16[2,128,128]{2,1,0:T(8,128)(2,1)S(1)} %get-tuple-element.26.refs_4_), channel_id=1, source_target_pairs={{0,8},{8,0},{16,24},{24,16},{1,9},{9,1},{17,25},{25,17},{2,10},{10... | collective-permute-start | bytes 196616 | tf_op jit(solution)/shard_map/ppermute | solution.py:342
  106.1 2.1 %shard_map.111 = (bf16[256,128]{1,0:T(8,128)(2,1)}, f32[8,128]{1,0:T(8,128)S(1)}) custom-call(bf16[256,256]{1,0:T(8,128)(2,1)S(1)} %collective-permute-done.2.refs_2_.refs_0_, bf16[256,256]{1,0:T(8,128)(2,1)S(1)} %collective-permute-done.3.refs_3_.refs_1_, bf16[256,256]{1,0:T(8,128)(2,1)S(1)} %get-tuple-element.16.refs_2_, bf16[3456,256]{1,0:T(8,128)(2,1)S(1)} %copy-done, ...), custom_call_target="tpu_custom_call" | custom-call | flops 452984832 | bytes 2228224 | tf_op jit(solution)/shard_map/pallas_call | solution.py:33
  108.2 2.5 %collective-permute-done.8.refs_3_ = bf16[2,128,128]{2,1,0:T(8,128)(2,1)S(1)} collective-permute-done((bf16[2,128,128]{2,1,0:T(8,128)(2,1)S(1)}, bf16[2,128,128]{2,1,0:T(8,128)(2,1)S(1)}, u32[]{:S(2)}, u32[]{:S(2)}) %collective-permute-start.8) | collective-permute-done | bytes 65568 | tf_op jit(solution)/shard_map/ppermute | solution.py:342
  110.8 1.3 %shard_map.112 = bf16[8,112,128]{2,1,0:T(8,128)(2,1)S(1)} custom-call(bf16[4,224,128]{2,1,0:T(8,128)(2,1)S(1)} %all-to-all-done.4.refs_0_, bf16[2,128,128]{2,1,0:T(8,128)(2,1)S(1)} %get-tuple-element.24.refs_2_.refs_1_, bf16[2,128,128]{2,1,0:T(8,128)(2,1)S(1)} %collective-permute-done.7.refs_3_.refs_2_, ...), custom_call_target="tpu_custom_call" | custom-call | bytes 693248 | tf_op jit(solution)/shard_map/pallas_call | solution.py:33
  112.1 9.6 %all_to_all.35.refs_0_ = bf16[8,112,128]{2,1,0:T(8,128)(2,1)S(1)} all-to-all(bf16[8,112,128]{2,1,0:T(8,128)(2,1)S(1)} %shard_map.112), channel_id=1, replica_groups=mesh['y'=4,'zh'=2,'zg'=2,'zl'=4,'x'=4,'c'=2] {'c','x'}, dimensions={0} | all-to-all | bytes 458752 | tf_op jit(solution)/shard_map/all_to_all | solution.py:57
  121.7 7.1 %all_to_all.36.refs_0_ = bf16[4,112,128]{2,1,0:T(8,128)(2,1)S(1)} all-to-all(bf16[4,112,128]{2,1,0:T(8,128)(2,1)S(1)} %shard_map.113), channel_id=1, replica_groups=mesh['y'=4,'zh'=2,'zg'=2,'zl'=4,'x'=4,'c'=2] {'y'}, dimensions={0} | all-to-all | bytes 229376 | tf_op jit(solution)/shard_map/all_to_all | solution.py:57
  (27 shorter events, 2.3 us)
Async XLA Ops:
  0.6 9.7 %copy-start.4 = (bf16[1,432,54]{1,2,0:T(8,128)(2,1)S(1)}, bf16[1,432,54]{1,2,0:T(8,128)(2,1)}, u32[]{:S(2)}) copy-start(bf16[1,432,54]{1,2,0:T(8,128)(2,1)} %param.13) | copy-start | bytes 139972
  0.6 9.7 %copy-start.7 = (f32[54]{0:T(128)S(1)}, f32[54]{0:T(128)}, u32[]{:S(2)}) copy-start(f32[54]{0:T(128)} %param.16) | copy-start | bytes 652
  0.7 10.7 %copy-start = (bf16[3456,256]{1,0:T(8,128)(2,1)S(1)}, bf16[3456,256]{1,0:T(8,128)(2,1)}, u32[]{:S(2)}) copy-start(bf16[3456,256]{1,0:T(8,128)(2,1)} %refs_3_.3) | copy-start | bytes 5308420
  0.7 10.7 %copy-start.2 = (bf16[1,1,16,16,256]{4,3,2,1,0:T(8,128)(2,1)S(1)}, bf16[1,1,16,16,256]{4,3,2,1,0:T(8,128)(2,1)}, u32[]{:S(2)}) copy-start(bf16[1,1,16,16,256]{4,3,2,1,0:T(8,128)(2,1)} %param.12) | copy-start | bytes 393220
  0.7 10.7 %copy-start.3 = (bf16[1,1,16,16,128]{4,3,2,1,0:T(8,128)(2,1)S(1)}, bf16[1,1,16,16,128]{4,3,2,1,0:T(8,128)(2,1)}, u32[]{:S(2)}) copy-start(bf16[1,1,16,16,128]{4,3,2,1,0:T(8,128)(2,1)} %param.9) | copy-start | bytes 196612
  0.7 10.7 %copy-start.5 = (f32[256]{0:T(256)S(1)}, f32[256]{0:T(256)}, u32[]{:S(2)}) copy-start(f32[256]{0:T(256)} %param.11) | copy-start | bytes 3076
  0.7 10.0 %collective-permute-start.1 = (bf16[256,128]{1,0:T(8,128)(2,1)}, bf16[256,128]{1,0:T(8,128)(2,1)S(1)}, u32[]{:S(2)}, u32[]{:S(2)}) collective-permute-start(bf16[256,128]{1,0:T(8,128)(2,1)} %bitcast.10), channel_id=1, source_target_pairs={{1,2},{3,4},{5,6},{7,8},{9,10},{11,12},{13,14},{15,16},{17,18},{19... | collective-permute-start | bytes 196616 | tf_op jit(solution)/shard_map/ppermute | solution.py:333
  5.3 6.0 %collective-permute-start = (bf16[256,128]{1,0:T(8,128)(2,1)}, bf16[256,128]{1,0:T(8,128)(2,1)S(1)}, u32[]{:S(2)}, u32[]{:S(2)}) collective-permute-start(bf16[256,128]{1,0:T(8,128)(2,1)} %bitcast.11), channel_id=1, source_target_pairs={{0,1},{1,0},{2,3},{3,2},{4,5},{5,4},{6,7},{7,6},{8,9},{9,8},{10,11... | collective-permute-start | bytes 196616 | tf_op jit(solution)/shard_map/ppermute | solution.py:331
  13.1 16.0 %all-to-all-start = ((bf16[8,384,128]{2,1,0:T(8,128)(2,1)}), bf16[8,384,128]{2,1,0:T(8,128)(2,1)S(1)}, u32[]{:S(2)}, u32[]{:S(2)}) async-start(bf16[8,384,128]{2,1,0:T(8,128)(2,1)} %get-tuple-element.17), calls=%async_computation | async-start | bytes 1572864 | tf_op jit(solution)/shard_map/all_to_all | solution.py:57
  17.0 58.5 %copy-start.8 = (s32[8]{0:T(128)S(1)}, s32[8]{0:T(128)}, u32[]{:S(2)}) copy-start(s32[8]{0:T(128)} %refs_0_.1) | copy-start | bytes 100
  17.0 7.5 %collective-permute-start.4 = (bf16[2,64,128]{2,1,0:T(8,128)(2,1)S(1)}, bf16[2,64,128]{2,1,0:T(8,128)(2,1)S(1)}, u32[]{:S(2)}, u32[]{:S(2)}) collective-permute-start(bf16[2,64,128]{2,1,0:T(8,128)(2,1)S(1)} %get-tuple-element.18), channel_id=1, source_target_pairs={{0,0},{8,128},{16,256},{24,384},{128,8},{136,136},{144,264},{152,3... | collective-permute-start | bytes 98312 | tf_op jit(solution)/shard_map/ppermute | solution.py:338
  17.8 8.6 %collective-permute-start.5 = (bf16[2,64,128]{2,1,0:T(8,128)(2,1)S(1)}, bf16[2,64,128]{2,1,0:T(8,128)(2,1)S(1)}, u32[]{:S(2)}, u32[]{:S(2)}) collective-permute-start(bf16[2,64,128]{2,1,0:T(8,128)(2,1)S(1)} %get-tuple-element.19), channel_id=1, source_target_pairs={{0,16},{8,144},{16,272},{24,400},{128,24},{136,152},{144,280},{152... | collective-permute-start | bytes 98312 | tf_op jit(solution)/shard_map/ppermute | solution.py:338
  31.3 17.5 %all-to-all-start.1 = ((bf16[16,56,128]{2,1,0:T(8,128)(2,1)}), bf16[16,56,128]{2,1,0:T(8,128)(2,1)S(1)}, u32[]{:S(2)}, u32[]{:S(2)}) async-start(bf16[16,56,128]{2,1,0:T(8,128)(2,1)} %get-tuple-element.20), calls=%async_computation.1 | async-start | bytes 458752 | tf_op jit(solution)/shard_map/all_to_all | solution.py:57
  39.3 6.4 %collective-permute-start.6 = (bf16[2,64,128]{2,1,0:T(8,128)(2,1)S(1)}, bf16[2,64,128]{2,1,0:T(8,128)(2,1)S(1)}, u32[]{:S(2)}, u32[]{:S(2)}) collective-permute-start(bf16[2,64,128]{2,1,0:T(8,128)(2,1)S(1)} %get-tuple-element.21), channel_id=1, source_target_pairs={{0,8},{8,0},{16,24},{24,16},{1,9},{9,1},{17,25},{25,17},{2,10},{10... | collective-permute-start | bytes 98312 | tf_op jit(solution)/shard_map/ppermute | solution.py:342
  49.5 26.0 %all-to-all-start.2 = ((bf16[4,272,128]{2,1,0:T(8,128)(2,1)}), bf16[4,272,128]{2,1,0:T(8,128)(2,1)S(1)}, u32[]{:S(2)}, u32[]{:S(2)}) async-start(bf16[4,272,128]{2,1,0:T(8,128)(2,1)} %shard_map.108), calls=%async_computation.2 | async-start | bytes 557056 | tf_op jit(solution)/shard_map/all_to_all | solution.py:57
  61.6 7.3 %collective-permute-start.3 = (bf16[256,256]{1,0:T(8,128)(2,1)S(1)}, bf16[256,256]{1,0:T(8,128)(2,1)S(1)}, u32[]{:S(2)}, u32[]{:S(2)}) collective-permute-start(bf16[256,256]{1,0:T(8,128)(2,1)S(1)} %get-tuple-element.16.refs_2_), channel_id=1, source_target_pairs={{1,2},{3,4},{5,6},{7,8},{9,10},{11,12},{13,14},{15,16},{17,18},{19... | collective-permute-start | bytes 393224 | tf_op jit(solution)/shard_map/ppermute | solution.py:333
  66.3 3.2 %collective-permute-start.2 = (bf16[256,256]{1,0:T(8,128)(2,1)S(1)}, bf16[256,256]{1,0:T(8,128)(2,1)S(1)}, u32[]{:S(2)}, u32[]{:S(2)}) collective-permute-start(bf16[256,256]{1,0:T(8,128)(2,1)S(1)} %get-tuple-element.16.refs_2_), channel_id=1, source_target_pairs={{0,1},{1,0},{2,3},{3,2},{4,5},{5,4},{6,7},{7,6},{8,9},{9,8},{10,11... | collective-permute-start | bytes 393224 | tf_op jit(solution)/shard_map/ppermute | solution.py:331
  76.9 20.2 %all-to-all-start.3 = ((bf16[32,56,128]{2,1,0:T(8,128)(2,1)}), bf16[32,56,128]{2,1,0:T(8,128)(2,1)S(1)}, u32[]{:S(2)}, u32[]{:S(2)}) async-start(bf16[32,56,128]{2,1,0:T(8,128)(2,1)} %get-tuple-element.22), calls=%async_computation.3 | async-start | bytes 917504 | tf_op jit(solution)/shard_map/all_to_all | solution.py:57
  86.5 7.2 %collective-permute-start.7 = (bf16[2,128,128]{2,1,0:T(8,128)(2,1)S(1)}, bf16[2,128,128]{2,1,0:T(8,128)(2,1)S(1)}, u32[]{:S(2)}, u32[]{:S(2)}) collective-permute-start(bf16[2,128,128]{2,1,0:T(8,128)(2,1)S(1)} %get-tuple-element.25), channel_id=1, source_target_pairs={{0,16},{8,24},{16,0},{24,8},{1,17},{9,25},{17,1},{25,9},{2,18},{10... | collective-permute-start | bytes 196616 | tf_op jit(solution)/shard_map/ppermute | solution.py:342
  97.1 13.7 %copy-start.1 = (f32[256,256]{1,0:T(8,128)S(1)}, f32[256,256]{1,0:T(8,128)}, u32[]{:S(2)}) copy-start(f32[256,256]{1,0:T(8,128)} %refs_4_.1) | copy-start | bytes 786436
  97.1 13.7 %copy-start.6 = (f32[256]{0:T(256)S(1)}, f32[256]{0:T(256)}, u32[]{:S(2)}) copy-start(f32[256]{0:T(256)} %param.17) | copy-start | bytes 3076
  98.1 12.6 %all-to-all-start.4 = ((bf16[4,224,128]{2,1,0:T(8,128)(2,1)}), bf16[4,224,128]{2,1,0:T(8,128)(2,1)S(1)}, u32[]{:S(2)}, u32[]{:S(2)}) async-start(bf16[4,224,128]{2,1,0:T(8,128)(2,1)} %get-tuple-element.28), calls=%async_computation.4 | async-start | bytes 458752 | tf_op jit(solution)/shard_map/all_to_all | solution.py:57
  102.4 8.3 %collective-permute-start.8 = (bf16[2,128,128]{2,1,0:T(8,128)(2,1)S(1)}, bf16[2,128,128]{2,1,0:T(8,128)(2,1)S(1)}, u32[]{:S(2)}, u32[]{:S(2)}) collective-permute-start(bf16[2,128,128]{2,1,0:T(8,128)(2,1)S(1)} %get-tuple-element.26.refs_4_), channel_id=1, source_target_pairs={{0,8},{8,0},{16,24},{24,16},{1,9},{9,1},{17,25},{25,17},{2,10},{10... | collective-permute-start | bytes 196616 | tf_op jit(solution)/shard_map/ppermute | solution.py:342

commit v17 on v16

--- a/solution.py
+++ b/solution.py
@@ -240,6 +240,21 @@
         out_ref[to] = total
 
 
+def two_terms(x):
+    high = x.astype(BF16)
+    return high, (x - high.astype(F32)).astype(BF16)
+
+
+def product(a, b, contract):
+    a_high, a_low = two_terms(a)
+    b_high, b_low = two_terms(b)
+
+    def dot(u, v):
+        return lax.dot_general(u, v, (contract, ((), ())), preferred_element_type=F32)
+
+    return dot(a_high, b_high) + (dot(a_high, b_low) + dot(a_low, b_high))
+
+
 def update_body(
     got_ref, here_ref, next_ref, pair_ref, out_basis_any, out_eigen_any,
     out_ref, panel, out_basis, out_eigen, ordered, sems,
@@ -252,7 +267,6 @@
         pltpu.make_async_copy(out_eigen_any, out_eigen, sems.at[1]),
     ]
     started(copies)
-    highest = lax.Precision.HIGHEST
     total = sum(got_ref[i].astype(F32) for i in range(4))
     none = jnp.zeros((8, 256), F32)
     parts = []
@@ -263,16 +277,12 @@
     rotated = jnp.concatenate(parts, axis=0)
     for copy in copies:
         copy.wait()
-    rotated = jnp.dot(rotated, out_basis[...], precision=highest, preferred_element_type=F32)
+    rotated = product(rotated, out_basis[...], ((1,), (0,)))
     terms = here_ref[0].astype(F32)
     eigen = (terms[:, 108:109] + terms[:, 109:110]) + terms[:, 110:111]
     scaled = rotated / (eigen * out_eigen[...] + DAMPING)
     scaled = jnp.where((iota((128, 256), 0) & 63) < 54, scaled, 0.0)
-    turned = lax.dot_general(
-        scaled, out_basis[...], (((1,), (1,)), ((), ())), precision=highest, preferred_element_type=F32
-    )
-    high = turned.astype(BF16)
-    rest = (turned - high.astype(F32)).astype(BF16)
+    high, rest = two_terms(product(scaled, out_basis[...], ((1,), (1,))))
     for r in range(4):
         block = panel[r].astype(F32).T.astype(BF16)
         rows = jnp.dot(block, high, preferred_element_type=F32) + jnp.dot(block, rest, preferred_element_type=F32)

time: 130 us -> 130 us (level)
  no operation moved by 1% of the time
where the time goes in v17:
time: 130 us; the launch traced here: 129 us
  starting transfers between devices  73.4 us (56%)
  waiting for transfers between devices  27 us (21%)
  blocking collectives  16.7 us (13%)
  Pallas kernels  11.2 us (9%)
    all_to_all x5, starting transfers between devices, exchange(): return lax.all_to_all(x, axes, 0, 0)  37.9 us
    all_to_all x2, blocking collectives, exchange(): return lax.all_to_all(x, axes, 0, 0)  16.7 us
    all_to_all x5, waiting for transfers between devices, exchange(): return lax.all_to_all(x, axes, 0, 0)  15.1 us
    ppermute x3, starting transfers between devices, across(): return lax.ppermute(block, 'zl', [(i, i ^ k) for i in range(4)])  11.9 us
    pallas_call x11, Pallas kernels, call(): pl.pallas_call(kernel, out_shape=out_shape, in_specs=[SMEM] * len(scalars...  11.2 us
    ppermute x2, starting transfers between devices, neighbours(): lax.ppermute(block, SPACE, pairs + [(j, i) for i, j in pairs])  9.32 us
    ppermute x3, waiting for transfers between devices, across(): return lax.ppermute(block, 'zl', [(i, i ^ k) for i in range(4)])  7.87 us
    ppermute x2, starting transfers between devices, turned(): return lax.ppermute(block, ('y', 'zl'), pairs)  7.44 us
  transfers between devices with their start and end apart: 14, of which 11 were waited for; matrix products, arithmetic and copies ran while one was open for 0% of the time, Pallas kernels for 2%

profile of v17, /device:TPU:1, one launch (start us, length us, event | category | flops | bytes accessed | tf_op | source)
XLA Modules:
  0.0 129.1 jit_solution(2081744703743116633)
XLA Ops:
  0.7 4.6 %collective-permute-start.1 = (bf16[256,128]{1,0:T(8,128)(2,1)}, bf16[256,128]{1,0:T(8,128)(2,1)S(1)}, u32[]{:S(2)}, u32[]{:S(2)}) collective-permute-start(bf16[256,128]{1,0:T(8,128)(2,1)} %bitcast.10), channel_id=1, source_target_pairs={{1,2},{3,4},{5,6},{7,8},{9,10},{11,12},{13,14},{15,16},{17,18},{19... | collective-permute-start | bytes 196616 | tf_op jit(solution)/shard_map/ppermute | solution.py:343
  5.3 4.9 %collective-permute-start = (bf16[256,128]{1,0:T(8,128)(2,1)}, bf16[256,128]{1,0:T(8,128)(2,1)S(1)}, u32[]{:S(2)}, u32[]{:S(2)}) collective-permute-start(bf16[256,128]{1,0:T(8,128)(2,1)} %bitcast.11), channel_id=1, source_target_pairs={{0,1},{1,0},{2,3},{3,2},{4,5},{5,4},{6,7},{7,6},{8,9},{9,8},{10,11... | collective-permute-start | bytes 196616 | tf_op jit(solution)/shard_map/ppermute | solution.py:341
  10.7 0.7 collective-permute-done.refs_0_
  11.4 1.7 %shard_map.106 = (bf16[256,256]{1,0:T(8,128)(2,1)S(1)}, bf16[8,384,128]{2,1,0:T(8,128)(2,1)}, bf16[2,64,128]{2,1,0:T(8,128)(2,1)S(1)}, bf16[2,64,128]{2,1,0:T(8,128)(2,1)S(1)}) custom-call(bf16[256,128]{1,0:T(8,128)(2,1)S(1)} %collective-permute-done.refs_0_, bf16[256,128]{1,0:T(8,128)(2,1)S(1)} %collective-permute-done.1.refs_1_, ...), custom_call_target="tpu_custom_call" | custom-call | flops 452984832 | bytes 2163712 | tf_op jit(solution)/shard_map/pallas_call | solution.py:33
  13.1 3.8 %all-to-all-start = ((bf16[8,384,128]{2,1,0:T(8,128)(2,1)}), bf16[8,384,128]{2,1,0:T(8,128)(2,1)S(1)}, u32[]{:S(2)}, u32[]{:S(2)}) async-start(bf16[8,384,128]{2,1,0:T(8,128)(2,1)} %get-tuple-element.17), calls=%async_computation | async-start | bytes 1572864 | tf_op jit(solution)/shard_map/all_to_all | solution.py:57
  17.0 0.8 collective-permute-start.4
  17.8 6.7 %collective-permute-start.5 = (bf16[2,64,128]{2,1,0:T(8,128)(2,1)S(1)}, bf16[2,64,128]{2,1,0:T(8,128)(2,1)S(1)}, u32[]{:S(2)}, u32[]{:S(2)}) collective-permute-start(bf16[2,64,128]{2,1,0:T(8,128)(2,1)S(1)} %get-tuple-element.19), channel_id=1, source_target_pairs={{0,16},{8,144},{16,272},{24,400},{128,24},{136,152},{144,280},{152... | collective-permute-start | bytes 98312 | tf_op jit(solution)/shard_map/ppermute | solution.py:348
  24.4 2.0 %collective-permute-done.5.refs_2_ = bf16[2,64,128]{2,1,0:T(8,128)(2,1)S(1)} collective-permute-done((bf16[2,64,128]{2,1,0:T(8,128)(2,1)S(1)}, bf16[2,64,128]{2,1,0:T(8,128)(2,1)S(1)}, u32[]{:S(2)}, u32[]{:S(2)}) %collective-permute-start.5) | collective-permute-done | bytes 32800 | tf_op jit(solution)/shard_map/ppermute | solution.py:348
  26.4 2.7 %all-to-all-done.refs_0_ = bf16[8,384,128]{2,1,0:T(8,128)(2,1)S(1)} async-done(((bf16[8,384,128]{2,1,0:T(8,128)(2,1)}), bf16[8,384,128]{2,1,0:T(8,128)(2,1)S(1)}, u32[]{:S(2)}, u32[]{:S(2)}) %all-to-all-start) | async-done | bytes 786464 | tf_op jit(solution)/shard_map/all_to_all | solution.py:57
  29.1 2.1 %shard_map.107 = (bf16[16,56,128]{2,1,0:T(8,128)(2,1)}, bf16[2,64,128]{2,1,0:T(8,128)(2,1)S(1)}) custom-call(bf16[8,384,128]{2,1,0:T(8,128)(2,1)S(1)} %all-to-all-done.refs_0_, bf16[2,64,128]{2,1,0:T(8,128)(2,1)S(1)} %collective-permute-done.4.refs_1_, bf16[2,64,128]{2,1,0:T(8,128)(2,1)S(1)} %collective-permute-done.5.refs_2_), custom_call_target="tpu_custom_call" | custom-call | flops 452984832 | bytes 851968 | tf_op jit(solution)/shard_map/pallas_call | solution.py:33
  31.3 8.1 %all-to-all-start.1 = ((bf16[16,56,128]{2,1,0:T(8,128)(2,1)}), bf16[16,56,128]{2,1,0:T(8,128)(2,1)S(1)}, u32[]{:S(2)}, u32[]{:S(2)}) async-start(bf16[16,56,128]{2,1,0:T(8,128)(2,1)} %get-tuple-element.20), calls=%async_computation.1 | async-start | bytes 458752 | tf_op jit(solution)/shard_map/all_to_all | solution.py:57
  39.3 3.3 %collective-permute-start.6 = (bf16[2,64,128]{2,1,0:T(8,128)(2,1)S(1)}, bf16[2,64,128]{2,1,0:T(8,128)(2,1)S(1)}, u32[]{:S(2)}, u32[]{:S(2)}) collective-permute-start(bf16[2,64,128]{2,1,0:T(8,128)(2,1)S(1)} %get-tuple-element.21), channel_id=1, source_target_pairs={{0,8},{8,0},{16,24},{24,16},{1,9},{9,1},{17,25},{25,17},{2,10},{10... | collective-permute-start | bytes 98312 | tf_op jit(solution)/shard_map/ppermute | solution.py:352
  42.6 3.1 %collective-permute-done.6.refs_3_ = bf16[2,64,128]{2,1,0:T(8,128)(2,1)S(1)} collective-permute-done((bf16[2,64,128]{2,1,0:T(8,128)(2,1)S(1)}, bf16[2,64,128]{2,1,0:T(8,128)(2,1)S(1)}, u32[]{:S(2)}, u32[]{:S(2)}) %collective-permute-start.6) | collective-permute-done | bytes 32800 | tf_op jit(solution)/shard_map/ppermute | solution.py:352
  45.7 3.1 %all-to-all-done.1.refs_0_ = bf16[16,56,128]{2,1,0:T(8,128)(2,1)S(1)} async-done(((bf16[16,56,128]{2,1,0:T(8,128)(2,1)}), bf16[16,56,128]{2,1,0:T(8,128)(2,1)S(1)}, u32[]{:S(2)}, u32[]{:S(2)}) %all-to-all-start.1) | async-done | bytes 229408 | tf_op jit(solution)/shard_map/all_to_all | solution.py:57
  48.8 0.8 shard_map.108
  49.5 12.1 %all-to-all-start.2 = ((bf16[4,272,128]{2,1,0:T(8,128)(2,1)}), bf16[4,272,128]{2,1,0:T(8,128)(2,1)S(1)}, u32[]{:S(2)}, u32[]{:S(2)}) async-start(bf16[4,272,128]{2,1,0:T(8,128)(2,1)} %shard_map.108), calls=%async_computation.2 | async-start | bytes 557056 | tf_op jit(solution)/shard_map/all_to_all | solution.py:57
  61.6 4.7 %collective-permute-start.3 = (bf16[256,256]{1,0:T(8,128)(2,1)S(1)}, bf16[256,256]{1,0:T(8,128)(2,1)S(1)}, u32[]{:S(2)}, u32[]{:S(2)}) collective-permute-start(bf16[256,256]{1,0:T(8,128)(2,1)S(1)} %get-tuple-element.16.refs_2_), channel_id=1, source_target_pairs={{1,2},{3,4},{5,6},{7,8},{9,10},{11,12},{13,14},{15,16},{17,18},{19... | collective-permute-start | bytes 393224 | tf_op jit(solution)/shard_map/ppermute | solution.py:343
  66.3 1.9 %collective-permute-start.2 = (bf16[256,256]{1,0:T(8,128)(2,1)S(1)}, bf16[256,256]{1,0:T(8,128)(2,1)S(1)}, u32[]{:S(2)}, u32[]{:S(2)}) collective-permute-start(bf16[256,256]{1,0:T(8,128)(2,1)S(1)} %get-tuple-element.16.refs_2_), channel_id=1, source_target_pairs={{0,1},{1,0},{2,3},{3,2},{4,5},{5,4},{6,7},{7,6},{8,9},{9,8},{10,11... | collective-permute-start | bytes 393224 | tf_op jit(solution)/shard_map/ppermute | solution.py:341
  69.5 5.9 %all-to-all-done.2.refs_1_ = bf16[4,272,128]{2,1,0:T(8,128)(2,1)S(1)} async-done(((bf16[4,272,128]{2,1,0:T(8,128)(2,1)}), bf16[4,272,128]{2,1,0:T(8,128)(2,1)S(1)}, u32[]{:S(2)}, u32[]{:S(2)}) %all-to-all-start.2) | async-done | bytes 278560 | tf_op jit(solution)/shard_map/all_to_all | solution.py:57
  75.5 1.4 %shard_map.109 = (bf16[32,56,128]{2,1,0:T(8,128)(2,1)}, bf16[8,128,128]{2,1,0:T(8,128)(2,1)S(1)}, bf16[2,128,128]{2,1,0:T(8,128)(2,1)S(1)}, bf16[2,128,128]{2,1,0:T(8,128)(2,1)S(1)}) custom-call(s32[8]{0:T(128)S(1)} %copy-done.8, bf16[4,272,128]{2,1,0:T(8,128)(2,1)S(1)} %all-to-all-done.2.refs_1_, ...), custom_call_target="tpu_custom_call" | custom-call | bytes 540704 | tf_op jit(solution)/shard_map/pallas_call | solution.py:33
  76.9 9.6 %all-to-all-start.3 = ((bf16[32,56,128]{2,1,0:T(8,128)(2,1)}), bf16[32,56,128]{2,1,0:T(8,128)(2,1)S(1)}, u32[]{:S(2)}, u32[]{:S(2)}) async-start(bf16[32,56,128]{2,1,0:T(8,128)(2,1)} %get-tuple-element.22), calls=%async_computation.3 | async-start | bytes 917504 | tf_op jit(solution)/shard_map/all_to_all | solution.py:57
  86.5 4.9 %collective-permute-start.7 = (bf16[2,128,128]{2,1,0:T(8,128)(2,1)S(1)}, bf16[2,128,128]{2,1,0:T(8,128)(2,1)S(1)}, u32[]{:S(2)}, u32[]{:S(2)}) collective-permute-start(bf16[2,128,128]{2,1,0:T(8,128)(2,1)S(1)} %get-tuple-element.25), channel_id=1, source_target_pairs={{0,16},{8,24},{16,0},{24,8},{1,17},{9,25},{17,1},{25,9},{2,18},{10... | collective-permute-start | bytes 196616 | tf_op jit(solution)/shard_map/ppermute | solution.py:352
  91.4 2.3 %collective-permute-done.7.refs_3_.refs_2_ = bf16[2,128,128]{2,1,0:T(8,128)(2,1)S(1)} collective-permute-done((bf16[2,128,128]{2,1,0:T(8,128)(2,1)S(1)}, bf16[2,128,128]{2,1,0:T(8,128)(2,1)S(1)}, u32[]{:S(2)}, u32[]{:S(2)}) %collective-permute-start.7) | collective-permute-done | bytes 65568 | tf_op jit(solution)/shard_map/ppermute | solution.py:352
  93.7 3.4 %all-to-all-done.3.refs_0_ = bf16[32,56,128]{2,1,0:T(8,128)(2,1)S(1)} async-done(((bf16[32,56,128]{2,1,0:T(8,128)(2,1)}), bf16[32,56,128]{2,1,0:T(8,128)(2,1)S(1)}, u32[]{:S(2)}, u32[]{:S(2)}) %all-to-all-start.3) | async-done | bytes 458784 | tf_op jit(solution)/shard_map/all_to_all | solution.py:57
  97.1 1.1 shard_map.110
  98.1 4.3 %all-to-all-start.4 = ((bf16[4,224,128]{2,1,0:T(8,128)(2,1)}), bf16[4,224,128]{2,1,0:T(8,128)(2,1)S(1)}, u32[]{:S(2)}, u32[]{:S(2)}) async-start(bf16[4,224,128]{2,1,0:T(8,128)(2,1)} %get-tuple-element.28), calls=%async_computation.4 | async-start | bytes 458752 | tf_op jit(solution)/shard_map/all_to_all | solution.py:57
  102.4 3.7 %collective-permute-start.8 = (bf16[2,128,128]{2,1,0:T(8,128)(2,1)S(1)}, bf16[2,128,128]{2,1,0:T(8,128)(2,1)S(1)}, u32[]{:S(2)}, u32[]{:S(2)}) collective-permute-start(bf16[2,128,128]{2,1,0:T(8,128)(2,1)S(1)} %get-tuple-element.26.refs_4_), channel_id=1, source_target_pairs={{0,8},{8,0},{16,24},{24,16},{1,9},{9,1},{17,25},{25,17},{2,10},{10... | collective-permute-start | bytes 196616 | tf_op jit(solution)/shard_map/ppermute | solution.py:352
  106.1 2.1 %shard_map.111 = (bf16[256,128]{1,0:T(8,128)(2,1)}, f32[8,128]{1,0:T(8,128)S(1)}) custom-call(bf16[256,256]{1,0:T(8,128)(2,1)S(1)} %collective-permute-done.2.refs_2_.refs_0_, bf16[256,256]{1,0:T(8,128)(2,1)S(1)} %collective-permute-done.3.refs_3_.refs_1_, bf16[256,256]{1,0:T(8,128)(2,1)S(1)} %get-tuple-element.16.refs_2_, bf16[3456,256]{1,0:T(8,128)(2,1)S(1)} %copy-done, ...), custom_call_target="tpu_custom_call" | custom-call | flops 452984832 | bytes 2228224 | tf_op jit(solution)/shard_map/pallas_call | solution.py:33
  108.2 2.5 %collective-permute-done.8.refs_3_ = bf16[2,128,128]{2,1,0:T(8,128)(2,1)S(1)} collective-permute-done((bf16[2,128,128]{2,1,0:T(8,128)(2,1)S(1)}, bf16[2,128,128]{2,1,0:T(8,128)(2,1)S(1)}, u32[]{:S(2)}, u32[]{:S(2)}) %collective-permute-start.8) | collective-permute-done | bytes 65568 | tf_op jit(solution)/shard_map/ppermute | solution.py:352
  110.8 0.9 shard_map.112
  111.7 9.6 %all_to_all.35.refs_0_ = bf16[8,112,128]{2,1,0:T(8,128)(2,1)S(1)} all-to-all(bf16[8,112,128]{2,1,0:T(8,128)(2,1)S(1)} %shard_map.112), channel_id=1, replica_groups=mesh['y'=4,'zh'=2,'zg'=2,'zl'=4,'x'=4,'c'=2] {'c','x'}, dimensions={0} | all-to-all | bytes 458752 | tf_op jit(solution)/shard_map/all_to_all | solution.py:57
  121.3 7.1 %all_to_all.36.refs_0_ = bf16[4,112,128]{2,1,0:T(8,128)(2,1)S(1)} all-to-all(bf16[4,112,128]{2,1,0:T(8,128)(2,1)S(1)} %shard_map.113), channel_id=1, replica_groups=mesh['y'=4,'zh'=2,'zg'=2,'zl'=4,'x'=4,'c'=2] {'y'}, dimensions={0} | all-to-all | bytes 229376 | tf_op jit(solution)/shard_map/all_to_all | solution.py:57
  (27 shorter events, 2.3 us)
Async XLA Ops:
  0.6 9.7 %copy-start.4 = (bf16[1,432,54]{1,2,0:T(8,128)(2,1)S(1)}, bf16[1,432,54]{1,2,0:T(8,128)(2,1)}, u32[]{:S(2)}) copy-start(bf16[1,432,54]{1,2,0:T(8,128)(2,1)} %param.13) | copy-start | bytes 139972
  0.6 9.7 %copy-start.7 = (f32[54]{0:T(128)S(1)}, f32[54]{0:T(128)}, u32[]{:S(2)}) copy-start(f32[54]{0:T(128)} %param.16) | copy-start | bytes 652
  0.7 10.7 %copy-start = (bf16[3456,256]{1,0:T(8,128)(2,1)S(1)}, bf16[3456,256]{1,0:T(8,128)(2,1)}, u32[]{:S(2)}) copy-start(bf16[3456,256]{1,0:T(8,128)(2,1)} %refs_3_.3) | copy-start | bytes 5308420
  0.7 10.7 %copy-start.2 = (bf16[1,1,16,16,256]{4,3,2,1,0:T(8,128)(2,1)S(1)}, bf16[1,1,16,16,256]{4,3,2,1,0:T(8,128)(2,1)}, u32[]{:S(2)}) copy-start(bf16[1,1,16,16,256]{4,3,2,1,0:T(8,128)(2,1)} %param.12) | copy-start | bytes 393220
  0.7 10.7 %copy-start.3 = (bf16[1,1,16,16,128]{4,3,2,1,0:T(8,128)(2,1)S(1)}, bf16[1,1,16,16,128]{4,3,2,1,0:T(8,128)(2,1)}, u32[]{:S(2)}) copy-start(bf16[1,1,16,16,128]{4,3,2,1,0:T(8,128)(2,1)} %param.9) | copy-start | bytes 196612
  0.7 10.7 %copy-start.5 = (f32[256]{0:T(256)S(1)}, f32[256]{0:T(256)}, u32[]{:S(2)}) copy-start(f32[256]{0:T(256)} %param.11) | copy-start | bytes 3076
  0.7 10.0 %collective-permute-start.1 = (bf16[256,128]{1,0:T(8,128)(2,1)}, bf16[256,128]{1,0:T(8,128)(2,1)S(1)}, u32[]{:S(2)}, u32[]{:S(2)}) collective-permute-start(bf16[256,128]{1,0:T(8,128)(2,1)} %bitcast.10), channel_id=1, source_target_pairs={{1,2},{3,4},{5,6},{7,8},{9,10},{11,12},{13,14},{15,16},{17,18},{19... | collective-permute-start | bytes 196616 | tf_op jit(solution)/shard_map/ppermute | solution.py:343
  5.3 6.0 %collective-permute-start = (bf16[256,128]{1,0:T(8,128)(2,1)}, bf16[256,128]{1,0:T(8,128)(2,1)S(1)}, u32[]{:S(2)}, u32[]{:S(2)}) collective-permute-start(bf16[256,128]{1,0:T(8,128)(2,1)} %bitcast.11), channel_id=1, source_target_pairs={{0,1},{1,0},{2,3},{3,2},{4,5},{5,4},{6,7},{7,6},{8,9},{9,8},{10,11... | collective-permute-start | bytes 196616 | tf_op jit(solution)/shard_map/ppermute | solution.py:341
  13.1 16.0 %all-to-all-start = ((bf16[8,384,128]{2,1,0:T(8,128)(2,1)}), bf16[8,384,128]{2,1,0:T(8,128)(2,1)S(1)}, u32[]{:S(2)}, u32[]{:S(2)}) async-start(bf16[8,384,128]{2,1,0:T(8,128)(2,1)} %get-tuple-element.17), calls=%async_computation | async-start | bytes 1572864 | tf_op jit(solution)/shard_map/all_to_all | solution.py:57
  17.0 58.5 %copy-start.8 = (s32[8]{0:T(128)S(1)}, s32[8]{0:T(128)}, u32[]{:S(2)}) copy-start(s32[8]{0:T(128)} %refs_0_.1) | copy-start | bytes 100
  17.0 7.5 %collective-permute-start.4 = (bf16[2,64,128]{2,1,0:T(8,128)(2,1)S(1)}, bf16[2,64,128]{2,1,0:T(8,128)(2,1)S(1)}, u32[]{:S(2)}, u32[]{:S(2)}) collective-permute-start(bf16[2,64,128]{2,1,0:T(8,128)(2,1)S(1)} %get-tuple-element.18), channel_id=1, source_target_pairs={{0,0},{8,128},{16,256},{24,384},{128,8},{136,136},{144,264},{152,3... | collective-permute-start | bytes 98312 | tf_op jit(solution)/shard_map/ppermute | solution.py:348
  17.8 8.6 %collective-permute-start.5 = (bf16[2,64,128]{2,1,0:T(8,128)(2,1)S(1)}, bf16[2,64,128]{2,1,0:T(8,128)(2,1)S(1)}, u32[]{:S(2)}, u32[]{:S(2)}) collective-permute-start(bf16[2,64,128]{2,1,0:T(8,128)(2,1)S(1)} %get-tuple-element.19), channel_id=1, source_target_pairs={{0,16},{8,144},{16,272},{24,400},{128,24},{136,152},{144,280},{152... | collective-permute-start | bytes 98312 | tf_op jit(solution)/shard_map/ppermute | solution.py:348
  31.3 17.5 %all-to-all-start.1 = ((bf16[16,56,128]{2,1,0:T(8,128)(2,1)}), bf16[16,56,128]{2,1,0:T(8,128)(2,1)S(1)}, u32[]{:S(2)}, u32[]{:S(2)}) async-start(bf16[16,56,128]{2,1,0:T(8,128)(2,1)} %get-tuple-element.20), calls=%async_computation.1 | async-start | bytes 458752 | tf_op jit(solution)/shard_map/all_to_all | solution.py:57
  39.3 6.4 %collective-permute-start.6 = (bf16[2,64,128]{2,1,0:T(8,128)(2,1)S(1)}, bf16[2,64,128]{2,1,0:T(8,128)(2,1)S(1)}, u32[]{:S(2)}, u32[]{:S(2)}) collective-permute-start(bf16[2,64,128]{2,1,0:T(8,128)(2,1)S(1)} %get-tuple-element.21), channel_id=1, source_target_pairs={{0,8},{8,0},{16,24},{24,16},{1,9},{9,1},{17,25},{25,17},{2,10},{10... | collective-permute-start | bytes 98312 | tf_op jit(solution)/shard_map/ppermute | solution.py:352
  49.5 26.0 %all-to-all-start.2 = ((bf16[4,272,128]{2,1,0:T(8,128)(2,1)}), bf16[4,272,128]{2,1,0:T(8,128)(2,1)S(1)}, u32[]{:S(2)}, u32[]{:S(2)}) async-start(bf16[4,272,128]{2,1,0:T(8,128)(2,1)} %shard_map.108), calls=%async_computation.2 | async-start | bytes 557056 | tf_op jit(solution)/shard_map/all_to_all | solution.py:57
  61.6 7.3 %collective-permute-start.3 = (bf16[256,256]{1,0:T(8,128)(2,1)S(1)}, bf16[256,256]{1,0:T(8,128)(2,1)S(1)}, u32[]{:S(2)}, u32[]{:S(2)}) collective-permute-start(bf16[256,256]{1,0:T(8,128)(2,1)S(1)} %get-tuple-element.16.refs_2_), channel_id=1, source_target_pairs={{1,2},{3,4},{5,6},{7,8},{9,10},{11,12},{13,14},{15,16},{17,18},{19... | collective-permute-start | bytes 393224 | tf_op jit(solution)/shard_map/ppermute | solution.py:343
  66.3 3.2 %collective-permute-start.2 = (bf16[256,256]{1,0:T(8,128)(2,1)S(1)}, bf16[256,256]{1,0:T(8,128)(2,1)S(1)}, u32[]{:S(2)}, u32[]{:S(2)}) collective-permute-start(bf16[256,256]{1,0:T(8,128)(2,1)S(1)} %get-tuple-element.16.refs_2_), channel_id=1, source_target_pairs={{0,1},{1,0},{2,3},{3,2},{4,5},{5,4},{6,7},{7,6},{8,9},{9,8},{10,11... | collective-permute-start | bytes 393224 | tf_op jit(solution)/shard_map/ppermute | solution.py:341
  76.9 20.2 %all-to-all-start.3 = ((bf16[32,56,128]{2,1,0:T(8,128)(2,1)}), bf16[32,56,128]{2,1,0:T(8,128)(2,1)S(1)}, u32[]{:S(2)}, u32[]{:S(2)}) async-start(bf16[32,56,128]{2,1,0:T(8,128)(2,1)} %get-tuple-element.22), calls=%async_computation.3 | async-start | bytes 917504 | tf_op jit(solution)/shard_map/all_to_all | solution.py:57
  86.5 7.2 %collective-permute-start.7 = (bf16[2,128,128]{2,1,0:T(8,128)(2,1)S(1)}, bf16[2,128,128]{2,1,0:T(8,128)(2,1)S(1)}, u32[]{:S(2)}, u32[]{:S(2)}) collective-permute-start(bf16[2,128,128]{2,1,0:T(8,128)(2,1)S(1)} %get-tuple-element.25), channel_id=1, source_target_pairs={{0,16},{8,24},{16,0},{24,8},{1,17},{9,25},{17,1},{25,9},{2,18},{10... | collective-permute-start | bytes 196616 | tf_op jit(solution)/shard_map/ppermute | solution.py:352
  97.1 13.7 %copy-start.1 = (f32[256,256]{1,0:T(8,128)S(1)}, f32[256,256]{1,0:T(8,128)}, u32[]{:S(2)}) copy-start(f32[256,256]{1,0:T(8,128)} %refs_4_.1) | copy-start | bytes 786436
  97.1 13.7 %copy-start.6 = (f32[256]{0:T(256)S(1)}, f32[256]{0:T(256)}, u32[]{:S(2)}) copy-start(f32[256]{0:T(256)} %param.17) | copy-start | bytes 3076
  98.1 12.6 %all-to-all-start.4 = ((bf16[4,224,128]{2,1,0:T(8,128)(2,1)}), bf16[4,224,128]{2,1,0:T(8,128)(2,1)S(1)}, u32[]{:S(2)}, u32[]{:S(2)}) async-start(bf16[4,224,128]{2,1,0:T(8,128)(2,1)} %get-tuple-element.28), calls=%async_computation.4 | async-start | bytes 458752 | tf_op jit(solution)/shard_map/all_to_all | solution.py:57
  102.4 8.3 %collective-permute-start.8 = (bf16[2,128,128]{2,1,0:T(8,128)(2,1)S(1)}, bf16[2,128,128]{2,1,0:T(8,128)(2,1)S(1)}, u32[]{:S(2)}, u32[]{:S(2)}) collective-permute-start(bf16[2,128,128]{2,1,0:T(8,128)(2,1)S(1)} %get-tuple-element.26.refs_4_), channel_id=1, source_target_pairs={{0,8},{8,0},{16,24},{24,16},{1,9},{9,1},{17,25},{25,17},{2,10},{10... | collective-permute-start | bytes 196616 | tf_op jit(solution)/shard_map/ppermute | solution.py:352

commit v18 on v17

--- a/solution.py
+++ b/solution.py
@@ -147,7 +147,7 @@
     return 4 * (e % 2) + e // 2
 
 
-def weight_grad_body(got_ref, even_ref, odd_ref, out_ref, pair_ref, moved, deltas, whole):
+def weight_grad_body(got_ref, odd_ref, even_ref, out_ref, pair_ref, moved, deltas, whole):
     pieces = []
     for plane, at in [(0, 64)] + [(e, 0) for e in range(8)] + [(7, 64)]:
         pieces.append(got_ref[slot(plane), at : at + 32].astype(F32))
@@ -384,11 +384,12 @@
         scratch=[pltpu.VMEM((256, 3456), BF16), pltpu.VMEM((3, 256, 128), BF16)],
         flops=2 * 256 * 3456 * 256,
     )
-    even, odd = turned(even, 0), turned(odd, 2)
+    odd = turned(odd, 2)
+    even = turned(even, 0)
     part, pair = call(
         weight_grad_body,
         [shape((16, 56, 128), BF16), shape((2, 64, 128), BF16)],
-        arrays=(exchange(send, CX), even, odd),
+        arrays=(exchange(send, CX), odd, even),
         scratch=[pltpu.VMEM((288, 2560), BF16), pltpu.VMEM((2048, 128), BF16), pltpu.VMEM((1024, 128), F32)],
         flops=2 * 864 * 2048 * 128,
     )

time: 130 us -> 130 us (level)
  starting transfers between devices: 73.4 us -> 70.5 us
  waiting for transfers between devices: 27 us -> 29.9 us
    ppermute x2, starting transfers between devices: 7.44 us -> 4.19 us  [turned(): return lax.ppermute(block, ('y', 'zl'), pairs)]
    all_to_all x5, waiting for transfers between devices: 15.1 us -> 18 us  [exchange(): return lax.all_to_all(x, axes, 0, 0)]
where the time goes in v18:
time: 130 us; the launch traced here: 129 us
  starting transfers between devices  70.5 us (54%)
  waiting for transfers between devices  29.9 us (23%)
  blocking collectives  16.7 us (13%)
  Pallas kernels  11.2 us (9%)
    all_to_all x5, starting transfers between devices, exchange(): return lax.all_to_all(x, axes, 0, 0)  37.9 us
    all_to_all x5, waiting for transfers between devices, exchange(): return lax.all_to_all(x, axes, 0, 0)  18 us
    all_to_all x2, blocking collectives, exchange(): return lax.all_to_all(x, axes, 0, 0)  16.7 us
    ppermute x3, starting transfers between devices, across(): return lax.ppermute(block, 'zl', [(i, i ^ k) for i in range(4)])  12.1 us
    pallas_call x11, Pallas kernels, call(): pl.pallas_call(kernel, out_shape=out_shape, in_specs=[SMEM] * len(scalars...  11.2 us
    ppermute x2, starting transfers between devices, neighbours(): lax.ppermute(block, SPACE, pairs + [(j, i) for i, j in pairs])  9.32 us
    ppermute x3, waiting for transfers between devices, across(): return lax.ppermute(block, 'zl', [(i, i ^ k) for i in range(4)])  7.54 us
    ppermute x2, starting transfers between devices, neighbours(): inside = lax.ppermute(block, 'c', [(0, 1), (1, 0)])  6.86 us
  transfers between devices with their start and end apart: 14, of which 11 were waited for; matrix products, arithmetic and copies ran while one was open for 0% of the time, Pallas kernels for 2%

profile of v18, /device:TPU:1, one launch (start us, length us, event | category | flops | bytes accessed | tf_op | source)
XLA Modules:
  0.0 129.1 jit_solution(11086958872919383659)
XLA Ops:
  0.7 4.6 %collective-permute-start.1 = (bf16[256,128]{1,0:T(8,128)(2,1)}, bf16[256,128]{1,0:T(8,128)(2,1)S(1)}, u32[]{:S(2)}, u32[]{:S(2)}) collective-permute-start(bf16[256,128]{1,0:T(8,128)(2,1)} %bitcast.10), channel_id=1, source_target_pairs={{1,2},{3,4},{5,6},{7,8},{9,10},{11,12},{13,14},{15,16},{17,18},{19... | collective-permute-start | bytes 196616 | tf_op jit(solution)/shard_map/ppermute | solution.py:343
  5.3 4.9 %collective-permute-start = (bf16[256,128]{1,0:T(8,128)(2,1)}, bf16[256,128]{1,0:T(8,128)(2,1)S(1)}, u32[]{:S(2)}, u32[]{:S(2)}) collective-permute-start(bf16[256,128]{1,0:T(8,128)(2,1)} %bitcast.11), channel_id=1, source_target_pairs={{0,1},{1,0},{2,3},{3,2},{4,5},{5,4},{6,7},{7,6},{8,9},{9,8},{10,11... | collective-permute-start | bytes 196616 | tf_op jit(solution)/shard_map/ppermute | solution.py:341
  10.7 0.7 collective-permute-done.refs_0_
  11.4 1.7 %shard_map.106 = (bf16[256,256]{1,0:T(8,128)(2,1)S(1)}, bf16[8,384,128]{2,1,0:T(8,128)(2,1)}, bf16[2,64,128]{2,1,0:T(8,128)(2,1)S(1)}, bf16[2,64,128]{2,1,0:T(8,128)(2,1)S(1)}) custom-call(bf16[256,128]{1,0:T(8,128)(2,1)S(1)} %collective-permute-done.refs_0_, bf16[256,128]{1,0:T(8,128)(2,1)S(1)} %collective-permute-done.1.refs_1_, ...), custom_call_target="tpu_custom_call" | custom-call | flops 452984832 | bytes 2163712 | tf_op jit(solution)/shard_map/pallas_call | solution.py:33
  13.1 3.8 %all-to-all-start = ((bf16[8,384,128]{2,1,0:T(8,128)(2,1)}), bf16[8,384,128]{2,1,0:T(8,128)(2,1)S(1)}, u32[]{:S(2)}, u32[]{:S(2)}) async-start(bf16[8,384,128]{2,1,0:T(8,128)(2,1)} %get-tuple-element.17), calls=%async_computation | async-start | bytes 1572864 | tf_op jit(solution)/shard_map/all_to_all | solution.py:57
  17.0 3.5 %collective-permute-start.4 = (bf16[2,64,128]{2,1,0:T(8,128)(2,1)S(1)}, bf16[2,64,128]{2,1,0:T(8,128)(2,1)S(1)}, u32[]{:S(2)}, u32[]{:S(2)}) collective-permute-start(bf16[2,64,128]{2,1,0:T(8,128)(2,1)S(1)} %get-tuple-element.18), channel_id=1, source_target_pairs={{0,16},{8,144},{16,272},{24,400},{128,24},{136,152},{144,280},{152... | collective-permute-start | bytes 98312 | tf_op jit(solution)/shard_map/ppermute | solution.py:348
  21.2 2.4 %collective-permute-done.4.refs_1_.refs_2_ = bf16[2,64,128]{2,1,0:T(8,128)(2,1)S(1)} collective-permute-done((bf16[2,64,128]{2,1,0:T(8,128)(2,1)S(1)}, bf16[2,64,128]{2,1,0:T(8,128)(2,1)S(1)}, u32[]{:S(2)}, u32[]{:S(2)}) %collective-permute-start.4) | collective-permute-done | bytes 32800 | tf_op jit(solution)/shard_map/ppermute | solution.py:348
  23.5 5.6 %all-to-all-done.refs_0_ = bf16[8,384,128]{2,1,0:T(8,128)(2,1)S(1)} async-done(((bf16[8,384,128]{2,1,0:T(8,128)(2,1)}), bf16[8,384,128]{2,1,0:T(8,128)(2,1)S(1)}, u32[]{:S(2)}, u32[]{:S(2)}) %all-to-all-start) | async-done | bytes 786464 | tf_op jit(solution)/shard_map/all_to_all | solution.py:57
  29.1 2.1 %shard_map.107 = (bf16[16,56,128]{2,1,0:T(8,128)(2,1)}, bf16[2,64,128]{2,1,0:T(8,128)(2,1)S(1)}) custom-call(bf16[8,384,128]{2,1,0:T(8,128)(2,1)S(1)} %all-to-all-done.refs_0_, bf16[2,64,128]{2,1,0:T(8,128)(2,1)S(1)} %collective-permute-done.4.refs_1_.refs_2_, bf16[2,64,128]{2,1,0:T(8,128)(2,1)S(1)} %collective-permute-done.5.refs_2_.refs_1_), custom_call_target="tpu_custom_call" | custom-call | flops 452984832 | bytes 851968 | tf_op jit(solution)/shard_map/pallas_call | solution.py:33
  31.3 8.1 %all-to-all-start.1 = ((bf16[16,56,128]{2,1,0:T(8,128)(2,1)}), bf16[16,56,128]{2,1,0:T(8,128)(2,1)S(1)}, u32[]{:S(2)}, u32[]{:S(2)}) async-start(bf16[16,56,128]{2,1,0:T(8,128)(2,1)} %get-tuple-element.20), calls=%async_computation.1 | async-start | bytes 458752 | tf_op jit(solution)/shard_map/all_to_all | solution.py:57
  39.3 3.3 %collective-permute-start.6 = (bf16[2,64,128]{2,1,0:T(8,128)(2,1)S(1)}, bf16[2,64,128]{2,1,0:T(8,128)(2,1)S(1)}, u32[]{:S(2)}, u32[]{:S(2)}) collective-permute-start(bf16[2,64,128]{2,1,0:T(8,128)(2,1)S(1)} %get-tuple-element.21), channel_id=1, source_target_pairs={{0,8},{8,0},{16,24},{24,16},{1,9},{9,1},{17,25},{25,17},{2,10},{10... | collective-permute-start | bytes 98312 | tf_op jit(solution)/shard_map/ppermute | solution.py:352
  42.6 3.1 %collective-permute-done.6.refs_3_ = bf16[2,64,128]{2,1,0:T(8,128)(2,1)S(1)} collective-permute-done((bf16[2,64,128]{2,1,0:T(8,128)(2,1)S(1)}, bf16[2,64,128]{2,1,0:T(8,128)(2,1)S(1)}, u32[]{:S(2)}, u32[]{:S(2)}) %collective-permute-start.6) | collective-permute-done | bytes 32800 | tf_op jit(solution)/shard_map/ppermute | solution.py:352
  45.7 3.1 %all-to-all-done.1.refs_0_ = bf16[16,56,128]{2,1,0:T(8,128)(2,1)S(1)} async-done(((bf16[16,56,128]{2,1,0:T(8,128)(2,1)}), bf16[16,56,128]{2,1,0:T(8,128)(2,1)S(1)}, u32[]{:S(2)}, u32[]{:S(2)}) %all-to-all-start.1) | async-done | bytes 229408 | tf_op jit(solution)/shard_map/all_to_all | solution.py:57
  48.8 0.8 shard_map.108
  49.5 12.1 %all-to-all-start.2 = ((bf16[4,272,128]{2,1,0:T(8,128)(2,1)}), bf16[4,272,128]{2,1,0:T(8,128)(2,1)S(1)}, u32[]{:S(2)}, u32[]{:S(2)}) async-start(bf16[4,272,128]{2,1,0:T(8,128)(2,1)} %shard_map.108), calls=%async_computation.2 | async-start | bytes 557056 | tf_op jit(solution)/shard_map/all_to_all | solution.py:57
  61.6 4.7 %collective-permute-start.3 = (bf16[256,256]{1,0:T(8,128)(2,1)S(1)}, bf16[256,256]{1,0:T(8,128)(2,1)S(1)}, u32[]{:S(2)}, u32[]{:S(2)}) collective-permute-start(bf16[256,256]{1,0:T(8,128)(2,1)S(1)} %get-tuple-element.16.refs_2_), channel_id=1, source_target_pairs={{1,2},{3,4},{5,6},{7,8},{9,10},{11,12},{13,14},{15,16},{17,18},{19... | collective-permute-start | bytes 393224 | tf_op jit(solution)/shard_map/ppermute | solution.py:343
  66.3 1.9 %collective-permute-start.2 = (bf16[256,256]{1,0:T(8,128)(2,1)S(1)}, bf16[256,256]{1,0:T(8,128)(2,1)S(1)}, u32[]{:S(2)}, u32[]{:S(2)}) collective-permute-start(bf16[256,256]{1,0:T(8,128)(2,1)S(1)} %get-tuple-element.16.refs_2_), channel_id=1, source_target_pairs={{0,1},{1,0},{2,3},{3,2},{4,5},{5,4},{6,7},{7,6},{8,9},{9,8},{10,11... | collective-permute-start | bytes 393224 | tf_op jit(solution)/shard_map/ppermute | solution.py:341
  68.2 0.7 collective-permute-done.3.refs_3_.refs_1_
  69.5 5.9 %all-to-all-done.2.refs_1_ = bf16[4,272,128]{2,1,0:T(8,128)(2,1)S(1)} async-done(((bf16[4,272,128]{2,1,0:T(8,128)(2,1)}), bf16[4,272,128]{2,1,0:T(8,128)(2,1)S(1)}, u32[]{:S(2)}, u32[]{:S(2)}) %all-to-all-start.2) | async-done | bytes 278560 | tf_op jit(solution)/shard_map/all_to_all | solution.py:57
  75.5 1.4 %shard_map.109 = (bf16[32,56,128]{2,1,0:T(8,128)(2,1)}, bf16[8,128,128]{2,1,0:T(8,128)(2,1)S(1)}, bf16[2,128,128]{2,1,0:T(8,128)(2,1)S(1)}, bf16[2,128,128]{2,1,0:T(8,128)(2,1)S(1)}) custom-call(s32[8]{0:T(128)S(1)} %copy-done.8, bf16[4,272,128]{2,1,0:T(8,128)(2,1)S(1)} %all-to-all-done.2.refs_1_, ...), custom_call_target="tpu_custom_call" | custom-call | bytes 540704 | tf_op jit(solution)/shard_map/pallas_call | solution.py:33
  76.9 9.6 %all-to-all-start.3 = ((bf16[32,56,128]{2,1,0:T(8,128)(2,1)}), bf16[32,56,128]{2,1,0:T(8,128)(2,1)S(1)}, u32[]{:S(2)}, u32[]{:S(2)}) async-start(bf16[32,56,128]{2,1,0:T(8,128)(2,1)} %get-tuple-element.22), calls=%async_computation.3 | async-start | bytes 917504 | tf_op jit(solution)/shard_map/all_to_all | solution.py:57
  86.5 4.9 %collective-permute-start.7 = (bf16[2,128,128]{2,1,0:T(8,128)(2,1)S(1)}, bf16[2,128,128]{2,1,0:T(8,128)(2,1)S(1)}, u32[]{:S(2)}, u32[]{:S(2)}) collective-permute-start(bf16[2,128,128]{2,1,0:T(8,128)(2,1)S(1)} %get-tuple-element.25), channel_id=1, source_target_pairs={{0,16},{8,24},{16,0},{24,8},{1,17},{9,25},{17,1},{25,9},{2,18},{10... | collective-permute-start | bytes 196616 | tf_op jit(solution)/shard_map/ppermute | solution.py:352
  91.4 2.3 %collective-permute-done.7.refs_3_.refs_2_ = bf16[2,128,128]{2,1,0:T(8,128)(2,1)S(1)} collective-permute-done((bf16[2,128,128]{2,1,0:T(8,128)(2,1)S(1)}, bf16[2,128,128]{2,1,0:T(8,128)(2,1)S(1)}, u32[]{:S(2)}, u32[]{:S(2)}) %collective-permute-start.7) | collective-permute-done | bytes 65568 | tf_op jit(solution)/shard_map/ppermute | solution.py:352
  93.7 3.4 %all-to-all-done.3.refs_0_ = bf16[32,56,128]{2,1,0:T(8,128)(2,1)S(1)} async-done(((bf16[32,56,128]{2,1,0:T(8,128)(2,1)}), bf16[32,56,128]{2,1,0:T(8,128)(2,1)S(1)}, u32[]{:S(2)}, u32[]{:S(2)}) %all-to-all-start.3) | async-done | bytes 458784 | tf_op jit(solution)/shard_map/all_to_all | solution.py:57
  97.1 1.1 shard_map.110
  98.1 4.3 %all-to-all-start.4 = ((bf16[4,224,128]{2,1,0:T(8,128)(2,1)}), bf16[4,224,128]{2,1,0:T(8,128)(2,1)S(1)}, u32[]{:S(2)}, u32[]{:S(2)}) async-start(bf16[4,224,128]{2,1,0:T(8,128)(2,1)} %get-tuple-element.28), calls=%async_computation.4 | async-start | bytes 458752 | tf_op jit(solution)/shard_map/all_to_all | solution.py:57
  102.5 4.0 %collective-permute-start.8 = (bf16[2,128,128]{2,1,0:T(8,128)(2,1)S(1)}, bf16[2,128,128]{2,1,0:T(8,128)(2,1)S(1)}, u32[]{:S(2)}, u32[]{:S(2)}) collective-permute-start(bf16[2,128,128]{2,1,0:T(8,128)(2,1)S(1)} %get-tuple-element.26.refs_4_), channel_id=1, source_target_pairs={{0,8},{8,0},{16,24},{24,16},{1,9},{9,1},{17,25},{25,17},{2,10},{10... | collective-permute-start | bytes 196616 | tf_op jit(solution)/shard_map/ppermute | solution.py:352
  106.5 2.1 %shard_map.111 = (bf16[256,128]{1,0:T(8,128)(2,1)}, f32[8,128]{1,0:T(8,128)S(1)}) custom-call(bf16[256,256]{1,0:T(8,128)(2,1)S(1)} %collective-permute-done.2.refs_2_.refs_0_, bf16[256,256]{1,0:T(8,128)(2,1)S(1)} %collective-permute-done.3.refs_3_.refs_1_, bf16[256,256]{1,0:T(8,128)(2,1)S(1)} %get-tuple-element.16.refs_2_, bf16[3456,256]{1,0:T(8,128)(2,1)S(1)} %copy-done, ...), custom_call_target="tpu_custom_call" | custom-call | flops 452984832 | bytes 2228224 | tf_op jit(solution)/shard_map/pallas_call | solution.py:33
  108.6 2.2 %collective-permute-done.8.refs_3_ = bf16[2,128,128]{2,1,0:T(8,128)(2,1)S(1)} collective-permute-done((bf16[2,128,128]{2,1,0:T(8,128)(2,1)S(1)}, bf16[2,128,128]{2,1,0:T(8,128)(2,1)S(1)}, u32[]{:S(2)}, u32[]{:S(2)}) %collective-permute-start.8) | collective-permute-done | bytes 65568 | tf_op jit(solution)/shard_map/ppermute | solution.py:352
  110.8 0.9 shard_map.112
  111.8 9.6 %all_to_all.35.refs_0_ = bf16[8,112,128]{2,1,0:T(8,128)(2,1)S(1)} all-to-all(bf16[8,112,128]{2,1,0:T(8,128)(2,1)S(1)} %shard_map.112), channel_id=1, replica_groups=mesh['y'=4,'zh'=2,'zg'=2,'zl'=4,'x'=4,'c'=2] {'c','x'}, dimensions={0} | all-to-all | bytes 458752 | tf_op jit(solution)/shard_map/all_to_all | solution.py:57
  121.4 7.1 %all_to_all.36.refs_0_ = bf16[4,112,128]{2,1,0:T(8,128)(2,1)S(1)} all-to-all(bf16[4,112,128]{2,1,0:T(8,128)(2,1)S(1)} %shard_map.113), channel_id=1, replica_groups=mesh['y'=4,'zh'=2,'zg'=2,'zl'=4,'x'=4,'c'=2] {'y'}, dimensions={0} | all-to-all | bytes 229376 | tf_op jit(solution)/shard_map/all_to_all | solution.py:57
  (27 shorter events, 2.3 us)
Async XLA Ops:
  0.6 9.7 %copy-start.4 = (bf16[1,432,54]{1,2,0:T(8,128)(2,1)S(1)}, bf16[1,432,54]{1,2,0:T(8,128)(2,1)}, u32[]{:S(2)}) copy-start(bf16[1,432,54]{1,2,0:T(8,128)(2,1)} %param.13) | copy-start | bytes 139972
  0.6 9.7 %copy-start.7 = (f32[54]{0:T(128)S(1)}, f32[54]{0:T(128)}, u32[]{:S(2)}) copy-start(f32[54]{0:T(128)} %param.16) | copy-start | bytes 652
  0.7 10.7 %copy-start = (bf16[3456,256]{1,0:T(8,128)(2,1)S(1)}, bf16[3456,256]{1,0:T(8,128)(2,1)}, u32[]{:S(2)}) copy-start(bf16[3456,256]{1,0:T(8,128)(2,1)} %refs_3_.3) | copy-start | bytes 5308420
  0.7 10.7 %copy-start.2 = (bf16[1,1,16,16,256]{4,3,2,1,0:T(8,128)(2,1)S(1)}, bf16[1,1,16,16,256]{4,3,2,1,0:T(8,128)(2,1)}, u32[]{:S(2)}) copy-start(bf16[1,1,16,16,256]{4,3,2,1,0:T(8,128)(2,1)} %param.12) | copy-start | bytes 393220
  0.7 10.7 %copy-start.3 = (bf16[1,1,16,16,128]{4,3,2,1,0:T(8,128)(2,1)S(1)}, bf16[1,1,16,16,128]{4,3,2,1,0:T(8,128)(2,1)}, u32[]{:S(2)}) copy-start(bf16[1,1,16,16,128]{4,3,2,1,0:T(8,128)(2,1)} %param.9) | copy-start | bytes 196612
  0.7 10.7 %copy-start.5 = (f32[256]{0:T(256)S(1)}, f32[256]{0:T(256)}, u32[]{:S(2)}) copy-start(f32[256]{0:T(256)} %param.11) | copy-start | bytes 3076
  0.7 10.0 %collective-permute-start.1 = (bf16[256,128]{1,0:T(8,128)(2,1)}, bf16[256,128]{1,0:T(8,128)(2,1)S(1)}, u32[]{:S(2)}, u32[]{:S(2)}) collective-permute-start(bf16[256,128]{1,0:T(8,128)(2,1)} %bitcast.10), channel_id=1, source_target_pairs={{1,2},{3,4},{5,6},{7,8},{9,10},{11,12},{13,14},{15,16},{17,18},{19... | collective-permute-start | bytes 196616 | tf_op jit(solution)/shard_map/ppermute | solution.py:343
  5.3 6.0 %collective-permute-start = (bf16[256,128]{1,0:T(8,128)(2,1)}, bf16[256,128]{1,0:T(8,128)(2,1)S(1)}, u32[]{:S(2)}, u32[]{:S(2)}) collective-permute-start(bf16[256,128]{1,0:T(8,128)(2,1)} %bitcast.11), channel_id=1, source_target_pairs={{0,1},{1,0},{2,3},{3,2},{4,5},{5,4},{6,7},{7,6},{8,9},{9,8},{10,11... | collective-permute-start | bytes 196616 | tf_op jit(solution)/shard_map/ppermute | solution.py:341
  13.1 16.0 %all-to-all-start = ((bf16[8,384,128]{2,1,0:T(8,128)(2,1)}), bf16[8,384,128]{2,1,0:T(8,128)(2,1)S(1)}, u32[]{:S(2)}, u32[]{:S(2)}) async-start(bf16[8,384,128]{2,1,0:T(8,128)(2,1)} %get-tuple-element.17), calls=%async_computation | async-start | bytes 1572864 | tf_op jit(solution)/shard_map/all_to_all | solution.py:57
  17.0 58.5 %copy-start.8 = (s32[8]{0:T(128)S(1)}, s32[8]{0:T(128)}, u32[]{:S(2)}) copy-start(s32[8]{0:T(128)} %refs_0_.1) | copy-start | bytes 100
  17.0 6.6 %collective-permute-start.4 = (bf16[2,64,128]{2,1,0:T(8,128)(2,1)S(1)}, bf16[2,64,128]{2,1,0:T(8,128)(2,1)S(1)}, u32[]{:S(2)}, u32[]{:S(2)}) collective-permute-start(bf16[2,64,128]{2,1,0:T(8,128)(2,1)S(1)} %get-tuple-element.18), channel_id=1, source_target_pairs={{0,16},{8,144},{16,272},{24,400},{128,24},{136,152},{144,280},{152... | collective-permute-start | bytes 98312 | tf_op jit(solution)/shard_map/ppermute | solution.py:348
  20.5 3.0 %collective-permute-start.5 = (bf16[2,64,128]{2,1,0:T(8,128)(2,1)S(1)}, bf16[2,64,128]{2,1,0:T(8,128)(2,1)S(1)}, u32[]{:S(2)}, u32[]{:S(2)}) collective-permute-start(bf16[2,64,128]{2,1,0:T(8,128)(2,1)S(1)} %get-tuple-element.19), channel_id=1, source_target_pairs={{0,0},{8,128},{16,256},{24,384},{128,8},{136,136},{144,264},{152,3... | collective-permute-start | bytes 98312 | tf_op jit(solution)/shard_map/ppermute | solution.py:348
  31.3 17.5 %all-to-all-start.1 = ((bf16[16,56,128]{2,1,0:T(8,128)(2,1)}), bf16[16,56,128]{2,1,0:T(8,128)(2,1)S(1)}, u32[]{:S(2)}, u32[]{:S(2)}) async-start(bf16[16,56,128]{2,1,0:T(8,128)(2,1)} %get-tuple-element.20), calls=%async_computation.1 | async-start | bytes 458752 | tf_op jit(solution)/shard_map/all_to_all | solution.py:57
  39.3 6.4 %collective-permute-start.6 = (bf16[2,64,128]{2,1,0:T(8,128)(2,1)S(1)}, bf16[2,64,128]{2,1,0:T(8,128)(2,1)S(1)}, u32[]{:S(2)}, u32[]{:S(2)}) collective-permute-start(bf16[2,64,128]{2,1,0:T(8,128)(2,1)S(1)} %get-tuple-element.21), channel_id=1, source_target_pairs={{0,8},{8,0},{16,24},{24,16},{1,9},{9,1},{17,25},{25,17},{2,10},{10... | collective-permute-start | bytes 98312 | tf_op jit(solution)/shard_map/ppermute | solution.py:352
  49.5 26.0 %all-to-all-start.2 = ((bf16[4,272,128]{2,1,0:T(8,128)(2,1)}), bf16[4,272,128]{2,1,0:T(8,128)(2,1)S(1)}, u32[]{:S(2)}, u32[]{:S(2)}) async-start(bf16[4,272,128]{2,1,0:T(8,128)(2,1)} %shard_map.108), calls=%async_computation.2 | async-start | bytes 557056 | tf_op jit(solution)/shard_map/all_to_all | solution.py:57
  61.6 7.3 %collective-permute-start.3 = (bf16[256,256]{1,0:T(8,128)(2,1)S(1)}, bf16[256,256]{1,0:T(8,128)(2,1)S(1)}, u32[]{:S(2)}, u32[]{:S(2)}) collective-permute-start(bf16[256,256]{1,0:T(8,128)(2,1)S(1)} %get-tuple-element.16.refs_2_), channel_id=1, source_target_pairs={{1,2},{3,4},{5,6},{7,8},{9,10},{11,12},{13,14},{15,16},{17,18},{19... | collective-permute-start | bytes 393224 | tf_op jit(solution)/shard_map/ppermute | solution.py:343
  66.3 3.2 %collective-permute-start.2 = (bf16[256,256]{1,0:T(8,128)(2,1)S(1)}, bf16[256,256]{1,0:T(8,128)(2,1)S(1)}, u32[]{:S(2)}, u32[]{:S(2)}) collective-permute-start(bf16[256,256]{1,0:T(8,128)(2,1)S(1)} %get-tuple-element.16.refs_2_), channel_id=1, source_target_pairs={{0,1},{1,0},{2,3},{3,2},{4,5},{5,4},{6,7},{7,6},{8,9},{9,8},{10,11... | collective-permute-start | bytes 393224 | tf_op jit(solution)/shard_map/ppermute | solution.py:341
  76.9 20.2 %all-to-all-start.3 = ((bf16[32,56,128]{2,1,0:T(8,128)(2,1)}), bf16[32,56,128]{2,1,0:T(8,128)(2,1)S(1)}, u32[]{:S(2)}, u32[]{:S(2)}) async-start(bf16[32,56,128]{2,1,0:T(8,128)(2,1)} %get-tuple-element.22), calls=%async_computation.3 | async-start | bytes 917504 | tf_op jit(solution)/shard_map/all_to_all | solution.py:57
  86.5 7.2 %collective-permute-start.7 = (bf16[2,128,128]{2,1,0:T(8,128)(2,1)S(1)}, bf16[2,128,128]{2,1,0:T(8,128)(2,1)S(1)}, u32[]{:S(2)}, u32[]{:S(2)}) collective-permute-start(bf16[2,128,128]{2,1,0:T(8,128)(2,1)S(1)} %get-tuple-element.25), channel_id=1, source_target_pairs={{0,16},{8,24},{16,0},{24,8},{1,17},{9,25},{17,1},{25,9},{2,18},{10... | collective-permute-start | bytes 196616 | tf_op jit(solution)/shard_map/ppermute | solution.py:352
  97.1 13.7 %copy-start.1 = (f32[256,256]{1,0:T(8,128)S(1)}, f32[256,256]{1,0:T(8,128)}, u32[]{:S(2)}) copy-start(f32[256,256]{1,0:T(8,128)} %refs_4_.1) | copy-start | bytes 786436
  97.1 13.7 %copy-start.6 = (f32[256]{0:T(256)S(1)}, f32[256]{0:T(256)}, u32[]{:S(2)}) copy-start(f32[256]{0:T(256)} %param.17) | copy-start | bytes 3076
  98.1 12.6 %all-to-all-start.4 = ((bf16[4,224,128]{2,1,0:T(8,128)(2,1)}), bf16[4,224,128]{2,1,0:T(8,128)(2,1)S(1)}, u32[]{:S(2)}, u32[]{:S(2)}) async-start(bf16[4,224,128]{2,1,0:T(8,128)(2,1)} %get-tuple-element.28), calls=%async_computation.4 | async-start | bytes 458752 | tf_op jit(solution)/shard_map/all_to_all | solution.py:57
  102.5 8.3 %collective-permute-start.8 = (bf16[2,128,128]{2,1,0:T(8,128)(2,1)S(1)}, bf16[2,128,128]{2,1,0:T(8,128)(2,1)S(1)}, u32[]{:S(2)}, u32[]{:S(2)}) collective-permute-start(bf16[2,128,128]{2,1,0:T(8,128)(2,1)S(1)} %get-tuple-element.26.refs_4_), channel_id=1, source_target_pairs={{0,8},{8,0},{16,24},{24,16},{1,9},{9,1},{17,25},{25,17},{2,10},{10... | collective-permute-start | bytes 196616 | tf_op jit(solution)/shard_map/ppermute | solution.py:352
